TPU v7x, 32 devices: a whole 2x2x4 slice. The times are simulated.
32 devices in a mesh: seq: 8 (over z, y), stream: 4 (over x, core).
Axes of the slice: x: 2, y: 2, z: 4, core: 2. Of those that a mesh axis runs over, the one named last changes fastest.
Arguments:
- resid_in: bfloat16 [4, 4096, 2048], P('stream', 'seq'), may hold values from -6 to 6
- out_grad: bfloat16 [4, 4096, 2048], P('stream', 'seq'), may hold values from -6 to 6
- row_lengths: int32 [4, 16], P('stream'), may hold values from 0 to 4096, as said below
- norm_gain: bfloat16 [2048], P(('seq', 'stream')), may hold values from 0.099609375 to 1.8984375
- in_weight: bfloat16 [2048, 8192], P(('seq', 'stream')), may hold values from -0.125 to 0.125
- conv_weight: bfloat16 [4, 4096], P(None, ('seq', 'stream')), may hold values from -3 to 3
- conv_bias: bfloat16 [4096], P(('seq', 'stream')), may hold values from -3 to 3
- xproj_weight: bfloat16 [4096, 160], P(('seq', 'stream')), may hold values from -0.09375 to 0.09375
- dt_weight: bfloat16 [128, 4096], P(None, ('seq', 'stream')), may hold values from -0.5 to 0.5
- dt_bias: bfloat16 [4096], P(('seq', 'stream')), may hold values from -4.59375 to -3.390625
- a_log: bfloat16 [4096, 16], P(('seq', 'stream')), may hold values from -12 to 1
- skip_gain: bfloat16 [4096], P(('seq', 'stream')), may hold values from 0.5 to 1.5
- out_weight: bfloat16 [4096, 2048], P(('seq', 'stream')), may hold values from -0.09375 to 0.09375
Outputs:
- output: bfloat16 [4, 4096, 2048], P('stream', 'seq')
- in_grad: bfloat16 [4, 4096, 2048], P('stream', 'seq')
- grad_norm_gain: float32 [2048], P(('seq', 'stream'))
- grad_in_weight: float32 [2048, 8192], P(('seq', 'stream'))
- grad_conv_weight: float32 [4, 4096], P(None, ('seq', 'stream'))
- grad_conv_bias: float32 [4096], P(('seq', 'stream'))
- grad_xproj_weight: float32 [4096, 160], P(('seq', 'stream'))
- grad_dt_weight: float32 [128, 4096], P(None, ('seq', 'stream'))
- grad_dt_bias: float32 [4096], P(('seq', 'stream'))
- grad_a_log: float32 [4096, 16], P(('seq', 'stream'))
- grad_skip_gain: float32 [4096], P(('seq', 'stream'))
- grad_out_weight: float32 [4096, 2048], P(('seq', 'stream'))
Inputs may be any that keep to these rules, and one draw needn't show every extreme that they name: `row_lengths`: slots hold the documents in order from position 0; unused slots at the end are 0; after the documents fewer than 256 padding positions remain; in one stream a single document fills all 4096 positions.
All inputs are finite; a program needn't handle non-finite values.
Results may differ from a plain program's by a relative error of at most 0.012.
Values may be sent and summed in bfloat16 or wider, within the bound.
A program may use at most 512 MiB of HBM per device.

v0:
```python
import jax
import jax.numpy as jnp
from jax import lax
from jax.sharding import PartitionSpec as P

CONV = 4


EPSILON = 1e-05
HIGHEST = lax.Precision.HIGHEST


def passed_along(block, axis, distance):
    devices = range(lax.axis_size(axis))
    route = [(i - distance, i) for i in devices if i - distance in devices]
    return lax.ppermute(block, axis, route)


def prefix(array, axis, join, neutral, backward):
    count = lax.axis_size(axis)
    place = lax.axis_index(axis)
    ahead = count - 1 - place if backward else place
    gathered = jax.tree.map(
        lambda a, kind: lax.all_gather(a.astype(kind), axis), array, (jnp.bfloat16, jnp.bfloat16)
    )
    state = jax.tree.map(lambda a, e: jnp.zeros_like(a) + jnp.asarray(e, a.dtype), array, neutral)

    def one(step, state):
        source = count - 1 - step if backward else step
        return join(
            state,
            jax.tree.map(
                lambda a, own: lax.dynamic_index_in_dim(a, source, 0, False).astype(own.dtype),
                gathered,
                array,
            ),
        )

    return lax.fori_loop(0, ahead, one, state)


def as_sent(array):
    return jax.tree.map(lambda a: a.astype(jnp.bfloat16) if a.dtype == jnp.float32 else a, array)


def silu_slope(values_in):
    sigmoid_v = jax.nn.sigmoid(values_in)
    return sigmoid_v * (1.0 + values_in * (1.0 - sigmoid_v))


def norm_rows(residual, norm_scale):
    inv_rms = lax.rsqrt(jnp.mean(residual * residual, axis=-1, keepdims=True) + EPSILON)
    return residual * inv_rms * norm_scale[None, :]


def token_layout(lengths, first_pos, n_tokens):
    doc_ends = jnp.cumsum(lengths)
    begins = doc_ends - lengths
    positions = first_pos + jnp.arange(n_tokens, dtype=jnp.int32)
    live_slot = (lengths > 0)[None, :]
    doc_ids = jnp.sum(
        ((begins[None, :] <= positions[:, None]) & live_slot).astype(jnp.int32), axis=1
    )
    start_flags = jnp.sum(
        ((begins[None, :] == positions[:, None]) & live_slot).astype(jnp.float32), axis=1
    )
    valid_mask = (positions < doc_ends[-1]).astype(jnp.float32)
    return (doc_ids, start_flags, valid_mask)


def contract_rows(left_mat, right_mat):
    return lax.dot_general(
        left_mat, right_mat, (((0,), (0,)), ((), ())), preferred_element_type=jnp.float32
    )


def contract_cols(left_mat, right_mat):
    return lax.dot_general(
        left_mat, right_mat, (((1,), (1,)), ((), ())), preferred_element_type=jnp.float32
    )


def block_states(decay_rates, state_now, pieces):
    dt_step, act_in, kept_mask, write_in, readout = pieces
    results = []
    for token_at in range(dt_step.shape[0]):
        decay_now = jnp.exp(dt_step[token_at][:, None] * decay_rates) * kept_mask[token_at]
        state_now = (
            decay_now * state_now
            + (dt_step[token_at] * act_in[token_at])[:, None] * write_in[token_at][None, :]
        )
        results.append(jnp.sum(state_now * readout[token_at][None, :], axis=1))
    return (state_now, jnp.stack(results))


def group_scan(dt_step, act_in, write_in, readout, log_rates, kept_mask, start_state, block_len):
    n_tokens, inner_dim = dt_step.shape
    blocks = n_tokens // block_len
    decay_rates = -jnp.exp(log_rates)
    walk_block = jax.checkpoint(block_states)

    def run_block(state_now, piece):
        return walk_block(decay_rates, state_now, piece)

    pieces = (
        dt_step.reshape(blocks, block_len, inner_dim),
        act_in.reshape(blocks, block_len, inner_dim),
        kept_mask.reshape(blocks, block_len),
        write_in.reshape(blocks, block_len, -1),
        readout.reshape(blocks, block_len, -1),
    )
    final_state, results = lax.scan(run_block, start_state, pieces)
    return (results.reshape(n_tokens, inner_dim), final_state)


def carry_rows(dt_step, readout, log_rates, carry_state, alive_mask, block_len):
    n_tokens, inner_dim = dt_step.shape
    blocks = n_tokens // block_len
    decay_rates = -jnp.exp(log_rates)
    lower_tri = (jnp.arange(block_len)[:, None] >= jnp.arange(block_len)[None, :]).astype(
        jnp.float32
    )

    def one_block(offset, pieces):
        block_step, block_read, block_alive = pieces
        partial_sums = offset[None, :] + jnp.dot(lower_tri, block_step, precision=HIGHEST)
        decay_now = (
            jnp.exp(partial_sums[:, :, None] * decay_rates[None]) * block_alive[:, None, None]
        )
        rows = jnp.einsum("tdn,dn,tn->td", decay_now, carry_state, block_read, precision=HIGHEST)
        return (partial_sums[block_len - 1], rows)

    walk_block = jax.checkpoint(one_block)
    pieces = (
        dt_step.reshape(blocks, block_len, inner_dim),
        readout.reshape(blocks, block_len, -1),
        alive_mask.reshape(blocks, block_len),
    )
    offset, rows = lax.scan(walk_block, jnp.zeros((inner_dim,), jnp.float32), pieces)
    end_extra = jnp.exp(decay_rates * offset[:, None]) * alive_mask[n_tokens - 1] * carry_state
    return (rows.reshape(n_tokens, inner_dim), end_extra)


def carry_weights(dt_step, d_ssm, readout, alive_mask, decay_rates, block_len):
    n_tokens, inner_dim = dt_step.shape
    blocks = n_tokens // block_len
    lower_tri = (jnp.arange(block_len)[:, None] >= jnp.arange(block_len)[None, :]).astype(
        jnp.float32
    )

    def visit_block(carry, pieces):
        running, offset = carry
        block_step, block_grad, block_read, block_alive = pieces
        partial_sums = offset[None, :] + jnp.dot(lower_tri, block_step, precision=HIGHEST)
        decay_now = (
            jnp.exp(partial_sums[:, :, None] * decay_rates[None]) * block_alive[:, None, None]
        )
        running = running + jnp.einsum(
            "tdn,td,tn->dn", decay_now, block_grad, block_read, precision=HIGHEST
        )
        return ((running, partial_sums[block_len - 1]), None)

    start_carry = (
        jnp.zeros((inner_dim, decay_rates.shape[1]), jnp.float32),
        jnp.zeros((inner_dim,), jnp.float32),
    )
    pieces = (
        dt_step.reshape(blocks, block_len, inner_dim),
        d_ssm.reshape(blocks, block_len, inner_dim),
        readout.reshape(blocks, block_len, -1),
        alive_mask.reshape(blocks, block_len),
    )
    (running, offset), unused = lax.scan(visit_block, start_carry, pieces)
    return running


def join_forward(earlier, later):
    return (earlier[0] * later[0], later[0] * earlier[1] + later[1])


def join_backward(earlier, later):
    return (earlier[0] * later[0], later[1] + later[0] * earlier[1])


def local(
    resid_in,
    out_grad,
    row_lengths,
    norm_gain,
    in_weight,
    conv_weight,
    conv_bias,
    xproj_weight,
    dt_weight,
    dt_bias,
    a_log,
    skip_gain,
    out_weight,
):
    gathered = (
        lax.all_gather(norm_gain, ("seq", "stream"), axis=0, tiled=True),
        lax.all_gather(in_weight, ("seq", "stream"), axis=0, tiled=True),
        lax.all_gather(conv_weight, ("seq", "stream"), axis=1, tiled=True),
        lax.all_gather(conv_bias, ("seq", "stream"), axis=0, tiled=True),
        lax.all_gather(xproj_weight, ("seq", "stream"), axis=0, tiled=True),
        lax.all_gather(dt_weight, ("seq", "stream"), axis=1, tiled=True),
        lax.all_gather(dt_bias, ("seq", "stream"), axis=0, tiled=True),
        lax.all_gather(a_log, ("seq", "stream"), axis=0, tiled=True),
        lax.all_gather(skip_gain, ("seq", "stream"), axis=0, tiled=True),
        lax.all_gather(out_weight, ("seq", "stream"), axis=0, tiled=True),
    )
    (
        gain_full,
        in_full,
        conv_full,
        cbias_full,
        xproj_full,
        dtw_full,
        dbias_full,
        alog_full,
        skip_full,
        out_full,
    ) = gathered
    norm_scale = gain_full.astype(jnp.float32)
    conv_taps = conv_full.astype(jnp.float32)
    conv_shift = cbias_full.astype(jnp.float32)
    dt_shift = dbias_full.astype(jnp.float32)
    log_rates = alog_full.astype(jnp.float32)
    skip_vec = skip_full.astype(jnp.float32)
    residual = resid_in[0].astype(jnp.float32)
    n_tokens = residual.shape[0]
    block_len = min(32, n_tokens)
    inner_dim = dtw_full.shape[1]
    rank_dim = dtw_full.shape[0]
    state_dim = alog_full.shape[1]
    rim_width = CONV - 1
    first_pos = lax.axis_index("seq") * n_tokens
    doc_ids, start_flags, valid_mask = token_layout(
        row_lengths[0], first_pos - rim_width, n_tokens + 2 * rim_width
    )
    own_ids = doc_ids[rim_width : rim_width + n_tokens]
    kept_mask = 1.0 - start_flags[rim_width : rim_width + n_tokens]
    valid_mask = valid_mask[rim_width : rim_width + n_tokens]
    alive_mask = (own_ids == doc_ids[rim_width - 1]).astype(jnp.float32)
    normed_f, norm_pull = jax.vjp(norm_rows, residual, norm_scale)
    normed_in = normed_f.astype(jnp.bfloat16)
    mixed_in = jnp.dot(normed_in, in_full, preferred_element_type=jnp.float32)
    conv_in = mixed_in[:, :inner_dim]
    gate_in = mixed_in[:, inner_dim:]
    earlier_rows = passed_along(
        conv_in[n_tokens - rim_width :].astype(jnp.bfloat16), "seq", 1
    ).astype(jnp.float32)
    padded_in = jnp.concatenate([earlier_rows, conv_in], axis=0)
    matches = [
        (doc_ids[tap_index : tap_index + n_tokens] == own_ids).astype(jnp.float32)[:, None]
        for tap_index in range(CONV)
    ]
    conv_out = conv_shift[None, :]
    for tap_index in range(CONV):
        conv_out = (
            conv_out
            + conv_taps[tap_index][None, :]
            * padded_in[tap_index : tap_index + n_tokens]
            * matches[tap_index]
        )
    activated = jax.nn.silu(conv_out).astype(jnp.bfloat16)
    act_float = activated.astype(jnp.float32)
    projected = jnp.dot(activated, xproj_full, preferred_element_type=jnp.float32)
    low_rank = projected[:, :rank_dim].astype(jnp.bfloat16)
    write_in = projected[:, rank_dim : rank_dim + state_dim]
    readout = projected[:, rank_dim + state_dim :]
    dt_pre = jnp.dot(low_rank, dtw_full, preferred_element_type=jnp.float32) + dt_shift[None, :]
    dt_step = jax.nn.softplus(dt_pre)
    decay_rates = -jnp.exp(log_rates)
    zero_state = jnp.zeros((inner_dim, state_dim), jnp.float32)

    def local_part(step_in, act_in, write_vec, read_vec, log_in):
        return group_scan(
            step_in, act_in, write_vec, read_vec, log_in, kept_mask, zero_state, block_len
        )

    (local_rows, local_end), scan_pull = jax.vjp(
        local_part, dt_step, act_float, write_in, readout, log_rates
    )
    through_decay = (
        jnp.exp(decay_rates * jnp.sum(dt_step, axis=0)[:, None]) * alive_mask[n_tokens - 1]
    )
    carry_in = prefix(
        (through_decay, local_end),
        "seq",
        join_forward,
        (jnp.ones_like(through_decay), jnp.zeros_like(local_end)),
        False,
    )
    carry_state = carry_in[1]

    def carried_part(step_in, read_vec, log_in):
        return carry_rows(step_in, read_vec, log_in, carry_state, alive_mask, block_len)

    (extra_rows, end_extra), carry_pull = jax.vjp(carried_part, dt_step, readout, log_rates)
    scanned = local_rows + extra_rows
    ssm_out = scanned + skip_vec[None, :] * act_float
    gate_act = jax.nn.silu(gate_in)
    gated = (ssm_out * gate_act * valid_mask[:, None]).astype(jnp.bfloat16)
    output = (residual + jnp.dot(gated, out_full, preferred_element_type=jnp.float32)).astype(
        jnp.bfloat16
    )
    cotangent = out_grad[0]
    d_gated = contract_cols(cotangent, out_full)
    g_out = contract_rows(gated, cotangent)
    d_masked = d_gated * valid_mask[:, None]
    d_ssm = d_masked * gate_act
    d_gate = d_masked * ssm_out * silu_slope(gate_in)
    g_skip = jnp.sum(d_ssm * act_float, axis=0)
    local_pull = carry_weights(dt_step, d_ssm, readout, alive_mask, decay_rates, block_len)
    later_sum = prefix(
        (through_decay, local_pull),
        "seq",
        join_backward,
        (jnp.ones_like(through_decay), jnp.zeros_like(local_pull)),
        True,
    )
    d_step_a, d_scan_act, d_write, d_read_a, g_log_a = scan_pull((d_ssm, later_sum[1]))
    d_step_b, d_read_b, g_log_b = carry_pull((d_ssm, later_sum[1]))
    d_step = d_step_a + d_step_b
    d_read = d_read_a + d_read_b
    g_log = g_log_a + g_log_b
    d_pre = d_step * jax.nn.sigmoid(dt_pre)
    g_dt_bias = jnp.sum(d_pre, axis=0)
    d_pre_low = d_pre.astype(jnp.bfloat16)
    g_dt = contract_rows(low_rank, d_pre_low)
    d_low = contract_cols(d_pre_low, dtw_full)
    d_proj = jnp.concatenate([d_low, d_write, d_read], axis=1).astype(jnp.bfloat16)
    g_xproj = contract_rows(activated, d_proj)
    d_act = d_scan_act + skip_vec[None, :] * d_ssm + contract_cols(d_proj, xproj_full)
    d_conv = d_act * silu_slope(conv_out)
    g_conv_bias = jnp.sum(d_conv, axis=0)
    g_conv = jnp.stack(
        [
            jnp.sum(
                d_conv * padded_in[tap_index : tap_index + n_tokens] * matches[tap_index], axis=0
            )
            for tap_index in range(CONV)
        ]
    )
    later_rows = passed_along(as_sent(d_conv[:rim_width]), "seq", -1)
    d_ext = jnp.concatenate([d_conv, later_rows], axis=0)
    d_conv_in = jnp.zeros_like(d_conv)
    for tap_index in range(CONV):
        offset = rim_width - tap_index
        match_back = (
            doc_ids[rim_width + offset : rim_width + offset + n_tokens] == own_ids
        ).astype(jnp.float32)[:, None]
        d_conv_in = (
            d_conv_in
            + conv_taps[tap_index][None, :] * d_ext[offset : offset + n_tokens] * match_back
        )
    d_mixed = jnp.concatenate([d_conv_in, d_gate], axis=1).astype(jnp.bfloat16)
    g_in = contract_rows(normed_in, d_mixed)
    d_normed = contract_cols(d_mixed, in_full)
    d_resid, g_gain = norm_pull(d_normed)
    in_grad = (d_resid + cotangent.astype(jnp.float32)).astype(jnp.bfloat16)
    grad_sums = tuple(
        (
            lax.psum_scatter(g_gain, ("seq", "stream"), scatter_dimension=0, tiled=True),
            lax.psum_scatter(g_in, ("seq", "stream"), scatter_dimension=0, tiled=True),
            lax.psum_scatter(g_conv, ("seq", "stream"), scatter_dimension=1, tiled=True),
            lax.psum_scatter(g_conv_bias, ("seq", "stream"), scatter_dimension=0, tiled=True),
            lax.psum_scatter(g_xproj, ("seq", "stream"), scatter_dimension=0, tiled=True),
            lax.psum_scatter(g_dt, ("seq", "stream"), scatter_dimension=1, tiled=True),
            lax.psum_scatter(g_dt_bias, ("seq", "stream"), scatter_dimension=0, tiled=True),
            lax.psum_scatter(g_log, ("seq", "stream"), scatter_dimension=0, tiled=True),
            lax.psum_scatter(g_skip, ("seq", "stream"), scatter_dimension=0, tiled=True),
            lax.psum_scatter(g_out, ("seq", "stream"), scatter_dimension=0, tiled=True),
        )
    )
    return (
        output[None],
        in_grad[None],
        grad_sums[0],
        grad_sums[1],
        grad_sums[2],
        grad_sums[3],
        grad_sums[4],
        grad_sums[5],
        grad_sums[6],
        grad_sums[7],
        grad_sums[8],
        grad_sums[9],
    )


def solution(mesh):
    in_specs = (
        P("stream", "seq", None),
        P("stream", "seq", None),
        P("stream", None),
        P(("seq", "stream")),
        P(("seq", "stream"), None),
        P(None, ("seq", "stream")),
        P(("seq", "stream")),
        P(("seq", "stream"), None),
        P(None, ("seq", "stream")),
        P(("seq", "stream")),
        P(("seq", "stream"), None),
        P(("seq", "stream")),
        P(("seq", "stream"), None),
    )
    out_specs = (
        P("stream", "seq", None),
        P("stream", "seq", None),
        P(("seq", "stream")),
        P(("seq", "stream"), None),
        P(None, ("seq", "stream")),
        P(("seq", "stream")),
        P(("seq", "stream"), None),
        P(None, ("seq", "stream")),
        P(("seq", "stream")),
        P(("seq", "stream"), None),
        P(("seq", "stream")),
        P(("seq", "stream"), None),
    )
    return jax.shard_map(local, mesh=mesh, in_specs=in_specs, out_specs=out_specs, check_vma=False)
```

profile of v0, /device:TPU:19, one launch (start us, length us, event | category | flops | bytes accessed | tf_op | source)
XLA Modules:
  0.0 6041.4 jit_solution(7286162727672869815)
XLA Ops:
  13.8 40.7 all-reduce.161
  59.5 32.8 all_gather.51
  92.5 115.2 %all-gather.14.cloned.1.call-done = bf16[2048,8192]{1,0:T(8,128)(2,1)} async-done(((bf16[64,8192]{1,0:T(8,128)(2,1)}), bf16[2048,8192]{1,0:T(8,128)(2,1)}) %all-gather.14.cloned.1.call-update) | async-done | bytes 33554448 | tf_op jit(solution)/shard_map/all_gather | solution.py:202
  207.8 27.4 fusion.151
  238.4 32.1 all_gather.57
  270.5 33.2 all-gather.3
  303.7 37.8 all-gather.5
  342.1 37.2 all-gather.4
  388.6 38.5 multiply_reduce_fusion.163
  455.0 918.4 %while.118 = (s32[]{:T(128)}, f32[4096,16]{0,1:T(8,128)S(1)}, f32[16,32,4096]{2,1,0:T(8,128)}, f32[16,4096,16]{1,2,0:T(8,128)}, f32[16,32,4096]{2,1,0:T(8,128)},...) while((s32[]{:T(128)}, f32[4096,16]{0,1:T(8,128)S(1)}, ...), condition=%wide.region_37.38_spmd.clone, body=%wide.region_4.37_spmd.clone.sunk | while | flops 22413344 | bytes 16498033 | solution.py:112
  1374.6 148.1 %while.119 = (s32[]{:T(128)}, f32[4096,16]{1,0:T(8,128)}, f32[4096]{0:T(1024)S(1)}, f32[16,32,4096]{2,1,0:T(8,128)}, f32[4096,16]{0,1:T(8,128)S(1)}, /*index=5*/...) while((s32[]{:T(128)}, f32[4096,16]{1,0:T(8,128)}, ...), condition=%wide.region_44.45_spmd.clone, body=%wide.region_43.44_spmd.clone.sunk | while | flops 61016064 | bytes 5036551 | solution.py:173
  1532.9 174.7 %while.117 = (s32[]{:T(128)}, f32[4096]{0:T(1024)S(1)}, f32[16,32,4096]{2,1,0:T(8,128)}, f32[16,4096]{1,0:T(8,128)}, f32[16,32,4096]{2,1,0:T(8,128)}, /*index=5*...) while((s32[]{:T(128)}, f32[4096]{0:T(1024)S(1)}, ...), condition=%wide.region_42.43_spmd.clone, body=%wide.region_41.42_spmd.clone.sunk | while | flops 81922048 | bytes 3758601 | solution.py:139
  1724.6 2280.4 %while.120 = (s32[]{:T(128)}, f32[4096,16]{0,1:T(8,128)}, f32[4096,16]{0,1:T(8,128)S(1)}, f32[16,32,4096]{2,1,0:T(8,128)}, f32[16,32,4096]{2,1,0:T(8,128)}, /*in...) while((s32[]{:T(128)}, f32[4096,16]{0,1:T(8,128)}, ...), condition=%wide.region_176.177_spmd.clone, body=%wide.region_47.176_spmd.clone.sunk | while | flops 101283840 | bytes 59315640 | solution.py:112
  1804.2 25.0 select_add_fusion.4
  1946.1 25.0 select_add_fusion.4
  2088.1 25.0 select_add_fusion.4
  2230.0 25.0 select_add_fusion.4
  2372.0 25.0 select_add_fusion.4
  2513.9 25.0 select_add_fusion.4
  2655.9 25.0 select_add_fusion.4
  2797.8 25.0 select_add_fusion.4
  2939.8 25.0 select_add_fusion.4
  4010.4 331.7 %while.121 = (s32[]{:T(128)}, f32[4096,16]{0,1:T(8,128)S(1)}, f32[4096]{0:T(1024)S(1)}, f32[16,32,4096]{2,1,0:T(8,128)}, f32[16,32,16]{1,2,0:T(8,128)S(1)}, /*in...) while((s32[]{:T(128)}, f32[4096,16]{0,1:T(8,128)S(1)}, ...), condition=%wide.region_182.183_spmd.clone, body=%wide.region_178.182_spmd.clone.sunk | while | flops 151451648 | bytes 9614019 | solution.py:139
  4376.0 36.8 fusion.169
  4472.3 29.4 fusion.126
  4516.6 25.7 fusion.131
  4542.3 48.8 all-reduce.166
  4600.3 62.8 %reduce-scatter.15.cloned.1.call-done = f32[128,16]{0,1:T(8,128)} async-done(((f32[4096,16]{0,1:T(8,128)}), f32[128,16]{0,1:T(8,128)}) %reduce-scatter.15.cloned.1.call-update) | async-done | bytes 8208 | tf_op jit(solution)/shard_map/reduce_scatter | solution.py:372
  4663.1 134.6 %reduce-scatter.13.cloned.1.call-done = f32[128,128]{1,0:T(8,128)} async-done(((f32[128,4096]{1,0:T(8,128)}), f32[128,128]{1,0:T(8,128)}) %reduce-scatter.13.cloned.1.call-update) | async-done | bytes 65552 | tf_op jit(solution)/shard_map/reduce_scatter | solution.py:370
  4797.7 136.5 %reduce-scatter.11.cloned.1.call-done = f32[128,160]{0,1:T(8,128)} async-done(((f32[4096,160]{0,1:T(8,128)}), f32[128,160]{0,1:T(8,128)}) %reduce-scatter.11.cloned.1.call-update) | async-done | bytes 81936 | tf_op jit(solution)/shard_map/reduce_scatter | solution.py:369
  4934.2 387.1 %reduce-scatter.17.cloned.1.call-done = f32[128,2048]{1,0:T(8,128)} async-done(((f32[4096,2048]{1,0:T(8,128)}), f32[128,2048]{1,0:T(8,128)}) %reduce-scatter.17.cloned.1.call-update) | async-done | bytes 1048592 | tf_op jit(solution)/shard_map/reduce_scatter | solution.py:374
  5321.3 713.3 %reduce-scatter.9.cloned.1.call-done = f32[64,8192]{1,0:T(8,128)} async-done(((f32[2048,8192]{1,0:T(8,128)}), f32[64,8192]{1,0:T(8,128)}) %reduce-scatter.9.cloned.1.call-update) | async-done | bytes 2097168 | tf_op jit(solution)/shard_map/reduce_scatter | solution.py:366
  (3144 shorter events, 3805.3 us)
Async XLA Ops:
  7.2 200.6 %all-gather.14.cloned.1.call-start = ((), (), s32[]{:S(2)}) async-start(), calls=%async_computation.6 | async-start | bytes 34603008 | tf_op jit(solution)/shard_map/all_gather | solution.py:202
  7.9 380.6 %all-gather.20.cloned.1.call-start = ((), (), s32[]{:S(2)}) async-start(), calls=%async_computation.9 | async-start | bytes 17301504 | tf_op jit(solution)/shard_map/all_gather | solution.py:210
  8.7 424.9 %all-gather.16.cloned.1.call-start = ((), (), s32[]{:S(2)}) async-start(), calls=%async_computation.7 | async-start | bytes 1351680 | tf_op jit(solution)/shard_map/all_gather | solution.py:205
  9.4 430.2 %all-gather.18.cloned.1.call-start = ((), (), s32[]{:S(2)}) async-start(), calls=%async_computation.8 | async-start | bytes 1081344 | tf_op jit(solution)/shard_map/all_gather | solution.py:206
  10.0 1515.5 %all-gather.22.cloned.1.call-start = ((), (), s32[]{:S(2)}) async-start(), calls=%async_computation.15 | async-start | bytes 1179648 | tf_op jit(solution)/shard_map/all_gather | solution.py:24
  54.5 180.6 %copy-start.10 = (f32[2048]{0:T(1024)}, f32[2048]{0:T(1024)S(1)}, u32[]{:S(2)}) copy-start(f32[2048]{0:T(1024)S(1)} %convert_element_type.151) | copy-start | bytes 24580
  56.9 178.3 %copy-start.13 = (f32[512]{0:T(512)}, f32[512]{0:T(512)S(1)}, u32[]{:S(2)}) copy-start(f32[512]{0:T(512)S(1)} %fusion.163) | copy-start | bytes 6148
  58.8 329.8 %copy-start.45 = (f32[512]{0:T(512)}, f32[512]{0:T(512)S(1)}, u32[]{:S(2)}) copy-start(f32[512]{0:T(512)S(1)} %get-tuple-element.2196) | copy-start | bytes 6148
  58.8 329.8 %copy-start.47 = (f32[512]{0:T(512)}, f32[512]{0:T(512)S(1)}, u32[]{:S(2)}) copy-start(f32[512]{0:T(512)S(1)} %get-tuple-element.2197) | copy-start | bytes 6148
  58.8 329.8 %copy-start.49 = (f32[512]{0:T(512)}, f32[512]{0:T(512)S(1)}, u32[]{:S(2)}) copy-start(f32[512]{0:T(512)S(1)} %get-tuple-element.2200) | copy-start | bytes 6148
  59.5 329.1 %copy-start.43 = (f32[512]{0:T(512)}, f32[512]{0:T(512)S(1)}, u32[]{:S(2)}) copy-start(f32[512]{0:T(512)S(1)} %slice_convert_fusion.5) | copy-start | bytes 6148
  92.4 296.2 %copy-start.25 = (f32[1,4096]{1,0:T(1,128)}, f32[1,4096]{1,0:T(1,128)S(1)}, u32[]{:S(2)}) copy-start(f32[1,4096]{1,0:T(1,128)S(1)} %get-tuple-element.2189) | copy-start | bytes 49156
  92.4 296.2 %copy-start.27 = (f32[1,4096]{1,0:T(1,128)}, f32[1,4096]{1,0:T(1,128)S(1)}, u32[]{:S(2)}) copy-start(f32[1,4096]{1,0:T(1,128)S(1)} %get-tuple-element.2190) | copy-start | bytes 49156
  92.4 296.2 %copy-start.29 = (f32[1,4096]{1,0:T(1,128)}, f32[1,4096]{1,0:T(1,128)S(1)}, u32[]{:S(2)}) copy-start(f32[1,4096]{1,0:T(1,128)S(1)} %get-tuple-element.2191) | copy-start | bytes 49156
  92.4 296.2 %copy-start.31 = (f32[1,4096]{1,0:T(1,128)}, f32[1,4096]{1,0:T(1,128)S(1)}, u32[]{:S(2)}) copy-start(f32[1,4096]{1,0:T(1,128)S(1)} %get-tuple-element.2192) | copy-start | bytes 49156
  92.5 145.8 %copy-start.42 = (bf16[128,16]{0,1:T(8,128)(2,1)S(1)}, bf16[128,16]{0,1:T(8,128)(2,1)}, u32[]{:S(2)}) copy-start(bf16[128,16]{0,1:T(8,128)(2,1)} %param.37) | copy-start | bytes 12292
  92.5 177.9 %copy-start.51 = (bf16[128]{0:T(256)(128)(2,1)S(1)}, bf16[128]{0:T(256)(128)(2,1)}, u32[]{:S(2)}) copy-start(bf16[128]{0:T(256)(128)(2,1)} %param.33) | copy-start | bytes 772
  92.5 211.2 %copy-start.52 = (bf16[128]{0:T(256)(128)(2,1)S(1)}, bf16[128]{0:T(256)(128)(2,1)}, u32[]{:S(2)}) copy-start(bf16[128]{0:T(256)(128)(2,1)} %param.38) | copy-start | bytes 772
  92.5 249.5 %copy-start.53 = (bf16[128]{0:T(256)(128)(2,1)S(1)}, bf16[128]{0:T(256)(128)(2,1)}, u32[]{:S(2)}) copy-start(bf16[128]{0:T(256)(128)(2,1)} %param.36) | copy-start | bytes 772
  236.1 152.4 %collective-permute-start = (bf16[3,4096]{1,0:T(4,128)(2,1)S(1)}, bf16[3,4096]{1,0:T(4,128)(2,1)S(1)}, u32[]{:S(2)}, u32[]{:S(2)}) collective-permute-start(bf16[3,4096]{1,0:T(4,128)(2,1)S(1)} %slice.2849), channel_id=1, source_target_pairs={{0,4},{4,8},{8,12},{12,16},{16,20},{20,24},{24,28},{1,5},{5,9},{9,... | collective-permute-start | bytes 73736 | tf_op jit(solution)/shard_map/ppermute | solution.py:16
  270.5 179.2 %copy-start.8 = (bf16[4096,16]{0,1:T(8,128)(2,1)}, bf16[4096,16]{0,1:T(8,128)(2,1)S(1)}, u32[]{:S(2)}) copy-start(bf16[4096,16]{0,1:T(8,128)(2,1)S(1)} %all_gather.57) | copy-start | bytes 393220
  450.5 1076.4 %all-gather.24.cloned.1.call-start = ((), (), s32[]{:S(2)}) async-start(), calls=%async_computation.16 | async-start | bytes 1179648 | tf_op jit(solution)/shard_map/all_gather | solution.py:24
  1374.0 333.6 %all-gather.26.cloned.1.call-start = ((), (), s32[]{:S(2)}) async-start(), calls=%async_computation.17 | async-start | bytes 9437184 | tf_op jit(solution)/shard_map/all_gather | solution.py:24
  1525.4 3073.4 %reduce-scatter.19.cloned.1.call-start = ((), (), s32[]{:S(2)}) async-start(), calls=%async_computation.18 | async-start | bytes 2162688
  4010.4 331.7 %copy-start.16 = (f32[16,32,16]{1,2,0:T(8,128)S(1)}, f32[16,32,16]{1,2,0:T(8,128)}, u32[]{:S(2)}) copy-start(f32[16,32,16]{1,2,0:T(8,128)} %get-tuple-element.880) | copy-start | bytes 98308
  4010.4 331.9 %copy-start.15 = (bf16[16,32,16]{2,1,0:T(8,128)(2,1)S(1)}, bf16[16,32,16]{2,1,0:T(8,128)(2,1)}, u32[]{:S(2)}) copy-start(bf16[16,32,16]{2,1,0:T(8,128)(2,1)} %get-tuple-element.879) | copy-start | bytes 49156
  4414.9 248.2 %reduce-scatter.15.cloned.1.call-start = ((), (), s32[]{:S(2)}) async-start(), calls=%async_computation.13 | async-start | bytes 270336 | tf_op jit(solution)/shard_map/reduce_scatter | solution.py:372
  4415.9 381.8 %reduce-scatter.13.cloned.1.call-start = ((), (), s32[]{:S(2)}) async-start(), calls=%async_computation.12 | async-start | bytes 2162688 | tf_op jit(solution)/shard_map/reduce_scatter | solution.py:370
  4420.3 513.9 %reduce-scatter.11.cloned.1.call-start = ((), (), s32[]{:S(2)}) async-start(), calls=%async_computation.11 | async-start | bytes 2703360 | tf_op jit(solution)/shard_map/reduce_scatter | solution.py:369
  4424.9 896.4 %reduce-scatter.17.cloned.1.call-start = ((), (), s32[]{:S(2)}) async-start(), calls=%async_computation.14 | async-start | bytes 34603008 | tf_op jit(solution)/shard_map/reduce_scatter | solution.py:374
  4442.9 1591.7 %reduce-scatter.9.cloned.1.call-start = ((), (), s32[]{:S(2)}) async-start(), calls=%async_computation.10 | async-start | bytes 69206016 | tf_op jit(solution)/shard_map/reduce_scatter | solution.py:366
  4444.0 6.9 collective-permute-start.1
  (69 other events, 1880.5 us)
Sparse Core Ops, SparseCore 0:
  10.9 196.8 all-gather.13
  210.6 113.8 all-gather.19
  327.4 48.4 all-gather.15
  378.6 47.9 all-gather.17
  450.6 46.6 all-gather.21
  1374.2 46.6 all-gather.23
  1525.5 132.0 all-gather.25
  4415.0 115.1 reduce-scatter.18
  4533.1 129.9 reduce-scatter.14
  4665.8 131.8 reduce-scatter.12
  4800.6 133.5 reduce-scatter.10
  4937.0 384.2 reduce-scatter.16
  5324.4 710.2 reduce-scatter.8
where the time goes:
time: 6100 us; the launch traced here: 6040 us
  other arithmetic  3030 us (50%)
  waiting for transfers between devices  1550 us (25%)
  local copies, waits for them, and re-layouts  572 us (9%)
  matrix products  568 us (9%)
  blocking collectives  263 us (4%)
    reduce_sum x160, other arithmetic, block_states(): results.append(jnp.sum(state_now * readout[token_at][None, :], axis=1))  1020 us
    reduce_sum x256, other arithmetic, block_states(): dt_step[token_at][:, None] * decay_rates  971 us
    reduce_scatter x1, waiting for transfers between devices, local(): lax.psum_scatter(g_in, ('seq', 'stream'), scatter_dimension=0, tiled=True)  713 us
    add_any x16, other arithmetic, run_block(): return walk_block(decay_rates, state_now, piece)  401 us
    reduce_scatter x1, waiting for transfers between devices, local(): lax.psum_scatter(g_out, ('seq', 'stream'), scatter_dimension=0, tiled=True)  387 us
    reduce_sum x176, other arithmetic, block_states(): (dt_step[token_at] * act_in[token_at])[:, None]  287 us
    dot_general x32, matrix products, one_block(): jnp.einsum('tdn,dn,tn->td', decay_now, carry_state, block_read, precision...  269 us
    reduce_scatter x1, waiting for transfers between devices, local(): lax.psum_scatter(g_xproj, ('seq', 'stream'), scatter_dimension=0, tiled=T...  137 us
  transfers between devices with their start and end apart: 15, of which 7 were waited for; matrix products, arithmetic and copies ran while one was open for 24% of the time, Pallas kernels for 0%

commit v1 on v0

v1 whole, which is shorter than its diff:
```python
import jax
import jax.numpy as jnp
from jax import lax
from jax.experimental import pallas as pl
from jax.experimental.pallas import tpu as pltpu
from jax.sharding import PartitionSpec as P

CONV = 4
EPSILON = 1e-05
AXES = ("seq", "stream")
RESET = 1e30
GROUP = 16
LN2 = 0.6931471805599453
NT = (((1,), (1,)), ((), ()))

def fwd_end_body(dte_ref, dtx_ref, wide_ref, rate_ref, end_ref):
    n_tok = dte_ref.shape[0]
    n = rate_ref.shape[0]
    rate = rate_ref[...]

    def group(g, h):
        for p in range(GROUP):
            t = g * GROUP + p
            w = wide_ref[pl.ds(t * n, n), :]
            w = jnp.concatenate([w] * (rate.shape[1] // w.shape[1]), axis=1)
            h = jnp.exp2(dte_ref[pl.ds(t, 1), :] * rate) * h + dtx_ref[pl.ds(t, 1), :] * w
        return h

    end_ref[...] = lax.fori_loop(0, n_tok // GROUP, group, jnp.zeros_like(rate))

def fwd_end(dte, dtx, wide, rate, width=512):
    n_tok, chans = dte.shape
    n = rate.shape[0]
    return pl.pallas_call(
        fwd_end_body, grid=(chans // width,),
        in_specs=[pl.BlockSpec((n_tok, width), lambda c: (0, c)), pl.BlockSpec((n_tok, width), lambda c: (0, c)),
                  pl.BlockSpec(wide.shape, lambda c: (0, 0)), pl.BlockSpec((n, width), lambda c: (0, c))],
        out_specs=pl.BlockSpec((n, width), lambda c: (0, c)),
        out_shape=jax.ShapeDtypeStruct((n, chans), jnp.float32),
        compiler_params=pltpu.CompilerParams(vmem_limit_bytes=48 << 20), name="fwd_end",
    )(dte, dtx, wide, rate)

def bwd_end_body(dte_ref, grad_ref, wide_ref, rate_ref, end_ref):
    n_tok = dte_ref.shape[0]
    n = rate_ref.shape[0]
    rate = rate_ref[...]
    groups = n_tok // GROUP

    def group(k, g):
        for p in reversed(range(GROUP)):
            t = (groups - 1 - k) * GROUP + p
            w = wide_ref[pl.ds(t * n, n), :]
            w = jnp.concatenate([w] * (rate.shape[1] // w.shape[1]), axis=1)
            g = jnp.exp2(dte_ref[pl.ds(t, 1), :] * rate) * (g + grad_ref[pl.ds(t, 1), :] * w)
        return g

    end_ref[...] = lax.fori_loop(0, groups, group, jnp.zeros_like(rate))

def bwd_end(dte, grad, wide, rate, width=512):
    n_tok, chans = dte.shape
    n = rate.shape[0]
    return pl.pallas_call(
        bwd_end_body, grid=(chans // width,),
        in_specs=[pl.BlockSpec((n_tok, width), lambda c: (0, c)), pl.BlockSpec((n_tok, width), lambda c: (0, c)),
                  pl.BlockSpec(wide.shape, lambda c: (0, 0)), pl.BlockSpec((n, width), lambda c: (0, c))],
        out_specs=pl.BlockSpec((n, width), lambda c: (0, c)),
        out_shape=jax.ShapeDtypeStruct((n, chans), jnp.float32),
        compiler_params=pltpu.CompilerParams(vmem_limit_bytes=48 << 20), name="bwd_end",
    )(dte, grad, wide, rate)

def fwd_full_body(dte_ref, dtx_ref, wide_ref, read_ref, rate_ref, start_ref, y_ref, hist_ref, h_ref):
    block = dte_ref.shape[0]
    n = rate_ref.shape[0]
    span = GROUP * n
    at = pl.program_id(1)
    rate = rate_ref[...]

    @pl.when(at == 0)
    def _():
        h_ref[...] = start_ref[...]

    h0 = h_ref[...]
    hist_ref[pl.ds(0, n), :] = h0.astype(jnp.bfloat16)

    def group(g, h):
        for p in range(GROUP):
            t = g * GROUP + p
            w = wide_ref[pl.ds((at * block + t) * n, n), :]
            w = jnp.concatenate([w] * (rate.shape[1] // w.shape[1]), axis=1)
            h = jnp.exp2(dte_ref[pl.ds(t, 1), :] * rate) * h + dtx_ref[pl.ds(t, 1), :] * w
            hist_ref[pl.ds((t + 1) * n, n), :] = h.astype(jnp.bfloat16)
        y_ref[pl.ds(g * GROUP, GROUP), :] = jnp.dot(
            read_ref[pl.ds(g * GROUP, GROUP), :], hist_ref[pl.ds(n + g * span, span), :],
            preferred_element_type=jnp.float32)
        return h

    h_ref[...] = lax.fori_loop(0, block // GROUP, group, h0)

def fwd_full(dte, dtx, wide, read, rate, start, width=1024, block=128):
    n_tok, chans = dte.shape
    n = rate.shape[0]
    blocks = n_tok // block
    return pl.pallas_call(
        fwd_full_body, grid=(chans // width, blocks),
        in_specs=[pl.BlockSpec((block, width), lambda c, t: (t, c)), pl.BlockSpec((block, width), lambda c, t: (t, c)),
                  pl.BlockSpec(wide.shape, lambda c, t: (0, 0)),
                  pl.BlockSpec((block, read.shape[1]), lambda c, t: (t, 0)),
                  pl.BlockSpec((n, width), lambda c, t: (0, c)), pl.BlockSpec((n, width), lambda c, t: (0, c))],
        out_specs=[pl.BlockSpec((block, width), lambda c, t: (t, c)),
                   pl.BlockSpec(((block + 1) * n, width), lambda c, t: (t, c))],
        out_shape=[jax.ShapeDtypeStruct((n_tok, chans), jnp.float32),
                   jax.ShapeDtypeStruct((blocks * (block + 1) * n, chans), jnp.bfloat16)],
        scratch_shapes=[pltpu.VMEM((n, width), jnp.float32)],
        compiler_params=pltpu.CompilerParams(vmem_limit_bytes=56 << 20), name="fwd_full",
    )(dte, dtx, wide, read, rate, start)

def bwd_full_body(dte_ref, dtx_ref, grad_ref, hist_ref, wide_ref, write_ref, ones_ref, rate_ref, start_ref,
                  s1_ref, s2_ref, grate_ref, dw_ref, dr_ref, g_ref, adj_ref, r_ref):
    block = dte_ref.shape[0]
    n = rate_ref.shape[0]
    span = GROUP * n
    blocks = pl.num_programs(1)
    step = pl.program_id(1)
    at = blocks - 1 - step
    rate = rate_ref[...]
    groups = block // GROUP
    bf = jnp.bfloat16

    @pl.when(step == 0)
    def _():
        g_ref[...] = start_ref[...]
        grate_ref[...] = jnp.zeros_like(grate_ref)

    @pl.when((step == 0) & (pl.program_id(0) == 0))
    def _():
        dw_ref[...] = jnp.zeros_like(dw_ref)
        dr_ref[...] = jnp.zeros_like(dr_ref)

    def group(k, g):
        q = groups - 1 - k
        for p in reversed(range(GROUP)):
            t = q * GROUP + p
            w = wide_ref[pl.ds((at * block + t) * n, n), :]
            w = jnp.concatenate([w] * (rate.shape[1] // w.shape[1]), axis=1)
            lam = dte_ref[pl.ds(t, 1), :] * rate
            adj = g + grad_ref[pl.ds(t, 1), :] * w
            g = jnp.exp2(lam) * adj
            adj_ref[pl.ds(p * n, n), :] = adj.astype(bf)
            r_ref[pl.ds(p * n, n), :] = g.astype(bf) * hist_ref[pl.ds(t * n, n), :] * lam.astype(bf)
        rows = pl.ds(q * GROUP, GROUP)
        adj_all = adj_ref[...]
        s1_ref[rows, :] = jnp.dot(write_ref[rows, :], adj_all, preferred_element_type=jnp.float32)
        sums = jnp.dot(ones_ref[...], r_ref[...], preferred_element_type=jnp.float32)
        s2_ref[rows, :] = sums[:GROUP]
        grate_ref[...] += sums[GROUP:]
        whole = pl.ds(at * block + q * GROUP, GROUP)
        dw_ref[whole, :] += lax.dot_general(dtx_ref[rows, :].astype(bf), adj_all, NT, preferred_element_type=jnp.float32)
        dr_ref[whole, :] += lax.dot_general(grad_ref[rows, :].astype(bf), hist_ref[pl.ds(n + q * span, span), :], NT,
                                            preferred_element_type=jnp.float32)
        return g

    g_ref[...] = lax.fori_loop(0, groups, group, g_ref[...])

def bwd_full(dte, dtx, grad, hist, wide, write, rate, start, width=1024, block=128):
    n_tok, chans = dte.shape
    n = rate.shape[0]
    blocks = n_tok // block
    span = GROUP * n
    col = jnp.arange(span)
    ones = jnp.concatenate([(col // n)[None, :] == jnp.arange(GROUP)[:, None], (col % n)[None, :] == jnp.arange(n)[:, None]]).astype(jnp.bfloat16)
    tok = lambda c, t: (blocks - 1 - t, c)
    return pl.pallas_call(
        bwd_full_body, grid=(chans // width, blocks),
        in_specs=[pl.BlockSpec((block, width), tok), pl.BlockSpec((block, width), tok), pl.BlockSpec((block, width), tok),
                  pl.BlockSpec(((block + 1) * n, width), tok),
                  pl.BlockSpec(wide.shape, lambda c, t: (0, 0)),
                  pl.BlockSpec((block, span), lambda c, t: (blocks - 1 - t, 0)),
                  pl.BlockSpec(ones.shape, lambda c, t: (0, 0)),
                  pl.BlockSpec((n, width), lambda c, t: (0, c)), pl.BlockSpec((n, width), lambda c, t: (0, c))],
        out_specs=[pl.BlockSpec((block, width), tok), pl.BlockSpec((block, width), tok),
                   pl.BlockSpec((n, width), lambda c, t: (0, c)),
                   pl.BlockSpec((n_tok, span), lambda c, t: (0, 0)), pl.BlockSpec((n_tok, span), lambda c, t: (0, 0))],
        out_shape=[jax.ShapeDtypeStruct((n_tok, chans), jnp.float32), jax.ShapeDtypeStruct((n_tok, chans), jnp.float32),
                   jax.ShapeDtypeStruct((n, chans), jnp.float32),
                   jax.ShapeDtypeStruct((n_tok, span), jnp.float32), jax.ShapeDtypeStruct((n_tok, span), jnp.float32)],
        scratch_shapes=[pltpu.VMEM((n, width), jnp.float32), pltpu.VMEM((span, width), jnp.bfloat16), pltpu.VMEM((span, width), jnp.bfloat16)],
        compiler_params=pltpu.CompilerParams(vmem_limit_bytes=56 << 20), name="bwd_full",
    )(dte, dtx, grad, hist, wide, write, ones, rate, start)

def widen(v):
    return jnp.broadcast_to(v.reshape(-1)[:, None], (v.size, 128))

def diag_rows(v):
    T, n = v.shape
    sel = (jnp.arange(T)[:, None] % GROUP == jnp.arange(GROUP)[None, :])
    return jnp.where(sel[:, :, None], v[:, None, :], 0).reshape(T, GROUP * n).astype(jnp.bfloat16)

def undiag(d, n):
    T = d.shape[0]
    sel = (jnp.arange(T)[:, None] % GROUP == jnp.arange(GROUP)[None, :])
    return jnp.sum(jnp.where(sel[:, :, None], d.reshape(T, GROUP, n), 0), axis=1)


def passed_along(block, axis, distance):
    devices = range(lax.axis_size(axis))
    route = [(i - distance, i) for i in devices if i - distance in devices]
    return lax.ppermute(block, axis, route)


def silu_slope(values_in):
    sigmoid_v = jax.nn.sigmoid(values_in)
    return sigmoid_v * (1.0 + values_in * (1.0 - sigmoid_v))


def norm_rows(residual, norm_scale):
    inv_rms = lax.rsqrt(jnp.mean(residual * residual, axis=-1, keepdims=True) + EPSILON)
    return residual * inv_rms * norm_scale[None, :]


def token_layout(lengths, first_pos, n_tokens):
    doc_ends = jnp.cumsum(lengths)
    begins = doc_ends - lengths
    positions = first_pos + jnp.arange(n_tokens, dtype=jnp.int32)
    live_slot = (lengths > 0)[None, :]
    doc_ids = jnp.sum(((begins[None, :] <= positions[:, None]) & live_slot).astype(jnp.int32), axis=1)
    start_flags = jnp.sum(((begins[None, :] == positions[:, None]) & live_slot).astype(jnp.float32), axis=1)
    valid_mask = (positions < doc_ends[-1]).astype(jnp.float32)
    return (doc_ids, start_flags, valid_mask)


def contract_rows(left_mat, right_mat):
    return lax.dot_general(left_mat, right_mat, (((0,), (0,)), ((), ())), preferred_element_type=jnp.float32)


def contract_cols(left_mat, right_mat):
    return lax.dot_general(left_mat, right_mat, NT, preferred_element_type=jnp.float32)


def carried(ends, step_sum, rate, backward):
    high = step_sum.astype(jnp.bfloat16)
    low = (step_sum - high.astype(jnp.float32)).astype(jnp.bfloat16)
    n = ends.shape[0]
    sent = jnp.concatenate([ends.astype(jnp.bfloat16), high[None], low[None]], axis=0)
    gathered = lax.all_gather(sent, "seq")
    count = lax.axis_size("seq")
    place = lax.axis_index("seq")
    state = jnp.zeros_like(ends)
    for step in range(count - 1):
        source = count - 1 - step if backward else step
        block = gathered[source].astype(jnp.float32)
        joined = jnp.exp2((block[n] + block[n + 1])[None, :] * rate) * state + block[:n]
        state = jnp.where(source > place if backward else source < place, joined, state)
    return state


def local(resid_in, out_grad, row_lengths, norm_gain, in_weight, conv_weight, conv_bias, xproj_weight, dt_weight,
          dt_bias, a_log, skip_gain, out_weight):
    bf, f32 = jnp.bfloat16, jnp.float32
    own_chans = conv_bias.shape[0]
    own_feats = norm_gain.shape[0]
    rank_dim = dt_weight.shape[0]
    state_dim = a_log.shape[1]
    proj_dim = xproj_weight.shape[1]
    half = in_weight.shape[1] // 2
    in_conv = lax.all_gather(in_weight[:, :half], AXES, axis=0, tiled=True)
    packed = jnp.concatenate(
        [xproj_weight, dt_weight.T, a_log, conv_weight.T, conv_bias[:, None], dt_bias[:, None], skip_gain[:, None],
         jnp.pad(norm_gain, (0, own_chans - own_feats))[:, None]], axis=1)
    packed = lax.all_gather(packed, AXES, axis=0, tiled=True)
    in_gate = lax.all_gather(in_weight[:, half:], AXES, axis=0, tiled=True)
    out_full = lax.all_gather(out_weight, AXES, axis=0, tiled=True)
    at = 0
    xproj_full = packed[:, :proj_dim]
    at = proj_dim
    dtw_cols = packed[:, at : at + rank_dim]
    at += rank_dim
    log_rates = packed[:, at : at + state_dim].astype(f32).T
    at += state_dim
    conv_taps = packed[:, at : at + CONV].astype(f32).T
    at += CONV
    conv_shift, dt_shift, skip_vec = (packed[:, at + i].astype(f32) for i in range(3))
    norm_scale = packed[:, at + 3].reshape(-1, own_chans)[:, :own_feats].reshape(-1).astype(f32)
    rate = -jnp.exp(log_rates) / LN2

    residual = resid_in[0].astype(f32)
    n_tokens = residual.shape[0]
    rim_width = CONV - 1
    first_pos = lax.axis_index("seq") * n_tokens
    doc_ids, start_flags, valid_mask = token_layout(row_lengths[0], first_pos - rim_width, n_tokens + 2 * rim_width)
    own_ids = doc_ids[rim_width : rim_width + n_tokens]
    starts = start_flags[rim_width : rim_width + n_tokens]
    valid_mask = valid_mask[rim_width : rim_width + n_tokens]
    normed_f, norm_pull = jax.vjp(norm_rows, residual, norm_scale)
    normed_in = normed_f.astype(bf)
    conv_in = jnp.dot(normed_in, in_conv, preferred_element_type=f32)
    gate_in = jnp.dot(normed_in, in_gate, preferred_element_type=f32)
    earlier_rows = passed_along(conv_in[n_tokens - rim_width :].astype(bf), "seq", 1).astype(f32)
    padded_in = jnp.concatenate([earlier_rows, conv_in], axis=0)
    matches = [(doc_ids[tap : tap + n_tokens] == own_ids).astype(f32)[:, None] for tap in range(CONV)]
    conv_out = conv_shift[None, :]
    for tap in range(CONV):
        conv_out = conv_out + conv_taps[tap][None, :] * padded_in[tap : tap + n_tokens] * matches[tap]
    activated = jax.nn.silu(conv_out).astype(bf)
    act_float = activated.astype(f32)
    projected = jnp.dot(activated, xproj_full, preferred_element_type=f32)
    low_rank = projected[:, :rank_dim].astype(bf)
    write_in = projected[:, rank_dim : rank_dim + state_dim]
    readout = projected[:, rank_dim + state_dim :]
    dt_pre = contract_cols(low_rank, dtw_cols) + dt_shift[None, :]
    dt_step = jax.nn.softplus(dt_pre)
    dt_reset = jnp.where(starts[:, None] > 0, RESET, dt_step)
    dt_act = dt_step * act_float
    write_wide, read_wide = widen(write_in), widen(readout)
    write_diag, read_diag = diag_rows(write_in), diag_rows(readout)

    step_sum = jnp.sum(dt_reset, axis=0)
    ends = fwd_end(dt_reset, dt_act, write_wide, rate)
    start_state = carried(ends, step_sum, rate, False)
    scanned, history = fwd_full(dt_reset, dt_act, write_wide, read_diag, rate, start_state)
    ssm_out = scanned + skip_vec[None, :] * act_float
    gate_act = jax.nn.silu(gate_in)
    gated = (ssm_out * gate_act * valid_mask[:, None]).astype(bf)
    output = (residual + jnp.dot(gated, out_full, preferred_element_type=f32)).astype(bf)
    cotangent = out_grad[0]
    d_gated = contract_cols(cotangent, out_full)
    g_out = lax.psum_scatter(contract_rows(gated, cotangent).astype(bf), AXES, scatter_dimension=0, tiled=True)
    d_masked = d_gated * valid_mask[:, None]
    d_ssm = d_masked * gate_act
    d_gate = (d_masked * ssm_out * silu_slope(gate_in)).astype(bf)
    g_in_gate = lax.psum_scatter(contract_rows(normed_in, d_gate).astype(bf), AXES, scatter_dimension=0, tiled=True)
    d_normed_gate = contract_cols(d_gate, in_gate)
    g_skip = jnp.sum(d_ssm * act_float, axis=0)
    back_ends = bwd_end(dt_reset, d_ssm, read_wide, rate)
    later_sum = carried(back_ends, step_sum, rate, True)
    sum_write, sum_rate, g_log, d_write, d_read = bwd_full(
        dt_reset, dt_act, d_ssm, history, read_wide, write_diag, rate, later_sum)
    d_write, d_read = undiag(d_write, state_dim), undiag(d_read, state_dim)
    g_log = g_log * LN2
    per_step = jnp.where(dt_step > 1e-30, sum_rate * LN2 / jnp.maximum(dt_step, 1e-30), 0.0)
    d_step = per_step + act_float * sum_write
    d_pre = d_step * jax.nn.sigmoid(dt_pre)
    g_dt_bias = jnp.sum(d_pre, axis=0)
    d_pre_low = d_pre.astype(bf)
    g_dt = contract_rows(d_pre_low, low_rank)
    d_low = jnp.dot(d_pre_low, dtw_cols, preferred_element_type=f32)
    d_proj = jnp.concatenate([d_low, d_write, d_read], axis=1).astype(bf)
    g_xproj = contract_rows(activated, d_proj)
    d_act = dt_step * sum_write + skip_vec[None, :] * d_ssm + contract_cols(d_proj, xproj_full)
    d_conv = d_act * silu_slope(conv_out)
    g_conv_bias = jnp.sum(d_conv, axis=0)
    g_conv = jnp.stack(
        [jnp.sum(d_conv * padded_in[tap : tap + n_tokens] * matches[tap], axis=0) for tap in range(CONV)], axis=1)
    later_rows = passed_along(d_conv[:rim_width].astype(bf), "seq", -1).astype(f32)
    d_ext = jnp.concatenate([d_conv, later_rows], axis=0)
    d_conv_in = jnp.zeros_like(d_conv)
    for tap in range(CONV):
        offset = rim_width - tap
        match_back = (doc_ids[rim_width + offset : rim_width + offset + n_tokens] == own_ids).astype(f32)[:, None]
        d_conv_in = d_conv_in + conv_taps[tap][None, :] * d_ext[offset : offset + n_tokens] * match_back
    d_conv_in = d_conv_in.astype(bf)
    g_in_conv = lax.psum_scatter(contract_rows(normed_in, d_conv_in).astype(bf), AXES, scatter_dimension=0, tiled=True)
    d_normed = contract_cols(d_conv_in, in_conv) + d_normed_gate
    d_resid, g_gain = norm_pull(d_normed)
    in_grad = (d_resid + cotangent.astype(f32)).astype(bf)
    g_gain = jnp.pad(g_gain.reshape(-1, own_feats), ((0, 0), (0, own_chans - own_feats))).reshape(-1)
    small = jnp.concatenate(
        [g_xproj, g_dt, g_log.T, g_conv, g_conv_bias[:, None], g_dt_bias[:, None], g_skip[:, None], g_gain[:, None]],
        axis=1)
    small = lax.psum_scatter(small, AXES, scatter_dimension=0, tiled=True)
    at = proj_dim + rank_dim
    return (
        output[None],
        in_grad[None],
        small[:own_feats, at + state_dim + CONV + 3],
        jnp.concatenate([g_in_conv, g_in_gate], axis=1).astype(f32),
        small[:, at + state_dim : at + state_dim + CONV].T,
        small[:, at + state_dim + CONV],
        small[:, :proj_dim],
        small[:, proj_dim:at].T,
        small[:, at + state_dim + CONV + 1],
        small[:, at : at + state_dim],
        small[:, at + state_dim + CONV + 2],
        g_out.astype(f32),
    )


def solution(mesh):
    in_specs = (
        P("stream", "seq", None),
        P("stream", "seq", None),
        P("stream", None),
        P(("seq", "stream")),
        P(("seq", "stream"), None),
        P(None, ("seq", "stream")),
        P(("seq", "stream")),
        P(("seq", "stream"), None),
        P(None, ("seq", "stream")),
        P(("seq", "stream")),
        P(("seq", "stream"), None),
        P(("seq", "stream")),
        P(("seq", "stream"), None),
    )
    out_specs = (
        P("stream", "seq", None),
        P("stream", "seq", None),
        P(("seq", "stream")),
        P(("seq", "stream"), None),
        P(None, ("seq", "stream")),
        P(("seq", "stream")),
        P(("seq", "stream"), None),
        P(None, ("seq", "stream")),
        P(("seq", "stream")),
        P(("seq", "stream"), None),
        P(("seq", "stream")),
        P(("seq", "stream"), None),
    )
    return jax.shard_map(local, mesh=mesh, in_specs=in_specs, out_specs=out_specs, check_vma=False)
```

time: 6100 us -> 1630 us (0.27)
  other arithmetic: 3030 us -> 71.9 us
  local copies, waits for them, and re-layouts: 572 us -> 42.7 us
  waiting for transfers between devices: 1550 us -> 1070 us
  matrix products: 568 us -> 204 us
  blocking collectives: 263 us -> 0 us
  Pallas kernels: 0 us -> 222 us
    reduce_sum x625 -> x1, other arithmetic: 2350 us -> 0.12 us  [undiag(): jnp.sum(jnp.where(sel[:, :, None], d.reshape(T, GROUP, n), 0), axis=1)]
    reduce_scatter x5 -> x4, waiting for transfers between devices: 1430 us -> 625 us  [the longest x1 204 us: local(): lax.psum_scatter(contract_rows(gated, cotangent).astype(bf), AXES, scatte...]
    add_any x32 -> x0, other arithmetic: 402 us -> none  [the longest x16 401 us: run_block(): return walk_block(decay_rates, state_now, piece)]
    dot_general x104 -> x10, matrix products: 512 us -> 156 us  [the longest x5 86.9 us: contract_cols(): lax.dot_general(left_mat, right_mat, NT, preferred_element_type=jnp.float32)]
    all_gather x7 -> x6, waiting for transfers between devices: 115 us -> 442 us  [the longest x1 114 us: local(): in_conv = lax.all_gather(in_weight[:, :half], AXES, axis=0, tiled=True)]
    pallas_call x0 -> x4, Pallas kernels: none -> 222 us  [the longest x1 108 us: bwd_full(): pl.pallas_call(bwd_full_body, grid=(chans // width, blocks), in_specs=[pl...]
    slice x230 -> x7, local copies, waits for them, and re-layouts: 219 us -> 6.18 us  [the longest x1 2.26 us: local(): in_conv = lax.all_gather(in_weight[:, :half], AXES, axis=0, tiled=True)]
    all_gather x5 -> x0, blocking collectives: 173 us -> none  [the longest x1 37.8 us: local(): lax.all_gather(skip_gain, ('seq', 'stream'), axis=0, tiled=True)]
  transfers between devices with their start and end apart: 15 -> 12, of which waited for: 7 -> 10; matrix products, arithmetic and copies ran while one was open for 24% -> 8% of each run, Pallas kernels for 0% -> 0%
where the time goes in v1:
time: 1630 us
  waiting for transfers between devices  1070 us (66%)
  Pallas kernels  222 us (14%)
  matrix products  204 us (13%)
  other arithmetic  71.9 us (4%)
  local copies, waits for them, and re-layouts  42.7 us (3%)
    reduce_scatter x1, waiting for transfers between devices, local(): lax.psum_scatter(contract_rows(gated, cotangent).astype(bf), AXES, scatte...  204 us
    reduce_scatter x1, waiting for transfers between devices, local(): lax.psum_scatter(contract_rows(normed_in, d_conv_in).astype(bf), AXES, sc...  187 us
    reduce_scatter x1, waiting for transfers between devices, local(): lax.psum_scatter(contract_rows(normed_in, d_gate).astype(bf), AXES, scatt...  185 us
    all_gather x1, waiting for transfers between devices, local(): in_conv = lax.all_gather(in_weight[:, :half], AXES, axis=0, tiled=True)  114 us
    pallas_call x1, Pallas kernels, bwd_full(): pl.pallas_call(bwd_full_body, grid=(chans // width, blocks), in_specs=[pl...  108 us
    all_gather x1, waiting for transfers between devices, local(): in_gate = lax.all_gather(in_weight[:, half:], AXES, axis=0, tiled=True)  101 us
    all_gather x1, waiting for transfers between devices, local(): out_full = lax.all_gather(out_weight, AXES, axis=0, tiled=True)  97.8 us
    dot_general x5, matrix products, contract_cols(): lax.dot_general(left_mat, right_mat, NT, preferred_element_type=jnp.float32)  86.9 us
  transfers between devices with their start and end apart: 12, of which 10 were waited for; matrix products, arithmetic and copies ran while one was open for 8% of the time, Pallas kernels for 0%

profile of v1, /device:TPU:19, one launch (start us, length us, event | category | flops | bytes accessed | tf_op | source)
XLA Modules:
  0.0 1628.7 jit_solution(2249161301130958831)
XLA Ops:
  7.9 5.3 concatenate.28
  23.9 45.2 %all-gather.11.cloned.1.call-done = bf16[4096,312]{0,1:T(8,128)(2,1)} async-done(((bf16[128,312]{0,1:T(8,128)(2,1)}), bf16[4096,312]{0,1:T(8,128)(2,1)}) %all-gather.11.cloned.1.call-update) | async-done | bytes 2555920 | tf_op jit(solution)/shard_map/all_gather | solution.py:269
  72.8 113.8 %all-gather.13.cloned.1.call-done = bf16[2048,4096]{1,0:T(8,128)(2,1)} async-done(((bf16[64,4096]{1,0:T(8,128)(2,1)}), bf16[2048,4096]{1,0:T(8,128)(2,1)}) %all-gather.13.cloned.1.call-update) | async-done | bytes 16777232 | tf_op jit(solution)/shard_map/all_gather | solution.py:265
  186.6 12.5 fusion.110
  199.0 3.3 copy-done.22
  202.4 2.7 collective-permute-start
  205.1 97.8 %all-gather.17.cloned.1.call-done = bf16[4096,2048]{1,0:T(8,128)(2,1)} async-done(((bf16[128,2048]{1,0:T(8,128)(2,1)}), bf16[4096,2048]{1,0:T(8,128)(2,1)}) %all-gather.17.cloned.1.call-update) | async-done | bytes 16777232 | tf_op jit(solution)/shard_map/all_gather | solution.py:271
  302.9 15.0 fusion.31
  317.9 101.3 %all-gather.15.cloned.1.call-done = bf16[2048,4096]{1,0:T(8,128)(2,1)} async-done(((bf16[64,4096]{1,0:T(8,128)(2,1)}), bf16[2048,4096]{1,0:T(8,128)(2,1)}) %all-gather.15.cloned.1.call-update) | async-done | bytes 16777232 | tf_op jit(solution)/shard_map/all_gather | solution.py:270
  419.2 36.0 %fusion.15 = (f32[4096]{0:T(1024)}, f32[512,4096]{1,0:T(8,128)}, bf16[512,4096]{1,0:T(8,128)(2,1)}, f32[512,4096]{1,0:T(8,128)}, f32[512,4096]{1,0:T(8,128)}) fusion(f32[512,4096]{1,0:T(8,128)} %fusion.31, f32[512]{0:T(512)S(1)} %get-tuple-element.91, f32[512,4096]{1,0:T(8,128)} %copy-done.22, f32[4096]{0:T(1024)S(1)} %bitcast.445, ...), kind=kOutput, calls=%fused_computation.27 | convolution fusion | flops 8652845056 | bytes 65177600 | tf_op jit(solution)/shard_map/dot_general | solution.py:296
  455.2 4.1 fusion.38
  459.4 13.6 fusion.114
  474.7 27.2 %fwd_end.1 = f32[16,4096]{1,0:T(8,128)S(1)} custom-call(f32[512,4096]{1,0:T(8,128)} %get-tuple-element.42.dte_ref, f32[512,4096]{1,0:T(8,128)} %get-tuple-element.45.dtx_ref, f32[8192,128]{1,0:T(8,128)S(1)} %broadcast_in_dim.96.wide_ref, f32[16,4096]{1,0:T(8,128)S(1)} %multiply_bitcast_fusion.1.rate_ref), custom_call_target="tpu_custom_call" | custom-call | tf_op jit(solution)/shard_map/fwd_end/pallas_call | solution.py:34
  503.1 27.4 %bwd_end.1 = f32[16,4096]{1,0:T(8,128)S(1)} custom-call(f32[512,4096]{1,0:T(8,128)} %get-tuple-element.42.dte_ref, f32[512,4096]{1,0:T(8,128)} %get-tuple-element.36.grad_ref, f32[8192,128]{1,0:T(8,128)S(1)} %broadcast_in_dim.102.wide_ref, f32[16,4096]{1,0:T(8,128)S(1)} %multiply_bitcast_fusion.1.rate_ref), custom_call_target="tpu_custom_call" | custom-call | tf_op jit(solution)/shard_map/bwd_end/pallas_call | solution.py:62
  533.9 39.9 %all-gather.19.cloned.1.call-done = bf16[8,18,4096]{2,1,0:T(8,128)(2,1)} async-done(((bf16[1,18,4096]{2,1,0:T(8,128)(2,1)}), bf16[8,18,4096]{2,1,0:T(8,128)(2,1)}) %all-gather.19.cloned.1.call-update) | async-done | bytes 1179664 | tf_op jit(solution)/shard_map/all_gather | solution.py:244
  575.8 43.7 %all-gather.21.cloned.1.call-done = bf16[8,18,4096]{2,1,0:T(8,128)(2,1)} async-done(((bf16[1,18,4096]{2,1,0:T(8,128)(2,1)}), bf16[8,18,4096]{2,1,0:T(8,128)(2,1)}) %all-gather.21.cloned.1.call-update) | async-done | bytes 1179664 | tf_op jit(solution)/shard_map/all_gather | solution.py:244
  623.5 59.5 %fwd_full.1 = (f32[512,4096]{1,0:T(8,128)}, bf16[8256,4096]{1,0:T(8,128)(2,1)}) custom-call(f32[512,4096]{1,0:T(8,128)} %get-tuple-element.42.dte_ref, f32[512,4096]{1,0:T(8,128)} %get-tuple-element.45.dtx_ref, f32[8192,128]{1,0:T(8,128)} %copy-done.1, bf16[512,256]{1,0:T(8,128)(2,1)} %copy.44.read_ref, f32[16,4096]{1,0:T(8,128)} %copy-done.2, ...), custom_call_target="tpu_custom_call" | custom-call | tf_op jit(solution)/shard_map/fwd_full/pallas_call | solution.py:103
  685.1 108.0 %bwd_full.1 = (f32[512,4096]{1,0:T(8,128)}, f32[512,4096]{1,0:T(8,128)}, f32[16,4096]{1,0:T(8,128)}, f32[512,256]{1,0:T(8,128)}, f32[512,256]{1,0:T(8,128)}) custom-call(f32[512,4096]{1,0:T(8,128)} %get-tuple-element.42.dte_ref, f32[512,4096]{1,0:T(8,128)} %get-tuple-element.45.dtx_ref, f32[512,4096]{1,0:T(8,128)} %get-tuple-element.36.grad_ref, ...), custom_call_target="tpu_custom_call" | custom-call | tf_op jit(solution)/shard_map/bwd_full/pallas_call | solution.py:172
  796.7 23.8 %fusion.112 = (f32[4096]{0:T(1024)S(1)}, bf16[512,4096]{1,0:T(8,128)(2,1)S(1)}, bf16[512,4096]{1,0:T(8,128)(2,1)}, bf16[512,4096]{1,0:T(8,128)(2,1)}) fusion(f32[512,4096]{1,0:T(8,128)} %get-tuple-element.21, bf16[512,4096]{1,0:T(8,128)(2,1)} %get-tuple-element.37, f32[512,4096]{1,0:T(8,128)} %get-tuple-element.22, f32[512,4096]{1,0:T(8,128)} %get-tuple-element.88, ...), kind=kLoop, calls=%fused_computation.251 | loop fusion | flops 79687680 | bytes 67160064 | tf_op jit(solution)/shard_map/reduce_sum | solution.py:342
  823.6 27.3 %multiply_reduce_fusion.1 = (f32[4096]{0:T(1024)S(1)}, f32[4096]{0:T(1024)S(1)}, f32[4096]{0:T(1024)S(1)}, f32[4096]{0:T(1024)S(1)}, f32[4096]{0:T(1024)S(1)}, /*index=5*/f32[512,4096]{1,0:T(8,128)}) fusion(f32[512,4096]{1,0:T(8,128)} %copy-done.22, f32[3,4096]{1,0:T(4,128)S(1)} %convert_element_type.264, f32[512]{0:T(512)S(1)} %get-tuple-element.83, ...), kind=kOutput, calls=%fused_computation.38 | convolution fusion | flops 742862848 | bytes 51992576 | tf_op jit(solution)/shard_map/dot_general | solution.py:236
  854.4 14.1 fusion.118
  870.6 21.6 %fusion.6 = bf16[512,4096]{1,0:T(8,128)(2,1)} fusion(f32[3,4096]{1,0:T(4,128)S(1)} %convert_element_type.303, f32[512,4096]{1,0:T(8,128)} %get-tuple-element.90, f32[512]{0:T(512)S(1)} %copy-done.19, f32[512]{0:T(512)S(1)} %copy-done.18, f32[512]{0:T(512)S(1)} %copy-done.17, f32[4096]{0:T(1024)S(1)} %bitcast.446, f32[4096]{0:T(1024)S(1)} %bitcast.448, ...), kind=kLoop, calls=%fused_computation.18 | loop fusion | flops 29360128 | bytes 12703744 | tf_op jit(solution)/shard_map/convert_element_type | solution.py:360
  892.2 16.9 %fusion.22 = (f32[2048]{0:T(1024)S(1)}, f32[512]{0:T(512)S(1)}, f32[512,2048]{1,0:T(8,128)}) fusion(bf16[1,512,2048]{2,1,0:T(8,128)(2,1)S(1)} %copy-done.5, f32[512]{0:T(512)S(1)} %copy-done.21, f32[2048]{0:T(1024)S(1)} %copy-done.13, f32[512,2048]{1,0:T(8,128)} %fusion.118, bf16[512,4096]{1,0:T(8,128)(2,1)} %fusion.6, ...), kind=kOutput, calls=%fused_computation.54 | convolution fusion | flops 8598321152 | bytes 31477760 | tf_op jit(solution)/shard_map/dot_general | solution.py:236
  909.1 11.0 concatenate.35
  920.2 15.0 convolution_convert_fusion
  936.8 14.8 convolution_convert_fusion.1
  951.6 15.1 convolution_convert_fusion.2
  966.7 14.8 fusion.28
  984.2 48.9 %reduce-scatter.5.cloned.1.call-done = f32[128,312]{0,1:T(8,128)} async-done(((f32[4096,312]{0,1:T(8,128)}), f32[128,312]{0,1:T(8,128)}) %reduce-scatter.5.cloned.1.call-update) | async-done | bytes 159760 | tf_op jit(solution)/shard_map/reduce_scatter | solution.py:369
  1041.2 204.1 %reduce-scatter.11.cloned.1.call-done = bf16[128,2048]{1,0:T(8,128)(2,1)} async-done(((bf16[4096,2048]{1,0:T(8,128)(2,1)}), bf16[128,2048]{1,0:T(8,128)(2,1)}) %reduce-scatter.11.cloned.1.call-update) | async-done | bytes 524304 | tf_op jit(solution)/shard_map/reduce_scatter | solution.py:326
  1247.4 184.8 %reduce-scatter.9.cloned.1.call-done = bf16[64,4096]{1,0:T(8,128)(2,1)} async-done(((bf16[2048,4096]{1,0:T(8,128)(2,1)}), bf16[64,4096]{1,0:T(8,128)(2,1)}) %reduce-scatter.9.cloned.1.call-update) | async-done | bytes 524304 | tf_op jit(solution)/shard_map/reduce_scatter | solution.py:330
  1432.2 186.7 %reduce-scatter.7.cloned.1.call-done = bf16[64,4096]{1,0:T(8,128)(2,1)} async-done(((bf16[2048,4096]{1,0:T(8,128)(2,1)}), bf16[64,4096]{1,0:T(8,128)(2,1)}) %reduce-scatter.7.cloned.1.call-update) | async-done | bytes 524304 | tf_op jit(solution)/shard_map/reduce_scatter | solution.py:361
  (152 shorter events, 58.4 us)
Async XLA Ops:
  7.2 61.9 %all-gather.11.cloned.1.call-start = ((), (), s32[]{:S(2)}) async-start(), calls=%async_computation.4 | async-start | bytes 2635776 | tf_op jit(solution)/shard_map/all_gather | solution.py:269
  13.3 173.3 %all-gather.13.cloned.1.call-start = ((), (), s32[]{:S(2)}) async-start(), calls=%async_computation.5 | async-start | bytes 17301504 | tf_op jit(solution)/shard_map/all_gather | solution.py:265
  15.6 287.3 %all-gather.17.cloned.1.call-start = ((), (), s32[]{:S(2)}) async-start(), calls=%async_computation.7 | async-start | bytes 17301504 | tf_op jit(solution)/shard_map/all_gather | solution.py:271
  16.3 402.9 %all-gather.15.cloned.1.call-start = ((), (), s32[]{:S(2)}) async-start(), calls=%async_computation.6 | async-start | bytes 17301504 | tf_op jit(solution)/shard_map/all_gather | solution.py:270
  16.9 557.0 %all-gather.19.cloned.1.call-start = ((), (), s32[]{:S(2)}) async-start(), calls=%async_computation.12 | async-start | bytes 1769472 | tf_op jit(solution)/shard_map/all_gather | solution.py:244
  23.2 396.0 %copy-start.20 = (f32[512]{0:T(512)}, f32[512]{0:T(512)S(1)}, u32[]{:S(2)}) copy-start(f32[512]{0:T(512)S(1)} %fusion.100) | copy-start | bytes 6148
  70.9 348.4 %copy-start.12 = (f32[2048]{0:T(1024)}, f32[2048]{0:T(1024)S(1)}, u32[]{:S(2)}) copy-start(f32[2048]{0:T(1024)S(1)} %reshape.347) | copy-start | bytes 24580
  72.7 430.3 %copy-start.2 = (f32[16,4096]{1,0:T(8,128)}, f32[16,4096]{1,0:T(8,128)S(1)}, u32[]{:S(2)}) copy-start(f32[16,4096]{1,0:T(8,128)S(1)} %multiply_bitcast_fusion.1.rate_ref) | copy-start | bytes 786436
  199.0 3.3 copy-start.22
  202.4 216.9 %copy-start.4 = (bf16[1,512,2048]{2,1,0:T(8,128)(2,1)S(1)}, bf16[1,512,2048]{2,1,0:T(8,128)(2,1)}, u32[]{:S(2)}) copy-start(bf16[1,512,2048]{2,1,0:T(8,128)(2,1)} %param.13) | copy-start | bytes 6291460
  202.4 115.5 %collective-permute-start = (bf16[3,4096]{1,0:T(4,128)(2,1)S(1)}, bf16[3,4096]{1,0:T(4,128)(2,1)S(1)}, u32[]{:S(2)}, u32[]{:S(2)}) collective-permute-start(bf16[3,4096]{1,0:T(4,128)(2,1)S(1)} %slice.950), channel_id=1, source_target_pairs={{0,4},{4,8},{8,12},{12,16},{16,20},{20,24},{24,28},{1,5},{5,9},{9,... | collective-permute-start | bytes 73736 | tf_op jit(solution)/shard_map/ppermute | solution.py:207
  474.7 27.2 %copy-start.1 = (f32[8192,128]{1,0:T(8,128)}, f32[8192,128]{1,0:T(8,128)S(1)}, u32[]{:S(2)}) copy-start(f32[8192,128]{1,0:T(8,128)S(1)} %broadcast_in_dim.96.wide_ref) | copy-start | bytes 12582916
  503.1 27.4 %copy-start = (f32[8192,128]{1,0:T(8,128)}, f32[8192,128]{1,0:T(8,128)S(1)}, u32[]{:S(2)}) copy-start(f32[8192,128]{1,0:T(8,128)S(1)} %broadcast_in_dim.102.wide_ref) | copy-start | bytes 12582916
  531.3 88.2 %all-gather.21.cloned.1.call-start = ((), (), s32[]{:S(2)}) async-start(), calls=%async_computation.13 | async-start | bytes 1769472 | tf_op jit(solution)/shard_map/all_gather | solution.py:244
  533.9 499.2 %reduce-scatter.5.cloned.1.call-start = ((), (), s32[]{:S(2)}) async-start(), calls=%async_computation.8 | async-start | bytes 5271552 | tf_op jit(solution)/shard_map/reduce_scatter | solution.py:369
  685.1 111.6 %copy-start.11 = (f32[4096,1]{0,1:T(1,128)S(1)}, f32[4096,1]{0,1:T(1,128)}, u32[]{:S(2)}) copy-start(f32[4096,1]{0,1:T(1,128)} %get-tuple-element.48) | copy-start | bytes 49156
  796.7 23.8 %copy-start.10 = (bf16[4096,312]{0,1:T(8,128)(2,1)S(1)}, bf16[4096,312]{0,1:T(8,128)(2,1)}, u32[]{:S(2)}) copy-start(bf16[4096,312]{0,1:T(8,128)(2,1)} %all-gather.11.cloned.1.call-done) | copy-start | bytes 7667716
  823.6 30.8 %copy-start.7 = (bf16[512,4096]{1,0:T(8,128)(2,1)S(1)}, bf16[512,4096]{1,0:T(8,128)(2,1)}, u32[]{:S(2)}) copy-start(bf16[512,4096]{1,0:T(8,128)(2,1)} %get-tuple-element.47) | copy-start | bytes 12582916
  851.8 18.8 %collective-permute-start.1 = (bf16[3,4096]{1,0:T(4,128)(2,1)S(1)}, bf16[3,4096]{1,0:T(4,128)(2,1)S(1)}, u32[]{:S(2)}, u32[]{:S(2)}) collective-permute-start(bf16[3,4096]{1,0:T(4,128)(2,1)S(1)} %slice.949), channel_id=1, source_target_pairs={{4,0},{8,4},{12,8},{16,12},{20,16},{24,20},{28,24},{5,1},{9,5},{13... | collective-permute-start | bytes 73736 | tf_op jit(solution)/shard_map/ppermute | solution.py:207
  854.3 16.2 copy-start.17
  854.4 16.2 copy-start.18
  854.4 16.2 copy-start.19
  868.5 23.7 %copy-start.5 = (bf16[1,512,2048]{2,1,0:T(8,128)(2,1)S(1)}, bf16[1,512,2048]{2,1,0:T(8,128)(2,1)}, u32[]{:S(2)}) copy-start(bf16[1,512,2048]{2,1,0:T(8,128)(2,1)} %param.13) | copy-start | bytes 6291460
  868.5 23.7 %copy-start.13 = (f32[2048]{0:T(1024)S(1)}, f32[2048]{0:T(1024)}, u32[]{:S(2)}) copy-start(f32[2048]{0:T(1024)} %copy-done.12) | copy-start | bytes 24580
  868.5 23.7 %copy-start.21 = (f32[512]{0:T(512)S(1)}, f32[512]{0:T(512)}, u32[]{:S(2)}) copy-start(f32[512]{0:T(512)} %copy-done.20) | copy-start | bytes 6148
  892.2 17.0 %copy-start.16 = (f32[4096]{0:T(1024)S(1)}, f32[4096]{0:T(1024)}, u32[]{:S(2)}) copy-start(f32[4096]{0:T(1024)} %get-tuple-element.35) | copy-start | bytes 49156
  920.1 325.1 %reduce-scatter.11.cloned.1.call-start = ((), (), s32[]{:S(2)}) async-start(), calls=%async_computation.11 | async-start | bytes 17301504 | tf_op jit(solution)/shard_map/reduce_scatter | solution.py:326
  935.2 497.1 %reduce-scatter.9.cloned.1.call-start = ((), (), s32[]{:S(2)}) async-start(), calls=%async_computation.10 | async-start | bytes 17301504 | tf_op jit(solution)/shard_map/reduce_scatter | solution.py:330
  951.6 667.3 %reduce-scatter.7.cloned.1.call-start = ((), (), s32[]{:S(2)}) async-start(), calls=%async_computation.9 | async-start | bytes 17301504 | tf_op jit(solution)/shard_map/reduce_scatter | solution.py:361
  966.7 14.9 copy-start.15
  966.7 14.9 copy-start.8
  966.7 14.9 copy-start.9
  (3 other events, 4.4 us)
Sparse Core Ops, SparseCore 0:
  13.4 55.6 all-gather.10
  72.5 113.9 all-gather.12
  189.4 113.3 all-gather.16
  306.2 113.0 all-gather.14
  531.5 42.3 all-gather.18
  576.5 42.9 all-gather.20
  920.3 112.7 reduce-scatter.4
  1035.4 209.8 reduce-scatter.10
  1247.6 184.6 reduce-scatter.8
  1434.4 184.4 reduce-scatter.6

commit v2 on v1

v2 whole, which is shorter than its diff:
```python
import functools

import jax
import jax.numpy as jnp
from jax import lax
from jax.experimental import pallas as pl
from jax.experimental.pallas import tpu as pltpu
from jax.sharding import PartitionSpec as P

CONV = 4
EPSILON = 1e-05
RESET = 1e30
GROUP = 16
LN2 = 0.6931471805599453
NT = (((1,), (1,)), ((), ()))
VMEM_LIMIT = 56 << 20


def across(rows, width):
    return jnp.concatenate([rows] * (width // rows.shape[1]), axis=1)


def fwd_end_body(dte_ref, dtx_ref, wide_ref, rate_ref, end_ref):
    n, width = rate_ref.shape
    rate = rate_ref[...]

    def group(at, state):
        for place in range(GROUP):
            t = at * GROUP + place
            write = across(wide_ref[pl.ds(t * n, n), :], width)
            state = jnp.exp2(dte_ref[pl.ds(t, 1), :] * rate) * state + dtx_ref[pl.ds(t, 1), :] * write
        return state

    end_ref[...] = lax.fori_loop(0, dte_ref.shape[0] // GROUP, group, jnp.zeros_like(rate))


def bwd_end_body(dte_ref, grad_ref, wide_ref, rate_ref, end_ref):
    n, width = rate_ref.shape
    rate = rate_ref[...]
    groups = dte_ref.shape[0] // GROUP

    def group(step, state):
        for place in reversed(range(GROUP)):
            t = (groups - 1 - step) * GROUP + place
            read = across(wide_ref[pl.ds(t * n, n), :], width)
            state = jnp.exp2(dte_ref[pl.ds(t, 1), :] * rate) * (state + grad_ref[pl.ds(t, 1), :] * read)
        return state

    end_ref[...] = lax.fori_loop(0, groups, group, jnp.zeros_like(rate))


def scan_end(body, dte, other, wide, rate, seqs, width=512):
    tokens, chans = dte.shape
    length = tokens // seqs
    n = rate.shape[0]
    width = min(width, chans)
    work = tokens * chans * n
    return pl.pallas_call(
        body,
        grid=(seqs, chans // width),
        in_specs=[
            pl.BlockSpec((length, width), lambda s, c: (s, c)),
            pl.BlockSpec((length, width), lambda s, c: (s, c)),
            pl.BlockSpec((length * n, wide.shape[1]), lambda s, c: (s, 0)),
            pl.BlockSpec((n, width), lambda s, c: (0, c)),
        ],
        out_specs=pl.BlockSpec((n, width), lambda s, c: (s, c)),
        out_shape=jax.ShapeDtypeStruct((seqs * n, chans), jnp.float32),
        compiler_params=pltpu.CompilerParams(vmem_limit_bytes=VMEM_LIMIT),
        cost_estimate=pl.CostEstimate(flops=4 * work, transcendentals=work, bytes_accessed=8 * tokens * chans),
        name=body.__name__[:7],
    )(dte, other, wide, rate)


def fwd_full_body(dte_ref, dtx_ref, wide_ref, read_ref, rate_ref, start_ref, y_ref, hist_ref, h_ref):
    block = dte_ref.shape[0]
    n, width = rate_ref.shape
    span = GROUP * n
    rate = rate_ref[...]

    @pl.when(pl.program_id(2) == 0)
    def _():
        h_ref[...] = start_ref[...]

    first = h_ref[...]
    hist_ref[pl.ds(0, n), :] = first.astype(jnp.bfloat16)

    def group(at, state):
        for place in range(GROUP):
            t = at * GROUP + place
            write = across(wide_ref[pl.ds(t * n, n), :], width)
            state = jnp.exp2(dte_ref[pl.ds(t, 1), :] * rate) * state + dtx_ref[pl.ds(t, 1), :] * write
            hist_ref[pl.ds((t + 1) * n, n), :] = state.astype(jnp.bfloat16)
        y_ref[pl.ds(at * GROUP, GROUP), :] = jnp.dot(
            read_ref[pl.ds(at * GROUP, GROUP), :],
            hist_ref[pl.ds(n + at * span, span), :],
            preferred_element_type=jnp.float32,
        )
        return state

    h_ref[...] = lax.fori_loop(0, block // GROUP, group, first)


def fwd_full(dte, dtx, wide, read, rate, start, seqs, width=1024, block=128):
    tokens, chans = dte.shape
    n = rate.shape[0]
    width = min(width, chans)
    blocks = tokens // seqs // block
    work = tokens * chans * n
    here = lambda c, s, t: (s * blocks + t, c)
    rows = lambda c, s, t: (s * blocks + t, 0)
    return pl.pallas_call(
        fwd_full_body,
        grid=(chans // width, seqs, blocks),
        in_specs=[
            pl.BlockSpec((block, width), here),
            pl.BlockSpec((block, width), here),
            pl.BlockSpec((block * n, wide.shape[1]), rows),
            pl.BlockSpec((block, read.shape[1]), rows),
            pl.BlockSpec((n, width), lambda c, s, t: (0, c)),
            pl.BlockSpec((n, width), lambda c, s, t: (s, c)),
        ],
        out_specs=[pl.BlockSpec((block, width), here), pl.BlockSpec(((block + 1) * n, width), here)],
        out_shape=[
            jax.ShapeDtypeStruct((tokens, chans), jnp.float32),
            jax.ShapeDtypeStruct((seqs * blocks * (block + 1) * n, chans), jnp.bfloat16),
        ],
        scratch_shapes=[pltpu.VMEM((n, width), jnp.float32)],
        compiler_params=pltpu.CompilerParams(vmem_limit_bytes=VMEM_LIMIT),
        cost_estimate=pl.CostEstimate(flops=8 * work, transcendentals=work, bytes_accessed=2 * work),
        name="fwd_full",
    )(dte, dtx, wide, read, rate, start)


def bwd_full_body(dte_ref, dtx_ref, grad_ref, hist_ref, wide_ref, write_ref, ones_ref, rate_ref, start_ref,
                  s1_ref, s2_ref, grate_ref, dw_ref, dr_ref, g_ref, adj_ref, r_ref):
    block = dte_ref.shape[0]
    n, width = rate_ref.shape
    span = GROUP * n
    rate = rate_ref[...]
    groups = block // GROUP
    bf = jnp.bfloat16

    @pl.when(pl.program_id(2) == 0)
    def _():
        g_ref[...] = start_ref[...]

    @pl.when((pl.program_id(2) == 0) & (pl.program_id(1) == 0))
    def _():
        grate_ref[...] = jnp.zeros_like(grate_ref)

    def group(step, state):
        at = groups - 1 - step
        for place in reversed(range(GROUP)):
            t = at * GROUP + place
            read = across(wide_ref[pl.ds(t * n, n), :], width)
            power = dte_ref[pl.ds(t, 1), :] * rate
            adjoint = state + grad_ref[pl.ds(t, 1), :] * read
            state = jnp.exp2(power) * adjoint
            adj_ref[pl.ds(place * n, n), :] = adjoint.astype(bf)
            r_ref[pl.ds(place * n, n), :] = state.astype(bf) * hist_ref[pl.ds(t * n, n), :] * power.astype(bf)
        rows = pl.ds(at * GROUP, GROUP)
        adj_all = adj_ref[...]
        s1_ref[rows, :] = jnp.dot(write_ref[rows, :], adj_all, preferred_element_type=jnp.float32)
        sums = jnp.dot(ones_ref[...], r_ref[...], preferred_element_type=jnp.float32)
        s2_ref[rows, :] = sums[:GROUP]
        grate_ref[...] += sums[GROUP:]
        dw_ref[rows, :] = lax.dot_general(
            dtx_ref[rows, :].astype(bf), adj_all, NT, preferred_element_type=jnp.float32)
        dr_ref[rows, :] = lax.dot_general(
            grad_ref[rows, :].astype(bf), hist_ref[pl.ds(n + at * span, span), :], NT,
            preferred_element_type=jnp.float32)
        return state

    g_ref[...] = lax.fori_loop(0, groups, group, g_ref[...])


def bwd_full(dte, dtx, grad, hist, wide, write, rate, start, seqs, width=1024, block=128):
    tokens, chans = dte.shape
    n = rate.shape[0]
    width = min(width, chans)
    strips = chans // width
    blocks = tokens // seqs // block
    span = GROUP * n
    work = tokens * chans * n
    column = jnp.arange(span)
    ones = jnp.concatenate(
        [(column // n)[None, :] == jnp.arange(GROUP)[:, None], (column % n)[None, :] == jnp.arange(n)[:, None]]
    ).astype(jnp.bfloat16)
    here = lambda c, s, t: (s * blocks + blocks - 1 - t, c)
    rows = lambda c, s, t: (s * blocks + blocks - 1 - t, 0)
    strip = lambda c, s, t: (c * seqs * blocks + s * blocks + blocks - 1 - t, 0)
    f32 = jnp.float32
    s1, s2, grate, dw, dr = pl.pallas_call(
        bwd_full_body,
        grid=(strips, seqs, blocks),
        in_specs=[
            pl.BlockSpec((block, width), here),
            pl.BlockSpec((block, width), here),
            pl.BlockSpec((block, width), here),
            pl.BlockSpec(((block + 1) * n, width), here),
            pl.BlockSpec((block * n, wide.shape[1]), rows),
            pl.BlockSpec((block, span), rows),
            pl.BlockSpec(ones.shape, lambda c, s, t: (0, 0)),
            pl.BlockSpec((n, width), lambda c, s, t: (0, c)),
            pl.BlockSpec((n, width), lambda c, s, t: (s, c)),
        ],
        out_specs=[
            pl.BlockSpec((block, width), here),
            pl.BlockSpec((block, width), here),
            pl.BlockSpec((n, width), lambda c, s, t: (0, c)),
            pl.BlockSpec((block, span), strip),
            pl.BlockSpec((block, span), strip),
        ],
        out_shape=[
            jax.ShapeDtypeStruct((tokens, chans), f32),
            jax.ShapeDtypeStruct((tokens, chans), f32),
            jax.ShapeDtypeStruct((n, chans), f32),
            jax.ShapeDtypeStruct((strips * tokens, span), f32),
            jax.ShapeDtypeStruct((strips * tokens, span), f32),
        ],
        scratch_shapes=[
            pltpu.VMEM((n, width), f32),
            pltpu.VMEM((span, width), jnp.bfloat16),
            pltpu.VMEM((span, width), jnp.bfloat16),
        ],
        compiler_params=pltpu.CompilerParams(vmem_limit_bytes=VMEM_LIMIT),
        cost_estimate=pl.CostEstimate(flops=14 * work, transcendentals=work, bytes_accessed=2 * work),
        name="bwd_full",
    )(dte, dtx, grad, hist, wide, write, ones, rate, start)
    return s1, s2, grate, diagonal(dw.reshape(strips, tokens, span).sum(0), n), diagonal(
        dr.reshape(strips, tokens, span).sum(0), n)


def widen(values):
    return jnp.broadcast_to(values.reshape(-1)[:, None], (values.size, 128))


def spread(values):
    tokens, n = values.shape
    own = jnp.arange(tokens)[:, None] % GROUP == jnp.arange(GROUP)[None, :]
    return jnp.where(own[:, :, None], values[:, None, :], 0).reshape(tokens, GROUP * n).astype(jnp.bfloat16)


def diagonal(sums, n):
    tokens = sums.shape[0]
    own = jnp.arange(tokens)[:, None] % GROUP == jnp.arange(GROUP)[None, :]
    return jnp.sum(jnp.where(own[:, :, None], sums.reshape(tokens, GROUP, n), 0), axis=1)


MESH = pl.DeviceIdType.MESH


class Grid:
    def __init__(self, axis, size, inner):
        self.axis, self.inner, self.outer = axis, inner, size // inner
        me = lax.axis_index(axis)
        self.row, self.col = me // inner, me % inner

    def device(self, row, col):
        return {self.axis: row * self.inner + col}

    def neighbours(self):
        row, col = self.row, self.col
        found = []
        if self.outer > 1:
            found += [(row > 0, self.device(row - 1, col)), (row < self.outer - 1, self.device(row + 1, col))]
        if self.inner > 1:
            found += [(col > 0, self.device(row, col - 1)), (col < self.inner - 1, self.device(row, col + 1))]
        return found


def greet(grids):
    barrier = pltpu.get_barrier_semaphore()
    count = 0
    for grid in grids:
        for there, device in grid.neighbours():

            @pl.when(there)
            def _(device=device):
                pl.semaphore_signal(barrier, inc=1, device_id=device, device_id_type=MESH)

            count = count + there.astype(jnp.int32)
    pl.semaphore_wait(barrier, count)


def gather_steps(grid, whole_ref, out_ref, send_sem, recv_sem, own_sem, waits, chunk, chunks):
    rows = whole_ref.shape[0]
    part = rows // chunks
    src_ref = whole_ref.at[pl.ds(chunk * part, part)]
    outer, inner = grid.outer, grid.inner
    row, col = grid.row, grid.col

    def place(r, c):
        return pl.ds(pl.multiple_of((r * inner + c) * rows + chunk * part, part), part)

    def send(there, way, r, c, device, source):
        copy = pltpu.make_async_remote_copy(
            src_ref=source, dst_ref=out_ref.at[place(r, c)], send_sem=send_sem.at[way, r * inner + c],
            recv_sem=recv_sem.at[r * inner + c], device_id=device, device_id_type=MESH)

        @pl.when(there)
        def _():
            copy.start()

        waits.append((there, copy))

    def across(there, r, c, source):
        if inner > 1:
            send(there & (c >= col) & (col > 0), 2, r, c, grid.device(row, col - 1), source)
            send(there & (c <= col) & (col < inner - 1), 3, r, c, grid.device(row, col + 1), source)

    def along(there, r, source):
        if outer > 1:
            send(there & (r >= row) & (row > 0), 0, r, col, grid.device(row - 1, col), source)
            send(there & (r <= row) & (row < outer - 1), 1, r, col, grid.device(row + 1, col), source)

    def arrive(there, r, c):
        copy = pltpu.make_async_remote_copy(
            src_ref=src_ref, dst_ref=out_ref.at[place(r, c)], send_sem=send_sem.at[0, 0],
            recv_sem=recv_sem.at[r * inner + c], device_id=grid.device(row, col), device_id_type=MESH)

        @pl.when(there)
        def _():
            copy.wait_recv()

    always = row >= 0
    along(always, row, src_ref)
    across(always, row, col, src_ref)
    own = pltpu.make_async_copy(src_ref, out_ref.at[place(row, col)], own_sem)
    own.start()
    waits.append((None, own))
    for _ in range(chunk + 1):
        yield
    for distance in range(1, outer):
        for r in (row - distance, row + distance):
            there = (r >= 0) & (r < outer)
            arrive(there, r, col)
            along(there, r, out_ref.at[place(r, col)])
            across(there, r, col, out_ref.at[place(r, col)])
        yield
    for step in range(1, inner):
        for distance in range(outer):
            for r in (row - distance, row + distance) if distance else (row,):
                for c in (col - step, col + step):
                    there = (r >= 0) & (r < outer) & (c >= 0) & (c < inner)
                    arrive(there, r, c)
                    if step < inner - 1:
                        across(there, r, c, out_ref.at[place(r, c)])
            yield


def finish(waits):
    for there, copy in waits:
        if there is None:
            copy.wait()
        else:

            @pl.when(there)
            def _(copy=copy):
                copy.wait_send()


def in_turn(runs):
    runs = list(runs)
    while runs:
        left = []
        for run in runs:
            if next(run, run) is not run:
                left.append(run)
        runs = left


def link_gather(arrays, sizes, collective_id):
    count = len(arrays)
    axes = sorted({entry[0] for entry in arrays})

    def kernel(*refs):
        sources, outs, sems = refs[:count], refs[count : 2 * count], refs[2 * count :]
        grids = {axis: Grid(axis, *sizes[axis]) for axis in axes}
        greet([grids[axis] for axis in axes])
        waits = []
        runs = []
        for i, (axis, _, chunks) in enumerate(arrays):
            for chunk in range(chunks):
                runs.append(gather_steps(grids[axis], sources[i], outs[i], *sems[:3], waits, chunk, chunks))
                sems = sems[3:]
        in_turn(runs)
        finish(waits)

    sems = []
    for axis, _, chunks in arrays:
        size = sizes[axis][0]
        sems += [pltpu.SemaphoreType.DMA((4, size)), pltpu.SemaphoreType.DMA((size,)), pltpu.SemaphoreType.DMA] * chunks
    return pl.pallas_call(
        kernel,
        in_specs=[pl.BlockSpec(memory_space=pl.ANY)] * count,
        out_specs=[pl.BlockSpec(memory_space=pl.ANY)] * count,
        out_shape=[
            jax.ShapeDtypeStruct((sizes[axis][0] * a.shape[0], *a.shape[1:]), a.dtype) for axis, a, _ in arrays],
        scratch_shapes=sems,
        compiler_params=pltpu.CompilerParams(collective_id=collective_id, has_side_effects=True),
        name="link_gather",
    )(*[a for _, a, _ in arrays])


def reduce_steps(grid, src_ref, out_ref, acc, inner_buf, outer_buf, sems, waits, chunk, chunks):
    outer, inner = grid.outer, grid.inner
    row, col = grid.row, grid.col
    rows, part = acc.shape[0] // (outer * inner), acc.shape[0] // (outer * inner * chunks)
    piece = min(part, 64)
    load_sem, inner_send, inner_recv, outer_send, outer_recv, out_sem = sems

    def place(r, c):
        return pl.ds(pl.multiple_of((r * inner + c) * rows + chunk * part, part), part)

    def add(r, c, buf):
        start = (r * inner + c) * rows + chunk * part

        @pl.loop(0, part // piece)
        def _(k):
            here = pl.ds(pl.multiple_of(start + k * piece, piece), piece)
            there = pl.ds(pl.multiple_of(k * piece, piece), piece)
            acc[here, :] = (acc[here, :].astype(jnp.float32) + buf[there, :].astype(jnp.float32)).astype(acc.dtype)

    def line(me, size, device, block, buf, send, recv):
        def hop(there, target, onward, slot):
            copy = pltpu.make_async_remote_copy(
                src_ref=acc.at[place(*block(target))], dst_ref=buf.at[slot], send_sem=send.at[target],
                recv_sem=recv.at[slot], device_id=device(onward), device_id_type=MESH)

            @pl.when(there)
            def _():
                copy.start()

            waits.append((there, copy))

        def from_low(target):
            return target if size > 2 else 0

        def from_high(target, owner):
            return jnp.where(target == owner, size, target) if size > 2 else 0

        def up(there, target):
            hop(there & (target > me), target, me + 1, from_low(target))

        def down(there, target):
            hop(there & (target < me), target, me - 1, from_high(target, me - 1))

        def arrive(there, target, slot):
            copy = pltpu.make_async_remote_copy(
                src_ref=acc.at[place(*block(target))], dst_ref=buf.at[slot], send_sem=send.at[target],
                recv_sem=recv.at[slot], device_id=device(me), device_id_type=MESH)

            @pl.when(there)
            def _():
                copy.wait_recv()
                add(*block(target), buf.at[slot])

        def begin(target):
            up(me == 0, target)
            down(me == size - 1, target)

        def go_on(target):
            arrive((me > 0) & (target >= me), target, from_low(target))
            arrive((me < size - 1) & (target <= me), target, from_high(target, me))
            up((me > 0) & (me < size - 1), target)
            down((me > 0) & (me < size - 1), target)

        return begin, go_on

    order = sorted(range(outer), key=lambda k: -abs(2 * k - outer + 1))
    lines = {}
    for r in order:
        loads = []
        for c in range(inner):
            load = pltpu.make_async_copy(src_ref.at[place(r, c)], acc.at[place(r, c)], load_sem.at[r * inner + c])
            load.start()
            loads.append(load)
        lines[r] = (loads, line(
            col, inner, lambda c: grid.device(row, c), lambda t, r=r: (r, t), inner_buf.at[r], inner_send.at[r],
            inner_recv.at[r]))
    for r in order:
        loads, (begin, _) = lines[r]
        for load in loads:
            load.wait()
        if inner > 1:
            for c in range(inner):
                begin(c)
    for _ in range(chunk + 1):
        yield
    begin_outer, go_on_outer = line(
        row, outer, lambda r: grid.device(r, col), lambda t: (t, col), outer_buf, outer_send, outer_recv)
    for r in order:
        if inner > 1:
            for c in range(inner):
                lines[r][1][1](c)
        if outer > 1:
            begin_outer(r)
        yield
    if outer > 1:
        for r in order:
            go_on_outer(r)
            yield
    last = pltpu.make_async_copy(acc.at[place(row, col)], out_ref.at[pl.ds(chunk * part, part)], out_sem)
    last.start()
    waits.append((None, last))


def link_reduce(arrays, sizes, collective_id):
    count = len(arrays)
    axes = sorted({entry[0] for entry in arrays})

    def kernel(*refs):
        sources, outs, scratch = refs[:count], refs[count : 2 * count], refs[2 * count :]
        grids = {axis: Grid(axis, *sizes[axis]) for axis in axes}
        greet([grids[axis] for axis in axes])
        waits = []
        runs = []
        for i, (axis, _, chunks) in enumerate(arrays):
            acc, scratch = scratch[0], scratch[1:]
            for chunk in range(chunks):
                inner_buf, outer_buf, sems, scratch = scratch[0], scratch[1], scratch[2:8], scratch[8:]
                runs.append(
                    reduce_steps(grids[axis], sources[i], outs[i], acc, inner_buf, outer_buf, sems, waits, chunk, chunks))
        in_turn(runs)
        finish(waits)

    scratch, shapes = [], []
    for axis, a, chunks in arrays:
        size, inner = sizes[axis]
        outer = size // inner
        part = a.shape[0] // size // chunks
        slots = [n + 1 if n > 2 else 1 for n in (inner, outer)]
        dma = pltpu.SemaphoreType.DMA
        shapes.append(jax.ShapeDtypeStruct((a.shape[0] // size, a.shape[1]), a.dtype))
        scratch.append(pltpu.VMEM(a.shape, a.dtype))
        for _ in range(chunks):
            scratch += [
                pltpu.VMEM((outer, slots[0], part, a.shape[1]), a.dtype),
                pltpu.VMEM((slots[1], part, a.shape[1]), a.dtype),
                dma((size,)), dma((outer, inner)), dma((outer, slots[0])), dma((outer,)), dma((slots[1],)), dma]
    return pl.pallas_call(
        kernel,
        in_specs=[pl.BlockSpec(memory_space=pl.ANY)] * count,
        out_specs=[pl.BlockSpec(memory_space=pl.ANY)] * count,
        out_shape=shapes,
        scratch_shapes=scratch,
        compiler_params=pltpu.CompilerParams(
            collective_id=collective_id, has_side_effects=True, vmem_limit_bytes=VMEM_LIMIT),
        name="link_reduce",
    )(*[a for _, a, _ in arrays])


def passed_along(block, axis, distance):
    devices = range(lax.axis_size(axis))
    route = [(i - distance, i) for i in devices if i - distance in devices]
    return lax.ppermute(block, axis, route)


def silu_slope(values_in):
    sigmoid_v = jax.nn.sigmoid(values_in)
    return sigmoid_v * (1.0 + values_in * (1.0 - sigmoid_v))


def token_layout(lengths, first_pos, n_tokens):
    doc_ends = jnp.cumsum(lengths)
    begins = doc_ends - lengths
    positions = first_pos + jnp.arange(n_tokens, dtype=jnp.int32)
    live_slot = (lengths > 0)[None, :]
    doc_ids = jnp.sum(((begins[None, :] <= positions[:, None]) & live_slot).astype(jnp.int32), axis=1)
    start_flags = jnp.sum(((begins[None, :] == positions[:, None]) & live_slot).astype(jnp.float32), axis=1)
    valid_mask = (positions < doc_ends[-1]).astype(jnp.float32)
    return (doc_ids, start_flags, valid_mask)


def contract_rows(left_mat, right_mat):
    return lax.dot_general(left_mat, right_mat, (((0,), (0,)), ((), ())), preferred_element_type=jnp.float32)


def contract_cols(left_mat, right_mat):
    return lax.dot_general(left_mat, right_mat, NT, preferred_element_type=jnp.float32)


def padded_rows(array, rows):
    return jnp.pad(array, ((0, -array.shape[0] % rows), (0, 0)))


def shared_sum(partial, sizes, collective_id):
    width = partial.shape[1]
    sent = jnp.pad(partial.astype(jnp.bfloat16), ((0, 0), (0, -width % 128)))
    (terms,) = link_gather([("stream", sent, 2)], sizes, collective_id)
    terms = terms.reshape(-1, *sent.shape)[:, :, :width].astype(jnp.float32)
    return jnp.sum(terms, axis=0)


def carried(ends, step_sum, rate, backward, sizes, collective_id):
    seqs, chans = step_sum.shape
    n = rate.shape[0]
    high = step_sum.astype(jnp.bfloat16)
    low = (step_sum - high.astype(jnp.float32)).astype(jnp.bfloat16)
    sent = padded_rows(jnp.concatenate([ends.astype(jnp.bfloat16), high, low], axis=0), 16)
    (gathered,) = link_gather([("seq", sent, 1)], sizes, collective_id)
    gathered = gathered.reshape(-1, *sent.shape)
    count = lax.axis_size("seq")
    place = lax.axis_index("seq")
    state = jnp.zeros((seqs, n, chans), jnp.float32)
    for step in range(count - 1):
        source = count - 1 - step if backward else step
        block = gathered[source].astype(jnp.float32)
        total = block[seqs * n : seqs * (n + 1)] + block[seqs * (n + 1) : seqs * (n + 2)]
        joined = jnp.exp2(total[:, None, :] * rate[None]) * state + block[: seqs * n].reshape(seqs, n, chans)
        state = jnp.where(source > place if backward else source < place, joined, state)
    return state.reshape(seqs * n, chans)


def local(sizes, resid_in, out_grad, row_lengths, norm_gain, in_weight, conv_weight, conv_bias, xproj_weight, dt_weight,
          dt_bias, a_log, skip_gain, out_weight):
    bf, f32 = jnp.bfloat16, jnp.float32
    seqs = lax.axis_size("stream")
    parts = lax.axis_size("seq")
    own = conv_bias.shape[0]
    own_feats = norm_gain.shape[0]
    chans = own * parts
    rank_dim = dt_weight.shape[0]
    state_dim = a_log.shape[1]
    proj_dim = xproj_weight.shape[1]
    length, feats = resid_in.shape[1:]
    tokens = seqs * length

    gain = norm_gain.astype(f32)
    scaled = (in_weight.astype(f32) * gain[:, None]).astype(bf).reshape(own_feats, 2, parts, seqs, own)
    scaled = scaled.transpose(3, 0, 1, 2, 4).reshape(seqs, own_feats, 2, chans)

    mine = lax.all_to_all(scaled.reshape(seqs * own_feats, 2 * chans), "stream", 0, 0, tiled=True)
    packed = jnp.concatenate(
        [xproj_weight, dt_weight.T, a_log, conv_weight.T, conv_bias[:, None], dt_bias[:, None], skip_gain[:, None]],
        axis=1)
    residual = resid_in[0].astype(f32)
    cotangent = out_grad[0]
    inv_rms = lax.rsqrt(jnp.mean(residual * residual, axis=-1, keepdims=True) + EPSILON)
    unit_own = residual * inv_rms
    slots = row_lengths.shape[1]
    in_conv, packed, unit, lengths = link_gather(
        [("seq", mine[:, :chans], 1), ("seq", jnp.pad(packed, ((0, 0), (0, -packed.shape[1] % 128))), 1),
         ("stream", unit_own.astype(bf), 4), ("stream", jnp.pad(row_lengths, ((0, 7), (0, -slots % 128))), 1)],
        sizes, 1)
    lengths = lengths[::8, :slots]
    in_gate = lax.all_gather(mine[:, chans:], "seq", axis=0, tiled=True)
    out_full = lax.all_gather(out_weight, "seq", axis=0, tiled=True)
    cot_all = lax.all_gather(cotangent, "stream", axis=0, tiled=True)
    xproj_full = packed[:, :proj_dim]
    dtw_cols = packed[:, proj_dim : proj_dim + rank_dim]
    at = proj_dim + rank_dim
    log_rates = packed[:, at : at + state_dim].astype(f32).T
    at += state_dim
    conv_taps = packed[:, at : at + CONV].astype(f32).T
    at += CONV
    conv_shift, dt_shift, skip_vec = (packed[:, at + i].astype(f32) for i in range(3))
    rate = -jnp.exp(log_rates) / LN2

    rim = CONV - 1
    first_pos = lax.axis_index("seq") * length
    doc_ids, start_flags, valid_mask = jax.vmap(
        lambda row: token_layout(row, first_pos - rim, length + 2 * rim))(lengths)
    own_ids = doc_ids[:, rim : rim + length]
    starts = start_flags[:, rim : rim + length].reshape(tokens, 1)
    valid = valid_mask[:, rim : rim + length].reshape(tokens, 1)
    matches = [(doc_ids[:, tap : tap + length] == own_ids).astype(f32)[:, :, None] for tap in range(CONV)]

    conv_in = jnp.dot(unit, in_conv, preferred_element_type=f32).reshape(seqs, length, chans)
    gate_in = jnp.dot(unit, in_gate, preferred_element_type=f32)
    earlier = passed_along(conv_in[:, length - rim :].astype(bf), "seq", 1).astype(f32)
    padded = jnp.concatenate([earlier, conv_in], axis=1)
    conv_out = conv_shift
    for tap in range(CONV):
        conv_out = conv_out + conv_taps[tap] * padded[:, tap : tap + length] * matches[tap]
    activated = jax.nn.silu(conv_out).astype(bf).reshape(tokens, chans)
    act_float = activated.astype(f32)
    projected = shared_sum(jnp.dot(activated, xproj_full, preferred_element_type=f32), sizes, 2)
    low_rank = projected[:, :rank_dim].astype(bf)
    write_in = projected[:, rank_dim : rank_dim + state_dim]
    readout = projected[:, rank_dim + state_dim :]
    dt_pre = contract_cols(low_rank, dtw_cols) + dt_shift
    dt_step = jax.nn.softplus(dt_pre)
    dt_reset = jnp.where(starts > 0, RESET, dt_step)
    dt_act = dt_step * act_float
    write_wide, read_wide = widen(write_in), widen(readout)
    write_diag, read_diag = spread(write_in), spread(readout)

    step_sum = jnp.sum(dt_reset.reshape(seqs, length, chans), axis=1)
    ends = scan_end(fwd_end_body, dt_reset, dt_act, write_wide, rate, seqs)
    start_state = carried(ends, step_sum, rate, False, sizes, 3)
    scanned, history = fwd_full(dt_reset, dt_act, write_wide, read_diag, rate, start_state, seqs)
    ssm_out = scanned + skip_vec * act_float
    gate_act = jax.nn.silu(gate_in)
    gated = (ssm_out * gate_act * valid).astype(bf)
    product = jnp.dot(gated, out_full, preferred_element_type=f32).astype(bf)
    output = (residual + lax.psum_scatter(product, "stream", scatter_dimension=0, tiled=True).astype(f32)).astype(bf)

    d_gated = contract_cols(cot_all, out_full)
    g_out = lax.psum_scatter(contract_rows(gated, cot_all).astype(bf), "seq", scatter_dimension=0, tiled=True)
    d_masked = d_gated * valid
    d_ssm = d_masked * gate_act
    d_gate = (d_masked * ssm_out * silu_slope(gate_in)).astype(bf)
    g_in_gate = lax.psum_scatter(contract_rows(unit, d_gate).astype(bf), "seq", scatter_dimension=0, tiled=True)
    g_skip = jnp.sum(d_ssm * act_float, axis=0)
    back_ends = scan_end(bwd_end_body, dt_reset, d_ssm, read_wide, rate, seqs)
    later_sum = carried(back_ends, step_sum, rate, True, sizes, 4)
    sum_write, sum_rate, g_log, d_write, d_read = bwd_full(
        dt_reset, dt_act, d_ssm, history, read_wide, write_diag, rate, later_sum, seqs)
    per_step = jnp.where(dt_step > 1e-30, sum_rate * LN2 / jnp.maximum(dt_step, 1e-30), 0.0)
    d_step = per_step + act_float * sum_write
    d_pre = d_step * jax.nn.sigmoid(dt_pre)
    g_dt_bias = jnp.sum(d_pre, axis=0)
    d_pre_low = d_pre.astype(bf)
    g_dt = contract_rows(d_pre_low, low_rank)
    d_low = jnp.dot(d_pre_low, dtw_cols, preferred_element_type=f32)
    d_proj = shared_sum(jnp.concatenate([d_low, d_write, d_read], axis=1), sizes, 5).astype(bf)
    g_xproj = contract_rows(activated, d_proj)
    d_act = dt_step * sum_write + skip_vec * d_ssm + contract_cols(d_proj, xproj_full)
    d_conv = d_act.reshape(seqs, length, chans) * silu_slope(conv_out)
    g_conv_bias = jnp.sum(d_conv, axis=(0, 1))
    g_conv = jnp.stack(
        [jnp.sum(d_conv * padded[:, tap : tap + length] * matches[tap], axis=(0, 1)) for tap in range(CONV)], axis=1)
    later = passed_along(d_conv[:, :rim].astype(bf), "seq", -1).astype(f32)
    d_ext = jnp.concatenate([d_conv, later], axis=1)
    d_conv_in = jnp.zeros_like(d_conv)
    for tap in range(CONV):
        offset = rim - tap
        match_back = (doc_ids[:, rim + offset : rim + offset + length] == own_ids).astype(f32)[:, :, None]
        d_conv_in = d_conv_in + conv_taps[tap] * d_ext[:, offset : offset + length] * match_back
    d_conv_in = d_conv_in.astype(bf).reshape(tokens, chans)
    g_in_conv = contract_rows(unit, d_conv_in).astype(bf)
    d_unit = (contract_cols(d_conv_in, in_conv) + contract_cols(d_gate, in_gate)).astype(bf)
    small = jnp.concatenate(
        [g_xproj, g_dt, g_log.T * LN2, g_conv, g_conv_bias[:, None], g_dt_bias[:, None], g_skip[:, None]], axis=1)
    small = jnp.pad(small, ((0, 0), (0, -small.shape[1] % 128))).astype(bf)
    g_in_conv, small, d_unit = link_reduce(
        [("seq", g_in_conv, 1), ("seq", small, 1), ("stream", d_unit, 4)], sizes, 6)
    small = small.astype(f32)
    d_unit = d_unit.astype(f32)
    in_grad = cotangent.astype(f32) + inv_rms * (d_unit - unit_own * jnp.mean(d_unit * unit_own, axis=-1, keepdims=True))

    def in_rows(block):
        shared = lax.all_to_all(block, "stream", 0, 0, tiled=True).reshape(seqs, own_feats, 2 * parts, own)
        return shared.transpose(1, 2, 0, 3).reshape(own_feats, 2 * parts * seqs * own).astype(f32)

    g_unit = in_rows(jnp.stack([g_in_conv, g_in_gate], axis=1).reshape(g_in_conv.shape[0], 2 * chans))
    at = proj_dim + rank_dim
    return (
        output[None],
        in_grad.astype(bf)[None],
        jnp.sum(g_unit * in_weight.astype(f32), axis=1),
        g_unit * gain[:, None],
        small[:, at + state_dim : at + state_dim + CONV].T,
        small[:, at + state_dim + CONV],
        small[:, :proj_dim],
        small[:, proj_dim:at].T,
        small[:, at + state_dim + CONV + 1],
        small[:, at : at + state_dim],
        small[:, at + state_dim + CONV + 2],
        g_out.astype(f32),
    )


def lines_of(mesh):
    devices = mesh.devices
    places = [getattr(device, "coords", None) for device in devices[:, 0]]
    seq = len(places)
    plane = 1
    if all(place is not None for place in places):
        plane = len({tuple(place)[1] for place in places})
    if seq % plane:
        plane = 1
    return {"seq": (seq, plane), "stream": (devices.shape[1], 1 if devices.shape[1] % 2 else 2)}


def solution(mesh):
    in_specs = (
        P("stream", "seq", None),
        P("stream", "seq", None),
        P("stream", None),
        P(("seq", "stream")),
        P(("seq", "stream"), None),
        P(None, ("seq", "stream")),
        P(("seq", "stream")),
        P(("seq", "stream"), None),
        P(None, ("seq", "stream")),
        P(("seq", "stream")),
        P(("seq", "stream"), None),
        P(("seq", "stream")),
        P(("seq", "stream"), None),
    )
    out_specs = (
        P("stream", "seq", None),
        P("stream", "seq", None),
        P(("seq", "stream")),
        P(("seq", "stream"), None),
        P(None, ("seq", "stream")),
        P(("seq", "stream")),
        P(("seq", "stream"), None),
        P(None, ("seq", "stream")),
        P(("seq", "stream")),
        P(("seq", "stream"), None),
        P(("seq", "stream")),
        P(("seq", "stream"), None),
    )
    return jax.shard_map(functools.partial(local, lines_of(mesh)), mesh=mesh, in_specs=in_specs, out_specs=out_specs, check_vma=False)
```

time: 1630 us -> 996 us (0.61)
  waiting for transfers between devices: 1070 us -> 9.44 us
  Pallas kernels: 222 us -> 551 us
  local copies, waits for them, and re-layouts: 42.7 us -> 90.8 us
  other arithmetic: 71.9 us -> 117 us
  matrix products: 204 us -> 171 us
  starting transfers between devices: 5.69 us -> 29.4 us
    reduce_scatter x4 -> x3, waiting for transfers between devices: 625 us -> 0.04 us  [the longest x1 0.02 us: local(): lax.psum_scatter(contract_rows(gated, cot_all).astype(bf), 'seq', scatter...]
    all_gather x6 -> x3, waiting for transfers between devices: 442 us -> 0.02 us  [the longest x1 0.01 us: local(): cot_all = lax.all_gather(cotangent, 'stream', axis=0, tiled=True)]
    pallas_call x4 -> x10, Pallas kernels: 222 us -> 551 us  [the longest x5 211 us: link_gather(): pl.pallas_call(kernel, in_specs=[pl.BlockSpec(memory_space=pl.ANY)] * cou...]
    broadcast_in_dim x5 -> x10, local copies, waits for them, and re-layouts: 3.19 us -> 32.5 us  [the longest x4 31.5 us: widen(): return jnp.broadcast_to(values.reshape(-1)[:, None], (values.size, 128))]
    dot_general x5, matrix products: 86.9 us -> 62.5 us  [contract_cols(): lax.dot_general(left_mat, right_mat, NT, preferred_element_type=jnp.float32)]
    all_to_all x0 -> x2, starting transfers between devices: none -> 23 us  [the longest x1 18.7 us: in_rows(): lax.all_to_all(block, 'stream', 0, 0, tiled=True)]
    reduce_sum x2 -> x6, other arithmetic: 2.19 us -> 24.2 us  [the longest x1 13.2 us: local(): g_conv_bias = jnp.sum(d_conv, axis=(0, 1))]
    convert_element_type x9 -> x11, other arithmetic: 25.7 us -> 44.3 us  [the longest x1 18.7 us: local(): activated = jax.nn.silu(conv_out).astype(bf).reshape(tokens, chans)]
  transfers between devices with their start and end apart: 12 -> 10, of which waited for: 10 -> 1; matrix products, arithmetic and copies ran while one was open for 8% -> 33% of each run, Pallas kernels for 0% -> 56%
where the time goes in v2:
time: 996 us; the launch traced here: 984 us
  Pallas kernels  551 us (55%)
  matrix products  171 us (17%)
  other arithmetic  117 us (12%)
  local copies, waits for them, and re-layouts  90.8 us (9%)
  starting transfers between devices  29.4 us (3%)
  between operations  15.6 us (2%)
    pallas_call x5, Pallas kernels, link_gather(): pl.pallas_call(kernel, in_specs=[pl.BlockSpec(memory_space=pl.ANY)] * cou...  211 us
    pallas_call x1, Pallas kernels, link_reduce(): pl.pallas_call(kernel, in_specs=[pl.BlockSpec(memory_space=pl.ANY)] * cou...  118 us
    pallas_call x1, Pallas kernels, bwd_full(): pl.pallas_call(bwd_full_body, grid=(strips, seqs, blocks), in_specs=[pl.B...  107 us
    dot_general x5, matrix products, contract_cols(): lax.dot_general(left_mat, right_mat, NT, preferred_element_type=jnp.float32)  62.5 us
    pallas_call x1, Pallas kernels, fwd_full(): pl.pallas_call(fwd_full_body, grid=(chans // width, seqs, blocks), in_spe...  57.9 us
    pallas_call x2, Pallas kernels, scan_end(): pl.pallas_call(body, grid=(seqs, chans // width), in_specs=[pl.BlockSpec(...  56.1 us
    dot_general x5, matrix products, contract_rows(): lax.dot_general(left_mat, right_mat, (((0,), (0,)), ((), ())), preferred_...  48.7 us
    broadcast_in_dim x4, local copies, waits for them, and re-layouts, widen(): return jnp.broadcast_to(values.reshape(-1)[:, None], (values.size, 128))  31.5 us
  transfers between devices with their start and end apart: 10, of which 1 were waited for; matrix products, arithmetic and copies ran while one was open for 33% of the time, Pallas kernels for 56%

profile of v2, /device:TPU:19, one launch (start us, length us, event | category | flops | bytes accessed | tf_op | source)
XLA Modules:
  0.0 983.5 jit_solution(1778829421761517193)
XLA Ops:
  24.1 7.9 all-to-all-done
  33.1 86.7 %link_gather.5 = (bf16[2048,1024]{1,0:T(8,128)(2,1)}, bf16[1024,384]{1,0:T(8,128)(2,1)}, bf16[2048,2048]{1,0:T(8,128)(2,1)}, s32[32,128]{1,0:T(8,128)}) custom-call(bf16[256,1024]{1,0:T(8,128)(2,1)} %get-tuple-element.168.refs_0_, bf16[128,384]{1,0:T(8,128)(2,1)} %pad.27.refs_1_, bf16[512,2048]{1,0:T(8,128)(2,1)} %fusion.25.refs_2_, s32[8,128]{1,0:T(8,128)} %pad.28.refs_3_), custom_call_target="tpu_custom_call" | custom-call | tf_op jit(solution)/shard_map/link_gather/pallas_call | solution.py:395
  122.3 14.0 %fusion.86 = f32[2048,1024]{1,0:T(8,128)S(1)} fusion(bf16[2048,2048]{1,0:T(8,128)(2,1)} %get-tuple-element.28, bf16[2048,1024]{1,0:T(8,128)(2,1)} %get-tuple-element.29), kind=kOutput, calls=%fused_computation.247 | convolution fusion | flops 8589934592 | bytes 20971520 | tf_op jit(solution)/shard_map/dot_general | solution.py:671
  146.9 18.7 %multiply_convert_fusion.2 = (bf16[4,512,1024]{2,1,0:T(8,128)(2,1)S(1)}, f32[4,512,1024]{2,1,0:T(8,128)}) fusion(f32[4,512,1024]{2,1,0:T(8,128)} %bitcast.237, f32[1024]{0:T(1024)S(1)} %get-tuple-element.124, f32[4,512]{1,0:T(4,128)S(1)} %get-tuple-element.187, f32[4,3,1024]{2,1,0:T(4,128)S(1)} %convert_element_type.265, f32[1024]{0:T(1024)S(1)} %get-tuple-element.125, ...), kind=kLoop, calls=%fused_computation.46 | loop fusion | flops 39845888 | bytes 21065728 | tf_op jit(solution)/shard_map/convert_element_type | solution.py:678
  170.9 34.2 %link_gather.6 = bf16[8192,256]{1,0:T(8,128)(2,1)} custom-call(bf16[2048,256]{1,0:T(8,128)(2,1)} %pad.29.refs_0_), custom_call_target="tpu_custom_call" | custom-call | tf_op jit(solution)/shard_map/link_gather/pallas_call | solution.py:395
  218.5 7.9 bitcast_reduce_fusion
  226.5 7.5 convert_multiply_fusion.3.dtx_ref
  234.0 14.8 %broadcast_in_dim.89.wide_ref = f32[32768,128]{1,0:T(8,128)} broadcast(f32[32768]{0:T(1024)S(1)} %broadcast_in_dim.88), dimensions={0} | broadcast | bytes 16908288 | tf_op jit(solution)/shard_map/broadcast_in_dim | solution.py:236
  248.9 27.9 %fwd_end.1 = f32[64,1024]{1,0:T(8,128)} custom-call(f32[2048,1024]{1,0:T(8,128)} %get-tuple-element.140.dte_ref, f32[2048,1024]{1,0:T(8,128)} %convert_multiply_fusion.3.dtx_ref, f32[32768,128]{1,0:T(8,128)} %broadcast_in_dim.89.wide_ref, f32[16,1024]{1,0:T(8,128)} %multiply_bitcast_fusion.rate_ref), custom_call_target="tpu_custom_call" | custom-call | flops 134217728 | bytes 16777216 | tf_op jit(solution)/shard_map/fwd_end/pallas_call | solution.py:58
  278.4 24.5 %link_gather.7 = bf16[640,1024]{1,0:T(8,128)(2,1)} custom-call(bf16[80,1024]{1,0:T(8,128)(2,1)} %pad.30.refs_0_), custom_call_target="tpu_custom_call" | custom-call | tf_op jit(solution)/shard_map/link_gather/pallas_call | solution.py:395
  306.0 57.9 %fwd_full.1 = (f32[2048,1024]{1,0:T(8,128)}, bf16[33024,1024]{1,0:T(8,128)(2,1)}) custom-call(f32[2048,1024]{1,0:T(8,128)} %get-tuple-element.140.dte_ref, f32[2048,1024]{1,0:T(8,128)} %convert_multiply_fusion.3.dtx_ref, f32[32768,128]{1,0:T(8,128)} %broadcast_in_dim.89.wide_ref, bf16[2048,256]{1,0:T(8,128)(2,1)} %copy.194.read_ref, ...), custom_call_target="tpu_custom_call" | custom-call | flops 268435456 | bytes 67108864 | tf_op jit(solution)/shard_map/fwd_full/pallas_call | solution.py:112
  363.9 14.6 %fusion.20 = f32[2048,1024]{1,0:T(8,128)} fusion(bf16[1024,2048]{1,0:T(8,128)(2,1)} %all-gather.7.cloned.1.call-done, bf16[1,2048,2048]{2,1,0:T(8,128)(2,1)} %all-gather.9.cloned.1.call-done), kind=kOutput, calls=%fused_computation.32 | convolution fusion | flops 8589934592 | bytes 20971520 | tf_op jit(solution)/shard_map/dot_general | solution.py:582
  378.5 26.7 %multiply_convert_fusion = (bf16[2048,1024]{1,0:T(8,128)(2,1)}, bf16[2048,1024]{1,0:T(8,128)(2,1)}, bf16[1024]{0:T(1024)(128)(2,1)}, f32[2048,1024]{1,0:T(8,128)}) fusion(f32[2048,1024]{1,0:T(8,128)} %fusion.20, f32[2048,1024]{1,0:T(8,128)} %get-tuple-element.30, f32[2048]{0:T(1024)S(1)} %bitcast.258, f32[1024]{0:T(1024)S(1)} %get-tuple-element.120, ...), kind=kOutput, calls=%fused_computation.35 | convolution fusion | flops 8633973760 | bytes 50345984 | tf_op jit(solution)/shard_map/dot_general | solution.py:672
  405.1 14.2 %convolution_convert_fusion.1 = bf16[2048,1024]{1,0:T(8,128)(2,1)} fusion(bf16[2048,2048]{1,0:T(8,128)(2,1)} %get-tuple-element.28, bf16[2048,1024]{1,0:T(8,128)(2,1)} %get-tuple-element.143), kind=kOutput, calls=%fused_computation.67 | convolution fusion | flops 8592031744 | bytes 16777216 | tf_op jit(solution)/shard_map/dot_general | solution.py:578
  419.5 14.2 %fusion.32 = bf16[1024,2048]{1,0:T(8,128)(2,1)} fusion(bf16[2048,1024]{1,0:T(8,128)(2,1)} %get-tuple-element.144, bf16[1,2048,2048]{2,1,0:T(8,128)(2,1)} %all-gather.9.cloned.1.call-done), kind=kOutput, calls=%fused_computation.66 | convolution fusion | flops 8592031744 | bytes 16777216 | tf_op jit(solution)/shard_map/dot_general | solution.py:578
  436.0 14.8 %broadcast_in_dim.99.wide_ref = f32[32768,128]{1,0:T(8,128)} broadcast(f32[32768]{0:T(1024)S(1)} %broadcast_in_dim.98), dimensions={0} | broadcast | bytes 16908288 | tf_op jit(solution)/shard_map/broadcast_in_dim | solution.py:236
  450.8 28.2 %bwd_end.1 = f32[64,1024]{1,0:T(8,128)} custom-call(f32[2048,1024]{1,0:T(8,128)} %get-tuple-element.140.dte_ref, f32[2048,1024]{1,0:T(8,128)} %get-tuple-element.146.grad_ref, f32[32768,128]{1,0:T(8,128)} %broadcast_in_dim.99.wide_ref, f32[16,1024]{1,0:T(8,128)} %multiply_bitcast_fusion.rate_ref), custom_call_target="tpu_custom_call" | custom-call | flops 134217728 | bytes 16777216 | tf_op jit(solution)/shard_map/bwd_end/pallas_call | solution.py:58
  480.7 29.1 %link_gather.8 = bf16[640,1024]{1,0:T(8,128)(2,1)} custom-call(bf16[80,1024]{1,0:T(8,128)(2,1)} %pad.31.refs_0_), custom_call_target="tpu_custom_call" | custom-call | tf_op jit(solution)/shard_map/link_gather/pallas_call | solution.py:395
  512.9 106.9 %bwd_full.1 = (f32[2048,1024]{1,0:T(8,128)}, f32[2048,1024]{1,0:T(8,128)}, f32[16,1024]{1,0:T(8,128)}, f32[2048,256]{1,0:T(8,128)}, f32[2048,256]{1,0:T(8,128)}) custom-call(f32[2048,1024]{1,0:T(8,128)} %get-tuple-element.140.dte_ref, f32[2048,1024]{1,0:T(8,128)} %convert_multiply_fusion.3.dtx_ref, f32[2048,1024]{1,0:T(8,128)} %get-tuple-element.146.grad_ref, ...), custom_call_target="tpu_custom_call" | custom-call | flops 469762048 | bytes 67108864 | tf_op jit(solution)/shard_map/bwd_full/pallas_call | solution.py:194
  624.6 14.0 %convolution_convert_fusion = bf16[2048,2048]{1,0:T(8,128)(2,1)} fusion(bf16[2048,1024]{1,0:T(8,128)(2,1)} %get-tuple-element.144, bf16[1024,2048]{1,0:T(8,128)(2,1)} %all-gather.7.cloned.1.call-done), kind=kOutput, calls=%fused_computation.50 | convolution fusion | flops 8594128896 | bytes 16777216 | tf_op jit(solution)/shard_map/dot_general | solution.py:698
  638.6 16.3 %fusion.82 = (bf16[1024]{0:T(1024)(128)(2,1)}, bf16[2048,1024]{1,0:T(8,128)(2,1)}) fusion(f32[2048,1024]{1,0:T(8,128)} %get-tuple-element.32, bf16[4,512,1024]{2,1,0:T(8,128)(2,1)} %copy-done, f32[2048,1024]{1,0:T(8,128)} %get-tuple-element.33, f32[2048,1024]{1,0:T(8,128)} %copy-done.4, f32[1024]{0:T(1024)S(1)} %copy-done.29), kind=kLoop, calls=%fused_computation.244 | loop fusion | flops 44039168 | bytes 33560576 | tf_op jit(solution)/shard_map/reduce_sum | solution.py:715
  663.2 36.9 %link_gather.9 = bf16[8192,256]{1,0:T(8,128)(2,1)} custom-call(bf16[2048,256]{1,0:T(8,128)(2,1)} %fusion.49.refs_0_), custom_call_target="tpu_custom_call" | custom-call | tf_op jit(solution)/shard_map/link_gather/pallas_call | solution.py:395
  703.1 13.9 %add_add_fusion = f32[2048,1024]{1,0:T(8,128)} fusion(f32[2048,1024]{1,0:T(8,128)} %get-tuple-element.146.grad_ref, f32[2048,1024]{1,0:T(8,128)} %get-tuple-element.32, bf16[2048,160]{1,0:T(8,128)(2,1)S(1)} %slice_reduce_fusion, f32[1024]{0:T(1024)S(1)} %copy-done.46, bf16[1024,384]{1,0:T(8,128)(2,1)S(1)} %copy-done.11, f32[2048,1024]{1,0:T(8,128)} %copy-done.4, ...), kind=kOutput, calls=%fused_computation.41 | convolution fusion | flops 694157312 | bytes 35135488 | tf_op jit(solution)/shard_map/dot_general | solution.py:582
  717.1 13.2 %fusion.81 = (bf16[1024]{0:T(1024)(128)(2,1)}, bf16[1024]{0:T(1024)(128)(2,1)}, bf16[1024]{0:T(1024)(128)(2,1)}, bf16[1024]{0:T(1024)(128)(2,1)}, bf16[1024]{0:T(1024)(128)(2,1)}, /*index=5*/f32[4,512,1024]{2,1,0:T(8,128)S(1)}) fusion(f32[2048,1024]{1,0:T(8,128)S(1)} %bitcast.239, f32[4,512]{1,0:T(4,128)} %copy-done.26, f32[4,512,1024]{2,1,0:T(8,128)S(1)} %bitcast.240, ...), kind=kLoop, calls=%fused_computation.243 | loop fusion | flops 48229376 | bytes 42027008 | tf_op jit(solution)/shard_map/reduce_sum | solution.py:723
  733.8 5.5 fusion.45
  741.1 11.9 %fusion.87 = f32[2048,2048]{1,0:T(8,128)} fusion(bf16[2048,1024]{1,0:T(8,128)(2,1)S(1)} %copy-done.62, bf16[2048,1024]{1,0:T(8,128)(2,1)S(1)} %copy-done.61), kind=kOutput, calls=%fused_computation.248 | convolution fusion | flops 8589934592 | bytes 25165824 | tf_op jit(solution)/shard_map/dot_general | solution.py:582
  761.4 17.0 %fusion.6 = bf16[4,512,1024]{2,1,0:T(8,128)(2,1)S(1)} fusion(f32[4,3,1024]{2,1,0:T(4,128)S(1)} %convert_element_type.309, f32[4,512,1024]{2,1,0:T(8,128)} %copy-done.5, f32[4,512]{1,0:T(4,128)S(1)} %copy-done.44, f32[4,512]{1,0:T(4,128)S(1)} %copy-done.43, f32[4,512]{1,0:T(4,128)S(1)} %copy-done.42, f32[1024]{0:T(1024)S(1)} %copy-done.34, ...), kind=kLoop, calls=%fused_computation.16 | loop fusion | flops 29360128 | bytes 12673024 | tf_op jit(solution)/shard_map/convert_element_type | solution.py:733
  778.5 13.1 %convolution_convert_fusion.2.refs_0_ = bf16[2048,1024]{1,0:T(8,128)(2,1)} fusion(bf16[2048,2048]{1,0:T(8,128)(2,1)} %get-tuple-element.28, bf16[2048,1024]{1,0:T(8,128)(2,1)S(1)} %bitcast.251), kind=kOutput, calls=%fused_computation.68 | convolution fusion | flops 8592031744 | bytes 16777216 | tf_op jit(solution)/shard_map/dot_general | solution.py:578
  791.6 14.2 %add_convert_fusion.refs_2_ = bf16[2048,2048]{1,0:T(8,128)(2,1)} fusion(f32[2048,2048]{1,0:T(8,128)} %fusion.87, bf16[2048,1024]{1,0:T(8,128)(2,1)S(1)} %bitcast.252, bf16[2048,1024]{1,0:T(8,128)(2,1)S(1)} %copy-done.60), kind=kOutput, calls=%fused_computation.1 | convolution fusion | flops 8598323200 | bytes 33554432 | tf_op jit(solution)/shard_map/dot_general | solution.py:582
  805.8 118.4 %link_reduce.1 = (bf16[256,1024]{1,0:T(8,128)(2,1)}, bf16[128,384]{1,0:T(8,128)(2,1)}, bf16[512,2048]{1,0:T(8,128)(2,1)}) custom-call(bf16[2048,1024]{1,0:T(8,128)(2,1)} %convolution_convert_fusion.2.refs_0_, bf16[1024,384]{1,0:T(8,128)(2,1)} %pad.33.refs_1_, bf16[2048,2048]{1,0:T(8,128)(2,1)} %add_convert_fusion.refs_2_), custom_call_target="tpu_custom_call" | custom-call | tf_op jit(solution)/shard_map/link_reduce/pallas_call | solution.py:543
  929.3 18.7 %all-to-all-start.1 = ((bf16[4,64,2048]{2,1,0:T(8,128)(2,1)}), bf16[4,64,2048]{2,1,0:T(8,128)(2,1)S(1)}, u32[]{:S(2)}, u32[]{:S(2)}) async-start(bf16[4,64,2048]{2,1,0:T(8,128)(2,1)} %all_to_all.17), calls=%async_computation.3 | async-start | bytes 2097152 | tf_op jit(solution)/shard_map/all_to_all | solution.py:746
  970.9 5.5 fusion.38
  (281 shorter events, 118.3 us)
Async XLA Ops:
  7.3 356.6 %all-gather.7.cloned.1.call-start = ((), (), s32[]{:S(2)}) async-start(), calls=%async_computation.6 | async-start | bytes 4718592 | tf_op jit(solution)/shard_map/all_gather | solution.py:650
  8.0 355.9 %all-gather.9.cloned.1.call-start = ((), (), s32[]{:S(2)}) async-start(), calls=%async_computation.10 | async-start | bytes 10485760 | tf_op jit(solution)/shard_map/all_gather | solution.py:651
  15.1 17.0 %all-to-all-start = ((bf16[4,64,2048]{2,1,0:T(8,128)(2,1)}), bf16[4,64,2048]{2,1,0:T(8,128)(2,1)S(1)}, u32[]{:S(2)}, u32[]{:S(2)}) async-start(bf16[4,64,2048]{2,1,0:T(8,128)(2,1)} %all_to_all.14), calls=%async_computation | async-start | bytes 2097152 | tf_op jit(solution)/shard_map/all_to_all | solution.py:635
  19.4 359.1 %all-gather.5.cloned.1.call-start = ((), (), s32[]{:S(2)}) async-start(), calls=%async_computation.5 | async-start | bytes 4718592 | tf_op jit(solution)/shard_map/all_gather | solution.py:649
  19.9 194.6 %copy-start.21 = (pred[2048,16]{0,1:T(8,128)(4,1)}, pred[2048,16]{0,1:T(8,128)(4,1)S(1)}, u32[]{:S(2)}) copy-start(pred[2048,16]{0,1:T(8,128)(4,1)S(1)} %iota_compare_fusion.1) | copy-start | bytes 98308
  22.4 114.0 %copy-start.39 = (f32[512]{0:T(512)}, f32[512]{0:T(512)S(1)}, u32[]{:S(2)}) copy-start(f32[512]{0:T(512)S(1)} %add_rsqrt_fusion) | copy-start | bytes 6148
  122.3 21.0 %copy-start.10 = (bf16[1024,384]{1,0:T(8,128)(2,1)S(1)}, bf16[1024,384]{1,0:T(8,128)(2,1)}, u32[]{:S(2)}) copy-start(bf16[1024,384]{1,0:T(8,128)(2,1)} %get-tuple-element.27) | copy-start | bytes 2359300
  139.7 7.1 collective-permute-start
  144.5 21.1 %copy-start.31 = (f32[1024]{0:T(1024)}, f32[1024]{0:T(1024)S(1)}, u32[]{:S(2)}) copy-start(f32[1024]{0:T(1024)S(1)} %get-tuple-element.123) | copy-start | bytes 12292
  144.5 21.1 %copy-start.33 = (f32[1024]{0:T(1024)}, f32[1024]{0:T(1024)S(1)}, u32[]{:S(2)}) copy-start(f32[1024]{0:T(1024)S(1)} %get-tuple-element.124) | copy-start | bytes 12292
  144.5 21.1 %copy-start.35 = (f32[1024]{0:T(1024)}, f32[1024]{0:T(1024)S(1)}, u32[]{:S(2)}) copy-start(f32[1024]{0:T(1024)S(1)} %get-tuple-element.125) | copy-start | bytes 12292
  144.5 21.1 %copy-start.37 = (f32[1024]{0:T(1024)}, f32[1024]{0:T(1024)S(1)}, u32[]{:S(2)}) copy-start(f32[1024]{0:T(1024)S(1)} %get-tuple-element.126) | copy-start | bytes 12292
  145.4 20.2 %copy-start.23 = (f32[4,512]{1,0:T(4,128)}, f32[4,512]{1,0:T(4,128)S(1)}, u32[]{:S(2)}) copy-start(f32[4,512]{1,0:T(4,128)S(1)} %get-tuple-element.187) | copy-start | bytes 24580
  145.4 20.2 %copy-start.25 = (f32[4,512]{1,0:T(4,128)}, f32[4,512]{1,0:T(4,128)S(1)}, u32[]{:S(2)}) copy-start(f32[4,512]{1,0:T(4,128)S(1)} %get-tuple-element.188) | copy-start | bytes 24580
  145.4 20.2 %copy-start.26 = (f32[4,512]{1,0:T(4,128)}, f32[4,512]{1,0:T(4,128)S(1)}, u32[]{:S(2)}) copy-start(f32[4,512]{1,0:T(4,128)S(1)} %get-tuple-element.190) | copy-start | bytes 24580
  146.6 79.9 %copy-start.28 = (f32[1024]{0:T(1024)}, f32[1024]{0:T(1024)S(1)}, u32[]{:S(2)}) copy-start(f32[1024]{0:T(1024)S(1)} %get-tuple-element.121) | copy-start | bytes 12292
  146.6 231.9 %copy-start.45 = (f32[1024]{0:T(1024)}, f32[1024]{0:T(1024)S(1)}, u32[]{:S(2)}) copy-start(f32[1024]{0:T(1024)S(1)} %get-tuple-element.120) | copy-start | bytes 12292
  146.6 778.7 %reduce-scatter.6.cloned.1.call-start = ((), (), s32[]{:S(2)}) async-start(), calls=%async_computation.8 | async-start | bytes 4718592 | tf_op jit(solution)/shard_map/reduce_scatter | solution.py:706
  146.9 18.8 %copy-start.19 = (f32[4,3,1024]{2,1,0:T(4,128)}, f32[4,3,1024]{2,1,0:T(4,128)S(1)}, u32[]{:S(2)}) copy-start(f32[4,3,1024]{2,1,0:T(4,128)S(1)} %convert_element_type.265) | copy-start | bytes 147460
  208.3 18.2 %copy-start.8 = (f32[2048,160]{1,0:T(8,128)}, f32[2048,160]{1,0:T(8,128)S(1)}, u32[]{:S(2)}) copy-start(f32[2048,160]{1,0:T(8,128)S(1)} %convert_reduce_fusion) | copy-start | bytes 3932164
  248.9 55.7 %copy-start.16 = (f32[16,1024]{1,0:T(8,128)S(1)}, f32[16,1024]{1,0:T(8,128)}, u32[]{:S(2)}) copy-start(f32[16,1024]{1,0:T(8,128)} %multiply_bitcast_fusion.rate_ref) | copy-start | bytes 196612
  419.3 539.3 %reduce-scatter.8.cloned.1.call-start = ((), (), s32[]{:S(2)}) async-start(), calls=%async_computation.9 | async-start | bytes 4718592 | tf_op jit(solution)/shard_map/reduce_scatter | solution.py:702
  433.7 537.2 %reduce-scatter.4.cloned.1.call-start = ((), (), s32[]{:S(2)}) async-start(), calls=%async_computation.7 | async-start | bytes 10485760 | tf_op jit(solution)/shard_map/reduce_scatter | solution.py:699
  450.8 60.7 %copy-start.17 = (f32[16,1024]{1,0:T(8,128)S(1)}, f32[16,1024]{1,0:T(8,128)}, u32[]{:S(2)}) copy-start(f32[16,1024]{1,0:T(8,128)} %multiply_bitcast_fusion.rate_ref) | copy-start | bytes 196612
  658.2 44.9 %copy-start.46 = (f32[1024]{0:T(1024)S(1)}, f32[1024]{0:T(1024)}, u32[]{:S(2)}) copy-start(f32[1024]{0:T(1024)} %copy-done.45) | copy-start | bytes 12292
  717.1 22.3 %copy-start.2 = (bf16[4,512,1024]{2,1,0:T(8,128)(2,1)S(1)}, bf16[4,512,1024]{2,1,0:T(8,128)(2,1)}, u32[]{:S(2)}) copy-start(bf16[4,512,1024]{2,1,0:T(8,128)(2,1)} %copy-done) | copy-start | bytes 12582916
  730.3 22.7 %copy-start.5 = (f32[4,512,1024]{2,1,0:T(8,128)}, f32[4,512,1024]{2,1,0:T(8,128)S(1)}, u32[]{:S(2)}) copy-start(f32[4,512,1024]{2,1,0:T(8,128)S(1)} %get-tuple-element.136) | copy-start | bytes 25165828
  730.9 29.7 %collective-permute-start.1 = (bf16[4,3,1024]{2,1,0:T(4,128)(2,1)}, bf16[4,3,1024]{2,1,0:T(4,128)(2,1)}, u32[]{:S(2)}, u32[]{:S(2)}) collective-permute-start(bf16[4,3,1024]{2,1,0:T(4,128)(2,1)} %slice.782), channel_id=1, source_target_pairs={{4,0},{8,4},{12,8},{16,12},{20,16},{24,20},{28,24},{5,1},{9,5},{13... | collective-permute-start | bytes 73736 | tf_op jit(solution)/shard_map/ppermute | solution.py:558
  805.8 150.4 %copy-start.7 = (bf16[1,512,2048]{2,1,0:T(8,128)(2,1)S(1)}, bf16[1,512,2048]{2,1,0:T(8,128)(2,1)}, u32[]{:S(2)}) copy-start(bf16[1,512,2048]{2,1,0:T(8,128)(2,1)} %param.13) | copy-start | bytes 6291460
  805.8 150.4 %copy-start.40 = (f32[512]{0:T(512)S(1)}, f32[512]{0:T(512)}, u32[]{:S(2)}) copy-start(f32[512]{0:T(512)} %copy-done.39) | copy-start | bytes 6148
  924.2 24.5 %copy-start.18 = (bf16[128,384]{1,0:T(8,128)(2,1)S(1)}, bf16[128,384]{1,0:T(8,128)(2,1)}, u32[]{:S(2)}) copy-start(bf16[128,384]{1,0:T(8,128)(2,1)} %get-tuple-element.39) | copy-start | bytes 294916
  929.3 31.5 %all-to-all-start.1 = ((bf16[4,64,2048]{2,1,0:T(8,128)(2,1)}), bf16[4,64,2048]{2,1,0:T(8,128)(2,1)S(1)}, u32[]{:S(2)}, u32[]{:S(2)}) async-start(bf16[4,64,2048]{2,1,0:T(8,128)(2,1)} %all_to_all.17), calls=%async_computation.3 | async-start | bytes 2097152 | tf_op jit(solution)/shard_map/all_to_all | solution.py:746
  (43 other events, 474.2 us)
Sparse Core Ops, SparseCore 0:
  10.2 98.7 all-gather.6
  110.6 59.8 all-gather.8
  172.7 72.6 all-gather.4
  419.5 93.8 reduce-scatter.5
  517.3 89.0 reduce-scatter.7
  655.1 82.0 reduce-scatter.3

commit v3 on v2

--- a/solution.py
+++ b/solution.py
@@ -16,40 +16,63 @@
 VMEM_LIMIT = 56 << 20
 
 
-def across(rows, width):
-    return jnp.concatenate([rows] * (width // rows.shape[1]), axis=1)
-
-
-def fwd_end_body(dte_ref, dtx_ref, wide_ref, rate_ref, end_ref):
+def across(slab, place, width):
+    return jnp.concatenate([jnp.broadcast_to(slab[:, place : place + 1], (slab.shape[0], 128))] * (width // 128), axis=1)
+
+
+def decays(dte_ref, rate_ref, at, buf, power_buf=None):
+    n = rate_ref.shape[0]
+    for place in range(GROUP):
+        power = dte_ref[pl.ds(at * GROUP + place, 1), :] * rate_ref[...]
+        buf[pl.ds(place * n, n), :] = jnp.exp2(power)
+        if power_buf is not None:
+            power_buf[pl.ds(place * n, n), :] = power.astype(jnp.bfloat16)
+
+
+def fwd_end_body(dte_ref, dtx_ref, slab_ref, rate_ref, end_ref, even_ref, odd_ref):
     n, width = rate_ref.shape
-    rate = rate_ref[...]
-
-    def group(at, state):
+    groups = dte_ref.shape[0] // GROUP
+
+    def walk(at, state, decay_ref):
+        slab = slab_ref[pl.ds(at * n, n), :]
         for place in range(GROUP):
-            t = at * GROUP + place
-            write = across(wide_ref[pl.ds(t * n, n), :], width)
-            state = jnp.exp2(dte_ref[pl.ds(t, 1), :] * rate) * state + dtx_ref[pl.ds(t, 1), :] * write
+            write = across(slab, place, width)
+            state = decay_ref[pl.ds(place * n, n), :] * state + dtx_ref[pl.ds(at * GROUP + place, 1), :] * write
         return state
 
-    end_ref[...] = lax.fori_loop(0, dte_ref.shape[0] // GROUP, group, jnp.zeros_like(rate))
-
-
-def bwd_end_body(dte_ref, grad_ref, wide_ref, rate_ref, end_ref):
+    def pair(step, state):
+        decays(dte_ref, rate_ref, 2 * step + 1, odd_ref)
+        state = walk(2 * step, state, even_ref)
+        decays(dte_ref, rate_ref, jnp.minimum(2 * step + 2, groups - 1), even_ref)
+        return walk(2 * step + 1, state, odd_ref)
+
+    decays(dte_ref, rate_ref, 0, even_ref)
+    end_ref[...] = lax.fori_loop(0, groups // 2, pair, jnp.zeros_like(end_ref))
+
+
+def bwd_end_body(dte_ref, grad_ref, slab_ref, rate_ref, end_ref, even_ref, odd_ref):
     n, width = rate_ref.shape
-    rate = rate_ref[...]
     groups = dte_ref.shape[0] // GROUP
 
-    def group(step, state):
+    def walk(at, state, decay_ref):
+        slab = slab_ref[pl.ds(at * n, n), :]
         for place in reversed(range(GROUP)):
-            t = (groups - 1 - step) * GROUP + place
-            read = across(wide_ref[pl.ds(t * n, n), :], width)
-            state = jnp.exp2(dte_ref[pl.ds(t, 1), :] * rate) * (state + grad_ref[pl.ds(t, 1), :] * read)
+            read = across(slab, place, width)
+            state = decay_ref[pl.ds(place * n, n), :] * (state + grad_ref[pl.ds(at * GROUP + place, 1), :] * read)
         return state
 
-    end_ref[...] = lax.fori_loop(0, groups, group, jnp.zeros_like(rate))
-
-
-def scan_end(body, dte, other, wide, rate, seqs, width=512):
+    def pair(step, state):
+        at = groups - 1 - 2 * step
+        decays(dte_ref, rate_ref, at - 1, odd_ref)
+        state = walk(at, state, even_ref)
+        decays(dte_ref, rate_ref, jnp.maximum(at - 2, 0), even_ref)
+        return walk(at - 1, state, odd_ref)
+
+    decays(dte_ref, rate_ref, groups - 1, even_ref)
+    end_ref[...] = lax.fori_loop(0, groups // 2, pair, jnp.zeros_like(end_ref))
+
+
+def scan_end(body, dte, other, slabs, rate, seqs, width=512):
     tokens, chans = dte.shape
     length = tokens // seqs
     n = rate.shape[0]
@@ -61,18 +84,19 @@
         in_specs=[
             pl.BlockSpec((length, width), lambda s, c: (s, c)),
             pl.BlockSpec((length, width), lambda s, c: (s, c)),
-            pl.BlockSpec((length * n, wide.shape[1]), lambda s, c: (s, 0)),
+            pl.BlockSpec((length // GROUP * n, GROUP), lambda s, c: (s, 0)),
             pl.BlockSpec((n, width), lambda s, c: (0, c)),
         ],
         out_specs=pl.BlockSpec((n, width), lambda s, c: (s, c)),
         out_shape=jax.ShapeDtypeStruct((seqs * n, chans), jnp.float32),
+        scratch_shapes=[pltpu.VMEM((GROUP * n, width), jnp.float32)] * 2,
         compiler_params=pltpu.CompilerParams(vmem_limit_bytes=VMEM_LIMIT),
         cost_estimate=pl.CostEstimate(flops=4 * work, transcendentals=work, bytes_accessed=8 * tokens * chans),
         name=body.__name__[:7],
-    )(dte, other, wide, rate)
-
-
-def fwd_full_body(dte_ref, dtx_ref, wide_ref, read_ref, rate_ref, start_ref, y_ref, hist_ref, h_ref):
+    )(dte, other, slabs, rate)
+
+
+def fwd_full_body(dte_ref, dtx_ref, slab_ref, read_ref, rate_ref, start_ref, y_ref, hist_ref, h_ref, even_ref, odd_ref):
     block = dte_ref.shape[0]
     n, width = rate_ref.shape
     span = GROUP * n
@@ -85,23 +109,33 @@
     first = h_ref[...]
     hist_ref[pl.ds(0, n), :] = first.astype(jnp.bfloat16)
 
-    def group(at, state):
+    def rows_out(at, buf):
+        y_ref[pl.ds(at * GROUP, GROUP), :] = jnp.dot(
+            read_ref[pl.ds(at * GROUP, GROUP), :], buf[...], preferred_element_type=jnp.float32)
+
+    def group(at, state, buf):
+        slab = slab_ref[pl.ds(at * n, n), :]
         for place in range(GROUP):
             t = at * GROUP + place
-            write = across(wide_ref[pl.ds(t * n, n), :], width)
+            write = across(slab, place, width)
             state = jnp.exp2(dte_ref[pl.ds(t, 1), :] * rate) * state + dtx_ref[pl.ds(t, 1), :] * write
-            hist_ref[pl.ds((t + 1) * n, n), :] = state.astype(jnp.bfloat16)
-        y_ref[pl.ds(at * GROUP, GROUP), :] = jnp.dot(
-            read_ref[pl.ds(at * GROUP, GROUP), :],
-            hist_ref[pl.ds(n + at * span, span), :],
-            preferred_element_type=jnp.float32,
-        )
+            kept = state.astype(jnp.bfloat16)
+            hist_ref[pl.ds((t + 1) * n, n), :] = kept
+            buf[pl.ds(place * n, n), :] = kept
         return state
 
-    h_ref[...] = lax.fori_loop(0, block // GROUP, group, first)
-
-
-def fwd_full(dte, dtx, wide, read, rate, start, seqs, width=1024, block=128):
+    def pair(step, state):
+        at = 2 * step
+        rows_out(jnp.maximum(at - 1, 0), odd_ref)
+        state = group(at, state, even_ref)
+        rows_out(at, even_ref)
+        return group(at + 1, state, odd_ref)
+
+    h_ref[...] = lax.fori_loop(0, block // GROUP // 2, pair, first)
+    rows_out(block // GROUP - 1, odd_ref)
+
+
+def fwd_full(dte, dtx, slabs, read, rate, start, seqs, width=512, block=256):
     tokens, chans = dte.shape
     n = rate.shape[0]
     width = min(width, chans)
@@ -115,7 +149,7 @@
         in_specs=[
             pl.BlockSpec((block, width), here),
             pl.BlockSpec((block, width), here),
-            pl.BlockSpec((block * n, wide.shape[1]), rows),
+            pl.BlockSpec((block // GROUP * n, GROUP), rows),
             pl.BlockSpec((block, read.shape[1]), rows),
             pl.BlockSpec((n, width), lambda c, s, t: (0, c)),
             pl.BlockSpec((n, width), lambda c, s, t: (s, c)),
@@ -125,21 +159,21 @@
             jax.ShapeDtypeStruct((tokens, chans), jnp.float32),
             jax.ShapeDtypeStruct((seqs * blocks * (block + 1) * n, chans), jnp.bfloat16),
         ],
-        scratch_shapes=[pltpu.VMEM((n, width), jnp.float32)],
+        scratch_shapes=[pltpu.VMEM((n, width), jnp.float32)] + [pltpu.VMEM((GROUP * n, width), jnp.bfloat16)] * 2,
         compiler_params=pltpu.CompilerParams(vmem_limit_bytes=VMEM_LIMIT),
         cost_estimate=pl.CostEstimate(flops=8 * work, transcendentals=work, bytes_accessed=2 * work),
         name="fwd_full",
-    )(dte, dtx, wide, read, rate, start)
-
-
-def bwd_full_body(dte_ref, dtx_ref, grad_ref, hist_ref, wide_ref, write_ref, ones_ref, rate_ref, start_ref,
-                  s1_ref, s2_ref, grate_ref, dw_ref, dr_ref, g_ref, adj_ref, r_ref):
+    )(dte, dtx, slabs, read, rate, start)
+
+
+def bwd_full_body(dte_ref, dtx_ref, grad_ref, hist_ref, slab_ref, write_ref, ones_ref, rate_ref, start_ref,
+                  s1_ref, s2_ref, grate_ref, dw_ref, dr_ref, g_ref, *scratch):
     block = dte_ref.shape[0]
     n, width = rate_ref.shape
-    span = GROUP * n
-    rate = rate_ref[...]
     groups = block // GROUP
-    bf = jnp.bfloat16
+    bf, f32 = jnp.bfloat16, jnp.float32
+    even, odd = scratch[:5], scratch[5:]
+    unit = jnp.ones((GROUP, 128), bf)
 
     @pl.when(pl.program_id(2) == 0)
     def _():
@@ -149,33 +183,51 @@
     def _():
         grate_ref[...] = jnp.zeros_like(grate_ref)
 
-    def group(step, state):
-        at = groups - 1 - step
+    def sums_out(at, bufs):
+        _, _, adj_ref, rated_ref, dw_part = bufs
+        rows = pl.ds(at * GROUP, GROUP)
+        s1_ref[rows, :] = jnp.dot(write_ref[rows, :], adj_ref[...], preferred_element_type=f32)
+        sums = jnp.dot(ones_ref[...], rated_ref[...], preferred_element_type=f32)
+        s2_ref[rows, :] = sums[:GROUP]
+        dw_ref[pl.ds(at, 1), :] = lax.dot_general(unit, dw_part[...], NT, preferred_element_type=f32)[:1]
+        dr_ref[rows, :] = lax.dot_general(
+            grad_ref[rows, :].astype(bf), hist_ref[pl.ds(n + at * GROUP * n, GROUP * n), :], NT,
+            preferred_element_type=f32)
+        return sums[GROUP:]
+
+    def strips(values):
+        parts = [values[:, k * 128 : (k + 1) * 128] for k in range(width // 128)]
+        while len(parts) > 1:
+            parts = [a + b for a, b in zip(parts[::2], parts[1::2])] + parts[len(parts) // 2 * 2 :]
+        return parts[0]
+
+    def walk(at, state, bufs):
+        decay_ref, power_ref, adj_ref, rated_ref, dw_part = bufs
+        slab = slab_ref[pl.ds(at * n, n), :]
         for place in reversed(range(GROUP)):
             t = at * GROUP + place
-            read = across(wide_ref[pl.ds(t * n, n), :], width)
-            power = dte_ref[pl.ds(t, 1), :] * rate
+            here = pl.ds(place * n, n)
+            read = across(slab, place, width)
             adjoint = state + grad_ref[pl.ds(t, 1), :] * read
+            power = dte_ref[pl.ds(t, 1), :] * rate_ref[...]
             state = jnp.exp2(power) * adjoint
-            adj_ref[pl.ds(place * n, n), :] = adjoint.astype(bf)
-            r_ref[pl.ds(place * n, n), :] = state.astype(bf) * hist_ref[pl.ds(t * n, n), :] * power.astype(bf)
-        rows = pl.ds(at * GROUP, GROUP)
-        adj_all = adj_ref[...]
-        s1_ref[rows, :] = jnp.dot(write_ref[rows, :], adj_all, preferred_element_type=jnp.float32)
-        sums = jnp.dot(ones_ref[...], r_ref[...], preferred_element_type=jnp.float32)
-        s2_ref[rows, :] = sums[:GROUP]
-        grate_ref[...] += sums[GROUP:]
-        dw_ref[rows, :] = lax.dot_general(
-            dtx_ref[rows, :].astype(bf), adj_all, NT, preferred_element_type=jnp.float32)
-        dr_ref[rows, :] = lax.dot_general(
-            grad_ref[rows, :].astype(bf), hist_ref[pl.ds(n + at * span, span), :], NT,
-            preferred_element_type=jnp.float32)
+            low = adjoint.astype(bf)
+            adj_ref[here, :] = low
+            rated_ref[here, :] = state.astype(bf) * hist_ref[pl.ds(t * n, n), :] * power.astype(bf)
+            dw_part[here, :] = strips(adjoint * dtx_ref[pl.ds(t, 1), :]).astype(bf)
         return state
 
-    g_ref[...] = lax.fori_loop(0, groups, group, g_ref[...])
-
-
-def bwd_full(dte, dtx, grad, hist, wide, write, rate, start, seqs, width=1024, block=128):
+    def pair(step, state):
+        at = groups - 1 - 2 * step
+        old = sums_out(jnp.minimum(at + 1, groups - 1), odd)
+        state = walk(at, state, even)
+        grate_ref[...] += jnp.where(step > 0, old, 0.0) + sums_out(at, even)
+        return walk(at - 1, state, odd)
+    g_ref[...] = lax.fori_loop(0, groups // 2, pair, g_ref[...])
+    grate_ref[...] += sums_out(0, odd)
+
+
+def bwd_full(dte, dtx, grad, hist, slabs, write, rate, start, seqs, width=512, block=256):
     tokens, chans = dte.shape
     n = rate.shape[0]
     width = min(width, chans)
@@ -199,7 +251,7 @@
             pl.BlockSpec((block, width), here),
             pl.BlockSpec((block, width), here),
             pl.BlockSpec(((block + 1) * n, width), here),
-            pl.BlockSpec((block * n, wide.shape[1]), rows),
+            pl.BlockSpec((block // GROUP * n, GROUP), rows),
             pl.BlockSpec((block, span), rows),
             pl.BlockSpec(ones.shape, lambda c, s, t: (0, 0)),
             pl.BlockSpec((n, width), lambda c, s, t: (0, c)),
@@ -209,43 +261,43 @@
             pl.BlockSpec((block, width), here),
             pl.BlockSpec((block, width), here),
             pl.BlockSpec((n, width), lambda c, s, t: (0, c)),
-            pl.BlockSpec((block, span), strip),
+            pl.BlockSpec((block // GROUP, span), strip),
             pl.BlockSpec((block, span), strip),
         ],
         out_shape=[
             jax.ShapeDtypeStruct((tokens, chans), f32),
             jax.ShapeDtypeStruct((tokens, chans), f32),
             jax.ShapeDtypeStruct((n, chans), f32),
-            jax.ShapeDtypeStruct((strips * tokens, span), f32),
+            jax.ShapeDtypeStruct((strips * tokens // GROUP, span), f32),
             jax.ShapeDtypeStruct((strips * tokens, span), f32),
         ],
         scratch_shapes=[
             pltpu.VMEM((n, width), f32),
-            pltpu.VMEM((span, width), jnp.bfloat16),
-            pltpu.VMEM((span, width), jnp.bfloat16),
+            *[
+                pltpu.VMEM((span, width), f32),
+                *[pltpu.VMEM((span, width), jnp.bfloat16)] * 3,
+                pltpu.VMEM((span, 128), jnp.bfloat16),
+            ] * 2,
         ],
         compiler_params=pltpu.CompilerParams(vmem_limit_bytes=VMEM_LIMIT),
         cost_estimate=pl.CostEstimate(flops=14 * work, transcendentals=work, bytes_accessed=2 * work),
         name="bwd_full",
-    )(dte, dtx, grad, hist, wide, write, ones, rate, start)
-    return s1, s2, grate, diagonal(dw.reshape(strips, tokens, span).sum(0), n), diagonal(
-        dr.reshape(strips, tokens, span).sum(0), n)
-
-
-def widen(values):
-    return jnp.broadcast_to(values.reshape(-1)[:, None], (values.size, 128))
+    )(dte, dtx, grad, hist, slabs, write, ones, rate, start)
+    dw = dw.reshape(strips, tokens, n).sum(0).T
+    own = jnp.arange(tokens)[:, None] % GROUP == jnp.arange(GROUP)[None, :]
+    dr = jnp.where(own[None, :, :, None], dr.reshape(strips, tokens, GROUP, n), 0).sum((0, 2)).T
+    return s1, s2, grate, dw, dr
+
+
+def slabs_of(values):
+    n, tokens = values.shape
+    return values.reshape(n, tokens // GROUP, GROUP).transpose(1, 0, 2).reshape(tokens // GROUP * n, GROUP)
 
 
 def spread(values):
-    tokens, n = values.shape
+    n, tokens = values.shape
     own = jnp.arange(tokens)[:, None] % GROUP == jnp.arange(GROUP)[None, :]
-    return jnp.where(own[:, :, None], values[:, None, :], 0).reshape(tokens, GROUP * n).astype(jnp.bfloat16)
-
-
-def diagonal(sums, n):
-    tokens = sums.shape[0]
-    own = jnp.arange(tokens)[:, None] % GROUP == jnp.arange(GROUP)[None, :]
-    return jnp.sum(jnp.where(own[:, :, None], sums.reshape(tokens, GROUP, n), 0), axis=1)
+    return jnp.where(own[:, :, None], values.T[:, None, :], 0).reshape(tokens, GROUP * n).astype(jnp.bfloat16)
 
 
 MESH = pl.DeviceIdType.MESH
@@ -269,12 +321,17 @@
             found += [(col > 0, self.device(row, col - 1)), (col < self.inner - 1, self.device(row, col + 1))]
         return found
 
-
-def greet(grids):
+    def everyone(self):
+        size = self.inner * self.outer
+        me = self.row * self.inner + self.col
+        return [(me >= 0, {self.axis: (me + step) % size}) for step in range(1, size)]
+
+
+def greet(grids, all_of=()):
     barrier = pltpu.get_barrier_semaphore()
     count = 0
     for grid in grids:
-        for there, device in grid.neighbours():
+        for there, device in grid.everyone() if grid.axis in all_of else grid.neighbours():
 
             @pl.when(there)
             def _(device=device):
@@ -284,20 +341,23 @@
     pl.semaphore_wait(barrier, count)
 
 
-def gather_steps(grid, whole_ref, out_ref, send_sem, recv_sem, own_sem, waits, chunk, chunks):
+def gather_steps(grid, whole_ref, out_ref, send_sem, recv_sem, own_sem, waits, chunk, chunks, across_too=True, ways=(True, True)):
     rows = whole_ref.shape[0]
     part = rows // chunks
     src_ref = whole_ref.at[pl.ds(chunk * part, part)]
-    outer, inner = grid.outer, grid.inner
+    outer, inner = grid.outer, grid.inner if across_too else 1
     row, col = grid.row, grid.col
 
+    def number(r, c):
+        return r * inner + c if across_too else r
+
     def place(r, c):
-        return pl.ds(pl.multiple_of((r * inner + c) * rows + chunk * part, part), part)
+        return pl.ds(pl.multiple_of(number(r, c) * rows + chunk * part, part), part)
 
     def send(there, way, r, c, device, source):
         copy = pltpu.make_async_remote_copy(
-            src_ref=source, dst_ref=out_ref.at[place(r, c)], send_sem=send_sem.at[way, r * inner + c],
-            recv_sem=recv_sem.at[r * inner + c], device_id=device, device_id_type=MESH)
+            src_ref=source, dst_ref=out_ref.at[place(r, c)], send_sem=send_sem.at[way, number(r, c)],
+            recv_sem=recv_sem.at[number(r, c)], device_id=device, device_id_type=MESH)
 
         @pl.when(there)
         def _():
@@ -312,13 +372,15 @@
 
     def along(there, r, source):
         if outer > 1:
-            send(there & (r >= row) & (row > 0), 0, r, col, grid.device(row - 1, col), source)
-            send(there & (r <= row) & (row < outer - 1), 1, r, col, grid.device(row + 1, col), source)
+            if ways[0]:
+                send(there & (r >= row) & (row > 0), 0, r, col, grid.device(row - 1, col), source)
+            if ways[1]:
+                send(there & (r <= row) & (row < outer - 1), 1, r, col, grid.device(row + 1, col), source)
 
     def arrive(there, r, c):
         copy = pltpu.make_async_remote_copy(
             src_ref=src_ref, dst_ref=out_ref.at[place(r, c)], send_sem=send_sem.at[0, 0],
-            recv_sem=recv_sem.at[r * inner + c], device_id=grid.device(row, col), device_id_type=MESH)
+            recv_sem=recv_sem.at[number(r, c)], device_id=grid.device(row, col), device_id_type=MESH)
 
         @pl.when(there)
         def _():
@@ -332,8 +394,12 @@
     waits.append((None, own))
     for _ in range(chunk + 1):
         yield
+
+    def rows_at(distance):
+        return [row - distance] * ways[1] + [row + distance] * ways[0]
+
     for distance in range(1, outer):
-        for r in (row - distance, row + distance):
+        for r in rows_at(distance):
             there = (r >= 0) & (r < outer)
             arrive(there, r, col)
             along(there, r, out_ref.at[place(r, col)])
@@ -341,7 +407,7 @@
         yield
     for step in range(1, inner):
         for distance in range(outer):
-            for r in (row - distance, row + distance) if distance else (row,):
+            for r in rows_at(distance) if distance else (row,):
                 for c in (col - step, col + step):
                     there = (r >= 0) & (r < outer) & (c >= 0) & (c < inner)
                     arrive(there, r, c)
@@ -371,7 +437,7 @@
         runs = left
 
 
-def link_gather(arrays, sizes, collective_id):
+def link_gather(arrays, sizes, collective_id, ways=(True, True)):
     count = len(arrays)
     axes = sorted({entry[0] for entry in arrays})
 
@@ -383,7 +449,7 @@
         runs = []
         for i, (axis, _, chunks) in enumerate(arrays):
             for chunk in range(chunks):
-                runs.append(gather_steps(grids[axis], sources[i], outs[i], *sems[:3], waits, chunk, chunks))
+                runs.append(gather_steps(grids[axis], sources[i], outs[i], *sems[:3], waits, chunk, chunks, ways=ways))
                 sems = sems[3:]
         in_turn(runs)
         finish(waits)
@@ -404,7 +470,7 @@
     )(*[a for _, a, _ in arrays])
 
 
-def reduce_steps(grid, src_ref, out_ref, acc, inner_buf, outer_buf, sems, waits, chunk, chunks):
+def reduce_steps(grid, src_ref, out_ref, acc, inner_buf, outer_buf, sems, waits, chunk, chunks, share=None):
     outer, inner = grid.outer, grid.inner
     row, col = grid.row, grid.col
     rows, part = acc.shape[0] // (outer * inner), acc.shape[0] // (outer * inner * chunks)
@@ -491,50 +557,92 @@
         yield
     begin_outer, go_on_outer = line(
         row, outer, lambda r: grid.device(r, col), lambda t: (t, col), outer_buf, outer_send, outer_recv)
+    late = []
     for r in order:
         if inner > 1:
             for c in range(inner):
                 lines[r][1][1](c)
         if outer > 1:
             begin_outer(r)
+            yield
+            for earlier in late:
+                go_on_outer(earlier)
+            late = [r]
         yield
-    if outer > 1:
-        for r in order:
-            go_on_outer(r)
-            yield
-    last = pltpu.make_async_copy(acc.at[place(row, col)], out_ref.at[pl.ds(chunk * part, part)], out_sem)
-    last.start()
-    waits.append((None, last))
+    for earlier in late:
+        go_on_outer(earlier)
+    if share is None:
+        last = pltpu.make_async_copy(acc.at[place(row, col)], out_ref.at[pl.ds(chunk * part, part)], out_sem)
+        last.start()
+        waits.append((None, last))
+        return
+    other, strip, send_sem, recv_sem = share
+    count, me = other.outer * other.inner, other.row * other.inner + other.col
+    take = rows // count
+    strips = acc.shape[1] // strip
+    first = (row * inner + col) * rows
+    for step in range(count):
+        mate = (me + step) % count
+        source_rows = pl.ds(pl.multiple_of(first + mate * take, take), take)
+        for k in range(strips):
+            piece_ref = acc.at[source_rows, pl.ds(k * strip, strip)]
+            target = out_ref.at[:, pl.ds(pl.multiple_of((k * count + me) * strip, strip), strip)]
+            if step == 0:
+                copy = pltpu.make_async_copy(piece_ref, target, send_sem.at[step, k])
+                copy.start()
+                waits.append((None, copy))
+            else:
+                copy = pltpu.make_async_remote_copy(
+                    src_ref=piece_ref, dst_ref=target, send_sem=send_sem.at[step, k], recv_sem=recv_sem.at[step, k],
+                    device_id={other.axis: mate}, device_id_type=MESH)
+                copy.start()
+                waits.append((me >= 0, copy))
+    for step in range(1, count):
+        mate = (me + count - step) % count
+        for k in range(strips):
+            copy = pltpu.make_async_remote_copy(
+                src_ref=acc.at[pl.ds(0, take), pl.ds(k * strip, strip)],
+                dst_ref=out_ref.at[:, pl.ds(pl.multiple_of((k * count + mate) * strip, strip), strip)],
+                send_sem=send_sem.at[step, k], recv_sem=recv_sem.at[step, k], device_id={other.axis: me},
+                device_id_type=MESH)
+            copy.wait_recv()
 
 
 def link_reduce(arrays, sizes, collective_id):
     count = len(arrays)
-    axes = sorted({entry[0] for entry in arrays})
 
     def kernel(*refs):
         sources, outs, scratch = refs[:count], refs[count : 2 * count], refs[2 * count :]
-        grids = {axis: Grid(axis, *sizes[axis]) for axis in axes}
-        greet([grids[axis] for axis in axes])
+        grids = {axis: Grid(axis, *sizes[axis]) for axis in ("seq", "stream")}
+        greet(list(grids.values()), ("stream",))
         waits = []
         runs = []
-        for i, (axis, _, chunks) in enumerate(arrays):
+        for i, (axis, _, chunks, strip) in enumerate(arrays):
             acc, scratch = scratch[0], scratch[1:]
+            share = None
+            if strip:
+                share, scratch = (grids["stream"], strip, *scratch[:2]), scratch[2:]
             for chunk in range(chunks):
                 inner_buf, outer_buf, sems, scratch = scratch[0], scratch[1], scratch[2:8], scratch[8:]
-                runs.append(
-                    reduce_steps(grids[axis], sources[i], outs[i], acc, inner_buf, outer_buf, sems, waits, chunk, chunks))
+                runs.append(reduce_steps(
+                    grids[axis], sources[i], outs[i], acc, inner_buf, outer_buf, sems, waits, chunk, chunks, share))
         in_turn(runs)
         finish(waits)
 
     scratch, shapes = [], []
-    for axis, a, chunks in arrays:
+    for axis, a, chunks, strip in arrays:
         size, inner = sizes[axis]
         outer = size // inner
         part = a.shape[0] // size // chunks
         slots = [n + 1 if n > 2 else 1 for n in (inner, outer)]
         dma = pltpu.SemaphoreType.DMA
-        shapes.append(jax.ShapeDtypeStruct((a.shape[0] // size, a.shape[1]), a.dtype))
         scratch.append(pltpu.VMEM(a.shape, a.dtype))
+        if strip:
+            mates = sizes["stream"][0]
+            shapes.append(jax.ShapeDtypeStruct((a.shape[0] // size // mates, a.shape[1] * mates), a.dtype))
+            scratch += [dma((mates, a.shape[1] // strip))] * 2
+        else:
+            shapes.append(jax.ShapeDtypeStruct((a.shape[0] // size, a.shape[1]), a.dtype))
         for _ in range(chunks):
             scratch += [
                 pltpu.VMEM((outer, slots[0], part, a.shape[1]), a.dtype),
@@ -549,7 +657,143 @@
         compiler_params=pltpu.CompilerParams(
             collective_id=collective_id, has_side_effects=True, vmem_limit_bytes=VMEM_LIMIT),
         name="link_reduce",
-    )(*[a for _, a, _ in arrays])
+    )(*[entry[1] for entry in arrays])
+
+
+def link_sum(partial, sizes, collective_id):
+    rows, width = partial.shape
+    size, inner = sizes["stream"]
+    outer = size // inner
+    assert inner == 2
+    half = rows // 2
+    bf, f32 = jnp.bfloat16, jnp.float32
+    dma = pltpu.SemaphoreType.DMA
+
+    def kernel(own_ref, out_ref, mate_buf, pair_ref, terms_ref, total_ref, send, recv, line_send, line_recv, own_sem):
+        grid = Grid("stream", size, inner)
+        row, col = grid.row, grid.col
+        greet([grid])
+        mate = grid.device(row, 1 - col)
+        mine = pl.ds(pl.multiple_of(col * half, half), half)
+        swap = pltpu.make_async_remote_copy(
+            src_ref=own_ref, dst_ref=mate_buf, send_sem=send.at[0], recv_sem=recv.at[0], device_id=mate,
+            device_id_type=MESH)
+        swap.start()
+        swap.wait_recv()
+        pair_ref[...] = (own_ref[mine, :].astype(f32) + mate_buf[mine, :].astype(f32)).astype(bf)
+        waits = []
+        line = Grid("stream", size, inner)
+        in_turn([gather_steps(
+            line, pair_ref, terms_ref, line_send, line_recv, own_sem, waits, 0, 1, across_too=False)])
+        finish(waits)
+        total = terms_ref[pl.ds(0, half), :].astype(f32)
+        for r in range(1, outer):
+            total = total + terms_ref[pl.ds(r * half, half), :].astype(f32)
+        total_ref[...] = total
+        out_ref[mine, :] = total
+        swap_back = pltpu.make_async_remote_copy(
+            src_ref=total_ref, dst_ref=out_ref.at[mine], send_sem=send.at[1], recv_sem=recv.at[1], device_id=mate,
+            device_id_type=MESH)
+        swap_back.start()
+        theirs = pltpu.make_async_remote_copy(
+            src_ref=total_ref, dst_ref=out_ref.at[pl.ds(pl.multiple_of((1 - col) * half, half), half)],
+            send_sem=send.at[1], recv_sem=recv.at[1], device_id=mate, device_id_type=MESH)
+        theirs.wait_recv()
+        swap.wait_send()
+        swap_back.wait_send()
+
+    return pl.pallas_call(
+        kernel,
+        in_specs=[pl.BlockSpec(memory_space=pltpu.VMEM)],
+        out_specs=pl.BlockSpec(memory_space=pltpu.VMEM),
+        out_shape=jax.ShapeDtypeStruct((rows, width), f32),
+        scratch_shapes=[
+            pltpu.VMEM((rows, width), bf), pltpu.VMEM((half, width), bf), pltpu.VMEM((outer * half, width), bf),
+            pltpu.VMEM((half, width), f32), dma((2,)), dma((2,)), dma((2, outer)), dma((outer,)), dma],
+        compiler_params=pltpu.CompilerParams(
+            collective_id=collective_id, has_side_effects=True, vmem_limit_bytes=VMEM_LIMIT),
+        name="link_sum",
+    )(partial.astype(bf))
+
+
+def link_open(conv, gate, arrays, sizes, collective_id):
+    count = len(arrays)
+    mates = sizes["stream"][0]
+    take = conv.shape[0] // mates
+    dma = pltpu.SemaphoreType.DMA
+
+    def kernel(conv_ref, gate_ref, *refs):
+        sources, refs = refs[:count], refs[count:]
+        conv_all, conv_own, gate_own, outs, refs = *refs[:3], refs[3 : 3 + count], refs[3 + count :]
+        hand_send, hand_recv, sems = refs[0], refs[1], refs[2:]
+        grids = {axis: Grid(axis, *sizes[axis]) for axis in ("seq", "stream")}
+        greet(list(grids.values()), ("stream",))
+        me = grids["stream"].row * grids["stream"].inner + grids["stream"].col
+        waits = []
+
+        def rows(mate):
+            return pl.ds(pl.multiple_of(mate * take, take), take)
+
+        def hand(kind, source, target):
+            copy = pltpu.make_async_copy(source.at[rows(me)], target.at[rows(me)], hand_send.at[kind, 0])
+            copy.start()
+            waits_own = [copy]
+            for step in range(1, mates):
+                mate = (me + step) % mates
+                copy = pltpu.make_async_remote_copy(
+                    src_ref=source.at[rows(mate)], dst_ref=target.at[rows(me)], send_sem=hand_send.at[kind, step],
+                    recv_sem=hand_recv.at[kind, step], device_id={"stream": mate}, device_id_type=MESH)
+                copy.start()
+                waits.append((me >= 0, copy))
+            return waits_own
+
+        def handed(kind, source, target, own):
+            for copy in own:
+                copy.wait()
+            for step in range(1, mates):
+                mate = (me + mates - step) % mates
+                pltpu.make_async_remote_copy(
+                    src_ref=source.at[rows(me)], dst_ref=target.at[rows(mate)], send_sem=hand_send.at[kind, step],
+                    recv_sem=hand_recv.at[kind, step], device_id={"stream": me}, device_id_type=MESH).wait_recv()
+
+        own = hand(0, conv_ref, conv_own)
+
+        def main():
+            for i, (axis, _, chunks) in enumerate(arrays):
+                for chunk in range(chunks):
+                    at = 3 * (1 + sum(entry[2] for entry in arrays[:i]) + chunk)
+                    yield gather_steps(grids[axis], sources[i], outs[i], *sems[at : at + 3], waits, chunk, chunks)
+
+        runs = list(main())
+        for run in runs:
+            next(run)
+        own_gate = hand(1, gate_ref, gate_own)
+        handed(0, conv_ref, conv_own, own)
+        first = gather_steps(grids["seq"], conv_own, conv_all, *sems[:3], waits, 0, 1)
+        next(first)
+        in_turn([first, *runs])
+        handed(1, gate_ref, gate_own, own_gate)
+        finish(waits)
+
+    entries = [("seq", conv, 1), *arrays]
+    sems = []
+    for axis, _, chunks in entries:
+        size = sizes[axis][0]
+        sems += [dma((4, size)), dma((size,)), dma] * chunks
+    result = pl.pallas_call(
+        kernel,
+        in_specs=[pl.BlockSpec(memory_space=pl.ANY)] * (count + 2),
+        out_specs=[pl.BlockSpec(memory_space=pl.ANY)] * (count + 3),
+        out_shape=[
+            jax.ShapeDtypeStruct((sizes["seq"][0] * conv.shape[0], conv.shape[1]), conv.dtype),
+            jax.ShapeDtypeStruct(conv.shape, conv.dtype),
+            jax.ShapeDtypeStruct(gate.shape, gate.dtype),
+            *[jax.ShapeDtypeStruct((sizes[axis][0] * a.shape[0], *a.shape[1:]), a.dtype) for axis, a, _ in arrays]],
+        scratch_shapes=[dma((2, mates)), dma((2, mates)), *sems],
+        compiler_params=pltpu.CompilerParams(collective_id=collective_id, has_side_effects=True),
+        name="link_open",
+    )(conv, gate, *[a for _, a, _ in arrays])
+    return result[0], result[2], *result[3:]
 
 
 def passed_along(block, axis, distance):
@@ -586,21 +830,13 @@
     return jnp.pad(array, ((0, -array.shape[0] % rows), (0, 0)))
 
 
-def shared_sum(partial, sizes, collective_id):
-    width = partial.shape[1]
-    sent = jnp.pad(partial.astype(jnp.bfloat16), ((0, 0), (0, -width % 128)))
-    (terms,) = link_gather([("stream", sent, 2)], sizes, collective_id)
-    terms = terms.reshape(-1, *sent.shape)[:, :, :width].astype(jnp.float32)
-    return jnp.sum(terms, axis=0)
-
-
 def carried(ends, step_sum, rate, backward, sizes, collective_id):
     seqs, chans = step_sum.shape
     n = rate.shape[0]
     high = step_sum.astype(jnp.bfloat16)
     low = (step_sum - high.astype(jnp.float32)).astype(jnp.bfloat16)
     sent = padded_rows(jnp.concatenate([ends.astype(jnp.bfloat16), high, low], axis=0), 16)
-    (gathered,) = link_gather([("seq", sent, 1)], sizes, collective_id)
+    (gathered,) = link_gather([("seq", sent, 1)], sizes, collective_id, (backward, not backward))
     gathered = gathered.reshape(-1, *sent.shape)
     count = lax.axis_size("seq")
     place = lax.axis_index("seq")
@@ -630,9 +866,7 @@
 
     gain = norm_gain.astype(f32)
     scaled = (in_weight.astype(f32) * gain[:, None]).astype(bf).reshape(own_feats, 2, parts, seqs, own)
-    scaled = scaled.transpose(3, 0, 1, 2, 4).reshape(seqs, own_feats, 2, chans)
-
-    mine = lax.all_to_all(scaled.reshape(seqs * own_feats, 2 * chans), "stream", 0, 0, tiled=True)
+    scaled = scaled.transpose(1, 3, 0, 2, 4).reshape(2, seqs * own_feats, chans)
     packed = jnp.concatenate(
         [xproj_weight, dt_weight.T, a_log, conv_weight.T, conv_bias[:, None], dt_bias[:, None], skip_gain[:, None]],
         axis=1)
@@ -641,14 +875,20 @@
     inv_rms = lax.rsqrt(jnp.mean(residual * residual, axis=-1, keepdims=True) + EPSILON)
     unit_own = residual * inv_rms
     slots = row_lengths.shape[1]
-    in_conv, packed, unit, lengths = link_gather(
-        [("seq", mine[:, :chans], 1), ("seq", jnp.pad(packed, ((0, 0), (0, -packed.shape[1] % 128))), 1),
-         ("stream", unit_own.astype(bf), 4), ("stream", jnp.pad(row_lengths, ((0, 7), (0, -slots % 128))), 1)],
-        sizes, 1)
+    arrays = [
+        ("stream", jnp.pad(row_lengths, ((0, 7), (0, -slots % 128))), 1), ("stream", unit_own.astype(bf), 4),
+        ("seq", jnp.pad(packed, ((0, 0), (0, -packed.shape[1] % 128))), 1)]
+    if own_feats % 16:
+        mine = lax.all_to_all(scaled, "stream", 1, 1, tiled=True)
+        gate_own = mine[1]
+        lengths, unit, packed, in_conv = link_gather([*arrays, ("seq", mine[0], 1)], sizes, 1)
+    else:
+        in_conv, gate_own, lengths, unit, packed = link_open(scaled[0], scaled[1], arrays, sizes, 1)
     lengths = lengths[::8, :slots]
-    in_gate = lax.all_gather(mine[:, chans:], "seq", axis=0, tiled=True)
-    out_full = lax.all_gather(out_weight, "seq", axis=0, tiled=True)
-    cot_all = lax.all_gather(cotangent, "stream", axis=0, tiled=True)
+    unit, gate_own, out_own, cot_own = lax.optimization_barrier((unit, gate_own, out_weight, cotangent))
+    in_gate = lax.all_gather(gate_own, "seq", axis=0, tiled=True)
+    out_full = lax.all_gather(out_own, "seq", axis=0, tiled=True)
+    cot_all = lax.all_gather(cot_own, "stream", axis=0, tiled=True)
     xproj_full = packed[:, :proj_dim]
     dtw_cols = packed[:, proj_dim : proj_dim + rank_dim]
     at = proj_dim + rank_dim
@@ -677,21 +917,22 @@
         conv_out = conv_out + conv_taps[tap] * padded[:, tap : tap + length] * matches[tap]
     activated = jax.nn.silu(conv_out).astype(bf).reshape(tokens, chans)
     act_float = activated.astype(f32)
-    projected = shared_sum(jnp.dot(activated, xproj_full, preferred_element_type=f32), sizes, 2)
-    low_rank = projected[:, :rank_dim].astype(bf)
-    write_in = projected[:, rank_dim : rank_dim + state_dim]
-    readout = projected[:, rank_dim + state_dim :]
-    dt_pre = contract_cols(low_rank, dtw_cols) + dt_shift
+    projected = link_sum(
+        lax.dot_general(xproj_full, activated, (((0,), (1,)), ((), ())), preferred_element_type=f32), sizes, 2)
+    low_rank = projected[:rank_dim].astype(bf)
+    write_in = projected[rank_dim : rank_dim + state_dim]
+    readout = projected[rank_dim + state_dim :]
+    dt_pre = lax.dot_general(low_rank, dtw_cols, (((0,), (1,)), ((), ())), preferred_element_type=f32) + dt_shift
     dt_step = jax.nn.softplus(dt_pre)
     dt_reset = jnp.where(starts > 0, RESET, dt_step)
     dt_act = dt_step * act_float
-    write_wide, read_wide = widen(write_in), widen(readout)
+    write_slabs, read_slabs = slabs_of(write_in), slabs_of(readout)
     write_diag, read_diag = spread(write_in), spread(readout)
 
     step_sum = jnp.sum(dt_reset.reshape(seqs, length, chans), axis=1)
-    ends = scan_end(fwd_end_body, dt_reset, dt_act, write_wide, rate, seqs)
+    ends = scan_end(fwd_end_body, dt_reset, dt_act, write_slabs, rate, seqs)
     start_state = carried(ends, step_sum, rate, False, sizes, 3)
-    scanned, history = fwd_full(dt_reset, dt_act, write_wide, read_diag, rate, start_state, seqs)
+    scanned, history = fwd_full(dt_reset, dt_act, write_slabs, read_diag, rate, start_state, seqs)
     ssm_out = scanned + skip_vec * act_float
     gate_act = jax.nn.silu(gate_in)
     gated = (ssm_out * gate_act * valid).astype(bf)
@@ -705,20 +946,21 @@
     d_gate = (d_masked * ssm_out * silu_slope(gate_in)).astype(bf)
     g_in_gate = lax.psum_scatter(contract_rows(unit, d_gate).astype(bf), "seq", scatter_dimension=0, tiled=True)
     g_skip = jnp.sum(d_ssm * act_float, axis=0)
-    back_ends = scan_end(bwd_end_body, dt_reset, d_ssm, read_wide, rate, seqs)
+    back_ends = scan_end(bwd_end_body, dt_reset, d_ssm, read_slabs, rate, seqs)
     later_sum = carried(back_ends, step_sum, rate, True, sizes, 4)
     sum_write, sum_rate, g_log, d_write, d_read = bwd_full(
-        dt_reset, dt_act, d_ssm, history, read_wide, write_diag, rate, later_sum, seqs)
+        dt_reset, dt_act, d_ssm, history, read_slabs, write_diag, rate, later_sum, seqs)
     per_step = jnp.where(dt_step > 1e-30, sum_rate * LN2 / jnp.maximum(dt_step, 1e-30), 0.0)
     d_step = per_step + act_float * sum_write
     d_pre = d_step * jax.nn.sigmoid(dt_pre)
     g_dt_bias = jnp.sum(d_pre, axis=0)
     d_pre_low = d_pre.astype(bf)
-    g_dt = contract_rows(d_pre_low, low_rank)
-    d_low = jnp.dot(d_pre_low, dtw_cols, preferred_element_type=f32)
-    d_proj = shared_sum(jnp.concatenate([d_low, d_write, d_read], axis=1), sizes, 5).astype(bf)
-    g_xproj = contract_rows(activated, d_proj)
-    d_act = dt_step * sum_write + skip_vec * d_ssm + contract_cols(d_proj, xproj_full)
+    g_dt = lax.dot_general(d_pre_low, low_rank, (((0,), (1,)), ((), ())), preferred_element_type=f32)
+    d_low = lax.dot_general(dtw_cols, d_pre_low, (((0,), (1,)), ((), ())), preferred_element_type=f32)
+    d_proj = link_sum(jnp.concatenate([d_low, d_write, d_read], axis=0), sizes, 5).astype(bf)
+    g_xproj = lax.dot_general(activated, d_proj, (((0,), (1,)), ((), ())), preferred_element_type=f32)
+    d_act = dt_step * sum_write + skip_vec * d_ssm + lax.dot_general(
+        d_proj, xproj_full, (((0,), (1,)), ((), ())), preferred_element_type=f32)
     d_conv = d_act.reshape(seqs, length, chans) * silu_slope(conv_out)
     g_conv_bias = jnp.sum(d_conv, axis=(0, 1))
     g_conv = jnp.stack(
@@ -737,16 +979,17 @@
         [g_xproj, g_dt, g_log.T * LN2, g_conv, g_conv_bias[:, None], g_dt_bias[:, None], g_skip[:, None]], axis=1)
     small = jnp.pad(small, ((0, 0), (0, -small.shape[1] % 128))).astype(bf)
     g_in_conv, small, d_unit = link_reduce(
-        [("seq", g_in_conv, 1), ("seq", small, 1), ("stream", d_unit, 4)], sizes, 6)
+        [("seq", g_in_conv, 1, 0 if own_feats % 16 else own), ("seq", small, 1, 0), ("stream", d_unit, 4, 0)], sizes, 6)
     small = small.astype(f32)
     d_unit = d_unit.astype(f32)
     in_grad = cotangent.astype(f32) + inv_rms * (d_unit - unit_own * jnp.mean(d_unit * unit_own, axis=-1, keepdims=True))
 
     def in_rows(block):
-        shared = lax.all_to_all(block, "stream", 0, 0, tiled=True).reshape(seqs, own_feats, 2 * parts, own)
-        return shared.transpose(1, 2, 0, 3).reshape(own_feats, 2 * parts * seqs * own).astype(f32)
-
-    g_unit = in_rows(jnp.stack([g_in_conv, g_in_gate], axis=1).reshape(g_in_conv.shape[0], 2 * chans))
+        shared = lax.all_to_all(block, "stream", 0, 0, tiled=True).reshape(seqs, own_feats, parts, own)
+        return shared.transpose(1, 2, 0, 3).reshape(own_feats, parts * seqs * own)
+
+    g_in_conv = in_rows(g_in_conv) if own_feats % 16 else g_in_conv
+    g_unit = jnp.concatenate([g_in_conv, in_rows(g_in_gate)], axis=1).astype(f32)
     at = proj_dim + rank_dim
     return (
         output[None],

time: 996 us -> 888 us (0.89)
  Pallas kernels: 551 us -> 487 us
  local copies, waits for them, and re-layouts: 90.8 us -> 66.8 us
  starting transfers between devices: 29.4 us -> 15.2 us
    pallas_call x5 -> x2, Pallas kernels: 211 us -> 27.4 us  [link_gather(): pl.pallas_call(kernel, in_specs=[pl.BlockSpec(memory_space=pl.ANY)] * cou...]
    pallas_call x0 -> x3, Pallas kernels: none -> 134 us  [the longest x1 94.8 us: link_open(): pl.pallas_call(kernel, in_specs=[pl.BlockSpec(memory_space=pl.ANY)] * (co...]
    broadcast_in_dim x4 -> x0, local copies, waits for them, and re-layouts: 31.5 us -> none  [widen(): return jnp.broadcast_to(values.reshape(-1)[:, None], (values.size, 128))]
    dot_general x2 -> x6, matrix products: 5.11 us -> 32.6 us  [the longest x1 15.2 us: local(): lax.dot_general(d_proj, xproj_full, (((0,), (1,)), ((), ())), preferred_e...]
    dot_general x5 -> x3, matrix products: 62.5 us -> 40.7 us  [contract_cols(): lax.dot_general(left_mat, right_mat, NT, preferred_element_type=jnp.float32)]
    pallas_call x1, Pallas kernels: 57.9 us -> 41.9 us  [fwd_full(): pl.pallas_call(fwd_full_body, grid=(chans // width, seqs, blocks), in_spe...]
    all_to_all x1, starting transfers between devices: 18.7 us -> 4.43 us  [in_rows(): lax.all_to_all(block, 'stream', 0, 0, tiled=True)]
    pallas_call x1, Pallas kernels: 107 us -> 93.1 us  [bwd_full(): pl.pallas_call(bwd_full_body, grid=(strips, seqs, blocks), in_specs=[pl.B...]
  transfers between devices with their start and end apart: 10 -> 9, of which waited for: 1 -> 1; matrix products, arithmetic and copies ran while one was open for 33% -> 32% of each run, Pallas kernels for 56% -> 45%
where the time goes in v3:
time: 888 us; the launch traced here: 877 us
  Pallas kernels  487 us (55%)
  matrix products  168 us (19%)
  other arithmetic  113 us (13%)
  local copies, waits for them, and re-layouts  66.8 us (8%)
  between operations  15.8 us (2%)
  starting transfers between devices  15.2 us (2%)
  waiting for transfers between devices  10.6 us (1%)
    pallas_call x1, Pallas kernels, link_reduce(): pl.pallas_call(kernel, in_specs=[pl.BlockSpec(memory_space=pl.ANY)] * cou...  128 us
    pallas_call x1, Pallas kernels, link_open(): pl.pallas_call(kernel, in_specs=[pl.BlockSpec(memory_space=pl.ANY)] * (co...  94.8 us
    pallas_call x1, Pallas kernels, bwd_full(): pl.pallas_call(bwd_full_body, grid=(strips, seqs, blocks), in_specs=[pl.B...  93.1 us
    pallas_call x2, Pallas kernels, scan_end(): pl.pallas_call(body, grid=(seqs, chans // width), in_specs=[pl.BlockSpec(...  62.5 us
    pallas_call x1, Pallas kernels, fwd_full(): pl.pallas_call(fwd_full_body, grid=(chans // width, seqs, blocks), in_spe...  41.9 us
    dot_general x3, matrix products, contract_rows(): lax.dot_general(left_mat, right_mat, (((0,), (0,)), ((), ())), preferred_...  41.4 us
    dot_general x3, matrix products, contract_cols(): lax.dot_general(left_mat, right_mat, NT, preferred_element_type=jnp.float32)  40.7 us
    pallas_call x2, Pallas kernels, link_sum(): pl.pallas_call(kernel, in_specs=[pl.BlockSpec(memory_space=pltpu.VMEM)],...  39.2 us
  transfers between devices with their start and end apart: 9, of which 1 were waited for; matrix products, arithmetic and copies ran while one was open for 32% of the time, Pallas kernels for 45%

profile of v3, /device:TPU:19, one launch (start us, length us, event | category | flops | bytes accessed | tf_op | source)
XLA Modules:
  0.0 876.6 jit_solution(12518711122716431145)
XLA Ops:
  25.0 94.8 %link_open.1 = (bf16[2048,1024]{1,0:T(8,128)(2,1)}, bf16[256,1024]{1,0:T(8,128)(2,1)}, bf16[256,1024]{1,0:T(8,128)(2,1)}, s32[32,128]{1,0:T(8,128)}, bf16[2048,2...) custom-call(bf16[256,1024]{1,0:T(8,128)(2,1)} %get-tuple-element.191.conv_ref, bf16[256,1024]{1,0:T(8,128)(2,1)} %get-tuple-element.190.gate_ref, ...), custom_call_target="tpu_custom_call" | custom-call | tf_op jit(solution)/shard_map/link_open/pallas_call | solution.py:783
  120.6 12.5 %fusion.76 = f32[2048,1024]{1,0:T(8,128)S(1)} fusion(bf16[2048,2048]{1,0:T(8,128)(2,1)} %get-tuple-element.35, bf16[2048,1024]{1,0:T(8,128)(2,1)} %get-tuple-element.36), kind=kOutput, calls=%fused_computation.243 | convolution fusion | flops 8589934592 | bytes 20971520 | tf_op jit(solution)/shard_map/dot_general | solution.py:911
  145.1 18.9 %multiply_convert_fusion.2 = (bf16[4,512,1024]{2,1,0:T(8,128)(2,1)S(1)}, f32[4,512,1024]{2,1,0:T(8,128)}) fusion(f32[4,512,1024]{2,1,0:T(8,128)} %bitcast.244, f32[1024]{0:T(1024)S(1)} %get-tuple-element.122, f32[4,512]{1,0:T(4,128)S(1)} %get-tuple-element.185, f32[4,3,1024]{2,1,0:T(4,128)S(1)} %convert_element_type.250, f32[1024]{0:T(1024)S(1)} %get-tuple-element.123, ...), kind=kLoop, calls=%fused_computation.41 | loop fusion | flops 39845888 | bytes 21065728 | tf_op jit(solution)/shard_map/convert_element_type | solution.py:918
  168.6 15.9 %link_sum.2 = f32[160,2048]{1,0:T(8,128)} custom-call(bf16[160,2048]{1,0:T(8,128)(2,1)} %convolution_convert_fusion.4.own_ref), custom_call_target="tpu_custom_call" | custom-call | tf_op jit(solution)/shard_map/link_sum/pallas_call | solution.py:705
  194.7 8.2 bitcast_reduce_fusion
  202.9 7.5 convert_multiply_fusion.3.dtx_ref
  210.4 31.2 %fwd_end.1 = f32[64,1024]{1,0:T(8,128)} custom-call(f32[2048,1024]{1,0:T(8,128)} %get-tuple-element.136.dte_ref, f32[2048,1024]{1,0:T(8,128)} %convert_multiply_fusion.3.dtx_ref, f32[2048,16]{1,0:T(8,128)} %bitcast.262, f32[16,1024]{1,0:T(8,128)} %multiply_bitcast_fusion.rate_ref), custom_call_target="tpu_custom_call" | custom-call | flops 134217728 | bytes 16777216 | tf_op jit(solution)/shard_map/fwd_end/pallas_call | solution.py:81
  243.3 14.3 %link_gather.2 = bf16[640,1024]{1,0:T(8,128)(2,1)} custom-call(bf16[80,1024]{1,0:T(8,128)(2,1)} %pad.22.refs_0_), custom_call_target="tpu_custom_call" | custom-call | tf_op jit(solution)/shard_map/link_gather/pallas_call | solution.py:461
  260.7 41.9 %fwd_full.1 = (f32[2048,1024]{1,0:T(8,128)}, bf16[32896,1024]{1,0:T(8,128)(2,1)}) custom-call(f32[2048,1024]{1,0:T(8,128)} %get-tuple-element.136.dte_ref, f32[2048,1024]{1,0:T(8,128)} %convert_multiply_fusion.3.dtx_ref, f32[2048,16]{1,0:T(8,128)} %bitcast.263, bf16[2048,256]{1,0:T(8,128)(2,1)} %copy.153.read_ref, f32[16,1024]{1,0:T(8,128)} %multiply_bitcast_fusion.rate_ref, ...), custom_call_target="tpu_custom_call" | custom-call | flops 268435456 | bytes 67108864 | tf_op jit(solution)/shard_map/fwd_full/pallas_call | solution.py:146
  302.6 14.5 %fusion.77 = f32[2048,1024]{1,0:T(8,128)} fusion(bf16[2048,2048]{1,0:T(8,128)(2,1)} %all-gather.8.cloned.1.call-done, bf16[1024,2048]{1,0:T(8,128)(2,1)} %all-gather.6.cloned.1.call-done), kind=kOutput, calls=%fused_computation.244 | convolution fusion | flops 8589934592 | bytes 20971520 | tf_op jit(solution)/shard_map/dot_general | solution.py:826
  317.1 9.7 %all-gather.4.cloned.1.call-done = bf16[2048,1024]{1,0:T(8,128)(2,1)} async-done(((bf16[256,1024]{1,0:T(8,128)(2,1)}), bf16[2048,1024]{1,0:T(8,128)(2,1)}) %all-gather.4.cloned.1.call-update) | async-done | bytes 4194320 | tf_op jit(solution)/shard_map/all_gather | solution.py:889
  326.8 26.4 %multiply_convert_fusion = (bf16[2048,1024]{1,0:T(8,128)(2,1)}, bf16[2048,1024]{1,0:T(8,128)(2,1)}, bf16[1024]{0:T(1024)(128)(2,1)}, f32[2048,1024]{1,0:T(8,128)}) fusion(f32[2048,1024]{1,0:T(8,128)} %fusion.77, f32[2048,1024]{1,0:T(8,128)} %get-tuple-element.37, f32[2048]{0:T(1024)S(1)} %bitcast.269, f32[1024]{0:T(1024)S(1)} %get-tuple-element.118, ...), kind=kOutput, calls=%fused_computation.31 | convolution fusion | flops 8633973760 | bytes 50345984 | tf_op jit(solution)/shard_map/dot_general | solution.py:912
  353.3 14.2 %convolution_convert_fusion.2 = bf16[2048,1024]{1,0:T(8,128)(2,1)} fusion(bf16[2048,2048]{1,0:T(8,128)(2,1)} %get-tuple-element.35, bf16[2048,1024]{1,0:T(8,128)(2,1)} %get-tuple-element.139), kind=kOutput, calls=%fused_computation.62 | convolution fusion | flops 8592031744 | bytes 16777216 | tf_op jit(solution)/shard_map/dot_general | solution.py:822
  367.5 14.1 %convolution_convert_fusion.1 = bf16[1024,2048]{1,0:T(8,128)(2,1)} fusion(bf16[2048,1024]{1,0:T(8,128)(2,1)} %get-tuple-element.140, bf16[2048,2048]{1,0:T(8,128)(2,1)} %all-gather.8.cloned.1.call-done), kind=kOutput, calls=%fused_computation.61 | convolution fusion | flops 8592031744 | bytes 16777216 | tf_op jit(solution)/shard_map/dot_general | solution.py:822
  385.6 31.3 %bwd_end.1 = f32[64,1024]{1,0:T(8,128)} custom-call(f32[2048,1024]{1,0:T(8,128)} %get-tuple-element.136.dte_ref, f32[2048,1024]{1,0:T(8,128)} %get-tuple-element.142.grad_ref, f32[2048,16]{1,0:T(8,128)} %bitcast.249, f32[16,1024]{1,0:T(8,128)} %multiply_bitcast_fusion.rate_ref), custom_call_target="tpu_custom_call" | custom-call | flops 134217728 | bytes 16777216 | tf_op jit(solution)/shard_map/bwd_end/pallas_call | solution.py:81
  418.6 13.1 %link_gather.3 = bf16[640,1024]{1,0:T(8,128)(2,1)} custom-call(bf16[80,1024]{1,0:T(8,128)(2,1)} %pad.23.refs_0_), custom_call_target="tpu_custom_call" | custom-call | tf_op jit(solution)/shard_map/link_gather/pallas_call | solution.py:461
  433.4 14.4 %convolution_convert_fusion = bf16[2048,2048]{1,0:T(8,128)(2,1)} fusion(bf16[2048,1024]{1,0:T(8,128)(2,1)} %get-tuple-element.140, bf16[1024,2048]{1,0:T(8,128)(2,1)} %all-gather.6.cloned.1.call-done), kind=kOutput, calls=%fused_computation.45 | convolution fusion | flops 8594128896 | bytes 16777216 | tf_op jit(solution)/shard_map/dot_general | solution.py:939
  450.0 93.1 %bwd_full.1 = (f32[2048,1024]{1,0:T(8,128)}, f32[2048,1024]{1,0:T(8,128)}, f32[16,1024]{1,0:T(8,128)}, f32[256,256]{1,0:T(8,128)}, f32[4096,256]{1,0:T(8,128)}) custom-call(f32[2048,1024]{1,0:T(8,128)} %get-tuple-element.136.dte_ref, f32[2048,1024]{1,0:T(8,128)} %convert_multiply_fusion.3.dtx_ref, f32[2048,1024]{1,0:T(8,128)} %get-tuple-element.142.grad_ref, ...), custom_call_target="tpu_custom_call" | custom-call | flops 469762048 | bytes 67108864 | tf_op jit(solution)/shard_map/bwd_full/pallas_call | solution.py:246
  543.2 14.6 %fusion.72 = (bf16[1024]{0:T(1024)(128)(2,1)S(1)}, bf16[2048,1024]{1,0:T(8,128)(2,1)}) fusion(f32[2048,1024]{1,0:T(8,128)} %get-tuple-element.42, bf16[4,512,1024]{2,1,0:T(8,128)(2,1)S(1)} %copy-done.2, f32[2048,1024]{1,0:T(8,128)} %get-tuple-element.43, f32[2048,1024]{1,0:T(8,128)} %copy-done.5, f32[1024]{0:T(1024)S(1)} %copy-done.31), kind=kLoop, calls=%fused_computation.240 | loop fusion | flops 44039168 | bytes 33560576 | tf_op jit(solution)/shard_map/reduce_sum | solution.py:956
  559.1 6.1 copy.157
  565.2 7.0 reshape.393
  576.1 5.3 select_reduce_fusion
  582.3 23.4 %link_sum.3 = f32[160,2048]{1,0:T(8,128)} custom-call(bf16[160,2048]{1,0:T(8,128)(2,1)} %pad_maximum_fusion.3.own_ref), custom_call_target="tpu_custom_call" | custom-call | tf_op jit(solution)/shard_map/link_sum/pallas_call | solution.py:705
  605.7 15.2 %add_add_fusion = f32[2048,1024]{1,0:T(8,128)} fusion(f32[2048,1024]{1,0:T(8,128)} %get-tuple-element.142.grad_ref, f32[2048,1024]{1,0:T(8,128)} %get-tuple-element.42, f32[1024]{0:T(1024)S(1)} %get-tuple-element.118, bf16[1024,384]{1,0:T(8,128)(2,1)S(1)} %copy-done.10, f32[160,2048]{1,0:T(8,128)} %link_sum.3, f32[2048,1024]{1,0:T(8,128)} %copy-done.5, ...), kind=kOutput, calls=%fused_computation.37 | convolution fusion | flops 694484992 | bytes 35397632 | tf_op jit(solution)/shard_map/dot_general | solution.py:962
  621.1 15.0 %fusion.71 = (bf16[1024]{0:T(1024)(128)(2,1)S(1)}, bf16[1024]{0:T(1024)(128)(2,1)S(1)}, bf16[1024]{0:T(1024)(128)(2,1)S(1)}, bf16[1024]{0:T(1024)(128)(2,1)S(1)}...) fusion(f32[2048,1024]{1,0:T(8,128)S(1)} %bitcast.246, f32[4,512]{1,0:T(4,128)S(1)} %copy-done.28, ...), kind=kLoop, calls=%fused_computation.239 | loop fusion | flops 48229376 | bytes 42027008 | tf_op jit(solution)/shard_map/reduce_sum | solution.py:965
  637.2 7.0 collective-permute-start.1
  647.2 11.9 %fusion.78 = f32[2048,2048]{1,0:T(8,128)} fusion(bf16[2048,1024]{1,0:T(8,128)(2,1)S(1)} %copy-done.51, bf16[2048,1024]{1,0:T(8,128)(2,1)S(1)} %copy-done.50), kind=kOutput, calls=%fused_computation.245 | convolution fusion | flops 8589934592 | bytes 25165824 | tf_op jit(solution)/shard_map/dot_general | solution.py:826
  664.7 16.7 %fusion.6 = bf16[4,512,1024]{2,1,0:T(8,128)(2,1)S(1)} fusion(f32[4,3,1024]{2,1,0:T(4,128)S(1)} %convert_element_type.294, f32[4,512,1024]{2,1,0:T(8,128)} %get-tuple-element.132, f32[4,512]{1,0:T(4,128)S(1)} %copy-done.44, f32[4,512]{1,0:T(4,128)S(1)} %copy-done.43, f32[4,512]{1,0:T(4,128)S(1)} %copy-done.42, f32[1024]{0:T(1024)S(1)} %copy-done.35, ...), kind=kLoop, calls=%fused_computation.16 | loop fusion | flops 29360128 | bytes 12673024 | tf_op jit(solution)/shard_map/convert_element_type | solution.py:975
  681.4 13.1 %convolution_convert_fusion.3.refs_0_ = bf16[2048,1024]{1,0:T(8,128)(2,1)} fusion(bf16[2048,2048]{1,0:T(8,128)(2,1)} %get-tuple-element.35, bf16[2048,1024]{1,0:T(8,128)(2,1)S(1)} %bitcast.256), kind=kOutput, calls=%fused_computation.63 | convolution fusion | flops 8592031744 | bytes 16777216 | tf_op jit(solution)/shard_map/dot_general | solution.py:822
  694.5 14.3 %add_convert_fusion.refs_2_ = bf16[2048,2048]{1,0:T(8,128)(2,1)} fusion(f32[2048,2048]{1,0:T(8,128)} %fusion.78, bf16[2048,1024]{1,0:T(8,128)(2,1)S(1)} %bitcast.257, bf16[2048,1024]{1,0:T(8,128)(2,1)S(1)} %copy-done.49), kind=kOutput, calls=%fused_computation.1 | convolution fusion | flops 8598323200 | bytes 33554432 | tf_op jit(solution)/shard_map/dot_general | solution.py:826
  708.8 128.2 %link_reduce.1 = (bf16[64,4096]{1,0:T(8,128)(2,1)}, bf16[128,384]{1,0:T(8,128)(2,1)}, bf16[512,2048]{1,0:T(8,128)(2,1)}) custom-call(bf16[2048,1024]{1,0:T(8,128)(2,1)} %convolution_convert_fusion.3.refs_0_, bf16[1024,384]{1,0:T(8,128)(2,1)} %pad.24.refs_1_, bf16[2048,2048]{1,0:T(8,128)(2,1)} %add_convert_fusion.refs_2_), custom_call_target="tpu_custom_call" | custom-call | tf_op jit(solution)/shard_map/link_reduce/pallas_call | solution.py:651
  863.8 5.5 fusion.31
  (254 shorter events, 101.3 us)
Async XLA Ops:
  7.2 295.4 %all-gather.6.cloned.1.call-start = ((), (), s32[]{:S(2)}) async-start(), calls=%async_computation.5 | async-start | bytes 4718592 | tf_op jit(solution)/shard_map/all_gather | solution.py:890
  10.1 109.6 %copy-start.40 = (f32[512]{0:T(512)}, f32[512]{0:T(512)S(1)}, u32[]{:S(2)}) copy-start(f32[512]{0:T(512)S(1)} %add_rsqrt_fusion) | copy-start | bytes 6148
  119.8 182.8 %all-gather.8.cloned.1.call-start = ((), (), s32[]{:S(2)}) async-start(), calls=%async_computation.7 | async-start | bytes 10485760 | tf_op jit(solution)/shard_map/all_gather | solution.py:891
  120.5 206.3 %all-gather.4.cloned.1.call-start = ((), (), s32[]{:S(2)}) async-start(), calls=%async_computation.4 | async-start | bytes 4718592 | tf_op jit(solution)/shard_map/all_gather | solution.py:889
  120.6 20.8 %copy-start.9 = (bf16[1024,384]{1,0:T(8,128)(2,1)S(1)}, bf16[1024,384]{1,0:T(8,128)(2,1)}, u32[]{:S(2)}) copy-start(bf16[1024,384]{1,0:T(8,128)(2,1)} %get-tuple-element.32) | copy-start | bytes 2359300
  136.4 8.7 collective-permute-start
  139.6 701.0 %reduce-scatter.6.cloned.1.call-start = ((), (), s32[]{:S(2)}) async-start(), calls=%async_computation.8 | async-start | bytes 4718592 | tf_op jit(solution)/shard_map/reduce_scatter | solution.py:947
  141.9 48.8 %copy-start.20 = (pred[2048,16]{0,1:T(8,128)(4,1)}, pred[2048,16]{0,1:T(8,128)(4,1)S(1)}, u32[]{:S(2)}) copy-start(pred[2048,16]{0,1:T(8,128)(4,1)S(1)} %iota_compare_fusion) | copy-start | bytes 98308
  142.7 21.3 %copy-start.23 = (f32[4,512]{1,0:T(4,128)}, f32[4,512]{1,0:T(4,128)S(1)}, u32[]{:S(2)}) copy-start(f32[4,512]{1,0:T(4,128)S(1)} %get-tuple-element.185) | copy-start | bytes 24580
  142.7 21.3 %copy-start.25 = (f32[4,512]{1,0:T(4,128)}, f32[4,512]{1,0:T(4,128)S(1)}, u32[]{:S(2)}) copy-start(f32[4,512]{1,0:T(4,128)S(1)} %get-tuple-element.186) | copy-start | bytes 24580
  142.7 21.3 %copy-start.27 = (f32[4,512]{1,0:T(4,128)}, f32[4,512]{1,0:T(4,128)S(1)}, u32[]{:S(2)}) copy-start(f32[4,512]{1,0:T(4,128)S(1)} %get-tuple-element.188) | copy-start | bytes 24580
  143.7 20.3 %copy-start.32 = (f32[1024]{0:T(1024)}, f32[1024]{0:T(1024)S(1)}, u32[]{:S(2)}) copy-start(f32[1024]{0:T(1024)S(1)} %get-tuple-element.121) | copy-start | bytes 12292
  143.7 20.3 %copy-start.34 = (f32[1024]{0:T(1024)}, f32[1024]{0:T(1024)S(1)}, u32[]{:S(2)}) copy-start(f32[1024]{0:T(1024)S(1)} %get-tuple-element.122) | copy-start | bytes 12292
  143.7 20.3 %copy-start.36 = (f32[1024]{0:T(1024)}, f32[1024]{0:T(1024)S(1)}, u32[]{:S(2)}) copy-start(f32[1024]{0:T(1024)S(1)} %get-tuple-element.123) | copy-start | bytes 12292
  143.7 20.3 %copy-start.38 = (f32[1024]{0:T(1024)}, f32[1024]{0:T(1024)S(1)}, u32[]{:S(2)}) copy-start(f32[1024]{0:T(1024)S(1)} %get-tuple-element.124) | copy-start | bytes 12292
  145.0 57.9 %copy-start.30 = (f32[1024]{0:T(1024)}, f32[1024]{0:T(1024)S(1)}, u32[]{:S(2)}) copy-start(f32[1024]{0:T(1024)S(1)} %get-tuple-element.119) | copy-start | bytes 12292
  210.4 49.0 %copy-start.16 = (f32[16,1024]{1,0:T(8,128)S(1)}, f32[16,1024]{1,0:T(8,128)}, u32[]{:S(2)}) copy-start(f32[16,1024]{1,0:T(8,128)} %multiply_bitcast_fusion.rate_ref) | copy-start | bytes 196612
  367.5 485.8 %reduce-scatter.8.cloned.1.call-start = ((), (), s32[]{:S(2)}) async-start(), calls=%async_computation.9 | async-start | bytes 4718592 | tf_op jit(solution)/shard_map/reduce_scatter | solution.py:943
  381.6 482.1 %reduce-scatter.4.cloned.1.call-start = ((), (), s32[]{:S(2)}) async-start(), calls=%async_computation.6 | async-start | bytes 10485760 | tf_op jit(solution)/shard_map/reduce_scatter | solution.py:940
  450.0 93.1 %copy-start.2 = (bf16[4,512,1024]{2,1,0:T(8,128)(2,1)S(1)}, bf16[4,512,1024]{2,1,0:T(8,128)(2,1)}, u32[]{:S(2)}) copy-start(bf16[4,512,1024]{2,1,0:T(8,128)(2,1)} %copy-done) | copy-start | bytes 12582916
  450.0 93.2 %copy-start.31 = (f32[1024]{0:T(1024)S(1)}, f32[1024]{0:T(1024)}, u32[]{:S(2)}) copy-start(f32[1024]{0:T(1024)} %copy-done.30) | copy-start | bytes 12292
  576.1 44.9 %slice-start = ((s8[8388608]{0:T(1024)(128)(4,1)}), s8[4194304]{0:T(1024)(128)(4,1)S(1)}, s32[]{:S(2)}) async-start(s8[8388608]{0:T(1024)(128)(4,1)} %bitcast.245), calls=%async_computation.10 | async-start | bytes 8388608
  621.0 23.2 %copy-start.3 = (bf16[4,512,1024]{2,1,0:T(8,128)(2,1)S(1)}, bf16[4,512,1024]{2,1,0:T(8,128)(2,1)}, u32[]{:S(2)}) copy-start(bf16[4,512,1024]{2,1,0:T(8,128)(2,1)} %copy-done) | copy-start | bytes 12582916
  621.0 23.2 %copy-start.11 = (f32[160,2048]{1,0:T(8,128)S(1)}, f32[160,2048]{1,0:T(8,128)}, u32[]{:S(2)}) copy-start(f32[160,2048]{1,0:T(8,128)} %link_sum.3) | copy-start | bytes 3932164
  621.1 24.1 %copy-start.6 = (bf16[2048,1024]{1,0:T(8,128)(2,1)S(1)}, bf16[2048,1024]{1,0:T(8,128)(2,1)}, u32[]{:S(2)}) copy-start(bf16[2048,1024]{1,0:T(8,128)(2,1)} %get-tuple-element.131) | copy-start | bytes 12582916
  621.1 24.1 %copy-start.13 = (f32[160,2048]{1,0:T(8,128)S(1)}, f32[160,2048]{1,0:T(8,128)}, u32[]{:S(2)}) copy-start(f32[160,2048]{1,0:T(8,128)} %link_sum.2) | copy-start | bytes 3932164
  637.2 27.4 %collective-permute-start.1 = (bf16[4,3,1024]{2,1,0:T(4,128)(2,1)S(1)}, bf16[4,3,1024]{2,1,0:T(4,128)(2,1)S(1)}, u32[]{:S(2)}, u32[]{:S(2)}) collective-permute-start(bf16[4,3,1024]{2,1,0:T(4,128)(2,1)S(1)} %slice.772), channel_id=1, source_target_pairs={{4,0},{8,4},{12,8},{16,12},{20,16},{24,20},{28,24},{5,1},{9,5},{13... | collective-permute-start | bytes 73736 | tf_op jit(solution)/shard_map/ppermute | solution.py:802
  708.8 129.3 %copy-start.8 = (bf16[1,512,2048]{2,1,0:T(8,128)(2,1)S(1)}, bf16[1,512,2048]{2,1,0:T(8,128)(2,1)}, u32[]{:S(2)}) copy-start(bf16[1,512,2048]{2,1,0:T(8,128)(2,1)} %param.13) | copy-start | bytes 6291460
  708.8 129.3 %copy-start.41 = (f32[512]{0:T(512)S(1)}, f32[512]{0:T(512)}, u32[]{:S(2)}) copy-start(f32[512]{0:T(512)} %copy-done.40) | copy-start | bytes 6148
  837.0 23.2 %copy-start.14 = (bf16[64,8192]{1,0:T(8,128)(2,1)S(1)}, bf16[64,8192]{1,0:T(8,128)(2,1)}, u32[]{:S(2)}) copy-start(bf16[64,8192]{1,0:T(8,128)(2,1)} %param.17) | copy-start | bytes 3145732
  837.0 23.2 %copy-start.47 = (f32[64]{0:T(128)S(1)}, f32[64]{0:T(128)}, u32[]{:S(2)}) copy-start(f32[64]{0:T(128)} %copy-done.46) | copy-start | bytes 772
  840.6 14.8 %all-to-all-start = ((bf16[4,64,1024]{2,1,0:T(8,128)(2,1)}), bf16[4,64,1024]{2,1,0:T(8,128)(2,1)}, u32[]{:S(2)}, u32[]{:S(2)}) async-start(bf16[4,64,1024]{2,1,0:T(8,128)(2,1)} %bitcast.264), calls=%async_computation.2 | async-start | bytes 1048576 | tf_op jit(solution)/shard_map/all_to_all | solution.py:988
  (31 other events, 326.3 us)
Sparse Core Ops, SparseCore 0:
  119.9 73.1 all-gather.5
  194.7 57.2 all-gather.7
  254.1 72.6 all-gather.3
  367.6 91.1 reduce-scatter.5
  462.7 87.7 reduce-scatter.7
  553.0 77.8 reduce-scatter.3

commit v4 on v3

--- a/solution.py
+++ b/solution.py
@@ -190,9 +190,11 @@
         sums = jnp.dot(ones_ref[...], rated_ref[...], preferred_element_type=f32)
         s2_ref[rows, :] = sums[:GROUP]
         dw_ref[pl.ds(at, 1), :] = lax.dot_general(unit, dw_part[...], NT, preferred_element_type=f32)[:1]
-        dr_ref[rows, :] = lax.dot_general(
+        reads = lax.dot_general(
             grad_ref[rows, :].astype(bf), hist_ref[pl.ds(n + at * GROUP * n, GROUP * n), :], NT,
             preferred_element_type=f32)
+        own = lax.broadcasted_iota(jnp.int32, reads.shape, 1) // n == lax.broadcasted_iota(jnp.int32, reads.shape, 0)
+        dr_ref[pl.ds(at, 1), :] = jnp.sum(jnp.where(own, reads, 0.0), axis=0, keepdims=True)
         return sums[GROUP:]
 
     def strips(values):
@@ -262,14 +264,14 @@
             pl.BlockSpec((block, width), here),
             pl.BlockSpec((n, width), lambda c, s, t: (0, c)),
             pl.BlockSpec((block // GROUP, span), strip),
-            pl.BlockSpec((block, span), strip),
+            pl.BlockSpec((block // GROUP, span), strip),
         ],
         out_shape=[
             jax.ShapeDtypeStruct((tokens, chans), f32),
             jax.ShapeDtypeStruct((tokens, chans), f32),
             jax.ShapeDtypeStruct((n, chans), f32),
             jax.ShapeDtypeStruct((strips * tokens // GROUP, span), f32),
-            jax.ShapeDtypeStruct((strips * tokens, span), f32),
+            jax.ShapeDtypeStruct((strips * tokens // GROUP, span), f32),
         ],
         scratch_shapes=[
             pltpu.VMEM((n, width), f32),
@@ -283,10 +285,9 @@
         cost_estimate=pl.CostEstimate(flops=14 * work, transcendentals=work, bytes_accessed=2 * work),
         name="bwd_full",
     )(dte, dtx, grad, hist, slabs, write, ones, rate, start)
-    dw = dw.reshape(strips, tokens, n).sum(0).T
-    own = jnp.arange(tokens)[:, None] % GROUP == jnp.arange(GROUP)[None, :]
-    dr = jnp.where(own[None, :, :, None], dr.reshape(strips, tokens, GROUP, n), 0).sum((0, 2)).T
-    return s1, s2, grate, dw, dr
+    both = jnp.stack([part.reshape(strips, tokens // GROUP, span).sum(0) for part in (dw, dr)])
+    both = both.reshape(2, tokens // GROUP, GROUP, n).transpose(0, 3, 1, 2).reshape(2, n, tokens)
+    return s1, s2, grate, both[0], both[1]
 
 
 def slabs_of(values):
@@ -341,7 +342,7 @@
     pl.semaphore_wait(barrier, count)
 
 
-def gather_steps(grid, whole_ref, out_ref, send_sem, recv_sem, own_sem, waits, chunk, chunks, across_too=True, ways=(True, True)):
+def gather_steps(grid, whole_ref, out_ref, send_sem, recv_sem, own, waits, chunk, chunks, across_too=True, ways=(True, True)):
     rows = whole_ref.shape[0]
     part = rows // chunks
     src_ref = whole_ref.at[pl.ds(chunk * part, part)]
@@ -389,11 +390,15 @@
     always = row >= 0
     along(always, row, src_ref)
     across(always, row, col, src_ref)
-    own = pltpu.make_async_copy(src_ref, out_ref.at[place(row, col)], own_sem)
-    own.start()
-    waits.append((None, own))
+    own_sem, own_buf = own
+    fetch = pltpu.make_async_copy(src_ref, own_buf, own_sem.at[0])
+    fetch.start()
     for _ in range(chunk + 1):
         yield
+    fetch.wait()
+    keep = pltpu.make_async_copy(own_buf, out_ref.at[place(row, col)], own_sem.at[1])
+    keep.start()
+    waits.append((None, keep))
 
     def rows_at(distance):
         return [row - distance] * ways[1] + [row + distance] * ways[0]
@@ -424,7 +429,16 @@
 
             @pl.when(there)
             def _(copy=copy):
-                copy.wait_send()
+                if copy.is_remote:
+                    copy.wait_send()
+                else:
+                    copy.wait()
+
+
+def gather_scratch(size, array, chunks):
+    dma = pltpu.SemaphoreType.DMA
+    own = pltpu.VMEM((array.shape[0] // chunks, *array.shape[1:]), array.dtype)
+    return [dma((4, size)), dma((size,)), dma((2,)), own] * chunks
 
 
 def in_turn(runs):
@@ -449,15 +463,15 @@
         runs = []
         for i, (axis, _, chunks) in enumerate(arrays):
             for chunk in range(chunks):
-                runs.append(gather_steps(grids[axis], sources[i], outs[i], *sems[:3], waits, chunk, chunks, ways=ways))
-                sems = sems[3:]
+                runs.append(gather_steps(
+                    grids[axis], sources[i], outs[i], sems[0], sems[1], sems[2:4], waits, chunk, chunks, ways=ways))
+                sems = sems[4:]
         in_turn(runs)
         finish(waits)
 
     sems = []
-    for axis, _, chunks in arrays:
-        size = sizes[axis][0]
-        sems += [pltpu.SemaphoreType.DMA((4, size)), pltpu.SemaphoreType.DMA((size,)), pltpu.SemaphoreType.DMA] * chunks
+    for axis, a, chunks in arrays:
+        sems += gather_scratch(sizes[axis][0], a, chunks)
     return pl.pallas_call(
         kernel,
         in_specs=[pl.BlockSpec(memory_space=pl.ANY)] * count,
@@ -465,34 +479,33 @@
         out_shape=[
             jax.ShapeDtypeStruct((sizes[axis][0] * a.shape[0], *a.shape[1:]), a.dtype) for axis, a, _ in arrays],
         scratch_shapes=sems,
-        compiler_params=pltpu.CompilerParams(collective_id=collective_id, has_side_effects=True),
+        compiler_params=pltpu.CompilerParams(
+            collective_id=collective_id, has_side_effects=True, vmem_limit_bytes=VMEM_LIMIT),
         name="link_gather",
     )(*[a for _, a, _ in arrays])
 
 
-def reduce_steps(grid, src_ref, out_ref, acc, inner_buf, outer_buf, sems, waits, chunk, chunks, share=None):
+def reduce_steps(grid, src_ref, out_ref, scratch, waits, chunks, share):
+    acc, inner_buf, outer_buf, load_sem, inner_send, inner_recv, outer_send, outer_recv, out_sem = scratch[:9]
     outer, inner = grid.outer, grid.inner
     row, col = grid.row, grid.col
-    rows, part = acc.shape[0] // (outer * inner), acc.shape[0] // (outer * inner * chunks)
+    rows = acc.shape[0] // (outer * inner)
+    part = rows // chunks
     piece = min(part, 64)
-    load_sem, inner_send, inner_recv, outer_send, outer_recv, out_sem = sems
-
-    def place(r, c):
-        return pl.ds(pl.multiple_of((r * inner + c) * rows + chunk * part, part), part)
-
-    def add(r, c, buf):
-        start = (r * inner + c) * rows + chunk * part
-
-        @pl.loop(0, part // piece)
-        def _(k):
-            here = pl.ds(pl.multiple_of(start + k * piece, piece), piece)
-            there = pl.ds(pl.multiple_of(k * piece, piece), piece)
-            acc[here, :] = (acc[here, :].astype(jnp.float32) + buf[there, :].astype(jnp.float32)).astype(acc.dtype)
+
+    def start_of(chunk, r, c):
+        return pl.multiple_of((r * inner + c) * rows + chunk * part, part)
 
     def line(me, size, device, block, buf, send, recv):
+        def from_low(target):
+            return target if size > 2 else 0
+
+        def from_high(target, owner):
+            return jnp.where(target == owner, size, target) if size > 2 else 0
+
         def hop(there, target, onward, slot):
             copy = pltpu.make_async_remote_copy(
-                src_ref=acc.at[place(*block(target))], dst_ref=buf.at[slot], send_sem=send.at[target],
+                src_ref=acc.at[pl.ds(block(target), part)], dst_ref=buf.at[slot], send_sem=send.at[target],
                 recv_sem=recv.at[slot], device_id=device(onward), device_id_type=MESH)
 
             @pl.when(there)
@@ -501,12 +514,6 @@
 
             waits.append((there, copy))
 
-        def from_low(target):
-            return target if size > 2 else 0
-
-        def from_high(target, owner):
-            return jnp.where(target == owner, size, target) if size > 2 else 0
-
         def up(there, target):
             hop(there & (target > me), target, me + 1, from_low(target))
 
@@ -514,14 +521,21 @@
             hop(there & (target < me), target, me - 1, from_high(target, me - 1))
 
         def arrive(there, target, slot):
+            at = block(target)
             copy = pltpu.make_async_remote_copy(
-                src_ref=acc.at[place(*block(target))], dst_ref=buf.at[slot], send_sem=send.at[target],
+                src_ref=acc.at[pl.ds(at, part)], dst_ref=buf.at[slot], send_sem=send.at[target],
                 recv_sem=recv.at[slot], device_id=device(me), device_id_type=MESH)
 
             @pl.when(there)
             def _():
                 copy.wait_recv()
-                add(*block(target), buf.at[slot])
+
+                @pl.loop(0, part // piece)
+                def _(k):
+                    here = pl.ds(pl.multiple_of(at + k * piece, piece), piece)
+                    there_rows = pl.ds(pl.multiple_of(k * piece, piece), piece)
+                    total = acc[here, :].astype(jnp.float32) + buf[slot, there_rows, :].astype(jnp.float32)
+                    acc[here, :] = total.astype(acc.dtype)
 
         def begin(target):
             up(me == 0, target)
@@ -530,82 +544,115 @@
         def go_on(target):
             arrive((me > 0) & (target >= me), target, from_low(target))
             arrive((me < size - 1) & (target <= me), target, from_high(target, me))
-            up((me > 0) & (me < size - 1), target)
-            down((me > 0) & (me < size - 1), target)
+            if size > 2:
+                up((me > 0) & (me < size - 1), target)
+                down((me > 0) & (me < size - 1), target)
 
         return begin, go_on
 
     order = sorted(range(outer), key=lambda k: -abs(2 * k - outer + 1))
-    lines = {}
-    for r in order:
-        loads = []
-        for c in range(inner):
-            load = pltpu.make_async_copy(src_ref.at[place(r, c)], acc.at[place(r, c)], load_sem.at[r * inner + c])
+    pieces = [(chunk, r) for chunk in range(chunks) for r in order]
+    loads = {}
+    for chunk, r in pieces:
+        loads[chunk, r] = [
+            pltpu.make_async_copy(
+                src_ref.at[pl.ds(start_of(chunk, r, c), part)], acc.at[pl.ds(start_of(chunk, r, c), part)],
+                load_sem.at[chunk, r * inner + c])
+            for c in range(inner)]
+        for load in loads[chunk, r]:
             load.start()
-            loads.append(load)
-        lines[r] = (loads, line(
-            col, inner, lambda c: grid.device(row, c), lambda t, r=r: (r, t), inner_buf.at[r], inner_send.at[r],
-            inner_recv.at[r]))
-    for r in order:
-        loads, (begin, _) = lines[r]
-        for load in loads:
-            load.wait()
+
+    def inner_line(chunk, r):
+        return line(
+            col, inner, lambda c: grid.device(row, c), lambda t: start_of(chunk, r, t), inner_buf.at[chunk, r],
+            inner_send.at[chunk, r], inner_recv.at[chunk, r])
+
+    def outer_line(chunk):
+        return line(
+            row, outer, lambda r: grid.device(r, col), lambda t: start_of(chunk, t, col), outer_buf.at[chunk],
+            outer_send.at[chunk], outer_recv.at[chunk])
+
+    def inner_start(k):
+        if k < len(pieces):
+            for load in loads[pieces[k]]:
+                load.wait()
+            if inner > 1:
+                for c in range(inner):
+                    inner_line(*pieces[k])[0](c)
+
+    def outer_rest(k):
+        if 0 <= k < len(pieces):
+            chunk, r = pieces[k]
+            if outer > 1:
+                outer_line(chunk)[1](r)
+            if r == order[-1]:
+                give(chunk)
+
+    def give(chunk):
+        first = start_of(chunk, row, col)
+        if share is None:
+            last = pltpu.make_async_copy(
+                acc.at[pl.ds(first, part)], out_ref.at[pl.ds(chunk * part, part)], out_sem.at[chunk])
+            last.start()
+            waits.append((None, last))
+            return
+        other, strip, send_sem, recv_sem = share
+        count, me = other.outer * other.inner, other.row * other.inner + other.col
+        take = rows // count
+        for mate in range(chunk * part // take, (chunk + 1) * part // take):
+            for k in range(acc.shape[1] // strip):
+                source = acc.at[
+                    pl.ds(pl.multiple_of((row * inner + col) * rows + mate * take, take), take),
+                    pl.ds(k * strip, strip)]
+                target = out_ref.at[:, pl.ds(pl.multiple_of((k * count + me) * strip, strip), strip)]
+                own = pltpu.make_async_copy(source, target, send_sem.at[mate, k])
+                sent = pltpu.make_async_remote_copy(
+                    src_ref=source, dst_ref=target, send_sem=send_sem.at[mate, k], recv_sem=recv_sem.at[me, k],
+                    device_id={other.axis: mate}, device_id_type=MESH)
+
+                @pl.when(mate == me)
+                def _(own=own):
+                    own.start()
+
+                @pl.when(mate != me)
+                def _(sent=sent):
+                    sent.start()
+
+                waits.append((mate != me, sent))
+                waits.append((mate == me, own))
+
+    window = 2
+    for k in range(window):
+        inner_start(k)
+    yield
+    for k in range(len(pieces)):
+        inner_start(k + window)
+        chunk, r = pieces[k]
         if inner > 1:
             for c in range(inner):
-                begin(c)
-    for _ in range(chunk + 1):
+                inner_line(chunk, r)[1](c)
+        if outer > 1:
+            outer_line(chunk)[0](r)
         yield
-    begin_outer, go_on_outer = line(
-        row, outer, lambda r: grid.device(r, col), lambda t: (t, col), outer_buf, outer_send, outer_recv)
-    late = []
-    for r in order:
-        if inner > 1:
-            for c in range(inner):
-                lines[r][1][1](c)
-        if outer > 1:
-            begin_outer(r)
-            yield
-            for earlier in late:
-                go_on_outer(earlier)
-            late = [r]
+        outer_rest(k - window)
         yield
-    for earlier in late:
-        go_on_outer(earlier)
-    if share is None:
-        last = pltpu.make_async_copy(acc.at[place(row, col)], out_ref.at[pl.ds(chunk * part, part)], out_sem)
-        last.start()
-        waits.append((None, last))
-        return
-    other, strip, send_sem, recv_sem = share
-    count, me = other.outer * other.inner, other.row * other.inner + other.col
-    take = rows // count
-    strips = acc.shape[1] // strip
-    first = (row * inner + col) * rows
-    for step in range(count):
-        mate = (me + step) % count
-        source_rows = pl.ds(pl.multiple_of(first + mate * take, take), take)
-        for k in range(strips):
-            piece_ref = acc.at[source_rows, pl.ds(k * strip, strip)]
-            target = out_ref.at[:, pl.ds(pl.multiple_of((k * count + me) * strip, strip), strip)]
-            if step == 0:
-                copy = pltpu.make_async_copy(piece_ref, target, send_sem.at[step, k])
-                copy.start()
-                waits.append((None, copy))
-            else:
+    for k in range(len(pieces) - window, len(pieces)):
+        outer_rest(k)
+        yield
+    if share is not None:
+        other, strip, send_sem, recv_sem = share
+        count, me = other.outer * other.inner, other.row * other.inner + other.col
+        take = rows // count
+        for mate in range(count):
+            for k in range(acc.shape[1] // strip):
                 copy = pltpu.make_async_remote_copy(
-                    src_ref=piece_ref, dst_ref=target, send_sem=send_sem.at[step, k], recv_sem=recv_sem.at[step, k],
-                    device_id={other.axis: mate}, device_id_type=MESH)
-                copy.start()
-                waits.append((me >= 0, copy))
-    for step in range(1, count):
-        mate = (me + count - step) % count
-        for k in range(strips):
-            copy = pltpu.make_async_remote_copy(
-                src_ref=acc.at[pl.ds(0, take), pl.ds(k * strip, strip)],
-                dst_ref=out_ref.at[:, pl.ds(pl.multiple_of((k * count + mate) * strip, strip), strip)],
-                send_sem=send_sem.at[step, k], recv_sem=recv_sem.at[step, k], device_id={other.axis: me},
-                device_id_type=MESH)
-            copy.wait_recv()
+                    src_ref=acc.at[pl.ds(0, take), pl.ds(k * strip, strip)],
+                    dst_ref=out_ref.at[:, pl.ds((k * count + mate) * strip, strip)], send_sem=send_sem.at[mate, k],
+                    recv_sem=recv_sem.at[mate, k], device_id={other.axis: me}, device_id_type=MESH)
+
+                @pl.when(mate != me)
+                def _(copy=copy):
+                    copy.wait_recv()
 
 
 def link_reduce(arrays, sizes, collective_id):
@@ -618,14 +665,9 @@
         waits = []
         runs = []
         for i, (axis, _, chunks, strip) in enumerate(arrays):
-            acc, scratch = scratch[0], scratch[1:]
-            share = None
-            if strip:
-                share, scratch = (grids["stream"], strip, *scratch[:2]), scratch[2:]
-            for chunk in range(chunks):
-                inner_buf, outer_buf, sems, scratch = scratch[0], scratch[1], scratch[2:8], scratch[8:]
-                runs.append(reduce_steps(
-                    grids[axis], sources[i], outs[i], acc, inner_buf, outer_buf, sems, waits, chunk, chunks, share))
+            share = (grids["stream"], strip, scratch[9], scratch[10]) if strip else None
+            runs.append(reduce_steps(grids[axis], sources[i], outs[i], scratch[:9], waits, chunks, share))
+            scratch = scratch[11 if strip else 9 :]
         in_turn(runs)
         finish(waits)
 
@@ -636,18 +678,18 @@
         part = a.shape[0] // size // chunks
         slots = [n + 1 if n > 2 else 1 for n in (inner, outer)]
         dma = pltpu.SemaphoreType.DMA
-        scratch.append(pltpu.VMEM(a.shape, a.dtype))
+        scratch += [
+            pltpu.VMEM(a.shape, a.dtype),
+            pltpu.VMEM((chunks, outer, slots[0], part, a.shape[1]), a.dtype),
+            pltpu.VMEM((chunks, slots[1], part, a.shape[1]), a.dtype),
+            dma((chunks, size)), dma((chunks, outer, inner)), dma((chunks, outer, slots[0])), dma((chunks, outer)),
+            dma((chunks, slots[1])), dma((chunks,))]
         if strip:
             mates = sizes["stream"][0]
             shapes.append(jax.ShapeDtypeStruct((a.shape[0] // size // mates, a.shape[1] * mates), a.dtype))
             scratch += [dma((mates, a.shape[1] // strip))] * 2
         else:
             shapes.append(jax.ShapeDtypeStruct((a.shape[0] // size, a.shape[1]), a.dtype))
-        for _ in range(chunks):
-            scratch += [
-                pltpu.VMEM((outer, slots[0], part, a.shape[1]), a.dtype),
-                pltpu.VMEM((slots[1], part, a.shape[1]), a.dtype),
-                dma((size,)), dma((outer, inner)), dma((outer, slots[0])), dma((outer,)), dma((slots[1],)), dma]
     return pl.pallas_call(
         kernel,
         in_specs=[pl.BlockSpec(memory_space=pl.ANY)] * count,
@@ -669,7 +711,7 @@
     bf, f32 = jnp.bfloat16, jnp.float32
     dma = pltpu.SemaphoreType.DMA
 
-    def kernel(own_ref, out_ref, mate_buf, pair_ref, terms_ref, total_ref, send, recv, line_send, line_recv, own_sem):
+    def kernel(own_ref, out_ref, mate_buf, pair_ref, terms_ref, total_ref, send, recv, line_send, line_recv, own_sem, own_buf):
         grid = Grid("stream", size, inner)
         row, col = grid.row, grid.col
         greet([grid])
@@ -684,7 +726,7 @@
         waits = []
         line = Grid("stream", size, inner)
         in_turn([gather_steps(
-            line, pair_ref, terms_ref, line_send, line_recv, own_sem, waits, 0, 1, across_too=False)])
+            line, pair_ref, terms_ref, line_send, line_recv, (own_sem, own_buf), waits, 0, 1, across_too=False)])
         finish(waits)
         total = terms_ref[pl.ds(0, half), :].astype(f32)
         for r in range(1, outer):
@@ -709,7 +751,8 @@
         out_shape=jax.ShapeDtypeStruct((rows, width), f32),
         scratch_shapes=[
             pltpu.VMEM((rows, width), bf), pltpu.VMEM((half, width), bf), pltpu.VMEM((outer * half, width), bf),
-            pltpu.VMEM((half, width), f32), dma((2,)), dma((2,)), dma((2, outer)), dma((outer,)), dma],
+            pltpu.VMEM((half, width), f32), dma((2,)), dma((2,)), dma((4, outer)), dma((outer,)), dma((2,)),
+            pltpu.VMEM((half, width), bf)],
         compiler_params=pltpu.CompilerParams(
             collective_id=collective_id, has_side_effects=True, vmem_limit_bytes=VMEM_LIMIT),
         name="link_sum",
@@ -725,7 +768,7 @@
     def kernel(conv_ref, gate_ref, *refs):
         sources, refs = refs[:count], refs[count:]
         conv_all, conv_own, gate_own, outs, refs = *refs[:3], refs[3 : 3 + count], refs[3 + count :]
-        hand_send, hand_recv, sems = refs[0], refs[1], refs[2:]
+        hand_send, hand_recv, hand_buf, sems = refs[0], refs[1], refs[2], refs[3:]
         grids = {axis: Grid(axis, *sizes[axis]) for axis in ("seq", "stream")}
         greet(list(grids.values()), ("stream",))
         me = grids["stream"].row * grids["stream"].inner + grids["stream"].col
@@ -735,9 +778,8 @@
             return pl.ds(pl.multiple_of(mate * take, take), take)
 
         def hand(kind, source, target):
-            copy = pltpu.make_async_copy(source.at[rows(me)], target.at[rows(me)], hand_send.at[kind, 0])
-            copy.start()
-            waits_own = [copy]
+            fetch = pltpu.make_async_copy(source.at[rows(me)], hand_buf.at[kind], hand_send.at[kind, 0])
+            fetch.start()
             for step in range(1, mates):
                 mate = (me + step) % mates
                 copy = pltpu.make_async_remote_copy(
@@ -745,11 +787,13 @@
                     recv_sem=hand_recv.at[kind, step], device_id={"stream": mate}, device_id_type=MESH)
                 copy.start()
                 waits.append((me >= 0, copy))
-            return waits_own
+            fetch.wait()
+            keep = pltpu.make_async_copy(hand_buf.at[kind], target.at[rows(me)], hand_recv.at[kind, 0])
+            keep.start()
+            return keep
 
         def handed(kind, source, target, own):
-            for copy in own:
-                copy.wait()
+            own.wait()
             for step in range(1, mates):
                 mate = (me + mates - step) % mates
                 pltpu.make_async_remote_copy(
@@ -761,15 +805,17 @@
         def main():
             for i, (axis, _, chunks) in enumerate(arrays):
                 for chunk in range(chunks):
-                    at = 3 * (1 + sum(entry[2] for entry in arrays[:i]) + chunk)
-                    yield gather_steps(grids[axis], sources[i], outs[i], *sems[at : at + 3], waits, chunk, chunks)
+                    at = 4 * (1 + sum(entry[2] for entry in arrays[:i]) + chunk)
+                    yield gather_steps(
+                        grids[axis], sources[i], outs[i], sems[at], sems[at + 1], sems[at + 2 : at + 4], waits, chunk,
+                        chunks)
 
         runs = list(main())
         for run in runs:
             next(run)
         own_gate = hand(1, gate_ref, gate_own)
         handed(0, conv_ref, conv_own, own)
-        first = gather_steps(grids["seq"], conv_own, conv_all, *sems[:3], waits, 0, 1)
+        first = gather_steps(grids["seq"], conv_own, conv_all, sems[0], sems[1], sems[2:4], waits, 0, 1)
         next(first)
         in_turn([first, *runs])
         handed(1, gate_ref, gate_own, own_gate)
@@ -777,9 +823,8 @@
 
     entries = [("seq", conv, 1), *arrays]
     sems = []
-    for axis, _, chunks in entries:
-        size = sizes[axis][0]
-        sems += [dma((4, size)), dma((size,)), dma] * chunks
+    for axis, a, chunks in entries:
+        sems += gather_scratch(sizes[axis][0], a, chunks)
     result = pl.pallas_call(
         kernel,
         in_specs=[pl.BlockSpec(memory_space=pl.ANY)] * (count + 2),
@@ -789,8 +834,10 @@
             jax.ShapeDtypeStruct(conv.shape, conv.dtype),
             jax.ShapeDtypeStruct(gate.shape, gate.dtype),
             *[jax.ShapeDtypeStruct((sizes[axis][0] * a.shape[0], *a.shape[1:]), a.dtype) for axis, a, _ in arrays]],
-        scratch_shapes=[dma((2, mates)), dma((2, mates)), *sems],
-        compiler_params=pltpu.CompilerParams(collective_id=collective_id, has_side_effects=True),
+        scratch_shapes=[
+            dma((2, mates)), dma((2, mates)), pltpu.VMEM((2, take, conv.shape[1]), conv.dtype), *sems],
+        compiler_params=pltpu.CompilerParams(
+            collective_id=collective_id, has_side_effects=True, vmem_limit_bytes=VMEM_LIMIT),
         name="link_open",
     )(conv, gate, *[a for _, a, _ in arrays])
     return result[0], result[2], *result[3:]
@@ -975,34 +1022,39 @@
     d_conv_in = d_conv_in.astype(bf).reshape(tokens, chans)
     g_in_conv = contract_rows(unit, d_conv_in).astype(bf)
     d_unit = (contract_cols(d_conv_in, in_conv) + contract_cols(d_gate, in_gate)).astype(bf)
-    small = jnp.concatenate(
-        [g_xproj, g_dt, g_log.T * LN2, g_conv, g_conv_bias[:, None], g_dt_bias[:, None], g_skip[:, None]], axis=1)
-    small = jnp.pad(small, ((0, 0), (0, -small.shape[1] % 128))).astype(bf)
-    g_in_conv, small, d_unit = link_reduce(
-        [("seq", g_in_conv, 1, 0 if own_feats % 16 else own), ("seq", small, 1, 0), ("stream", d_unit, 4, 0)], sizes, 6)
-    small = small.astype(f32)
-    d_unit = d_unit.astype(f32)
-    in_grad = cotangent.astype(f32) + inv_rms * (d_unit - unit_own * jnp.mean(d_unit * unit_own, axis=-1, keepdims=True))
-
     def in_rows(block):
         shared = lax.all_to_all(block, "stream", 0, 0, tiled=True).reshape(seqs, own_feats, parts, own)
         return shared.transpose(1, 2, 0, 3).reshape(own_feats, parts * seqs * own)
 
+    def padded_small(columns):
+        joined = jnp.concatenate(columns, axis=1)
+        return jnp.pad(joined, ((0, 0), (0, -joined.shape[1] % 128))).astype(bf)
+
+    small = padded_small([g_xproj, g_dt, g_log.T * LN2, g_dt_bias[:, None], g_skip[:, None]])
+    small = lax.psum_scatter(small, "seq", scatter_dimension=0, tiled=True).astype(f32)
+    taps = padded_small([g_conv, g_conv_bias[:, None]])
+    d_unit, g_in_gate = lax.optimization_barrier((d_unit, in_rows(g_in_gate)))
+    g_in_conv, taps, d_unit = link_reduce(
+        [("seq", g_in_conv, 2, 0 if own_feats % 16 else own), ("seq", taps, 1, 0), ("stream", d_unit, 4, 0)], sizes, 6)
+    taps = taps.astype(f32)
+    d_unit = d_unit.astype(f32)
+    in_grad = cotangent.astype(f32) + inv_rms * (d_unit - unit_own * jnp.mean(d_unit * unit_own, axis=-1, keepdims=True))
+
     g_in_conv = in_rows(g_in_conv) if own_feats % 16 else g_in_conv
-    g_unit = jnp.concatenate([g_in_conv, in_rows(g_in_gate)], axis=1).astype(f32)
+    g_unit = jnp.concatenate([g_in_conv, g_in_gate], axis=1).astype(f32)
     at = proj_dim + rank_dim
     return (
         output[None],
         in_grad.astype(bf)[None],
         jnp.sum(g_unit * in_weight.astype(f32), axis=1),
         g_unit * gain[:, None],
-        small[:, at + state_dim : at + state_dim + CONV].T,
-        small[:, at + state_dim + CONV],
+        taps[:, :CONV].T,
+        taps[:, CONV],
         small[:, :proj_dim],
         small[:, proj_dim:at].T,
-        small[:, at + state_dim + CONV + 1],
+        small[:, at + state_dim],
         small[:, at : at + state_dim],
-        small[:, at + state_dim + CONV + 2],
+        small[:, at + state_dim + 1],
         g_out.astype(f32),
     )
 

time: 888 us -> 927 us (1.044)
  waiting for transfers between devices: 10.6 us -> 104 us
  Pallas kernels: 487 us -> 461 us
  local copies, waits for them, and re-layouts: 66.8 us -> 48.9 us
    reduce_scatter x1, waiting for transfers between devices: 0.01 us -> 85.9 us  [local(): lax.psum_scatter(contract_rows(gated, cot_all).astype(bf), 'seq', scatter...]
    pallas_call x1, Pallas kernels: 94.8 us -> 63.5 us  [link_open(): pl.pallas_call(kernel, in_specs=[pl.BlockSpec(memory_space=pl.ANY)] * (co...]
    reduce_scatter x1, waiting for transfers between devices: 0.02 us -> 16.1 us  [local(): lax.psum_scatter(contract_rows(unit, d_gate).astype(bf), 'seq', scatter_d...]
  transfers between devices with their start and end apart: 9 -> 10, of which waited for: 1 -> 3; matrix products, arithmetic and copies ran while one was open for 32% -> 26% of each run, Pallas kernels for 45% -> 25%
where the time goes in v4:
time: 927 us; the launch traced here: 920 us
  Pallas kernels  461 us (50%)
  matrix products  165 us (18%)
  other arithmetic  110 us (12%)
  waiting for transfers between devices  104 us (11%)
  local copies, waits for them, and re-layouts  48.9 us (5%)
  starting transfers between devices  15.6 us (2%)
  between operations  15.6 us (2%)
    pallas_call x1, Pallas kernels, link_reduce(): pl.pallas_call(kernel, in_specs=[pl.BlockSpec(memory_space=pl.ANY)] * cou...  126 us
    pallas_call x1, Pallas kernels, bwd_full(): pl.pallas_call(bwd_full_body, grid=(strips, seqs, blocks), in_specs=[pl.B...  95.1 us
    reduce_scatter x1, waiting for transfers between devices, local(): lax.psum_scatter(contract_rows(gated, cot_all).astype(bf), 'seq', scatter...  85.9 us
    pallas_call x1, Pallas kernels, link_open(): pl.pallas_call(kernel, in_specs=[pl.BlockSpec(memory_space=pl.ANY)] * (co...  63.5 us
    pallas_call x2, Pallas kernels, scan_end(): pl.pallas_call(body, grid=(seqs, chans // width), in_specs=[pl.BlockSpec(...  62.5 us
    dot_general x3, matrix products, contract_cols(): lax.dot_general(left_mat, right_mat, NT, preferred_element_type=jnp.float32)  42.8 us
    pallas_call x1, Pallas kernels, fwd_full(): pl.pallas_call(fwd_full_body, grid=(chans // width, seqs, blocks), in_spe...  41.9 us
    dot_general x3, matrix products, contract_rows(): lax.dot_general(left_mat, right_mat, (((0,), (0,)), ((), ())), preferred_...  41.3 us
  transfers between devices with their start and end apart: 10, of which 3 were waited for; matrix products, arithmetic and copies ran while one was open for 26% of the time, Pallas kernels for 25%

profile of v4, /device:TPU:19, one launch (start us, length us, event | category | flops | bytes accessed | tf_op | source)
XLA Modules:
  0.0 919.9 jit_solution(16936428951071464062)
XLA Ops:
  25.0 63.5 %link_open.1 = (bf16[2048,1024]{1,0:T(8,128)(2,1)}, bf16[256,1024]{1,0:T(8,128)(2,1)}, bf16[256,1024]{1,0:T(8,128)(2,1)}, s32[32,128]{1,0:T(8,128)}, bf16[2048,2...) custom-call(bf16[256,1024]{1,0:T(8,128)(2,1)} %get-tuple-element.184.conv_ref, bf16[256,1024]{1,0:T(8,128)(2,1)} %get-tuple-element.183.gate_ref, ...), custom_call_target="tpu_custom_call" | custom-call | tf_op jit(solution)/shard_map/link_open/pallas_call | solution.py:828
  89.3 12.5 %fusion.79 = f32[2048,1024]{1,0:T(8,128)S(1)} fusion(bf16[2048,2048]{1,0:T(8,128)(2,1)} %get-tuple-element.37, bf16[2048,1024]{1,0:T(8,128)(2,1)} %get-tuple-element.38), kind=kOutput, calls=%fused_computation.244 | convolution fusion | flops 8589934592 | bytes 20971520 | tf_op jit(solution)/shard_map/dot_general | solution.py:958
  113.3 19.5 %multiply_convert_fusion.2 = (bf16[4,512,1024]{2,1,0:T(8,128)(2,1)S(1)}, f32[4,512,1024]{2,1,0:T(8,128)}) fusion(f32[4,512,1024]{2,1,0:T(8,128)} %bitcast.252, f32[1024]{0:T(1024)S(1)} %get-tuple-element.114, f32[4,512]{1,0:T(4,128)S(1)} %get-tuple-element.178, f32[4,3,1024]{2,1,0:T(4,128)S(1)} %convert_element_type.254, f32[1024]{0:T(1024)S(1)} %get-tuple-element.115, ...), kind=kLoop, calls=%fused_computation.41 | loop fusion | flops 39845888 | bytes 21065728 | tf_op jit(solution)/shard_map/convert_element_type | solution.py:965
  137.4 16.1 %link_sum.2 = f32[160,2048]{1,0:T(8,128)} custom-call(bf16[160,2048]{1,0:T(8,128)(2,1)} %convolution_convert_fusion.4.own_ref), custom_call_target="tpu_custom_call" | custom-call | tf_op jit(solution)/shard_map/link_sum/pallas_call | solution.py:747
  170.2 8.2 bitcast_reduce_fusion
  178.4 7.5 convert_multiply_fusion.3.dtx_ref
  185.9 31.1 %fwd_end.1 = f32[64,1024]{1,0:T(8,128)} custom-call(f32[2048,1024]{1,0:T(8,128)} %get-tuple-element.125.dte_ref, f32[2048,1024]{1,0:T(8,128)} %convert_multiply_fusion.3.dtx_ref, f32[2048,16]{1,0:T(8,128)} %bitcast.268, f32[16,1024]{1,0:T(8,128)} %multiply_bitcast_fusion.rate_ref), custom_call_target="tpu_custom_call" | custom-call | flops 134217728 | bytes 16777216 | tf_op jit(solution)/shard_map/fwd_end/pallas_call | solution.py:81
  218.7 17.5 %link_gather.2 = bf16[640,1024]{1,0:T(8,128)(2,1)} custom-call(bf16[80,1024]{1,0:T(8,128)(2,1)} %pad.27.refs_0_), custom_call_target="tpu_custom_call" | custom-call | tf_op jit(solution)/shard_map/link_gather/pallas_call | solution.py:475
  239.3 41.9 %fwd_full.1 = (f32[2048,1024]{1,0:T(8,128)}, bf16[32896,1024]{1,0:T(8,128)(2,1)}) custom-call(f32[2048,1024]{1,0:T(8,128)} %get-tuple-element.125.dte_ref, f32[2048,1024]{1,0:T(8,128)} %convert_multiply_fusion.3.dtx_ref, f32[2048,16]{1,0:T(8,128)} %bitcast.269, bf16[2048,256]{1,0:T(8,128)(2,1)} %copy.95.read_ref, f32[16,1024]{1,0:T(8,128)} %multiply_bitcast_fusion.rate_ref, ...), custom_call_target="tpu_custom_call" | custom-call | flops 268435456 | bytes 67108864 | tf_op jit(solution)/shard_map/fwd_full/pallas_call | solution.py:146
  281.2 14.6 %fusion.80 = f32[2048,1024]{1,0:T(8,128)} fusion(bf16[2048,2048]{1,0:T(8,128)(2,1)} %all-gather.8.cloned.1.call-done, bf16[1024,2048]{1,0:T(8,128)(2,1)} %all-gather.6.cloned.1.call-done), kind=kOutput, calls=%fused_computation.245 | convolution fusion | flops 8589934592 | bytes 20971520 | tf_op jit(solution)/shard_map/dot_general | solution.py:873
  296.8 25.9 %multiply_convert_fusion = (bf16[2048,1024]{1,0:T(8,128)(2,1)}, bf16[2048,1024]{1,0:T(8,128)(2,1)}, bf16[1024]{0:T(1024)(128)(2,1)S(1)}, f32[2048,1024]{1,0:T(8,128)}) fusion(f32[2048,1024]{1,0:T(8,128)} %fusion.80, f32[2048,1024]{1,0:T(8,128)} %get-tuple-element.39, f32[2048]{0:T(1024)S(1)} %bitcast.277, f32[1024]{0:T(1024)S(1)} %get-tuple-element.110, ...), kind=kOutput, calls=%fused_computation.31 | convolution fusion | flops 8633973760 | bytes 50345984 | tf_op jit(solution)/shard_map/dot_general | solution.py:959
  322.8 31.3 %bwd_end.1 = f32[64,1024]{1,0:T(8,128)} custom-call(f32[2048,1024]{1,0:T(8,128)} %get-tuple-element.125.dte_ref, f32[2048,1024]{1,0:T(8,128)} %get-tuple-element.131.grad_ref, f32[2048,16]{1,0:T(8,128)} %bitcast.255, f32[16,1024]{1,0:T(8,128)} %multiply_bitcast_fusion.rate_ref), custom_call_target="tpu_custom_call" | custom-call | flops 134217728 | bytes 16777216 | tf_op jit(solution)/shard_map/bwd_end/pallas_call | solution.py:81
  355.8 15.2 %link_gather.3 = bf16[640,1024]{1,0:T(8,128)(2,1)} custom-call(bf16[80,1024]{1,0:T(8,128)(2,1)} %pad.28.refs_0_), custom_call_target="tpu_custom_call" | custom-call | tf_op jit(solution)/shard_map/link_gather/pallas_call | solution.py:475
  374.0 95.1 %bwd_full.1 = (f32[2048,1024]{1,0:T(8,128)}, f32[2048,1024]{1,0:T(8,128)}, f32[16,1024]{1,0:T(8,128)}, f32[256,256]{1,0:T(8,128)}, f32[256,256]{1,0:T(8,128)}) custom-call(f32[2048,1024]{1,0:T(8,128)} %get-tuple-element.125.dte_ref, f32[2048,1024]{1,0:T(8,128)} %convert_multiply_fusion.3.dtx_ref, f32[2048,1024]{1,0:T(8,128)} %get-tuple-element.131.grad_ref, ...), custom_call_target="tpu_custom_call" | custom-call | flops 469762048 | bytes 67108864 | tf_op jit(solution)/shard_map/bwd_full/pallas_call | solution.py:248
  469.2 13.0 %fusion.74 = (bf16[1024]{0:T(1024)(128)(2,1)S(1)}, bf16[2048,1024]{1,0:T(8,128)(2,1)S(1)}) fusion(f32[2048,1024]{1,0:T(8,128)} %get-tuple-element.44, bf16[4,512,1024]{2,1,0:T(8,128)(2,1)S(1)} %copy-done.2, f32[2048,1024]{1,0:T(8,128)} %get-tuple-element.45, f32[2048,1024]{1,0:T(8,128)} %copy-done.4, f32[1024]{0:T(1024)S(1)} %get-tuple-element.111), kind=kLoop, calls=%fused_computation.240 | loop fusion | flops 44039168 | bytes 33560576 | tf_op jit(solution)/shard_map/reduce_sum | solution.py:1003
  488.2 23.4 %link_sum.3 = f32[160,2048]{1,0:T(8,128)} custom-call(bf16[160,2048]{1,0:T(8,128)(2,1)} %pad_maximum_fusion.3.own_ref), custom_call_target="tpu_custom_call" | custom-call | tf_op jit(solution)/shard_map/link_sum/pallas_call | solution.py:747
  517.0 14.0 %convolution_convert_fusion.2 = bf16[2048,1024]{1,0:T(8,128)(2,1)} fusion(bf16[2048,2048]{1,0:T(8,128)(2,1)} %get-tuple-element.37, bf16[2048,1024]{1,0:T(8,128)(2,1)} %get-tuple-element.128), kind=kOutput, calls=%fused_computation.61 | convolution fusion | flops 8592031744 | bytes 16777216 | tf_op jit(solution)/shard_map/dot_general | solution.py:869
  531.1 14.2 %convolution_convert_fusion.1 = bf16[1024,2048]{1,0:T(8,128)(2,1)} fusion(bf16[2048,1024]{1,0:T(8,128)(2,1)} %get-tuple-element.129, bf16[2048,2048]{1,0:T(8,128)(2,1)} %all-gather.8.cloned.1.call-done), kind=kOutput, calls=%fused_computation.60 | convolution fusion | flops 8592031744 | bytes 16777216 | tf_op jit(solution)/shard_map/dot_general | solution.py:869
  545.7 14.0 %convolution_convert_fusion = bf16[2048,2048]{1,0:T(8,128)(2,1)} fusion(bf16[2048,1024]{1,0:T(8,128)(2,1)} %get-tuple-element.129, bf16[1024,2048]{1,0:T(8,128)(2,1)} %all-gather.6.cloned.1.call-done), kind=kOutput, calls=%fused_computation.45 | convolution fusion | flops 8594128896 | bytes 16777216 | tf_op jit(solution)/shard_map/dot_general | solution.py:986
  561.1 11.7 %add_add_fusion = f32[2048,1024]{1,0:T(8,128)S(1)} fusion(f32[2048,1024]{1,0:T(8,128)} %get-tuple-element.131.grad_ref, f32[2048,1024]{1,0:T(8,128)} %get-tuple-element.44, f32[1024]{0:T(1024)S(1)} %get-tuple-element.110, bf16[1024,384]{1,0:T(8,128)(2,1)S(1)} %copy-done.9, f32[160,2048]{1,0:T(8,128)S(1)} %copy-done.10, f32[2048,1024]{1,0:T(8,128)} %copy-done.4, ...), kind=kOutput, calls=%fused_computation.37 | convolution fusion | flops 694484992 | bytes 35397632 | tf_op jit(solution)/shard_map/dot_general | solution.py:1009
  572.8 18.5 %fusion.73 = (bf16[1024]{0:T(1024)(128)(2,1)S(1)}, bf16[1024]{0:T(1024)(128)(2,1)S(1)}, bf16[1024]{0:T(1024)(128)(2,1)S(1)}, bf16[1024]{0:T(1024)(128)(2,1)S(1)}...) fusion(f32[2048,1024]{1,0:T(8,128)} %copy-done.3, f32[4,512]{1,0:T(4,128)S(1)} %copy-done.25, ...), kind=kLoop, calls=%fused_computation.239 | loop fusion | flops 48229376 | bytes 42027008 | tf_op jit(solution)/shard_map/reduce_sum | solution.py:1012
  591.4 8.2 collective-permute-start.1
  599.6 14.0 %fusion.81 = f32[2048,2048]{1,0:T(8,128)} fusion(bf16[2048,1024]{1,0:T(8,128)(2,1)} %get-tuple-element.128, bf16[2048,1024]{1,0:T(8,128)(2,1)S(1)} %copy-done.44), kind=kOutput, calls=%fused_computation.246 | convolution fusion | flops 8589934592 | bytes 25165824 | tf_op jit(solution)/shard_map/dot_general | solution.py:873
  614.7 17.0 %fusion.6 = bf16[4,512,1024]{2,1,0:T(8,128)(2,1)S(1)} fusion(f32[4,3,1024]{2,1,0:T(4,128)S(1)} %convert_element_type.298, f32[4,512,1024]{2,1,0:T(8,128)} %copy-done.5, f32[4,512]{1,0:T(4,128)S(1)} %copy-done.39, f32[4,512]{1,0:T(4,128)S(1)} %copy-done.38, f32[4,512]{1,0:T(4,128)S(1)} %copy-done.37, f32[1024]{0:T(1024)S(1)} %copy-done.30, ...), kind=kLoop, calls=%fused_computation.16 | loop fusion | flops 29360128 | bytes 12673024 | tf_op jit(solution)/shard_map/convert_element_type | solution.py:1022
  631.7 13.2 %convolution_convert_fusion.3.refs_0_ = bf16[2048,1024]{1,0:T(8,128)(2,1)} fusion(bf16[2048,2048]{1,0:T(8,128)(2,1)} %get-tuple-element.37, bf16[2048,1024]{1,0:T(8,128)(2,1)S(1)} %bitcast.262), kind=kOutput, calls=%fused_computation.62 | convolution fusion | flops 8592031744 | bytes 16777216 | tf_op jit(solution)/shard_map/dot_general | solution.py:869
  644.9 14.3 %add_convert_fusion.refs_2_ = bf16[2048,2048]{1,0:T(8,128)(2,1)} fusion(f32[2048,2048]{1,0:T(8,128)} %fusion.81, bf16[2048,1024]{1,0:T(8,128)(2,1)S(1)} %bitcast.263, bf16[2048,1024]{1,0:T(8,128)(2,1)S(1)} %copy-done.43), kind=kOutput, calls=%fused_computation.1 | convolution fusion | flops 8598323200 | bytes 33554432 | tf_op jit(solution)/shard_map/dot_general | solution.py:873
  661.5 16.1 %reduce-scatter.9.cloned.1.call-done = bf16[256,1024]{1,0:T(8,128)(2,1)} async-done(((bf16[2048,1024]{1,0:T(8,128)(2,1)}), bf16[256,1024]{1,0:T(8,128)(2,1)}) %reduce-scatter.9.cloned.1.call-update) | async-done | bytes 524304 | tf_op jit(solution)/shard_map/reduce_scatter | solution.py:994
  677.6 4.3 all-to-all-start
  683.0 85.9 %reduce-scatter.11.cloned.1.call-done = bf16[128,2048]{1,0:T(8,128)(2,1)} async-done(((bf16[1024,2048]{1,0:T(8,128)(2,1)}), bf16[128,2048]{1,0:T(8,128)(2,1)}) %reduce-scatter.11.cloned.1.call-update) | async-done | bytes 524304 | tf_op jit(solution)/shard_map/reduce_scatter | solution.py:990
  773.1 126.0 %link_reduce.1 = (bf16[64,4096]{1,0:T(8,128)(2,1)}, bf16[128,128]{1,0:T(8,128)(2,1)}, bf16[512,2048]{1,0:T(8,128)(2,1)}) custom-call(bf16[2048,1024]{1,0:T(8,128)(2,1)} %convolution_convert_fusion.3.refs_0_, bf16[1024,128]{1,0:T(8,128)(2,1)} %pad.29.refs_1_, bf16[2048,2048]{1,0:T(8,128)(2,1)} %add_convert_fusion.refs_2_), custom_call_target="tpu_custom_call" | custom-call | tf_op jit(solution)/shard_map/link_reduce/pallas_call | solution.py:693
  903.7 3.5 convert_multiply_fusion.6
  907.2 5.6 fusion.31
  (244 shorter events, 87.5 us)
Async XLA Ops:
  7.2 274.0 %all-gather.6.cloned.1.call-start = ((), (), s32[]{:S(2)}) async-start(), calls=%async_computation.6 | async-start | bytes 4718592 | tf_op jit(solution)/shard_map/all_gather | solution.py:937
  10.1 78.4 %copy-start.35 = (f32[512]{0:T(512)}, f32[512]{0:T(512)S(1)}, u32[]{:S(2)}) copy-start(f32[512]{0:T(512)S(1)} %add_rsqrt_fusion) | copy-start | bytes 6148
  88.5 192.7 %all-gather.8.cloned.1.call-start = ((), (), s32[]{:S(2)}) async-start(), calls=%async_computation.8 | async-start | bytes 10485760 | tf_op jit(solution)/shard_map/all_gather | solution.py:938
  89.3 207.6 %all-gather.4.cloned.1.call-start = ((), (), s32[]{:S(2)}) async-start(), calls=%async_computation.5 | async-start | bytes 4718592 | tf_op jit(solution)/shard_map/all_gather | solution.py:936
  105.2 8.1 collective-permute-start
  107.4 551.8 %reduce-scatter.13.cloned.1.call-start = ((), (), s32[]{:S(2)}) async-start(), calls=%async_computation.11 | async-start | bytes 884736
  110.8 22.0 %copy-start.20 = (f32[4,512]{1,0:T(4,128)}, f32[4,512]{1,0:T(4,128)S(1)}, u32[]{:S(2)}) copy-start(f32[4,512]{1,0:T(4,128)S(1)} %get-tuple-element.178) | copy-start | bytes 24580
  110.8 22.0 %copy-start.22 = (f32[4,512]{1,0:T(4,128)}, f32[4,512]{1,0:T(4,128)S(1)}, u32[]{:S(2)}) copy-start(f32[4,512]{1,0:T(4,128)S(1)} %get-tuple-element.179) | copy-start | bytes 24580
  110.8 22.0 %copy-start.24 = (f32[4,512]{1,0:T(4,128)}, f32[4,512]{1,0:T(4,128)S(1)}, u32[]{:S(2)}) copy-start(f32[4,512]{1,0:T(4,128)S(1)} %get-tuple-element.181) | copy-start | bytes 24580
  111.9 20.9 %copy-start.27 = (f32[1024]{0:T(1024)}, f32[1024]{0:T(1024)S(1)}, u32[]{:S(2)}) copy-start(f32[1024]{0:T(1024)S(1)} %get-tuple-element.113) | copy-start | bytes 12292
  111.9 20.9 %copy-start.29 = (f32[1024]{0:T(1024)}, f32[1024]{0:T(1024)S(1)}, u32[]{:S(2)}) copy-start(f32[1024]{0:T(1024)S(1)} %get-tuple-element.114) | copy-start | bytes 12292
  185.9 52.0 %copy-start.14 = (f32[16,1024]{1,0:T(8,128)S(1)}, f32[16,1024]{1,0:T(8,128)}, u32[]{:S(2)}) copy-start(f32[16,1024]{1,0:T(8,128)} %multiply_bitcast_fusion.rate_ref) | copy-start | bytes 196612
  322.8 49.9 %copy-start.15 = (f32[16,1024]{1,0:T(8,128)S(1)}, f32[16,1024]{1,0:T(8,128)}, u32[]{:S(2)}) copy-start(f32[16,1024]{1,0:T(8,128)} %multiply_bitcast_fusion.rate_ref) | copy-start | bytes 196612
  374.0 95.1 %copy-start.2 = (bf16[4,512,1024]{2,1,0:T(8,128)(2,1)S(1)}, bf16[4,512,1024]{2,1,0:T(8,128)(2,1)}, u32[]{:S(2)}) copy-start(bf16[4,512,1024]{2,1,0:T(8,128)(2,1)} %copy-done) | copy-start | bytes 12582916
  516.7 160.9 %reduce-scatter.9.cloned.1.call-start = ((), (), s32[]{:S(2)}) async-start(), calls=%async_computation.9 | async-start | bytes 4718592 | tf_op jit(solution)/shard_map/reduce_scatter | solution.py:994
  531.0 237.9 %reduce-scatter.11.cloned.1.call-start = ((), (), s32[]{:S(2)}) async-start(), calls=%async_computation.10 | async-start | bytes 4718592 | tf_op jit(solution)/shard_map/reduce_scatter | solution.py:990
  545.3 361.9 %reduce-scatter.7.cloned.1.call-start = ((), (), s32[]{:S(2)}) async-start(), calls=%async_computation.7 | async-start | bytes 10485760 | tf_op jit(solution)/shard_map/reduce_scatter | solution.py:987
  572.8 26.8 %copy-start.44 = (bf16[2048,1024]{1,0:T(8,128)(2,1)S(1)}, bf16[2048,1024]{1,0:T(8,128)(2,1)}, u32[]{:S(2)}) copy-start(bf16[2048,1024]{1,0:T(8,128)(2,1)} %all-gather.4.cloned.1.call-done) | copy-start | bytes 12582916
  591.3 22.2 %copy-start.5 = (f32[4,512,1024]{2,1,0:T(8,128)}, f32[4,512,1024]{2,1,0:T(8,128)S(1)}, u32[]{:S(2)}) copy-start(f32[4,512,1024]{2,1,0:T(8,128)S(1)} %get-tuple-element.121) | copy-start | bytes 25165828
  591.3 23.3 %copy-start.28 = (f32[1024]{0:T(1024)S(1)}, f32[1024]{0:T(1024)}, u32[]{:S(2)}) copy-start(f32[1024]{0:T(1024)} %copy-done.27) | copy-start | bytes 12292
  591.3 23.3 %copy-start.30 = (f32[1024]{0:T(1024)S(1)}, f32[1024]{0:T(1024)}, u32[]{:S(2)}) copy-start(f32[1024]{0:T(1024)} %copy-done.29) | copy-start | bytes 12292
  591.3 23.3 %copy-start.32 = (f32[1024]{0:T(1024)S(1)}, f32[1024]{0:T(1024)}, u32[]{:S(2)}) copy-start(f32[1024]{0:T(1024)} %copy-done.31) | copy-start | bytes 12292
  591.4 23.3 %copy-start.34 = (f32[1024]{0:T(1024)S(1)}, f32[1024]{0:T(1024)}, u32[]{:S(2)}) copy-start(f32[1024]{0:T(1024)} %copy-done.33) | copy-start | bytes 12292
  591.4 23.3 %copy-start.37 = (f32[4,512]{1,0:T(4,128)S(1)}, f32[4,512]{1,0:T(4,128)}, u32[]{:S(2)}) copy-start(f32[4,512]{1,0:T(4,128)} %get-tuple-element.176) | copy-start | bytes 24580
  591.4 23.3 %copy-start.38 = (f32[4,512]{1,0:T(4,128)S(1)}, f32[4,512]{1,0:T(4,128)}, u32[]{:S(2)}) copy-start(f32[4,512]{1,0:T(4,128)} %get-tuple-element.177) | copy-start | bytes 24580
  591.4 23.3 %copy-start.39 = (f32[4,512]{1,0:T(4,128)S(1)}, f32[4,512]{1,0:T(4,128)}, u32[]{:S(2)}) copy-start(f32[4,512]{1,0:T(4,128)} %get-tuple-element.180) | copy-start | bytes 24580
  591.4 23.2 %collective-permute-start.1 = (bf16[4,3,1024]{2,1,0:T(4,128)(2,1)S(1)}, bf16[4,3,1024]{2,1,0:T(4,128)(2,1)S(1)}, u32[]{:S(2)}, u32[]{:S(2)}) collective-permute-start(bf16[4,3,1024]{2,1,0:T(4,128)(2,1)S(1)} %slice.786), channel_id=1, source_target_pairs={{4,0},{8,4},{12,8},{16,12},{20,16},{24,20},{28,24},{5,1},{9,5},{13... | collective-permute-start | bytes 73736 | tf_op jit(solution)/shard_map/ppermute | solution.py:849
  677.6 93.5 %all-to-all-start = ((bf16[4,64,1024]{2,1,0:T(8,128)(2,1)}), bf16[4,64,1024]{2,1,0:T(8,128)(2,1)S(1)}, u32[]{:S(2)}, u32[]{:S(2)}) async-start(bf16[4,64,1024]{2,1,0:T(8,128)(2,1)} %bitcast.270), calls=%async_computation.2 | async-start | bytes 1048576 | tf_op jit(solution)/shard_map/all_to_all | solution.py:1026
  771.2 130.0 %copy-start.7 = (bf16[1,512,2048]{2,1,0:T(8,128)(2,1)S(1)}, bf16[1,512,2048]{2,1,0:T(8,128)(2,1)}, u32[]{:S(2)}) copy-start(bf16[1,512,2048]{2,1,0:T(8,128)(2,1)} %param.13) | copy-start | bytes 6291460
  771.2 130.0 %copy-start.36 = (f32[512]{0:T(512)S(1)}, f32[512]{0:T(512)}, u32[]{:S(2)}) copy-start(f32[512]{0:T(512)} %copy-done.35) | copy-start | bytes 6148
  773.1 130.5 %copy-start.13 = (bf16[64,8192]{1,0:T(8,128)(2,1)S(1)}, bf16[64,8192]{1,0:T(8,128)(2,1)}, u32[]{:S(2)}) copy-start(bf16[64,8192]{1,0:T(8,128)(2,1)} %param.17) | copy-start | bytes 3145732
  773.1 130.5 %copy-start.41 = (f32[64]{0:T(128)S(1)}, f32[64]{0:T(128)}, u32[]{:S(2)}) copy-start(f32[64]{0:T(128)} %copy-done.40) | copy-start | bytes 772
  (23 other events, 260.6 us)
Sparse Core Ops, SparseCore 0:
  88.6 72.4 all-gather.5
  162.7 57.2 all-gather.7
  222.2 74.5 all-gather.3
  516.9 67.1 reduce-scatter.12
  588.0 89.5 reduce-scatter.8
  681.1 87.8 reduce-scatter.10
  771.7 112.6 reduce-scatter.6

commit v5 on v4

--- a/solution.py
+++ b/solution.py
@@ -14,6 +14,7 @@
 LN2 = 0.6931471805599453
 NT = (((1,), (1,)), ((), ()))
 VMEM_LIMIT = 56 << 20
+LINK_COST = 20_000_000_000
 
 
 def across(slab, place, width):
@@ -91,7 +92,7 @@
         out_shape=jax.ShapeDtypeStruct((seqs * n, chans), jnp.float32),
         scratch_shapes=[pltpu.VMEM((GROUP * n, width), jnp.float32)] * 2,
         compiler_params=pltpu.CompilerParams(vmem_limit_bytes=VMEM_LIMIT),
-        cost_estimate=pl.CostEstimate(flops=4 * work, transcendentals=work, bytes_accessed=8 * tokens * chans),
+        cost_estimate=pl.CostEstimate(flops=1000 * work, transcendentals=work, bytes_accessed=8 * tokens * chans),
         name=body.__name__[:7],
     )(dte, other, slabs, rate)
 
@@ -161,7 +162,7 @@
         ],
         scratch_shapes=[pltpu.VMEM((n, width), jnp.float32)] + [pltpu.VMEM((GROUP * n, width), jnp.bfloat16)] * 2,
         compiler_params=pltpu.CompilerParams(vmem_limit_bytes=VMEM_LIMIT),
-        cost_estimate=pl.CostEstimate(flops=8 * work, transcendentals=work, bytes_accessed=2 * work),
+        cost_estimate=pl.CostEstimate(flops=1400 * work, transcendentals=work, bytes_accessed=2 * work),
         name="fwd_full",
     )(dte, dtx, slabs, read, rate, start)
 
@@ -282,7 +283,7 @@
             ] * 2,
         ],
         compiler_params=pltpu.CompilerParams(vmem_limit_bytes=VMEM_LIMIT),
-        cost_estimate=pl.CostEstimate(flops=14 * work, transcendentals=work, bytes_accessed=2 * work),
+        cost_estimate=pl.CostEstimate(flops=3200 * work, transcendentals=work, bytes_accessed=2 * work),
         name="bwd_full",
     )(dte, dtx, grad, hist, slabs, write, ones, rate, start)
     both = jnp.stack([part.reshape(strips, tokens // GROUP, span).sum(0) for part in (dw, dr)])
@@ -481,6 +482,7 @@
         scratch_shapes=sems,
         compiler_params=pltpu.CompilerParams(
             collective_id=collective_id, has_side_effects=True, vmem_limit_bytes=VMEM_LIMIT),
+        cost_estimate=pl.CostEstimate(flops=LINK_COST, transcendentals=0, bytes_accessed=0),
         name="link_gather",
     )(*[a for _, a, _ in arrays])
 
@@ -698,6 +700,7 @@
         scratch_shapes=scratch,
         compiler_params=pltpu.CompilerParams(
             collective_id=collective_id, has_side_effects=True, vmem_limit_bytes=VMEM_LIMIT),
+        cost_estimate=pl.CostEstimate(flops=4 * LINK_COST, transcendentals=0, bytes_accessed=0),
         name="link_reduce",
     )(*[entry[1] for entry in arrays])
 
@@ -755,6 +758,7 @@
             pltpu.VMEM((half, width), bf)],
         compiler_params=pltpu.CompilerParams(
             collective_id=collective_id, has_side_effects=True, vmem_limit_bytes=VMEM_LIMIT),
+        cost_estimate=pl.CostEstimate(flops=LINK_COST, transcendentals=0, bytes_accessed=0),
         name="link_sum",
     )(partial.astype(bf))
 
@@ -838,6 +842,7 @@
             dma((2, mates)), dma((2, mates)), pltpu.VMEM((2, take, conv.shape[1]), conv.dtype), *sems],
         compiler_params=pltpu.CompilerParams(
             collective_id=collective_id, has_side_effects=True, vmem_limit_bytes=VMEM_LIMIT),
+        cost_estimate=pl.CostEstimate(flops=4 * LINK_COST, transcendentals=0, bytes_accessed=0),
         name="link_open",
     )(conv, gate, *[a for _, a, _ in arrays])
     return result[0], result[2], *result[3:]
@@ -984,14 +989,16 @@
     gate_act = jax.nn.silu(gate_in)
     gated = (ssm_out * gate_act * valid).astype(bf)
     product = jnp.dot(gated, out_full, preferred_element_type=f32).astype(bf)
-    output = (residual + lax.psum_scatter(product, "stream", scatter_dimension=0, tiled=True).astype(f32)).astype(bf)
-
     d_gated = contract_cols(cot_all, out_full)
-    g_out = lax.psum_scatter(contract_rows(gated, cot_all).astype(bf), "seq", scatter_dimension=0, tiled=True)
+    g_out = contract_rows(gated, cot_all).astype(bf)
     d_masked = d_gated * valid
     d_ssm = d_masked * gate_act
     d_gate = (d_masked * ssm_out * silu_slope(gate_in)).astype(bf)
-    g_in_gate = lax.psum_scatter(contract_rows(unit, d_gate).astype(bf), "seq", scatter_dimension=0, tiled=True)
+    g_in_gate = contract_rows(unit, d_gate).astype(bf)
+    d_ssm, product, g_out, g_in_gate = lax.optimization_barrier((d_ssm, product, g_out, g_in_gate))
+    g_out = lax.psum_scatter(g_out, "seq", scatter_dimension=0, tiled=True)
+    g_in_gate = lax.psum_scatter(g_in_gate, "seq", scatter_dimension=0, tiled=True)
+    output = (residual + lax.psum_scatter(product, "stream", scatter_dimension=0, tiled=True).astype(f32)).astype(bf)
     g_skip = jnp.sum(d_ssm * act_float, axis=0)
     back_ends = scan_end(bwd_end_body, dt_reset, d_ssm, read_slabs, rate, seqs)
     later_sum = carried(back_ends, step_sum, rate, True, sizes, 4)
@@ -1030,13 +1037,12 @@
         joined = jnp.concatenate(columns, axis=1)
         return jnp.pad(joined, ((0, 0), (0, -joined.shape[1] % 128))).astype(bf)
 
-    small = padded_small([g_xproj, g_dt, g_log.T * LN2, g_dt_bias[:, None], g_skip[:, None]])
-    small = lax.psum_scatter(small, "seq", scatter_dimension=0, tiled=True).astype(f32)
-    taps = padded_small([g_conv, g_conv_bias[:, None]])
-    d_unit, g_in_gate = lax.optimization_barrier((d_unit, in_rows(g_in_gate)))
-    g_in_conv, taps, d_unit = link_reduce(
-        [("seq", g_in_conv, 2, 0 if own_feats % 16 else own), ("seq", taps, 1, 0), ("stream", d_unit, 4, 0)], sizes, 6)
-    taps = taps.astype(f32)
+    small = padded_small(
+        [g_xproj, g_dt, g_log.T * LN2, g_dt_bias[:, None], g_skip[:, None], g_conv, g_conv_bias[:, None]])
+    d_unit, g_in_gate, output, g_out = lax.optimization_barrier((d_unit, in_rows(g_in_gate), output, g_out))
+    g_in_conv, small, d_unit = link_reduce(
+        [("seq", g_in_conv, 2, 0 if own_feats % 16 else own), ("seq", small, 2, 0), ("stream", d_unit, 4, 0)], sizes, 6)
+    small = small.astype(f32)
     d_unit = d_unit.astype(f32)
     in_grad = cotangent.astype(f32) + inv_rms * (d_unit - unit_own * jnp.mean(d_unit * unit_own, axis=-1, keepdims=True))
 
@@ -1048,8 +1054,8 @@
         in_grad.astype(bf)[None],
         jnp.sum(g_unit * in_weight.astype(f32), axis=1),
         g_unit * gain[:, None],
-        taps[:, :CONV].T,
-        taps[:, CONV],
+        small[:, at + state_dim + 2 : at + state_dim + 2 + CONV].T,
+        small[:, at + state_dim + 2 + CONV],
         small[:, :proj_dim],
         small[:, proj_dim:at].T,
         small[:, at + state_dim],

time: 927 us -> 815 us (0.88)
  waiting for transfers between devices: 104 us -> 19.6 us
  Pallas kernels: 461 us -> 415 us
  other arithmetic: 110 us -> 125 us
    reduce_scatter x2, waiting for transfers between devices: 102 us -> 14.7 us  [the longest x1 14.7 us: local(): g_out = lax.psum_scatter(g_out, 'seq', scatter_dimension=0, tiled=True)]
    pallas_call x1, Pallas kernels: 126 us -> 86.6 us  [link_reduce(): pl.pallas_call(kernel, in_specs=[pl.BlockSpec(memory_space=pl.ANY)] * cou...]
  transfers between devices with their start and end apart: 10 -> 9, of which waited for: 3 -> 2; matrix products, arithmetic and copies ran while one was open for 26% -> 29% of each run, Pallas kernels for 25% -> 33%
where the time goes in v5:
time: 815 us; the launch traced here: 808 us
  Pallas kernels  415 us (51%)
  matrix products  170 us (21%)
  other arithmetic  125 us (15%)
  local copies, waits for them, and re-layouts  48 us (6%)
  waiting for transfers between devices  19.6 us (2%)
  between operations  15.5 us (2%)
  starting transfers between devices  15 us (2%)
    pallas_call x1, Pallas kernels, bwd_full(): pl.pallas_call(bwd_full_body, grid=(strips, seqs, blocks), in_specs=[pl.B...  95.3 us
    pallas_call x1, Pallas kernels, link_reduce(): pl.pallas_call(kernel, in_specs=[pl.BlockSpec(memory_space=pl.ANY)] * cou...  86.6 us
    pallas_call x1, Pallas kernels, link_open(): pl.pallas_call(kernel, in_specs=[pl.BlockSpec(memory_space=pl.ANY)] * (co...  63.5 us
    pallas_call x2, Pallas kernels, scan_end(): pl.pallas_call(body, grid=(seqs, chans // width), in_specs=[pl.BlockSpec(...  62.4 us
    dot_general x3, matrix products, contract_cols(): lax.dot_general(left_mat, right_mat, NT, preferred_element_type=jnp.float32)  44.3 us
    dot_general x3, matrix products, contract_rows(): lax.dot_general(left_mat, right_mat, (((0,), (0,)), ((), ())), preferred_...  42.4 us
    pallas_call x1, Pallas kernels, fwd_full(): pl.pallas_call(fwd_full_body, grid=(chans // width, seqs, blocks), in_spe...  41.9 us
    pallas_call x2, Pallas kernels, link_sum(): pl.pallas_call(kernel, in_specs=[pl.BlockSpec(memory_space=pltpu.VMEM)],...  34.6 us
  transfers between devices with their start and end apart: 9, of which 2 were waited for; matrix products, arithmetic and copies ran while one was open for 29% of the time, Pallas kernels for 33%

profile of v5, /device:TPU:19, one launch (start us, length us, event | category | flops | bytes accessed | tf_op | source)
XLA Modules:
  0.0 807.9 jit_solution(11380361966206505182)
XLA Ops:
  25.0 63.5 %link_open.1 = (bf16[2048,1024]{1,0:T(8,128)(2,1)}, bf16[256,1024]{1,0:T(8,128)(2,1)}, bf16[256,1024]{1,0:T(8,128)(2,1)}, s32[32,128]{1,0:T(8,128)}, bf16[2048,2...) custom-call(bf16[256,1024]{1,0:T(8,128)(2,1)} %get-tuple-element.205.conv_ref, bf16[256,1024]{1,0:T(8,128)(2,1)} %get-tuple-element.204.gate_ref, ...), custom_call_target="tpu_custom_call" | custom-call | flops 80000000000 | tf_op jit(solution)/shard_map/link_open/pallas_call | solution.py:832
  89.3 12.5 %fusion.77 = f32[2048,1024]{1,0:T(8,128)S(1)} fusion(bf16[2048,2048]{1,0:T(8,128)(2,1)} %get-tuple-element.42, bf16[2048,1024]{1,0:T(8,128)(2,1)} %get-tuple-element.43), kind=kOutput, calls=%fused_computation.242 | convolution fusion | flops 8589934592 | bytes 20971520 | tf_op jit(solution)/shard_map/dot_general | solution.py:963
  114.7 19.4 %multiply_convert_fusion.2 = (bf16[4,512,1024]{2,1,0:T(8,128)(2,1)S(1)}, f32[4,512,1024]{2,1,0:T(8,128)}) fusion(f32[4,512,1024]{2,1,0:T(8,128)} %bitcast.245, f32[1024]{0:T(1024)S(1)} %get-tuple-element.138, f32[4,512]{1,0:T(4,128)S(1)} %get-tuple-element.199, f32[4,3,1024]{2,1,0:T(4,128)S(1)} %convert_element_type.247, f32[1024]{0:T(1024)S(1)} %get-tuple-element.139, ...), kind=kLoop, calls=%fused_computation.41 | loop fusion | flops 39845888 | bytes 21065728 | tf_op jit(solution)/shard_map/convert_element_type | solution.py:970
  138.6 16.1 %link_sum.2 = f32[160,2048]{1,0:T(8,128)} custom-call(bf16[160,2048]{1,0:T(8,128)(2,1)} %convolution_convert_fusion.4.own_ref), custom_call_target="tpu_custom_call" | custom-call | flops 20000000000 | tf_op jit(solution)/shard_map/link_sum/pallas_call | solution.py:750
  159.3 9.3 %bitcast_reduce_fusion = (f32[4,1024]{1,0:T(4,128)S(1)}, f32[2048,1024]{1,0:T(8,128)}, f32[2048,1024]{1,0:T(8,128)S(1)}) fusion(f32[1024]{0:T(1024)S(1)} %get-tuple-element.135, pred[2048]{0:T(1024)(128)(4,1)S(1)} %bitcast.273, bf16[1024,384]{1,0:T(8,128)(2,1)S(1)} %copy-done.8, f32[160,2048]{1,0:T(8,128)} %link_sum.2), kind=kOutput, calls=%fused_computation.30 | convolution fusion | flops 555741184 | bytes 17586176 | tf_op jit(solution)/shard_map/dot_general | solution.py:977
  168.6 7.5 convert_multiply_fusion.3.dtx_ref
  176.6 31.1 %fwd_end.1 = f32[64,1024]{1,0:T(8,128)} custom-call(f32[2048,1024]{1,0:T(8,128)} %get-tuple-element.150.dte_ref, f32[2048,1024]{1,0:T(8,128)} %convert_multiply_fusion.3.dtx_ref, f32[2048,16]{1,0:T(8,128)} %bitcast.263, f32[16,1024]{1,0:T(8,128)} %multiply_bitcast_fusion.rate_ref), custom_call_target="tpu_custom_call" | custom-call | flops 33554432000 | bytes 16777216 | tf_op jit(solution)/shard_map/fwd_end/pallas_call | solution.py:82
  209.4 15.4 %link_gather.2 = bf16[640,1024]{1,0:T(8,128)(2,1)} custom-call(bf16[80,1024]{1,0:T(8,128)(2,1)} %pad.22.refs_0_), custom_call_target="tpu_custom_call" | custom-call | flops 20000000000 | tf_op jit(solution)/shard_map/link_gather/pallas_call | solution.py:476
  234.3 41.9 %fwd_full.1 = (f32[2048,1024]{1,0:T(8,128)}, bf16[32896,1024]{1,0:T(8,128)(2,1)}) custom-call(f32[2048,1024]{1,0:T(8,128)} %get-tuple-element.150.dte_ref, f32[2048,1024]{1,0:T(8,128)} %convert_multiply_fusion.3.dtx_ref, f32[2048,16]{1,0:T(8,128)} %bitcast.264, bf16[2048,256]{1,0:T(8,128)(2,1)} %copy.158.read_ref, f32[16,1024]{1,0:T(8,128)} %multiply_bitcast_fusion.rate_ref, ...), custom_call_target="tpu_custom_call" | custom-call | flops 46976204800 | bytes 67108864 | tf_op jit(solution)/shard_map/fwd_full/pallas_call | solution.py:147
  276.3 14.5 %fusion.78 = f32[2048,1024]{1,0:T(8,128)} fusion(bf16[2048,2048]{1,0:T(8,128)(2,1)} %all-gather.4.cloned.1.call-done, bf16[1024,2048]{1,0:T(8,128)(2,1)} %all-gather.6.cloned.1.call-done), kind=kOutput, calls=%fused_computation.243 | convolution fusion | flops 8589934592 | bytes 20971520 | tf_op jit(solution)/shard_map/dot_general | solution.py:878
  290.8 4.1 all-gather.8.cloned.1.call-done
  294.9 25.1 %multiply_convert_fusion.1 = (bf16[2048,1024]{1,0:T(8,128)(2,1)}, bf16[2048,1024]{1,0:T(8,128)(2,1)}, f32[2048,1024]{1,0:T(8,128)}) fusion(f32[2048,1024]{1,0:T(8,128)} %get-tuple-element.48, f32[1024]{0:T(1024)S(1)} %copy-done.48, f32[2048]{0:T(1024)S(1)} %bitcast.272, bf16[4,512,1024]{2,1,0:T(8,128)(2,1)} %copy-done, f32[2048,1024]{1,0:T(8,128)} %fusion.78, ...), kind=kOutput, calls=%fused_computation.38 | convolution fusion | flops 8629780480 | bytes 50343936 | tf_op jit(solution)/shard_map/dot_general | solution.py:964
  320.0 14.3 %convolution_convert_fusion.3 = bf16[2048,1024]{1,0:T(8,128)(2,1)} fusion(bf16[2048,2048]{1,0:T(8,128)(2,1)} %get-tuple-element.42, bf16[2048,1024]{1,0:T(8,128)(2,1)} %get-tuple-element.154), kind=kOutput, calls=%fused_computation.62 | convolution fusion | flops 8592031744 | bytes 16777216 | tf_op jit(solution)/shard_map/dot_general | solution.py:874
  334.3 14.0 %convolution_convert_fusion.1 = bf16[1024,2048]{1,0:T(8,128)(2,1)} fusion(bf16[2048,1024]{1,0:T(8,128)(2,1)} %get-tuple-element.153, bf16[2048,2048]{1,0:T(8,128)(2,1)} %all-gather.4.cloned.1.call-done), kind=kOutput, calls=%fused_computation.60 | convolution fusion | flops 8592031744 | bytes 16777216 | tf_op jit(solution)/shard_map/dot_general | solution.py:874
  348.3 14.4 %convolution_convert_fusion = bf16[2048,2048]{1,0:T(8,128)(2,1)} fusion(bf16[2048,1024]{1,0:T(8,128)(2,1)} %get-tuple-element.153, bf16[1024,2048]{1,0:T(8,128)(2,1)} %all-gather.6.cloned.1.call-done), kind=kOutput, calls=%fused_computation.45 | convolution fusion | flops 8594128896 | bytes 16777216 | tf_op jit(solution)/shard_map/dot_general | solution.py:991
  366.8 31.3 %bwd_end.1 = f32[64,1024]{1,0:T(8,128)} custom-call(f32[2048,1024]{1,0:T(8,128)} %get-tuple-element.150.dte_ref, f32[2048,1024]{1,0:T(8,128)} %get-tuple-element.49.grad_ref, f32[2048,16]{1,0:T(8,128)} %bitcast.261, f32[16,1024]{1,0:T(8,128)} %multiply_bitcast_fusion.rate_ref), custom_call_target="tpu_custom_call" | custom-call | flops 33554432000 | bytes 16777216 | tf_op jit(solution)/shard_map/bwd_end/pallas_call | solution.py:82
  399.8 15.4 %link_gather.3 = bf16[640,1024]{1,0:T(8,128)(2,1)} custom-call(bf16[80,1024]{1,0:T(8,128)(2,1)} %pad.23.refs_0_), custom_call_target="tpu_custom_call" | custom-call | flops 20000000000 | tf_op jit(solution)/shard_map/link_gather/pallas_call | solution.py:476
  418.5 95.3 %bwd_full.1 = (f32[2048,1024]{1,0:T(8,128)}, f32[2048,1024]{1,0:T(8,128)}, f32[16,1024]{1,0:T(8,128)}, f32[256,256]{1,0:T(8,128)}, f32[256,256]{1,0:T(8,128)}) custom-call(f32[2048,1024]{1,0:T(8,128)} %get-tuple-element.150.dte_ref, f32[2048,1024]{1,0:T(8,128)} %convert_multiply_fusion.3.dtx_ref, f32[2048,1024]{1,0:T(8,128)} %get-tuple-element.49.grad_ref, ...), custom_call_target="tpu_custom_call" | custom-call | flops 107374182400 | bytes 67108864 | tf_op jit(solution)/shard_map/bwd_full/pallas_call | solution.py:249
  518.2 16.0 %fusion.72 = (bf16[1024]{0:T(1024)(128)(2,1)S(1)}, bf16[2048,1024]{1,0:T(8,128)(2,1)S(1)}, bf16[1024]{0:T(1024)(128)(2,1)S(1)}) fusion(f32[2048,1024]{1,0:T(8,128)} %get-tuple-element.51, bf16[4,512,1024]{2,1,0:T(8,128)(2,1)} %copy-done, f32[2048,1024]{1,0:T(8,128)} %get-tuple-element.52, f32[2048,1024]{1,0:T(8,128)} %copy-done.4, f32[1024]{0:T(1024)S(1)} %copy-done.34, ...), kind=kLoop, calls=%fused_computation.238 | loop fusion | flops 48232448 | bytes 41951232 | tf_op jit(solution)/shard_map/reduce_sum | solution.py:1010
  536.7 18.5 %link_sum.3 = f32[160,2048]{1,0:T(8,128)} custom-call(bf16[160,2048]{1,0:T(8,128)(2,1)} %pad_maximum_fusion.3.own_ref), custom_call_target="tpu_custom_call" | custom-call | flops 20000000000 | tf_op jit(solution)/shard_map/link_sum/pallas_call | solution.py:750
  555.3 14.8 %add_add_fusion = f32[2048,1024]{1,0:T(8,128)} fusion(f32[2048,1024]{1,0:T(8,128)} %get-tuple-element.49.grad_ref, f32[2048,1024]{1,0:T(8,128)} %get-tuple-element.51, f32[1024]{0:T(1024)S(1)} %copy-done.49, bf16[1024,384]{1,0:T(8,128)(2,1)S(1)} %copy-done.9, f32[160,2048]{1,0:T(8,128)} %link_sum.3, f32[2048,1024]{1,0:T(8,128)} %copy-done.4, ...), kind=kOutput, calls=%fused_computation.36 | convolution fusion | flops 694484992 | bytes 35397632 | tf_op jit(solution)/shard_map/dot_general | solution.py:1016
  570.2 21.4 %fusion.71 = (bf16[1024]{0:T(1024)(128)(2,1)S(1)}, bf16[1024]{0:T(1024)(128)(2,1)S(1)}, bf16[1024]{0:T(1024)(128)(2,1)S(1)}, bf16[1024]{0:T(1024)(128)(2,1)S(1)}...) fusion(f32[2048,1024]{1,0:T(8,128)} %copy-done.3, f32[4,512]{1,0:T(4,128)S(1)} %copy-done.27, ...), kind=kLoop, calls=%fused_computation.237 | loop fusion | flops 48229376 | bytes 42027008 | tf_op jit(solution)/shard_map/reduce_sum | solution.py:1019
  591.7 6.4 collective-permute-start.1
  601.0 15.6 %fusion.79 = f32[2048,2048]{1,0:T(8,128)} fusion(bf16[2048,1024]{1,0:T(8,128)(2,1)} %get-tuple-element.154, bf16[2048,1024]{1,0:T(8,128)(2,1)} %all-gather.8.cloned.1.call-done), kind=kOutput, calls=%fused_computation.244 | convolution fusion | flops 8589934592 | bytes 25165824 | tf_op jit(solution)/shard_map/dot_general | solution.py:878
  622.2 17.0 %fusion.6 = bf16[4,512,1024]{2,1,0:T(8,128)(2,1)S(1)} fusion(f32[4,3,1024]{2,1,0:T(4,128)S(1)} %convert_element_type.292, f32[4,512,1024]{2,1,0:T(8,128)} %copy-done.7, f32[4,512]{1,0:T(4,128)S(1)} %copy-done.47, f32[4,512]{1,0:T(4,128)S(1)} %copy-done.46, f32[4,512]{1,0:T(4,128)S(1)} %copy-done.45, f32[1024]{0:T(1024)S(1)} %copy-done.38, ...), kind=kLoop, calls=%fused_computation.16 | loop fusion | flops 29360128 | bytes 12673024 | tf_op jit(solution)/shard_map/convert_element_type | solution.py:1029
  641.2 14.2 %add_convert_fusion.refs_2_ = bf16[2048,2048]{1,0:T(8,128)(2,1)} fusion(f32[2048,2048]{1,0:T(8,128)} %fusion.79, bf16[2048,1024]{1,0:T(8,128)(2,1)S(1)} %bitcast.253, bf16[2048,1024]{1,0:T(8,128)(2,1)S(1)} %copy-done.54), kind=kOutput, calls=%fused_computation.1 | convolution fusion | flops 8598323200 | bytes 33554432 | tf_op jit(solution)/shard_map/dot_general | solution.py:878
  655.4 5.6 all-to-all-start
  661.1 14.1 %convolution_convert_fusion.2.refs_0_ = bf16[2048,1024]{1,0:T(8,128)(2,1)} fusion(bf16[2048,2048]{1,0:T(8,128)(2,1)} %get-tuple-element.42, bf16[2048,1024]{1,0:T(8,128)(2,1)} %bitcast.254), kind=kOutput, calls=%fused_computation.61 | convolution fusion | flops 8592031744 | bytes 16777216 | tf_op jit(solution)/shard_map/dot_general | solution.py:874
  677.2 3.7 fusion.27
  680.9 14.7 %reduce-scatter.8.cloned.1.call-done = bf16[128,2048]{1,0:T(8,128)(2,1)} async-done(((bf16[1024,2048]{1,0:T(8,128)(2,1)}), bf16[128,2048]{1,0:T(8,128)(2,1)}) %reduce-scatter.8.cloned.1.call-update) | async-done | bytes 524304 | tf_op jit(solution)/shard_map/reduce_scatter | solution.py:999
  695.6 86.6 %link_reduce.1 = (bf16[64,4096]{1,0:T(8,128)(2,1)}, bf16[128,384]{1,0:T(8,128)(2,1)}, bf16[512,2048]{1,0:T(8,128)(2,1)}) custom-call(bf16[2048,1024]{1,0:T(8,128)(2,1)} %convolution_convert_fusion.2.refs_0_, bf16[1024,384]{1,0:T(8,128)(2,1)} %pad.24.refs_1_, bf16[2048,2048]{1,0:T(8,128)(2,1)} %add_convert_fusion.refs_2_), custom_call_target="tpu_custom_call" | custom-call | flops 80000000000 | tf_op jit(solution)/shard_map/link_reduce/pallas_call | solution.py:695
  788.3 4.1 fusion.30
  (260 shorter events, 94.3 us)
Async XLA Ops:
  7.2 269.0 %all-gather.6.cloned.1.call-start = ((), (), s32[]{:S(2)}) async-start(), calls=%async_computation.5 | async-start | bytes 4718592 | tf_op jit(solution)/shard_map/all_gather | solution.py:942
  10.1 78.4 %copy-start.43 = (f32[512]{0:T(512)}, f32[512]{0:T(512)S(1)}, u32[]{:S(2)}) copy-start(f32[512]{0:T(512)S(1)} %add_rsqrt_fusion) | copy-start | bytes 6148
  88.5 187.7 %all-gather.4.cloned.1.call-start = ((), (), s32[]{:S(2)}) async-start(), calls=%async_computation.4 | async-start | bytes 10485760 | tf_op jit(solution)/shard_map/all_gather | solution.py:943
  89.3 205.6 %all-gather.8.cloned.1.call-start = ((), (), s32[]{:S(2)}) async-start(), calls=%async_computation.6 | async-start | bytes 4718592 | tf_op jit(solution)/shard_map/all_gather | solution.py:941
  89.3 20.1 %copy-start.8 = (bf16[1024,384]{1,0:T(8,128)(2,1)S(1)}, bf16[1024,384]{1,0:T(8,128)(2,1)}, u32[]{:S(2)}) copy-start(bf16[1024,384]{1,0:T(8,128)(2,1)} %get-tuple-element.39) | copy-start | bytes 2359300
  105.2 9.5 %collective-permute-start = (bf16[4,3,1024]{2,1,0:T(4,128)(2,1)S(1)}, bf16[4,3,1024]{2,1,0:T(4,128)(2,1)S(1)}, u32[]{:S(2)}, u32[]{:S(2)}) collective-permute-start(bf16[4,3,1024]{2,1,0:T(4,128)(2,1)S(1)} %slice.787), channel_id=1, source_target_pairs={{0,4},{4,8},{8,12},{12,16},{16,20},{20,24},{24,28},{1,5},{5,9},{9,... | collective-permute-start | bytes 73736 | tf_op jit(solution)/shard_map/ppermute | solution.py:854
  107.4 548.0 %reduce-scatter.4.cloned.1.call-start = ((), (), s32[]{:S(2)}) async-start(), calls=%async_computation.7 | async-start | bytes 4718592 | tf_op jit(solution)/shard_map/reduce_scatter | solution.py:1000
  111.2 22.9 %copy-start.22 = (f32[4,512]{1,0:T(4,128)}, f32[4,512]{1,0:T(4,128)S(1)}, u32[]{:S(2)}) copy-start(f32[4,512]{1,0:T(4,128)S(1)} %get-tuple-element.199) | copy-start | bytes 24580
  111.2 22.9 %copy-start.24 = (f32[4,512]{1,0:T(4,128)}, f32[4,512]{1,0:T(4,128)S(1)}, u32[]{:S(2)}) copy-start(f32[4,512]{1,0:T(4,128)S(1)} %get-tuple-element.200) | copy-start | bytes 24580
  111.2 22.9 %copy-start.26 = (f32[4,512]{1,0:T(4,128)}, f32[4,512]{1,0:T(4,128)S(1)}, u32[]{:S(2)}) copy-start(f32[4,512]{1,0:T(4,128)S(1)} %get-tuple-element.202) | copy-start | bytes 24580
  112.3 21.8 %copy-start.35 = (f32[1024]{0:T(1024)}, f32[1024]{0:T(1024)S(1)}, u32[]{:S(2)}) copy-start(f32[1024]{0:T(1024)S(1)} %get-tuple-element.137) | copy-start | bytes 12292
  112.3 21.8 %copy-start.37 = (f32[1024]{0:T(1024)}, f32[1024]{0:T(1024)S(1)}, u32[]{:S(2)}) copy-start(f32[1024]{0:T(1024)S(1)} %get-tuple-element.138) | copy-start | bytes 12292
  112.3 21.8 %copy-start.39 = (f32[1024]{0:T(1024)}, f32[1024]{0:T(1024)S(1)}, u32[]{:S(2)}) copy-start(f32[1024]{0:T(1024)S(1)} %get-tuple-element.139) | copy-start | bytes 12292
  112.3 21.8 %copy-start.41 = (f32[1024]{0:T(1024)}, f32[1024]{0:T(1024)S(1)}, u32[]{:S(2)}) copy-start(f32[1024]{0:T(1024)S(1)} %get-tuple-element.140) | copy-start | bytes 12292
  114.1 54.5 %copy-start.33 = (f32[1024]{0:T(1024)}, f32[1024]{0:T(1024)S(1)}, u32[]{:S(2)}) copy-start(f32[1024]{0:T(1024)S(1)} %get-tuple-element.135) | copy-start | bytes 12292
  114.7 19.5 %copy-start.16 = (f32[4,3,1024]{2,1,0:T(4,128)}, f32[4,3,1024]{2,1,0:T(4,128)S(1)}, u32[]{:S(2)}) copy-start(f32[4,3,1024]{2,1,0:T(4,128)S(1)} %convert_element_type.247) | copy-start | bytes 147460
  168.6 40.0 %copy-start.28 = (bf16[4,1024]{1,0:T(4,128)(2,1)}, bf16[4,1024]{1,0:T(4,128)(2,1)S(1)}, u32[]{:S(2)}) copy-start(bf16[4,1024]{1,0:T(4,128)(2,1)S(1)} %get-tuple-element.147) | copy-start | bytes 24580
  168.6 40.0 %copy-start.30 = (bf16[4,1024]{1,0:T(4,128)(2,1)}, bf16[4,1024]{1,0:T(4,128)(2,1)S(1)}, u32[]{:S(2)}) copy-start(bf16[4,1024]{1,0:T(4,128)(2,1)S(1)} %get-tuple-element.148) | copy-start | bytes 24580
  209.3 20.1 %copy-start.21 = (pred[2048,16]{0,1:T(8,128)(4,1)S(1)}, pred[2048,16]{0,1:T(8,128)(4,1)}, u32[]{:S(2)}) copy-start(pred[2048,16]{0,1:T(8,128)(4,1)} %iota_compare_fusion) | copy-start | bytes 98308
  209.3 22.7 %copy-start.18 = (f32[16,1024]{1,0:T(8,128)S(1)}, f32[16,1024]{1,0:T(8,128)}, u32[]{:S(2)}) copy-start(f32[16,1024]{1,0:T(8,128)} %multiply_bitcast_fusion.rate_ref) | copy-start | bytes 196612
  362.8 314.4 %reduce-scatter.6.cloned.1.call-start = ((), (), s32[]{:S(2)}) async-start(), calls=%async_computation.8 | async-start | bytes 10485760 | tf_op jit(solution)/shard_map/reduce_scatter | solution.py:1001
  366.8 32.3 %copy-start.29 = (bf16[4,1024]{1,0:T(4,128)(2,1)S(1)}, bf16[4,1024]{1,0:T(4,128)(2,1)}, u32[]{:S(2)}) copy-start(bf16[4,1024]{1,0:T(4,128)(2,1)} %copy-done.28) | copy-start | bytes 24580
  366.8 32.3 %copy-start.31 = (bf16[4,1024]{1,0:T(4,128)(2,1)S(1)}, bf16[4,1024]{1,0:T(4,128)(2,1)}, u32[]{:S(2)}) copy-start(bf16[4,1024]{1,0:T(4,128)(2,1)} %copy-done.30) | copy-start | bytes 24580
  417.0 278.6 %reduce-scatter.8.cloned.1.call-start = ((), (), s32[]{:S(2)}) async-start(), calls=%async_computation.9 | async-start | bytes 4718592 | tf_op jit(solution)/shard_map/reduce_scatter | solution.py:999
  418.5 99.7 %copy-start.34 = (f32[1024]{0:T(1024)S(1)}, f32[1024]{0:T(1024)}, u32[]{:S(2)}) copy-start(f32[1024]{0:T(1024)} %copy-done.33) | copy-start | bytes 12292
  570.2 27.9 %copy-start.2 = (bf16[4,512,1024]{2,1,0:T(8,128)(2,1)S(1)}, bf16[4,512,1024]{2,1,0:T(8,128)(2,1)}, u32[]{:S(2)}) copy-start(bf16[4,512,1024]{2,1,0:T(8,128)(2,1)} %copy-done) | copy-start | bytes 12582916
  570.2 27.9 %copy-start.11 = (f32[160,2048]{1,0:T(8,128)S(1)}, f32[160,2048]{1,0:T(8,128)}, u32[]{:S(2)}) copy-start(f32[160,2048]{1,0:T(8,128)} %link_sum.3) | copy-start | bytes 3932164
  570.2 28.8 %copy-start.15 = (f32[160,2048]{1,0:T(8,128)S(1)}, f32[160,2048]{1,0:T(8,128)}, u32[]{:S(2)}) copy-start(f32[160,2048]{1,0:T(8,128)} %link_sum.2) | copy-start | bytes 3932164
  591.7 30.5 %collective-permute-start.1 = (bf16[4,3,1024]{2,1,0:T(4,128)(2,1)S(1)}, bf16[4,3,1024]{2,1,0:T(4,128)(2,1)S(1)}, u32[]{:S(2)}, u32[]{:S(2)}) collective-permute-start(bf16[4,3,1024]{2,1,0:T(4,128)(2,1)S(1)} %slice.786), channel_id=1, source_target_pairs={{4,0},{8,4},{12,8},{16,12},{20,16},{24,20},{28,24},{5,1},{9,5},{13... | collective-permute-start | bytes 73736 | tf_op jit(solution)/shard_map/ppermute | solution.py:854
  655.4 19.8 %all-to-all-start = ((bf16[4,64,1024]{2,1,0:T(8,128)(2,1)}), bf16[4,64,1024]{2,1,0:T(8,128)(2,1)S(1)}, u32[]{:S(2)}, u32[]{:S(2)}) async-start(bf16[4,64,1024]{2,1,0:T(8,128)(2,1)} %bitcast.265), calls=%async_computation.1 | async-start | bytes 1048576 | tf_op jit(solution)/shard_map/all_to_all | solution.py:1033
  680.9 104.9 %copy-start.44 = (f32[512]{0:T(512)S(1)}, f32[512]{0:T(512)}, u32[]{:S(2)}) copy-start(f32[512]{0:T(512)} %copy-done.43) | copy-start | bytes 6148
  695.6 92.7 %copy-start.10 = (bf16[1,512,2048]{2,1,0:T(8,128)(2,1)S(1)}, bf16[1,512,2048]{2,1,0:T(8,128)(2,1)}, u32[]{:S(2)}) copy-start(bf16[1,512,2048]{2,1,0:T(8,128)(2,1)} %param.14) | copy-start | bytes 6291460
  (32 other events, 362.7 us)
Sparse Core Ops, SparseCore 0:
  88.6 72.4 all-gather.5
  162.7 57.2 all-gather.3
  222.2 72.6 all-gather.7
  362.9 94.4 reduce-scatter.3
  460.0 70.7 reduce-scatter.5
  601.2 94.3 reduce-scatter.7

commit v6 on v5

--- a/solution.py
+++ b/solution.py
@@ -848,6 +848,106 @@
     return result[0], result[2], *result[3:]
 
 
+ROWS = 128
+
+
+def conv_fwd_body(x_ref, early_ref, masks_ref, taps_ref, act_ref, slope_ref, ext_ref):
+    length = x_ref.shape[0]
+    ext_ref[pl.ds(0, 8), :] = early_ref[...]
+
+    @pl.loop(0, length // ROWS)
+    def _(k):
+        here = pl.ds(pl.multiple_of(k * ROWS, ROWS), ROWS)
+        ext_ref[pl.ds(pl.multiple_of(k * ROWS + 8, 8), ROWS), :] = x_ref[here, :]
+        window = ext_ref[pl.ds(pl.multiple_of(k * ROWS, ROWS), ROWS + 8), :]
+        masks = masks_ref[here, :]
+        total = taps_ref[CONV : CONV + 1, :] + taps_ref[CONV - 1 : CONV, :] * window[8:]
+        for tap in range(CONV - 1):
+            shift = 8 - (CONV - 1) + tap
+            total = total + taps_ref[tap : tap + 1, :] * (window[shift : shift + ROWS] * masks[:, tap : tap + 1])
+        gate = jax.nn.sigmoid(total)
+        act_ref[here, :] = (total * gate).astype(act_ref.dtype)
+        slope_ref[here, :] = (gate * (1.0 + total * (1.0 - gate))).astype(slope_ref.dtype)
+
+
+def conv_bwd_body(grad_ref, slope_ref, late_ref, x_ref, masks_ref, taps_ref, out_ref, sums_ref, ext_ref):
+    length, width = x_ref.shape
+    ext_ref[pl.ds(length, 8), :] = late_ref[...]
+
+    @pl.loop(0, length // ROWS)
+    def _(k):
+        here = pl.ds(pl.multiple_of(k * ROWS, ROWS), ROWS)
+        ext_ref[here, :] = grad_ref[here, :] * slope_ref[here, :].astype(jnp.float32)
+
+    def some(k, sums):
+        start = pl.multiple_of(k * ROWS, ROWS)
+        here = pl.ds(start, ROWS)
+        window = ext_ref[pl.ds(start, ROWS + 8), :]
+        masks = masks_ref[here, :]
+        x = x_ref[here, :]
+        total = jnp.zeros((ROWS, width), jnp.float32)
+        parts = []
+        for tap in range(CONV):
+            ahead = CONV - 1 - tap
+            term = window[ahead : ahead + ROWS]
+            if ahead:
+                term = term * masks[:, CONV - 2 + ahead : CONV - 1 + ahead]
+            total = total + taps_ref[tap : tap + 1, :] * term
+            parts.append((term * x).reshape(ROWS // 8, 8, width).sum(0))
+        parts.append(window[:ROWS].reshape(ROWS // 8, 8, width).sum(0))
+        out_ref[here, :] = total.astype(out_ref.dtype)
+        return tuple(a + b for a, b in zip(sums, parts))
+
+    sums = lax.fori_loop(0, length // ROWS, some, (jnp.zeros((8, width), jnp.float32),) * (CONV + 1))
+    for tap in range(CONV + 1):
+        sums_ref[tap : tap + 1, :] = jnp.sum(sums[tap], axis=0, keepdims=True)
+    sums_ref[CONV + 1 :, :] = jnp.zeros((7 - CONV, width), jnp.float32)
+
+
+def conv_fwd(x, early, masks, taps, seqs, width=1024):
+    tokens, chans = x.shape
+    width = min(width, chans)
+    length = tokens // seqs
+    block = pl.BlockSpec((length, width), lambda s, c: (s, c))
+    return pl.pallas_call(
+        conv_fwd_body,
+        grid=(seqs, chans // width),
+        in_specs=[
+            block, pl.BlockSpec((8, width), lambda s, c: (s, c)), pl.BlockSpec((length, 8), lambda s, c: (s, 0)),
+            pl.BlockSpec((8, width), lambda s, c: (0, c))],
+        out_specs=[block, block],
+        out_shape=[jax.ShapeDtypeStruct((tokens, chans), jnp.bfloat16)] * 2,
+        scratch_shapes=[pltpu.VMEM((length + 8, width), jnp.float32)],
+        compiler_params=pltpu.CompilerParams(vmem_limit_bytes=VMEM_LIMIT),
+        cost_estimate=pl.CostEstimate(
+            flops=4000 * tokens * chans, transcendentals=tokens * chans, bytes_accessed=8 * tokens * chans),
+        name="conv_fwd",
+    )(x, early, masks, taps)
+
+
+def conv_bwd(grad, slope, late, x, masks, taps, seqs, width=512):
+    tokens, chans = x.shape
+    width = min(width, chans)
+    length = tokens // seqs
+    block = pl.BlockSpec((length, width), lambda s, c: (s, c))
+    rim = pl.BlockSpec((8, width), lambda s, c: (s, c))
+    return pl.pallas_call(
+        conv_bwd_body,
+        grid=(seqs, chans // width),
+        in_specs=[
+            block, block, rim, block, pl.BlockSpec((length, 8), lambda s, c: (s, 0)),
+            pl.BlockSpec((8, width), lambda s, c: (0, c))],
+        out_specs=[block, rim],
+        out_shape=[
+            jax.ShapeDtypeStruct((tokens, chans), jnp.bfloat16), jax.ShapeDtypeStruct((seqs * 8, chans), jnp.float32)],
+        scratch_shapes=[pltpu.VMEM((length + 8, width), jnp.float32)],
+        compiler_params=pltpu.CompilerParams(vmem_limit_bytes=VMEM_LIMIT),
+        cost_estimate=pl.CostEstimate(
+            flops=5000 * tokens * chans, transcendentals=0, bytes_accessed=12 * tokens * chans),
+        name="conv_bwd",
+    )(grad, slope, late, x, masks, taps)
+
+
 def passed_along(block, axis, distance):
     devices = range(lax.axis_size(axis))
     route = [(i - distance, i) for i in devices if i - distance in devices]
@@ -958,16 +1058,15 @@
     own_ids = doc_ids[:, rim : rim + length]
     starts = start_flags[:, rim : rim + length].reshape(tokens, 1)
     valid = valid_mask[:, rim : rim + length].reshape(tokens, 1)
-    matches = [(doc_ids[:, tap : tap + length] == own_ids).astype(f32)[:, :, None] for tap in range(CONV)]
-
-    conv_in = jnp.dot(unit, in_conv, preferred_element_type=f32).reshape(seqs, length, chans)
+    near = [doc_ids[:, tap : tap + length] == own_ids for tap in range(2 * rim + 1) if tap != rim]
+    masks = jnp.pad(jnp.stack(near, axis=-1).astype(f32), ((0, 0), (0, 0), (0, 8 - 2 * rim))).reshape(tokens, 8)
+
+    conv_in = jnp.dot(unit, in_conv, preferred_element_type=f32)
     gate_in = jnp.dot(unit, in_gate, preferred_element_type=f32)
-    earlier = passed_along(conv_in[:, length - rim :].astype(bf), "seq", 1).astype(f32)
-    padded = jnp.concatenate([earlier, conv_in], axis=1)
-    conv_out = conv_shift
-    for tap in range(CONV):
-        conv_out = conv_out + conv_taps[tap] * padded[:, tap : tap + length] * matches[tap]
-    activated = jax.nn.silu(conv_out).astype(bf).reshape(tokens, chans)
+    earlier = passed_along(conv_in.reshape(seqs, length, chans)[:, length - rim :].astype(bf), "seq", 1).astype(f32)
+    earlier = jnp.pad(earlier, ((0, 0), (8 - rim, 0), (0, 0))).reshape(seqs * 8, chans)
+    taps = jnp.pad(jnp.concatenate([conv_taps, conv_shift[None]]), ((0, 7 - CONV), (0, 0)))
+    activated, slope = conv_fwd(conv_in, earlier, masks, taps, seqs)
     act_float = activated.astype(f32)
     projected = link_sum(
         lax.dot_general(xproj_full, activated, (((0,), (1,)), ((), ())), preferred_element_type=f32), sizes, 2)
@@ -990,10 +1089,10 @@
     gated = (ssm_out * gate_act * valid).astype(bf)
     product = jnp.dot(gated, out_full, preferred_element_type=f32).astype(bf)
     d_gated = contract_cols(cot_all, out_full)
-    g_out = contract_rows(gated, cot_all).astype(bf)
     d_masked = d_gated * valid
     d_ssm = d_masked * gate_act
     d_gate = (d_masked * ssm_out * silu_slope(gate_in)).astype(bf)
+    g_out = contract_rows(gated, cot_all).astype(bf)
     g_in_gate = contract_rows(unit, d_gate).astype(bf)
     d_ssm, product, g_out, g_in_gate = lax.optimization_barrier((d_ssm, product, g_out, g_in_gate))
     g_out = lax.psum_scatter(g_out, "seq", scatter_dimension=0, tiled=True)
@@ -1012,21 +1111,16 @@
     g_dt = lax.dot_general(d_pre_low, low_rank, (((0,), (1,)), ((), ())), preferred_element_type=f32)
     d_low = lax.dot_general(dtw_cols, d_pre_low, (((0,), (1,)), ((), ())), preferred_element_type=f32)
     d_proj = link_sum(jnp.concatenate([d_low, d_write, d_read], axis=0), sizes, 5).astype(bf)
+    d_proj, g_out, g_in_gate = lax.optimization_barrier((d_proj, g_out, g_in_gate))
     g_xproj = lax.dot_general(activated, d_proj, (((0,), (1,)), ((), ())), preferred_element_type=f32)
     d_act = dt_step * sum_write + skip_vec * d_ssm + lax.dot_general(
         d_proj, xproj_full, (((0,), (1,)), ((), ())), preferred_element_type=f32)
-    d_conv = d_act.reshape(seqs, length, chans) * silu_slope(conv_out)
-    g_conv_bias = jnp.sum(d_conv, axis=(0, 1))
-    g_conv = jnp.stack(
-        [jnp.sum(d_conv * padded[:, tap : tap + length] * matches[tap], axis=(0, 1)) for tap in range(CONV)], axis=1)
-    later = passed_along(d_conv[:, :rim].astype(bf), "seq", -1).astype(f32)
-    d_ext = jnp.concatenate([d_conv, later], axis=1)
-    d_conv_in = jnp.zeros_like(d_conv)
-    for tap in range(CONV):
-        offset = rim - tap
-        match_back = (doc_ids[:, rim + offset : rim + offset + length] == own_ids).astype(f32)[:, :, None]
-        d_conv_in = d_conv_in + conv_taps[tap] * d_ext[:, offset : offset + length] * match_back
-    d_conv_in = d_conv_in.astype(bf).reshape(tokens, chans)
+    first = (d_act.reshape(seqs, length, chans)[:, :rim] * slope.reshape(seqs, length, chans)[:, :rim].astype(f32))
+    later = passed_along(first.astype(bf), "seq", -1).astype(f32)
+    later = jnp.pad(later, ((0, 0), (0, 8 - rim), (0, 0))).reshape(seqs * 8, chans)
+    d_conv_in, sums = conv_bwd(d_act, slope, later, conv_in, masks, taps, seqs)
+    sums = sums.reshape(seqs, 8, chans).sum(0)
+    g_conv, g_conv_bias = sums[:CONV].T, sums[CONV]
     g_in_conv = contract_rows(unit, d_conv_in).astype(bf)
     d_unit = (contract_cols(d_conv_in, in_conv) + contract_cols(d_gate, in_gate)).astype(bf)
     def in_rows(block):

time: 815 us -> 796 us (0.977)
  other arithmetic: 125 us -> 71.8 us
  Pallas kernels: 415 us -> 449 us
    convert_element_type x5 -> x2, other arithmetic: 37.1 us -> 2.56 us  [the longest x1 1.62 us: local(): link_sum(jnp.concatenate([d_low, d_write, d_read], axis=0), sizes, 5)]
    pallas_call x0 -> x2, Pallas kernels: none -> 31.2 us  [the longest x1 18.9 us: conv_bwd(): pl.pallas_call(conv_bwd_body, grid=(seqs, chans // width), in_specs=[bloc...]
    reduce_sum x1, other arithmetic: 21.4 us -> 0.01 us  [local(): sums = sums.reshape(seqs, 8, chans).sum(0)]
    reduce_scatter x1, waiting for transfers between devices: 14.7 us -> 0.01 us  [local(): g_out = lax.psum_scatter(g_out, 'seq', scatter_dimension=0, tiled=True)]
  transfers between devices with their start and end apart: 9 -> 9, of which waited for: 2 -> 1; matrix products, arithmetic and copies ran while one was open for 29% -> 24% of each run, Pallas kernels for 33% -> 38%
where the time goes in v6:
time: 796 us; the launch traced here: 786 us
  Pallas kernels  449 us (56%)
  matrix products  173 us (22%)
  other arithmetic  71.8 us (9%)
  local copies, waits for them, and re-layouts  46.8 us (6%)
  starting transfers between devices  16.8 us (2%)
  between operations  15.4 us (2%)
  waiting for transfers between devices  12.1 us (2%)
    pallas_call x1, Pallas kernels, bwd_full(): pl.pallas_call(bwd_full_body, grid=(strips, seqs, blocks), in_specs=[pl.B...  95.4 us
    pallas_call x1, Pallas kernels, link_reduce(): pl.pallas_call(kernel, in_specs=[pl.BlockSpec(memory_space=pl.ANY)] * cou...  90 us
    pallas_call x1, Pallas kernels, link_open(): pl.pallas_call(kernel, in_specs=[pl.BlockSpec(memory_space=pl.ANY)] * (co...  63.5 us
    pallas_call x2, Pallas kernels, scan_end(): pl.pallas_call(body, grid=(seqs, chans // width), in_specs=[pl.BlockSpec(...  62.7 us
    dot_general x3, matrix products, contract_cols(): lax.dot_general(left_mat, right_mat, NT, preferred_element_type=jnp.float32)  44.8 us
    pallas_call x1, Pallas kernels, fwd_full(): pl.pallas_call(fwd_full_body, grid=(chans // width, seqs, blocks), in_spe...  41.9 us
    dot_general x3, matrix products, contract_rows(): lax.dot_general(left_mat, right_mat, (((0,), (0,)), ((), ())), preferred_...  41.4 us
    pallas_call x2, Pallas kernels, link_sum(): pl.pallas_call(kernel, in_specs=[pl.BlockSpec(memory_space=pltpu.VMEM)],...  32.6 us
  transfers between devices with their start and end apart: 9, of which 1 were waited for; matrix products, arithmetic and copies ran while one was open for 24% of the time, Pallas kernels for 38%

profile of v6, /device:TPU:19, one launch (start us, length us, event | category | flops | bytes accessed | tf_op | source)
XLA Modules:
  0.0 785.5 jit_solution(9875520959652826133)
XLA Ops:
  25.0 63.5 %link_open.1 = (bf16[2048,1024]{1,0:T(8,128)(2,1)}, bf16[256,1024]{1,0:T(8,128)(2,1)}, bf16[256,1024]{1,0:T(8,128)(2,1)}, s32[32,128]{1,0:T(8,128)}, bf16[2048,2...) custom-call(bf16[256,1024]{1,0:T(8,128)(2,1)} %get-tuple-element.265.conv_ref, bf16[256,1024]{1,0:T(8,128)(2,1)} %get-tuple-element.264.gate_ref, ...), custom_call_target="tpu_custom_call" | custom-call | flops 80000000000 | tf_op jit(solution)/shard_map/link_open/pallas_call | solution.py:832
  89.4 14.5 %fusion.65 = (bf16[2048,1024]{1,0:T(8,128)(2,1)S(1)}, f32[2048,1024]{1,0:T(8,128)}) fusion(bf16[2048,2048]{1,0:T(8,128)(2,1)} %get-tuple-element.49, bf16[2048,1024]{1,0:T(8,128)(2,1)} %get-tuple-element.50), kind=kOutput, calls=%fused_computation.216 | convolution fusion | flops 8592031744 | bytes 25165824 | tf_op jit(solution)/shard_map/dot_general | solution.py:1064
  114.0 12.3 %conv_fwd.1 = (bf16[2048,1024]{1,0:T(8,128)(2,1)}, bf16[2048,1024]{1,0:T(8,128)(2,1)}) custom-call(f32[2048,1024]{1,0:T(8,128)} %get-tuple-element.262.x_ref, f32[32,1024]{1,0:T(8,128)} %bitcast_convert_fusion.1.early_ref, f32[2048,8]{1,0:T(8,128)} %bitcast.270, f32[8,1024]{1,0:T(8,128)} %fusion.47.taps_ref), custom_call_target="tpu_custom_call" | custom-call | flops 8388608000 | bytes 16777216 | tf_op jit(solution)/shard_map/conv_fwd/pallas_call | solution.py:912
  126.3 4.6 convolution_convert_fusion.4.own_ref
  130.8 16.2 %link_sum.2 = f32[160,2048]{1,0:T(8,128)} custom-call(bf16[160,2048]{1,0:T(8,128)(2,1)} %convolution_convert_fusion.4.own_ref), custom_call_target="tpu_custom_call" | custom-call | flops 20000000000 | tf_op jit(solution)/shard_map/link_sum/pallas_call | solution.py:750
  151.6 9.4 %bitcast_reduce_fusion = (f32[4,1024]{1,0:T(4,128)S(1)}, f32[2048,1024]{1,0:T(8,128)}, f32[2048,1024]{1,0:T(8,128)S(1)}) fusion(f32[1024]{0:T(1024)S(1)} %get-tuple-element.201, pred[2048]{0:T(1024)(128)(4,1)S(1)} %bitcast.286, bf16[1024,384]{1,0:T(8,128)(2,1)S(1)} %copy-done.6, f32[160,2048]{1,0:T(8,128)} %link_sum.2), kind=kOutput, calls=%fused_computation.10 | convolution fusion | flops 555741184 | bytes 17586176 | tf_op jit(solution)/shard_map/dot_general | solution.py:1076
  161.1 7.2 convert_multiply_fusion.3.dtx_ref
  168.3 31.4 %fwd_end.1 = f32[64,1024]{1,0:T(8,128)} custom-call(f32[2048,1024]{1,0:T(8,128)} %get-tuple-element.210.dte_ref, f32[2048,1024]{1,0:T(8,128)} %convert_multiply_fusion.3.dtx_ref, f32[2048,16]{1,0:T(8,128)} %bitcast.274, f32[16,1024]{1,0:T(8,128)} %multiply_bitcast_fusion.rate_ref), custom_call_target="tpu_custom_call" | custom-call | flops 33554432000 | bytes 16777216 | tf_op jit(solution)/shard_map/fwd_end/pallas_call | solution.py:82
  201.4 16.1 %link_gather.2 = bf16[640,1024]{1,0:T(8,128)(2,1)} custom-call(bf16[80,1024]{1,0:T(8,128)(2,1)} %pad.47.refs_0_), custom_call_target="tpu_custom_call" | custom-call | flops 20000000000 | tf_op jit(solution)/shard_map/link_gather/pallas_call | solution.py:476
  227.1 41.9 %fwd_full.1 = (f32[2048,1024]{1,0:T(8,128)}, bf16[32896,1024]{1,0:T(8,128)(2,1)}) custom-call(f32[2048,1024]{1,0:T(8,128)} %get-tuple-element.210.dte_ref, f32[2048,1024]{1,0:T(8,128)} %convert_multiply_fusion.3.dtx_ref, f32[2048,16]{1,0:T(8,128)} %bitcast.275, bf16[2048,256]{1,0:T(8,128)(2,1)} %copy.352.read_ref, f32[16,1024]{1,0:T(8,128)} %multiply_bitcast_fusion.rate_ref, ...), custom_call_target="tpu_custom_call" | custom-call | flops 46976204800 | bytes 67108864 | tf_op jit(solution)/shard_map/fwd_full/pallas_call | solution.py:147
  269.1 14.6 %fusion.66 = f32[2048,1024]{1,0:T(8,128)} fusion(bf16[2048,2048]{1,0:T(8,128)(2,1)} %all-gather.4.cloned.1.call-done, bf16[1024,2048]{1,0:T(8,128)(2,1)} %all-gather.6.cloned.1.call-done), kind=kOutput, calls=%fused_computation.217 | convolution fusion | flops 8589934592 | bytes 20971520 | tf_op jit(solution)/shard_map/dot_general | solution.py:978
  283.7 11.3 %all-gather.8.cloned.1.call-done = bf16[2048,1024]{1,0:T(8,128)(2,1)} async-done(((bf16[256,1024]{1,0:T(8,128)(2,1)}), bf16[2048,1024]{1,0:T(8,128)(2,1)}) %all-gather.8.cloned.1.call-update) | async-done | bytes 4194320 | tf_op jit(solution)/shard_map/all_gather | solution.py:1041
  294.9 25.1 %multiply_convert_fusion = (bf16[2048,1024]{1,0:T(8,128)(2,1)}, bf16[2048,1024]{1,0:T(8,128)(2,1)}, f32[2048,1024]{1,0:T(8,128)}) fusion(f32[2048,1024]{1,0:T(8,128)} %fusion.66, f32[2048,1024]{1,0:T(8,128)} %get-tuple-element.56, bf16[2048,1024]{1,0:T(8,128)(2,1)} %get-tuple-element.52, f32[1024]{0:T(1024)S(1)} %copy-done.27, f32[2048]{0:T(1024)S(1)} %bitcast.285, ...), kind=kOutput, calls=%fused_computation.12 | convolution fusion | flops 8629780480 | bytes 50343936 | tf_op jit(solution)/shard_map/dot_general | solution.py:1065
  320.0 14.2 %convolution_convert_fusion.3 = bf16[2048,1024]{1,0:T(8,128)(2,1)} fusion(bf16[2048,2048]{1,0:T(8,128)(2,1)} %get-tuple-element.49, bf16[2048,1024]{1,0:T(8,128)(2,1)} %get-tuple-element.211), kind=kOutput, calls=%fused_computation.34 | convolution fusion | flops 8592031744 | bytes 16777216 | tf_op jit(solution)/shard_map/dot_general | solution.py:974
  334.2 14.1 %convolution_convert_fusion.1 = bf16[1024,2048]{1,0:T(8,128)(2,1)} fusion(bf16[2048,1024]{1,0:T(8,128)(2,1)} %get-tuple-element.212, bf16[2048,2048]{1,0:T(8,128)(2,1)} %all-gather.4.cloned.1.call-done), kind=kOutput, calls=%fused_computation.32 | convolution fusion | flops 8592031744 | bytes 16777216 | tf_op jit(solution)/shard_map/dot_general | solution.py:974
  348.2 14.1 %convolution_convert_fusion = bf16[2048,2048]{1,0:T(8,128)(2,1)} fusion(bf16[2048,1024]{1,0:T(8,128)(2,1)} %get-tuple-element.212, bf16[1024,2048]{1,0:T(8,128)(2,1)} %all-gather.6.cloned.1.call-done), kind=kOutput, calls=%fused_computation.17 | convolution fusion | flops 8594128896 | bytes 16777216 | tf_op jit(solution)/shard_map/dot_general | solution.py:1090
  366.6 31.3 %bwd_end.1 = f32[64,1024]{1,0:T(8,128)} custom-call(f32[2048,1024]{1,0:T(8,128)} %get-tuple-element.210.dte_ref, f32[2048,1024]{1,0:T(8,128)} %get-tuple-element.57.grad_ref, f32[2048,16]{1,0:T(8,128)} %bitcast.272, f32[16,1024]{1,0:T(8,128)} %multiply_bitcast_fusion.rate_ref), custom_call_target="tpu_custom_call" | custom-call | flops 33554432000 | bytes 16777216 | tf_op jit(solution)/shard_map/bwd_end/pallas_call | solution.py:82
  399.6 16.0 %link_gather.3 = bf16[640,1024]{1,0:T(8,128)(2,1)} custom-call(bf16[80,1024]{1,0:T(8,128)(2,1)} %pad.48.refs_0_), custom_call_target="tpu_custom_call" | custom-call | flops 20000000000 | tf_op jit(solution)/shard_map/link_gather/pallas_call | solution.py:476
  418.8 95.4 %bwd_full.1 = (f32[2048,1024]{1,0:T(8,128)}, f32[2048,1024]{1,0:T(8,128)}, f32[16,1024]{1,0:T(8,128)}, f32[256,256]{1,0:T(8,128)}, f32[256,256]{1,0:T(8,128)}) custom-call(f32[2048,1024]{1,0:T(8,128)} %get-tuple-element.210.dte_ref, f32[2048,1024]{1,0:T(8,128)} %convert_multiply_fusion.3.dtx_ref, f32[2048,1024]{1,0:T(8,128)} %get-tuple-element.57.grad_ref, ...), custom_call_target="tpu_custom_call" | custom-call | flops 107374182400 | bytes 67108864 | tf_op jit(solution)/shard_map/bwd_full/pallas_call | solution.py:249
  518.8 18.3 %fusion.60 = (bf16[1024]{0:T(1024)(128)(2,1)S(1)}, bf16[2048,1024]{1,0:T(8,128)(2,1)}, bf16[1024]{0:T(1024)(128)(2,1)S(1)}) fusion(f32[2048,1024]{1,0:T(8,128)} %get-tuple-element.59, bf16[2048,1024]{1,0:T(8,128)(2,1)} %get-tuple-element.52, f32[2048,1024]{1,0:T(8,128)} %get-tuple-element.60, f32[2048,1024]{1,0:T(8,128)} %copy-done, ...), kind=kLoop, calls=%fused_computation.212 | loop fusion | flops 48232448 | bytes 41951232 | tf_op jit(solution)/shard_map/reduce_sum | solution.py:1109
  541.1 3.9 convolution_convert_fusion.5
  545.9 16.4 %link_sum.3 = f32[160,2048]{1,0:T(8,128)} custom-call(bf16[160,2048]{1,0:T(8,128)(2,1)} %pad_maximum_fusion.1.own_ref), custom_call_target="tpu_custom_call" | custom-call | flops 20000000000 | tf_op jit(solution)/shard_map/link_sum/pallas_call | solution.py:750
  566.0 12.5 %add_add_fusion.grad_ref = f32[2048,1024]{1,0:T(8,128)S(1)} fusion(f32[2048,1024]{1,0:T(8,128)} %get-tuple-element.57.grad_ref, f32[2048,1024]{1,0:T(8,128)} %get-tuple-element.59, bf16[160,2048]{1,0:T(8,128)(2,1)S(1)} %convert_element_type.268, f32[1024]{0:T(1024)S(1)} %copy-done.28, bf16[1024,384]{1,0:T(8,128)(2,1)S(1)} %copy-done.7, ...), kind=kOutput, calls=%fused_computation.11 | convolution fusion | flops 694157312 | bytes 34742272 | tf_op jit(solution)/shard_map/dot_general | solution.py:1116
  579.4 9.2 %collective-permute-start.1 = (bf16[4,3,1024]{2,1,0:T(4,128)(2,1)S(1)}, bf16[4,3,1024]{2,1,0:T(4,128)(2,1)S(1)}, u32[]{:S(2)}, u32[]{:S(2)}) collective-permute-start(bf16[4,3,1024]{2,1,0:T(4,128)(2,1)S(1)} %fusion.43), channel_id=1, source_target_pairs={{4,0},{8,4},{12,8},{16,12},{20,16},{24,20},{28,24},{5,1},{9,5},{13... | collective-permute-start | bytes 73736 | tf_op jit(solution)/shard_map/ppermute | solution.py:954
  589.5 5.3 all-to-all-start
  596.5 18.9 %conv_bwd.1 = (bf16[2048,1024]{1,0:T(8,128)(2,1)}, f32[32,1024]{1,0:T(8,128)}) custom-call(f32[2048,1024]{1,0:T(8,128)} %copy-done.8, bf16[2048,1024]{1,0:T(8,128)(2,1)} %get-tuple-element.66.slope_ref, f32[32,1024]{1,0:T(8,128)} %bitcast_convert_fusion.late_ref, f32[2048,1024]{1,0:T(8,128)} %get-tuple-element.262.x_ref, f32[2048,8]{1,0:T(8,128)} %bitcast.271, ...), custom_call_target="tpu_custom_call" | custom-call | flops 10485760000 | bytes 25165824 | tf_op jit(solution)/shard_map/conv_bwd/pallas_call | solution.py:934
  615.4 14.2 %fusion.67 = f32[2048,2048]{1,0:T(8,128)} fusion(bf16[2048,1024]{1,0:T(8,128)(2,1)} %get-tuple-element.67, bf16[2048,1024]{1,0:T(8,128)(2,1)S(1)} %copy-done.35), kind=kOutput, calls=%fused_computation.218 | convolution fusion | flops 8589934592 | bytes 25165824 | tf_op jit(solution)/shard_map/dot_general | solution.py:978
  629.6 16.0 %add_convert_fusion.refs_2_ = bf16[2048,2048]{1,0:T(8,128)(2,1)} fusion(f32[2048,2048]{1,0:T(8,128)} %fusion.67, bf16[2048,1024]{1,0:T(8,128)(2,1)} %get-tuple-element.211, bf16[2048,1024]{1,0:T(8,128)(2,1)S(1)} %copy-done.33), kind=kOutput, calls=%fused_computation.1 | convolution fusion | flops 8598323200 | bytes 33554432 | tf_op jit(solution)/shard_map/dot_general | solution.py:978
  645.6 13.2 %convolution_convert_fusion.2.refs_0_ = bf16[2048,1024]{1,0:T(8,128)(2,1)} fusion(bf16[2048,2048]{1,0:T(8,128)(2,1)} %get-tuple-element.49, bf16[2048,1024]{1,0:T(8,128)(2,1)S(1)} %copy-done.34), kind=kOutput, calls=%fused_computation.33 | convolution fusion | flops 8592031744 | bytes 16777216 | tf_op jit(solution)/shard_map/dot_general | solution.py:974
  660.6 3.6 concatenate.34
  667.1 3.7 fusion.13
  670.8 90.0 %link_reduce.1 = (bf16[64,4096]{1,0:T(8,128)(2,1)}, bf16[128,384]{1,0:T(8,128)(2,1)}, bf16[512,2048]{1,0:T(8,128)(2,1)}) custom-call(bf16[2048,1024]{1,0:T(8,128)(2,1)} %convolution_convert_fusion.2.refs_0_, bf16[1024,384]{1,0:T(8,128)(2,1)} %pad.50.refs_1_, bf16[2048,2048]{1,0:T(8,128)(2,1)} %add_convert_fusion.refs_2_), custom_call_target="tpu_custom_call" | custom-call | flops 80000000000 | tf_op jit(solution)/shard_map/link_reduce/pallas_call | solution.py:695
  (233 shorter events, 92.0 us)
Async XLA Ops:
  7.2 261.8 %all-gather.6.cloned.1.call-start = ((), (), s32[]{:S(2)}) async-start(), calls=%async_computation.5 | async-start | bytes 4718592 | tf_op jit(solution)/shard_map/all_gather | solution.py:1042
  7.9 12.6 %copy-start.30 = (f32[64]{0:T(128)}, f32[64]{0:T(128)S(1)}, u32[]{:S(2)}) copy-start(f32[64]{0:T(128)S(1)} %convert_element_type.223) | copy-start | bytes 772
  10.0 10.7 %copy-start.25 = (f32[512]{0:T(512)}, f32[512]{0:T(512)S(1)}, u32[]{:S(2)}) copy-start(f32[512]{0:T(512)S(1)} %add_rsqrt_fusion) | copy-start | bytes 6148
  88.5 180.5 %all-gather.4.cloned.1.call-start = ((), (), s32[]{:S(2)}) async-start(), calls=%async_computation.4 | async-start | bytes 10485760 | tf_op jit(solution)/shard_map/all_gather | solution.py:1043
  89.3 205.6 %all-gather.8.cloned.1.call-start = ((), (), s32[]{:S(2)}) async-start(), calls=%async_computation.6 | async-start | bytes 4718592 | tf_op jit(solution)/shard_map/all_gather | solution.py:1041
  89.3 17.9 %copy-start.6 = (bf16[1024,384]{1,0:T(8,128)(2,1)S(1)}, bf16[1024,384]{1,0:T(8,128)(2,1)}, u32[]{:S(2)}) copy-start(bf16[1024,384]{1,0:T(8,128)(2,1)} %get-tuple-element.46) | copy-start | bytes 2359300
  103.9 9.4 %collective-permute-start = (bf16[4,3,1024]{2,1,0:T(4,128)(2,1)S(1)}, bf16[4,3,1024]{2,1,0:T(4,128)(2,1)S(1)}, u32[]{:S(2)}, u32[]{:S(2)}) collective-permute-start(bf16[4,3,1024]{2,1,0:T(4,128)(2,1)S(1)} %slice.399), channel_id=1, source_target_pairs={{0,4},{4,8},{8,12},{12,16},{16,20},{20,24},{24,28},{1,5},{5,9},{9,... | collective-permute-start | bytes 73736 | tf_op jit(solution)/shard_map/ppermute | solution.py:954
  106.1 460.0 %reduce-scatter.4.cloned.1.call-start = ((), (), s32[]{:S(2)}) async-start(), calls=%async_computation.7 | async-start | bytes 4718592 | tf_op jit(solution)/shard_map/reduce_scatter | solution.py:1098
  108.4 52.7 %copy-start.23 = (f32[1024]{0:T(1024)}, f32[1024]{0:T(1024)S(1)}, u32[]{:S(2)}) copy-start(f32[1024]{0:T(1024)S(1)} %get-tuple-element.201) | copy-start | bytes 12292
  151.6 9.4 %copy-start.1 = (bf16[2048,1024]{1,0:T(8,128)(2,1)S(1)}, bf16[2048,1024]{1,0:T(8,128)(2,1)}, u32[]{:S(2)}) copy-start(bf16[2048,1024]{1,0:T(8,128)(2,1)} %get-tuple-element.52) | copy-start | bytes 12582916
  161.0 39.6 %copy-start.19 = (bf16[4,1024]{1,0:T(4,128)(2,1)}, bf16[4,1024]{1,0:T(4,128)(2,1)S(1)}, u32[]{:S(2)}) copy-start(bf16[4,1024]{1,0:T(4,128)(2,1)S(1)} %get-tuple-element.207) | copy-start | bytes 24580
  161.0 39.6 %copy-start.21 = (bf16[4,1024]{1,0:T(4,128)(2,1)}, bf16[4,1024]{1,0:T(4,128)(2,1)S(1)}, u32[]{:S(2)}) copy-start(bf16[4,1024]{1,0:T(4,128)(2,1)S(1)} %get-tuple-element.208) | copy-start | bytes 24580
  201.4 20.9 %copy-start.17 = (pred[2048,16]{0,1:T(8,128)(4,1)S(1)}, pred[2048,16]{0,1:T(8,128)(4,1)}, u32[]{:S(2)}) copy-start(pred[2048,16]{0,1:T(8,128)(4,1)} %iota_compare_fusion) | copy-start | bytes 98308
  269.0 25.9 %copy-start.27 = (f32[1024]{0:T(1024)S(1)}, f32[1024]{0:T(1024)}, u32[]{:S(2)}) copy-start(f32[1024]{0:T(1024)} %get-tuple-element.200) | copy-start | bytes 12292
  269.0 25.9 %copy-start.29 = (f32[1,4,4,128]{3,1,2,0:T(4,128)S(1)}, f32[1,4,4,128]{3,1,2,0:T(4,128)}, u32[]{:S(2)}) copy-start(f32[1,4,4,128]{3,1,2,0:T(4,128)} %copy.376) | copy-start | bytes 24580
  362.4 203.6 %reduce-scatter.6.cloned.1.call-start = ((), (), s32[]{:S(2)}) async-start(), calls=%async_computation.8 | async-start | bytes 4718592 | tf_op jit(solution)/shard_map/reduce_scatter | solution.py:1099
  366.5 32.3 %copy-start.20 = (bf16[4,1024]{1,0:T(4,128)(2,1)S(1)}, bf16[4,1024]{1,0:T(4,128)(2,1)}, u32[]{:S(2)}) copy-start(bf16[4,1024]{1,0:T(4,128)(2,1)} %copy-done.19) | copy-start | bytes 24580
  366.6 32.3 %copy-start.22 = (bf16[4,1024]{1,0:T(4,128)(2,1)S(1)}, bf16[4,1024]{1,0:T(4,128)(2,1)}, u32[]{:S(2)}) copy-start(bf16[4,1024]{1,0:T(4,128)(2,1)} %copy-done.21) | copy-start | bytes 24580
  417.4 249.7 %reduce-scatter.8.cloned.1.call-start = ((), (), s32[]{:S(2)}) async-start(), calls=%async_computation.9 | async-start | bytes 10485760 | tf_op jit(solution)/shard_map/reduce_scatter | solution.py:1100
  518.8 22.3 %copy-start.7 = (bf16[1024,384]{1,0:T(8,128)(2,1)S(1)}, bf16[1024,384]{1,0:T(8,128)(2,1)}, u32[]{:S(2)}) copy-start(bf16[1024,384]{1,0:T(8,128)(2,1)} %get-tuple-element.46) | copy-start | bytes 2359300
  545.9 18.1 %copy-start.5 = (bf16[2048,1024]{1,0:T(8,128)(2,1)S(1)}, bf16[2048,1024]{1,0:T(8,128)(2,1)}, u32[]{:S(2)}) copy-start(bf16[2048,1024]{1,0:T(8,128)(2,1)} %get-tuple-element.206) | copy-start | bytes 12582916
  545.9 18.1 %copy-start.13 = (f32[160,2048]{1,0:T(8,128)S(1)}, f32[160,2048]{1,0:T(8,128)}, u32[]{:S(2)}) copy-start(f32[160,2048]{1,0:T(8,128)} %link_sum.2) | copy-start | bytes 3932164
  566.0 22.6 %copy-start.2 = (bf16[2048,1024]{1,0:T(8,128)(2,1)S(1)}, bf16[2048,1024]{1,0:T(8,128)(2,1)}, u32[]{:S(2)}) copy-start(bf16[2048,1024]{1,0:T(8,128)(2,1)} %get-tuple-element.52) | copy-start | bytes 12582916
  578.5 11.0 %copy-start.8 = (f32[2048,1024]{1,0:T(8,128)}, f32[2048,1024]{1,0:T(8,128)S(1)}, u32[]{:S(2)}) copy-start(f32[2048,1024]{1,0:T(8,128)S(1)} %add_add_fusion.grad_ref) | copy-start | bytes 25165828
  579.4 16.4 %collective-permute-start.1 = (bf16[4,3,1024]{2,1,0:T(4,128)(2,1)S(1)}, bf16[4,3,1024]{2,1,0:T(4,128)(2,1)S(1)}, u32[]{:S(2)}, u32[]{:S(2)}) collective-permute-start(bf16[4,3,1024]{2,1,0:T(4,128)(2,1)S(1)} %fusion.43), channel_id=1, source_target_pairs={{4,0},{8,4},{12,8},{16,12},{20,16},{24,20},{28,24},{5,1},{9,5},{13... | collective-permute-start | bytes 73736 | tf_op jit(solution)/shard_map/ppermute | solution.py:954
  589.5 75.6 %all-to-all-start = ((bf16[4,64,1024]{2,1,0:T(8,128)(2,1)}), bf16[4,64,1024]{2,1,0:T(8,128)(2,1)S(1)}, u32[]{:S(2)}, u32[]{:S(2)}) async-start(bf16[4,64,1024]{2,1,0:T(8,128)(2,1)} %bitcast.51), calls=%async_computation.2 | async-start | bytes 1048576 | tf_op jit(solution)/shard_map/all_to_all | solution.py:1127
  596.5 18.9 %copy-start.35 = (bf16[2048,1024]{1,0:T(8,128)(2,1)S(1)}, bf16[2048,1024]{1,0:T(8,128)(2,1)}, u32[]{:S(2)}) copy-start(bf16[2048,1024]{1,0:T(8,128)(2,1)} %get-tuple-element.50) | copy-start | bytes 12582916
  615.4 14.2 %copy-start.33 = (bf16[2048,1024]{1,0:T(8,128)(2,1)S(1)}, bf16[2048,1024]{1,0:T(8,128)(2,1)}, u32[]{:S(2)}) copy-start(bf16[2048,1024]{1,0:T(8,128)(2,1)} %all-gather.8.cloned.1.call-done) | copy-start | bytes 12582916
  629.6 16.0 %copy-start.34 = (bf16[2048,1024]{1,0:T(8,128)(2,1)S(1)}, bf16[2048,1024]{1,0:T(8,128)(2,1)}, u32[]{:S(2)}) copy-start(bf16[2048,1024]{1,0:T(8,128)(2,1)} %get-tuple-element.67) | copy-start | bytes 12582916
  645.6 13.2 %copy-start.18 = (f32[32,1024]{1,0:T(8,128)S(1)}, f32[32,1024]{1,0:T(8,128)}, u32[]{:S(2)}) copy-start(f32[32,1024]{1,0:T(8,128)} %get-tuple-element.73) | copy-start | bytes 393220
  670.8 93.9 %copy-start.26 = (f32[512]{0:T(512)S(1)}, f32[512]{0:T(512)}, u32[]{:S(2)}) copy-start(f32[512]{0:T(512)} %copy-done.25) | copy-start | bytes 6148
  767.2 7.5 copy-start.11
  (13 other events, 60.0 us)
Sparse Core Ops, SparseCore 0:
  88.7 72.4 all-gather.5
  162.8 57.2 all-gather.3
  222.2 72.6 all-gather.7
  362.5 93.1 reduce-scatter.3
  459.6 87.8 reduce-scatter.5
  550.0 76.3 reduce-scatter.7

commit v7 on v6

--- a/solution.py
+++ b/solution.py
@@ -1061,9 +1061,12 @@
     near = [doc_ids[:, tap : tap + length] == own_ids for tap in range(2 * rim + 1) if tap != rim]
     masks = jnp.pad(jnp.stack(near, axis=-1).astype(f32), ((0, 0), (0, 0), (0, 8 - 2 * rim))).reshape(tokens, 8)
 
-    conv_in = jnp.dot(unit, in_conv, preferred_element_type=f32)
+    last_rows = unit.reshape(seqs, length, feats)[:, length - 16 :].reshape(seqs * 16, feats)
+    last_rows = jnp.dot(last_rows, in_conv, preferred_element_type=f32).reshape(seqs, 16, chans)[:, 16 - rim :]
+    last_rows, unit_main = lax.optimization_barrier((last_rows.astype(bf), unit))
+    earlier = passed_along(last_rows, "seq", 1).astype(f32)
+    conv_in = jnp.dot(unit_main, in_conv, preferred_element_type=f32)
     gate_in = jnp.dot(unit, in_gate, preferred_element_type=f32)
-    earlier = passed_along(conv_in.reshape(seqs, length, chans)[:, length - rim :].astype(bf), "seq", 1).astype(f32)
     earlier = jnp.pad(earlier, ((0, 0), (8 - rim, 0), (0, 0))).reshape(seqs * 8, chans)
     taps = jnp.pad(jnp.concatenate([conv_taps, conv_shift[None]]), ((0, 7 - CONV), (0, 0)))
     activated, slope = conv_fwd(conv_in, earlier, masks, taps, seqs)
@@ -1117,12 +1120,13 @@
         d_proj, xproj_full, (((0,), (1,)), ((), ())), preferred_element_type=f32)
     first = (d_act.reshape(seqs, length, chans)[:, :rim] * slope.reshape(seqs, length, chans)[:, :rim].astype(f32))
     later = passed_along(first.astype(bf), "seq", -1).astype(f32)
+    later, gate_part = lax.optimization_barrier((later, contract_cols(d_gate, in_gate)))
     later = jnp.pad(later, ((0, 0), (0, 8 - rim), (0, 0))).reshape(seqs * 8, chans)
     d_conv_in, sums = conv_bwd(d_act, slope, later, conv_in, masks, taps, seqs)
     sums = sums.reshape(seqs, 8, chans).sum(0)
     g_conv, g_conv_bias = sums[:CONV].T, sums[CONV]
     g_in_conv = contract_rows(unit, d_conv_in).astype(bf)
-    d_unit = (contract_cols(d_conv_in, in_conv) + contract_cols(d_gate, in_gate)).astype(bf)
+    d_unit = (contract_cols(d_conv_in, in_conv) + gate_part).astype(bf)
     def in_rows(block):
         shared = lax.all_to_all(block, "stream", 0, 0, tiled=True).reshape(seqs, own_feats, parts, own)
         return shared.transpose(1, 2, 0, 3).reshape(own_feats, parts * seqs * own)

time: 796 us -> 805 us (1.011)
  other arithmetic: 71.8 us -> 81 us
    convert_element_type x0 -> x1, other arithmetic: none -> 9.68 us  [local(): d_unit = (contract_cols(d_conv_in, in_conv) + gate_part).astype(bf)]
    dot_general x1 -> x2, matrix products: 14.5 us -> 17.6 us  [the longest x1 14.5 us: local(): conv_in = jnp.dot(unit_main, in_conv, preferred_element_type=f32)]
  transfers between devices with their start and end apart: 9 -> 9, of which waited for: 1 -> 1; matrix products, arithmetic and copies ran while one was open for 24% -> 25% of each run, Pallas kernels for 38% -> 37%
where the time goes in v7:
time: 805 us; the launch traced here: 794 us
  Pallas kernels  450 us (56%)
  matrix products  175 us (22%)
  other arithmetic  81 us (10%)
  local copies, waits for them, and re-layouts  47.7 us (6%)
  starting transfers between devices  17.6 us (2%)
  between operations  15.5 us (2%)
    pallas_call x1, Pallas kernels, bwd_full(): pl.pallas_call(bwd_full_body, grid=(strips, seqs, blocks), in_specs=[pl.B...  95.6 us
    pallas_call x1, Pallas kernels, link_reduce(): pl.pallas_call(kernel, in_specs=[pl.BlockSpec(memory_space=pl.ANY)] * cou...  89.5 us
    pallas_call x1, Pallas kernels, link_open(): pl.pallas_call(kernel, in_specs=[pl.BlockSpec(memory_space=pl.ANY)] * (co...  63.5 us
    pallas_call x2, Pallas kernels, scan_end(): pl.pallas_call(body, grid=(seqs, chans // width), in_specs=[pl.BlockSpec(...  62.6 us
    dot_general x3, matrix products, contract_cols(): lax.dot_general(left_mat, right_mat, NT, preferred_element_type=jnp.float32)  42.7 us
    dot_general x3, matrix products, contract_rows(): lax.dot_general(left_mat, right_mat, (((0,), (0,)), ((), ())), preferred_...  42.5 us
    pallas_call x1, Pallas kernels, fwd_full(): pl.pallas_call(fwd_full_body, grid=(chans // width, seqs, blocks), in_spe...  42 us
    pallas_call x2, Pallas kernels, link_gather(): pl.pallas_call(kernel, in_specs=[pl.BlockSpec(memory_space=pl.ANY)] * cou...  32.9 us
  transfers between devices with their start and end apart: 9, of which 1 were waited for; matrix products, arithmetic and copies ran while one was open for 25% of the time, Pallas kernels for 37%

profile of v7, /device:TPU:19, one launch (start us, length us, event | category | flops | bytes accessed | tf_op | source)
XLA Modules:
  0.0 794.5 jit_solution(7467289054203275118)
XLA Ops:
  25.0 63.5 %link_open.1 = (bf16[2048,1024]{1,0:T(8,128)(2,1)}, bf16[256,1024]{1,0:T(8,128)(2,1)}, bf16[256,1024]{1,0:T(8,128)(2,1)}, s32[32,128]{1,0:T(8,128)}, bf16[2048,2...) custom-call(bf16[256,1024]{1,0:T(8,128)(2,1)} %get-tuple-element.271.conv_ref, bf16[256,1024]{1,0:T(8,128)(2,1)} %get-tuple-element.270.gate_ref, ...), custom_call_target="tpu_custom_call" | custom-call | flops 80000000000 | tf_op jit(solution)/shard_map/link_open/pallas_call | solution.py:832
  99.3 14.5 %fusion.68.x_ref = f32[2048,1024]{1,0:T(8,128)} fusion(bf16[2048,2048]{1,0:T(8,128)(2,1)} %get-tuple-element.55, bf16[2048,1024]{1,0:T(8,128)(2,1)} %get-tuple-element.54), kind=kOutput, calls=%fused_computation.220 | convolution fusion | flops 8589934592 | bytes 20971520 | tf_op jit(solution)/shard_map/dot_general | solution.py:1068
  117.1 12.5 %conv_fwd.1 = (bf16[2048,1024]{1,0:T(8,128)(2,1)}, bf16[2048,1024]{1,0:T(8,128)(2,1)}) custom-call(f32[2048,1024]{1,0:T(8,128)} %fusion.68.x_ref, f32[32,1024]{1,0:T(8,128)} %bitcast_convert_fusion.early_ref, f32[2048,8]{1,0:T(8,128)} %bitcast.274, f32[8,1024]{1,0:T(8,128)} %fusion.50.taps_ref), custom_call_target="tpu_custom_call" | custom-call | flops 8388608000 | bytes 16777216 | tf_op jit(solution)/shard_map/conv_fwd/pallas_call | solution.py:912
  129.6 4.6 convolution_convert_fusion.4.own_ref
  134.2 15.9 %link_sum.2 = f32[160,2048]{1,0:T(8,128)} custom-call(bf16[160,2048]{1,0:T(8,128)(2,1)} %convolution_convert_fusion.4.own_ref), custom_call_target="tpu_custom_call" | custom-call | flops 20000000000 | tf_op jit(solution)/shard_map/link_sum/pallas_call | solution.py:750
  154.7 9.4 %bitcast_reduce_fusion = (f32[4,1024]{1,0:T(4,128)S(1)}, f32[2048,1024]{1,0:T(8,128)}, f32[2048,1024]{1,0:T(8,128)S(1)}) fusion(f32[1024]{0:T(1024)S(1)} %get-tuple-element.209, pred[2048]{0:T(1024)(128)(4,1)S(1)} %bitcast.291, bf16[1024,384]{1,0:T(8,128)(2,1)S(1)} %copy-done.6, f32[160,2048]{1,0:T(8,128)} %link_sum.2), kind=kOutput, calls=%fused_computation.10 | convolution fusion | flops 555741184 | bytes 17586176 | tf_op jit(solution)/shard_map/dot_general | solution.py:1079
  164.2 7.3 convert_multiply_fusion.3.dtx_ref
  171.5 31.3 %fwd_end.1 = f32[64,1024]{1,0:T(8,128)} custom-call(f32[2048,1024]{1,0:T(8,128)} %get-tuple-element.218.dte_ref, f32[2048,1024]{1,0:T(8,128)} %convert_multiply_fusion.3.dtx_ref, f32[2048,16]{1,0:T(8,128)} %bitcast.278, f32[16,1024]{1,0:T(8,128)} %multiply_bitcast_fusion.rate_ref), custom_call_target="tpu_custom_call" | custom-call | flops 33554432000 | bytes 16777216 | tf_op jit(solution)/shard_map/fwd_end/pallas_call | solution.py:82
  204.5 16.9 %link_gather.2 = bf16[640,1024]{1,0:T(8,128)(2,1)} custom-call(bf16[80,1024]{1,0:T(8,128)(2,1)} %pad.46.refs_0_), custom_call_target="tpu_custom_call" | custom-call | flops 20000000000 | tf_op jit(solution)/shard_map/link_gather/pallas_call | solution.py:476
  231.0 42.0 %fwd_full.1 = (f32[2048,1024]{1,0:T(8,128)}, bf16[32896,1024]{1,0:T(8,128)(2,1)}) custom-call(f32[2048,1024]{1,0:T(8,128)} %get-tuple-element.218.dte_ref, f32[2048,1024]{1,0:T(8,128)} %convert_multiply_fusion.3.dtx_ref, f32[2048,16]{1,0:T(8,128)} %bitcast.279, bf16[2048,256]{1,0:T(8,128)(2,1)} %copy.352.read_ref, f32[16,1024]{1,0:T(8,128)} %multiply_bitcast_fusion.rate_ref, ...), custom_call_target="tpu_custom_call" | custom-call | flops 46976204800 | bytes 67108864 | tf_op jit(solution)/shard_map/fwd_full/pallas_call | solution.py:147
  273.1 14.6 %fusion.69 = f32[2048,1024]{1,0:T(8,128)} fusion(bf16[2048,2048]{1,0:T(8,128)(2,1)} %all-gather.4.cloned.1.call-done, bf16[1024,2048]{1,0:T(8,128)(2,1)} %all-gather.6.cloned.1.call-done), kind=kOutput, calls=%fused_computation.221 | convolution fusion | flops 8589934592 | bytes 20971520 | tf_op jit(solution)/shard_map/dot_general | solution.py:978
  287.7 6.6 all-gather.8.cloned.1.call-done
  294.2 25.1 %multiply_convert_fusion = (bf16[2048,1024]{1,0:T(8,128)(2,1)}, bf16[2048,1024]{1,0:T(8,128)(2,1)}, f32[2048,1024]{1,0:T(8,128)}) fusion(f32[2048,1024]{1,0:T(8,128)} %fusion.69, f32[2048,1024]{1,0:T(8,128)} %get-tuple-element.62, bf16[2048,1024]{1,0:T(8,128)(2,1)} %get-tuple-element.58, f32[1024]{0:T(1024)S(1)} %copy-done.28, f32[2048]{0:T(1024)S(1)} %bitcast.290, ...), kind=kOutput, calls=%fused_computation.12 | convolution fusion | flops 8629780480 | bytes 50343936 | tf_op jit(solution)/shard_map/dot_general | solution.py:1069
  319.3 14.2 %convolution_convert_fusion.3 = bf16[2048,1024]{1,0:T(8,128)(2,1)} fusion(bf16[2048,2048]{1,0:T(8,128)(2,1)} %get-tuple-element.55, bf16[2048,1024]{1,0:T(8,128)(2,1)} %get-tuple-element.219), kind=kOutput, calls=%fused_computation.36 | convolution fusion | flops 8592031744 | bytes 16777216 | tf_op jit(solution)/shard_map/dot_general | solution.py:974
  333.5 14.1 %convolution_convert_fusion.1 = bf16[1024,2048]{1,0:T(8,128)(2,1)} fusion(bf16[2048,1024]{1,0:T(8,128)(2,1)} %get-tuple-element.220, bf16[2048,2048]{1,0:T(8,128)(2,1)} %all-gather.4.cloned.1.call-done), kind=kOutput, calls=%fused_computation.34 | convolution fusion | flops 8592031744 | bytes 16777216 | tf_op jit(solution)/shard_map/dot_general | solution.py:974
  347.6 14.2 %convolution_convert_fusion = bf16[2048,2048]{1,0:T(8,128)(2,1)} fusion(bf16[2048,1024]{1,0:T(8,128)(2,1)} %get-tuple-element.220, bf16[1024,2048]{1,0:T(8,128)(2,1)} %all-gather.6.cloned.1.call-done), kind=kOutput, calls=%fused_computation.17 | convolution fusion | flops 8594128896 | bytes 16777216 | tf_op jit(solution)/shard_map/dot_general | solution.py:1093
  365.9 31.3 %bwd_end.1 = f32[64,1024]{1,0:T(8,128)} custom-call(f32[2048,1024]{1,0:T(8,128)} %get-tuple-element.218.dte_ref, f32[2048,1024]{1,0:T(8,128)} %get-tuple-element.63.grad_ref, f32[2048,16]{1,0:T(8,128)} %bitcast.276, f32[16,1024]{1,0:T(8,128)} %multiply_bitcast_fusion.rate_ref), custom_call_target="tpu_custom_call" | custom-call | flops 33554432000 | bytes 16777216 | tf_op jit(solution)/shard_map/bwd_end/pallas_call | solution.py:82
  398.9 16.0 %link_gather.3 = bf16[640,1024]{1,0:T(8,128)(2,1)} custom-call(bf16[80,1024]{1,0:T(8,128)(2,1)} %pad.47.refs_0_), custom_call_target="tpu_custom_call" | custom-call | flops 20000000000 | tf_op jit(solution)/shard_map/link_gather/pallas_call | solution.py:476
  418.2 95.6 %bwd_full.1 = (f32[2048,1024]{1,0:T(8,128)}, f32[2048,1024]{1,0:T(8,128)}, f32[16,1024]{1,0:T(8,128)}, f32[256,256]{1,0:T(8,128)}, f32[256,256]{1,0:T(8,128)}) custom-call(f32[2048,1024]{1,0:T(8,128)} %get-tuple-element.218.dte_ref, f32[2048,1024]{1,0:T(8,128)} %convert_multiply_fusion.3.dtx_ref, f32[2048,1024]{1,0:T(8,128)} %get-tuple-element.63.grad_ref, ...), custom_call_target="tpu_custom_call" | custom-call | flops 107374182400 | bytes 67108864 | tf_op jit(solution)/shard_map/bwd_full/pallas_call | solution.py:249
  518.4 18.1 %fusion.63 = (bf16[1024]{0:T(1024)(128)(2,1)S(1)}, bf16[2048,1024]{1,0:T(8,128)(2,1)}, bf16[1024]{0:T(1024)(128)(2,1)S(1)}) fusion(f32[2048,1024]{1,0:T(8,128)} %get-tuple-element.65, bf16[2048,1024]{1,0:T(8,128)(2,1)} %get-tuple-element.58, f32[2048,1024]{1,0:T(8,128)} %get-tuple-element.66, f32[2048,1024]{1,0:T(8,128)} %copy-done, ...), kind=kLoop, calls=%fused_computation.216 | loop fusion | flops 48232448 | bytes 41951232 | tf_op jit(solution)/shard_map/reduce_sum | solution.py:1112
  540.5 3.9 convolution_convert_fusion.5
  545.3 16.9 %link_sum.3 = f32[160,2048]{1,0:T(8,128)} custom-call(bf16[160,2048]{1,0:T(8,128)(2,1)} %pad_maximum_fusion.1.own_ref), custom_call_target="tpu_custom_call" | custom-call | flops 20000000000 | tf_op jit(solution)/shard_map/link_sum/pallas_call | solution.py:750
  566.2 14.0 %fusion.70 = f32[2048,2048]{1,0:T(8,128)} fusion(bf16[2048,1024]{1,0:T(8,128)(2,1)} %get-tuple-element.219, bf16[2048,1024]{1,0:T(8,128)(2,1)S(1)} %copy-done.34), kind=kOutput, calls=%fused_computation.222 | convolution fusion | flops 8589934592 | bytes 25165824 | tf_op jit(solution)/shard_map/dot_general | solution.py:978
  580.2 12.1 %add_add_fusion.grad_ref = f32[2048,1024]{1,0:T(8,128)S(1)} fusion(f32[2048,1024]{1,0:T(8,128)} %get-tuple-element.63.grad_ref, f32[2048,1024]{1,0:T(8,128)} %get-tuple-element.65, bf16[160,2048]{1,0:T(8,128)(2,1)S(1)} %convert_element_type.270, f32[1024]{0:T(1024)S(1)} %copy-done.29, bf16[1024,384]{1,0:T(8,128)(2,1)S(1)} %copy-done.7, ...), kind=kOutput, calls=%fused_computation.11 | convolution fusion | flops 694157312 | bytes 34742272 | tf_op jit(solution)/shard_map/dot_general | solution.py:1119
  593.3 10.2 %collective-permute-start.1 = (bf16[4,3,1024]{2,1,0:T(4,128)(2,1)S(1)}, bf16[4,3,1024]{2,1,0:T(4,128)(2,1)S(1)}, u32[]{:S(2)}, u32[]{:S(2)}) collective-permute-start(bf16[4,3,1024]{2,1,0:T(4,128)(2,1)S(1)} %fusion.46), channel_id=1, source_target_pairs={{4,0},{8,4},{12,8},{16,12},{20,16},{24,20},{28,24},{5,1},{9,5},{13... | collective-permute-start | bytes 73736 | tf_op jit(solution)/shard_map/ppermute | solution.py:954
  604.4 5.0 all-to-all-start
  611.1 18.7 %conv_bwd.1 = (bf16[2048,1024]{1,0:T(8,128)(2,1)}, f32[32,1024]{1,0:T(8,128)}) custom-call(f32[2048,1024]{1,0:T(8,128)} %copy-done.8, bf16[2048,1024]{1,0:T(8,128)(2,1)} %get-tuple-element.72.slope_ref, f32[32,1024]{1,0:T(8,128)} %pad_bitcast_fusion.late_ref, f32[2048,1024]{1,0:T(8,128)} %fusion.68.x_ref, f32[2048,8]{1,0:T(8,128)} %bitcast.275, ...), custom_call_target="tpu_custom_call" | custom-call | flops 10485760000 | bytes 25165824 | tf_op jit(solution)/shard_map/conv_bwd/pallas_call | solution.py:934
  629.8 14.2 %convolution_convert_fusion.2.refs_0_ = bf16[2048,1024]{1,0:T(8,128)(2,1)} fusion(bf16[2048,2048]{1,0:T(8,128)(2,1)} %get-tuple-element.55, bf16[2048,1024]{1,0:T(8,128)(2,1)} %get-tuple-element.74), kind=kOutput, calls=%fused_computation.35 | convolution fusion | flops 8592031744 | bytes 16777216 | tf_op jit(solution)/shard_map/dot_general | solution.py:974
  644.0 14.1 %fusion.71 = f32[2048,2048]{1,0:T(8,128)} fusion(bf16[2048,1024]{1,0:T(8,128)(2,1)} %get-tuple-element.74, bf16[2048,1024]{1,0:T(8,128)(2,1)S(1)} %copy-done.11), kind=kOutput, calls=%fused_computation.223 | convolution fusion | flops 8589934592 | bytes 25165824 | tf_op jit(solution)/shard_map/dot_general | solution.py:978
  658.1 9.7 %add_convert_fusion.refs_2_ = bf16[2048,2048]{1,0:T(8,128)(2,1)} fusion(f32[2048,2048]{1,0:T(8,128)} %fusion.71, f32[2048,2048]{1,0:T(8,128)S(1)} %bitcast.261), kind=kLoop, calls=%fused_computation.1 | loop fusion | flops 8388608 | bytes 41943040 | tf_op jit(solution)/shard_map/convert_element_type | solution.py:1129
  669.6 3.8 concatenate.34
  680.2 89.5 %link_reduce.1 = (bf16[64,4096]{1,0:T(8,128)(2,1)}, bf16[128,384]{1,0:T(8,128)(2,1)}, bf16[512,2048]{1,0:T(8,128)(2,1)}) custom-call(bf16[2048,1024]{1,0:T(8,128)(2,1)} %convolution_convert_fusion.2.refs_0_, bf16[1024,384]{1,0:T(8,128)(2,1)} %pad.49.refs_1_, bf16[2048,2048]{1,0:T(8,128)(2,1)} %add_convert_fusion.refs_2_), custom_call_target="tpu_custom_call" | custom-call | flops 80000000000 | tf_op jit(solution)/shard_map/link_reduce/pallas_call | solution.py:695
  (243 shorter events, 99.1 us)
Async XLA Ops:
  7.2 265.9 %all-gather.6.cloned.1.call-start = ((), (), s32[]{:S(2)}) async-start(), calls=%async_computation.5 | async-start | bytes 4718592 | tf_op jit(solution)/shard_map/all_gather | solution.py:1042
  7.9 12.6 %copy-start.31 = (f32[64]{0:T(128)}, f32[64]{0:T(128)S(1)}, u32[]{:S(2)}) copy-start(f32[64]{0:T(128)S(1)} %convert_element_type.225) | copy-start | bytes 772
  10.0 10.7 %copy-start.26 = (f32[512]{0:T(512)}, f32[512]{0:T(512)S(1)}, u32[]{:S(2)}) copy-start(f32[512]{0:T(512)S(1)} %add_rsqrt_fusion) | copy-start | bytes 6148
  88.6 184.5 %all-gather.4.cloned.1.call-start = ((), (), s32[]{:S(2)}) async-start(), calls=%async_computation.4 | async-start | bytes 10485760 | tf_op jit(solution)/shard_map/all_gather | solution.py:1043
  89.3 204.9 %all-gather.8.cloned.1.call-start = ((), (), s32[]{:S(2)}) async-start(), calls=%async_computation.6 | async-start | bytes 4718592 | tf_op jit(solution)/shard_map/all_gather | solution.py:1041
  92.5 23.9 %collective-permute-start = (bf16[4,3,1024]{2,1,0:T(4,128)(2,1)S(1)}, bf16[4,3,1024]{2,1,0:T(4,128)(2,1)S(1)}, u32[]{:S(2)}, u32[]{:S(2)}) collective-permute-start(bf16[4,3,1024]{2,1,0:T(4,128)(2,1)S(1)} %slice.698), channel_id=1, source_target_pairs={{0,4},{4,8},{8,12},{12,16},{16,20},{20,24},{24,28},{1,5},{5,9},{9,... | collective-permute-start | bytes 73736 | tf_op jit(solution)/shard_map/ppermute | solution.py:954
  94.7 485.5 %reduce-scatter.4.cloned.1.call-start = ((), (), s32[]{:S(2)}) async-start(), calls=%async_computation.7 | async-start | bytes 4718592 | tf_op jit(solution)/shard_map/reduce_scatter | solution.py:1101
  97.0 67.1 %copy-start.24 = (f32[1024]{0:T(1024)}, f32[1024]{0:T(1024)S(1)}, u32[]{:S(2)}) copy-start(f32[1024]{0:T(1024)S(1)} %get-tuple-element.209) | copy-start | bytes 12292
  164.1 39.7 %copy-start.20 = (bf16[4,1024]{1,0:T(4,128)(2,1)}, bf16[4,1024]{1,0:T(4,128)(2,1)S(1)}, u32[]{:S(2)}) copy-start(bf16[4,1024]{1,0:T(4,128)(2,1)S(1)} %get-tuple-element.215) | copy-start | bytes 24580
  164.1 39.7 %copy-start.22 = (bf16[4,1024]{1,0:T(4,128)(2,1)}, bf16[4,1024]{1,0:T(4,128)(2,1)S(1)}, u32[]{:S(2)}) copy-start(bf16[4,1024]{1,0:T(4,128)(2,1)S(1)} %get-tuple-element.216) | copy-start | bytes 24580
  204.5 21.6 %copy-start.18 = (pred[2048,16]{0,1:T(8,128)(4,1)S(1)}, pred[2048,16]{0,1:T(8,128)(4,1)}, u32[]{:S(2)}) copy-start(pred[2048,16]{0,1:T(8,128)(4,1)} %iota_compare_fusion) | copy-start | bytes 98308
  273.0 21.2 %copy-start.28 = (f32[1024]{0:T(1024)S(1)}, f32[1024]{0:T(1024)}, u32[]{:S(2)}) copy-start(f32[1024]{0:T(1024)} %get-tuple-element.208) | copy-start | bytes 12292
  273.0 21.2 %copy-start.30 = (f32[1,4,4,128]{3,1,2,0:T(4,128)S(1)}, f32[1,4,4,128]{3,1,2,0:T(4,128)}, u32[]{:S(2)}) copy-start(f32[1,4,4,128]{3,1,2,0:T(4,128)} %copy.376) | copy-start | bytes 24580
  361.8 218.4 %reduce-scatter.6.cloned.1.call-start = ((), (), s32[]{:S(2)}) async-start(), calls=%async_computation.8 | async-start | bytes 4718592 | tf_op jit(solution)/shard_map/reduce_scatter | solution.py:1102
  365.9 32.3 %copy-start.21 = (bf16[4,1024]{1,0:T(4,128)(2,1)S(1)}, bf16[4,1024]{1,0:T(4,128)(2,1)}, u32[]{:S(2)}) copy-start(bf16[4,1024]{1,0:T(4,128)(2,1)} %copy-done.20) | copy-start | bytes 24580
  365.9 32.3 %copy-start.23 = (bf16[4,1024]{1,0:T(4,128)(2,1)S(1)}, bf16[4,1024]{1,0:T(4,128)(2,1)}, u32[]{:S(2)}) copy-start(bf16[4,1024]{1,0:T(4,128)(2,1)} %copy-done.22) | copy-start | bytes 24580
  416.7 259.7 %reduce-scatter.8.cloned.1.call-start = ((), (), s32[]{:S(2)}) async-start(), calls=%async_computation.9 | async-start | bytes 10485760 | tf_op jit(solution)/shard_map/reduce_scatter | solution.py:1103
  518.4 22.1 %copy-start.7 = (bf16[1024,384]{1,0:T(8,128)(2,1)S(1)}, bf16[1024,384]{1,0:T(8,128)(2,1)}, u32[]{:S(2)}) copy-start(bf16[1024,384]{1,0:T(8,128)(2,1)} %get-tuple-element.50) | copy-start | bytes 2359300
  545.3 18.9 %copy-start.5 = (bf16[2048,1024]{1,0:T(8,128)(2,1)S(1)}, bf16[2048,1024]{1,0:T(8,128)(2,1)}, u32[]{:S(2)}) copy-start(bf16[2048,1024]{1,0:T(8,128)(2,1)} %get-tuple-element.214) | copy-start | bytes 12582916
  545.3 18.9 %copy-start.14 = (f32[160,2048]{1,0:T(8,128)S(1)}, f32[160,2048]{1,0:T(8,128)}, u32[]{:S(2)}) copy-start(f32[160,2048]{1,0:T(8,128)} %link_sum.2) | copy-start | bytes 3932164
  566.2 14.0 %copy-start.29 = (f32[1024]{0:T(1024)S(1)}, f32[1024]{0:T(1024)}, u32[]{:S(2)}) copy-start(f32[1024]{0:T(1024)} %get-tuple-element.208) | copy-start | bytes 12292
  580.2 23.3 %copy-start.2 = (bf16[2048,1024]{1,0:T(8,128)(2,1)S(1)}, bf16[2048,1024]{1,0:T(8,128)(2,1)}, u32[]{:S(2)}) copy-start(bf16[2048,1024]{1,0:T(8,128)(2,1)} %get-tuple-element.58) | copy-start | bytes 12582916
  592.3 12.1 %copy-start.8 = (f32[2048,1024]{1,0:T(8,128)}, f32[2048,1024]{1,0:T(8,128)S(1)}, u32[]{:S(2)}) copy-start(f32[2048,1024]{1,0:T(8,128)S(1)} %add_add_fusion.grad_ref) | copy-start | bytes 25165828
  593.3 17.2 %collective-permute-start.1 = (bf16[4,3,1024]{2,1,0:T(4,128)(2,1)S(1)}, bf16[4,3,1024]{2,1,0:T(4,128)(2,1)S(1)}, u32[]{:S(2)}, u32[]{:S(2)}) collective-permute-start(bf16[4,3,1024]{2,1,0:T(4,128)(2,1)S(1)} %fusion.46), channel_id=1, source_target_pairs={{4,0},{8,4},{12,8},{16,12},{20,16},{24,20},{28,24},{5,1},{9,5},{13... | collective-permute-start | bytes 73736 | tf_op jit(solution)/shard_map/ppermute | solution.py:954
  604.4 70.1 %all-to-all-start = ((bf16[4,64,1024]{2,1,0:T(8,128)(2,1)}), bf16[4,64,1024]{2,1,0:T(8,128)(2,1)S(1)}, u32[]{:S(2)}, u32[]{:S(2)}) async-start(bf16[4,64,1024]{2,1,0:T(8,128)(2,1)} %bitcast.52), calls=%async_computation.2 | async-start | bytes 1048576 | tf_op jit(solution)/shard_map/all_to_all | solution.py:1131
  629.8 14.2 %copy-start.11 = (bf16[2048,1024]{1,0:T(8,128)(2,1)S(1)}, bf16[2048,1024]{1,0:T(8,128)(2,1)}, u32[]{:S(2)}) copy-start(bf16[2048,1024]{1,0:T(8,128)(2,1)} %get-tuple-element.54) | copy-start | bytes 12582916
  629.8 28.3 %slice-start = ((s8[16777216]{0:T(1024)(128)(4,1)}), s8[4194304]{0:T(1024)(128)(4,1)S(1)}, s32[]{:S(2)}) async-start(s8[16777216]{0:T(1024)(128)(4,1)} %bitcast.260), calls=%async_computation.10 | async-start | bytes 8388608
  629.8 28.3 %slice-start.1 = ((s8[16777216]{0:T(1024)(128)(4,1)}), s8[4194304]{0:T(1024)(128)(4,1)S(1)}, s32[]{:S(2)}) async-start(s8[16777216]{0:T(1024)(128)(4,1)} %bitcast.260), calls=%async_computation.11 | async-start | bytes 8388608
  644.0 14.1 %slice-start.2 = ((s8[16777216]{0:T(1024)(128)(4,1)}), s8[4194304]{0:T(1024)(128)(4,1)S(1)}, s32[]{:S(2)}) async-start(s8[16777216]{0:T(1024)(128)(4,1)} %bitcast.260), calls=%async_computation.12 | async-start | bytes 8388608
  644.0 14.1 %slice-start.3 = ((s8[16777216]{0:T(1024)(128)(4,1)}), s8[4194304]{0:T(1024)(128)(4,1)S(1)}, s32[]{:S(2)}) async-start(s8[16777216]{0:T(1024)(128)(4,1)} %bitcast.260), calls=%async_computation.13 | async-start | bytes 8388608
  658.1 9.7 %copy-start.19 = (f32[32,1024]{1,0:T(8,128)S(1)}, f32[32,1024]{1,0:T(8,128)}, u32[]{:S(2)}) copy-start(f32[32,1024]{1,0:T(8,128)} %get-tuple-element.81) | copy-start | bytes 393220
  680.2 93.5 %copy-start.27 = (f32[512]{0:T(512)S(1)}, f32[512]{0:T(512)}, u32[]{:S(2)}) copy-start(f32[512]{0:T(512)} %copy-done.26) | copy-start | bytes 6148
  (16 other events, 84.9 us)
Sparse Core Ops, SparseCore 0:
  88.7 71.8 all-gather.5
  162.1 57.2 all-gather.3
  221.5 72.6 all-gather.7
  361.9 93.1 reduce-scatter.3
  459.0 87.6 reduce-scatter.5
  549.2 76.3 reduce-scatter.7

commit v8 on v6

--- a/solution.py
+++ b/solution.py
@@ -1092,15 +1092,18 @@
     d_masked = d_gated * valid
     d_ssm = d_masked * gate_act
     d_gate = (d_masked * ssm_out * silu_slope(gate_in)).astype(bf)
+    product, d_ssm, gated, d_gate = lax.optimization_barrier((product, d_ssm, gated, d_gate))
+    product = lax.psum_scatter(product, "stream", scatter_dimension=0, tiled=True)
     g_out = contract_rows(gated, cot_all).astype(bf)
     g_in_gate = contract_rows(unit, d_gate).astype(bf)
-    d_ssm, product, g_out, g_in_gate = lax.optimization_barrier((d_ssm, product, g_out, g_in_gate))
-    g_out = lax.psum_scatter(g_out, "seq", scatter_dimension=0, tiled=True)
-    g_in_gate = lax.psum_scatter(g_in_gate, "seq", scatter_dimension=0, tiled=True)
-    output = (residual + lax.psum_scatter(product, "stream", scatter_dimension=0, tiled=True).astype(f32)).astype(bf)
+    d_ssm, g_out, g_in_gate = lax.optimization_barrier((d_ssm, g_out, g_in_gate))
     g_skip = jnp.sum(d_ssm * act_float, axis=0)
     back_ends = scan_end(bwd_end_body, dt_reset, d_ssm, read_slabs, rate, seqs)
     later_sum = carried(back_ends, step_sum, rate, True, sizes, 4)
+    later_sum, product, g_out, g_in_gate = lax.optimization_barrier((later_sum, product, g_out, g_in_gate))
+    output = (residual + product.astype(f32)).astype(bf)
+    g_out = lax.psum_scatter(g_out, "seq", scatter_dimension=0, tiled=True)
+    g_in_gate = lax.psum_scatter(g_in_gate, "seq", scatter_dimension=0, tiled=True)
     sum_write, sum_rate, g_log, d_write, d_read = bwd_full(
         dt_reset, dt_act, d_ssm, history, read_slabs, write_diag, rate, later_sum, seqs)
     per_step = jnp.where(dt_step > 1e-30, sum_rate * LN2 / jnp.maximum(dt_step, 1e-30), 0.0)
@@ -1111,7 +1114,7 @@
     g_dt = lax.dot_general(d_pre_low, low_rank, (((0,), (1,)), ((), ())), preferred_element_type=f32)
     d_low = lax.dot_general(dtw_cols, d_pre_low, (((0,), (1,)), ((), ())), preferred_element_type=f32)
     d_proj = link_sum(jnp.concatenate([d_low, d_write, d_read], axis=0), sizes, 5).astype(bf)
-    d_proj, g_out, g_in_gate = lax.optimization_barrier((d_proj, g_out, g_in_gate))
+    d_proj, g_out = lax.optimization_barrier((d_proj, g_out))
     g_xproj = lax.dot_general(activated, d_proj, (((0,), (1,)), ((), ())), preferred_element_type=f32)
     d_act = dt_step * sum_write + skip_vec * d_ssm + lax.dot_general(
         d_proj, xproj_full, (((0,), (1,)), ((), ())), preferred_element_type=f32)
@@ -1119,6 +1122,7 @@
     later = passed_along(first.astype(bf), "seq", -1).astype(f32)
     later = jnp.pad(later, ((0, 0), (0, 8 - rim), (0, 0))).reshape(seqs * 8, chans)
     d_conv_in, sums = conv_bwd(d_act, slope, later, conv_in, masks, taps, seqs)
+    d_conv_in, g_in_gate = lax.optimization_barrier((d_conv_in, g_in_gate))
     sums = sums.reshape(seqs, 8, chans).sum(0)
     g_conv, g_conv_bias = sums[:CONV].T, sums[CONV]
     g_in_conv = contract_rows(unit, d_conv_in).astype(bf)

time: 796 us -> 784 us (0.985)
  transfers between devices with their start and end apart: 9 -> 9, of which waited for: 1 -> 2; matrix products, arithmetic and copies ran while one was open for 24% -> 27% of each run, Pallas kernels for 38% -> 38%
where the time goes in v8:
time: 784 us; the launch traced here: 775 us
  Pallas kernels  446 us (57%)
  matrix products  175 us (22%)
  other arithmetic  64.1 us (8%)
  local copies, waits for them, and re-layouts  45.2 us (6%)
  starting transfers between devices  16.2 us (2%)
  between operations  15.6 us (2%)
  waiting for transfers between devices  12.6 us (2%)
    pallas_call x1, Pallas kernels, bwd_full(): pl.pallas_call(bwd_full_body, grid=(strips, seqs, blocks), in_specs=[pl.B...  95.2 us
    pallas_call x1, Pallas kernels, link_reduce(): pl.pallas_call(kernel, in_specs=[pl.BlockSpec(memory_space=pl.ANY)] * cou...  91.9 us
    pallas_call x1, Pallas kernels, link_open(): pl.pallas_call(kernel, in_specs=[pl.BlockSpec(memory_space=pl.ANY)] * (co...  63.5 us
    pallas_call x2, Pallas kernels, scan_end(): pl.pallas_call(body, grid=(seqs, chans // width), in_specs=[pl.BlockSpec(...  62.7 us
    dot_general x3, matrix products, contract_cols(): lax.dot_general(left_mat, right_mat, NT, preferred_element_type=jnp.float32)  45.8 us
    dot_general x3, matrix products, contract_rows(): lax.dot_general(left_mat, right_mat, (((0,), (0,)), ((), ())), preferred_...  42.8 us
    pallas_call x1, Pallas kernels, fwd_full(): pl.pallas_call(fwd_full_body, grid=(chans // width, seqs, blocks), in_spe...  42 us
    pallas_call x2, Pallas kernels, link_sum(): pl.pallas_call(kernel, in_specs=[pl.BlockSpec(memory_space=pltpu.VMEM)],...  34.5 us
  transfers between devices with their start and end apart: 9, of which 2 were waited for; matrix products, arithmetic and copies ran while one was open for 27% of the time, Pallas kernels for 38%

profile of v8, /device:TPU:19, one launch (start us, length us, event | category | flops | bytes accessed | tf_op | source)
XLA Modules:
  0.0 774.9 jit_solution(720618481454283052)
XLA Ops:
  25.0 63.5 %link_open.1 = (bf16[2048,1024]{1,0:T(8,128)(2,1)}, bf16[256,1024]{1,0:T(8,128)(2,1)}, bf16[256,1024]{1,0:T(8,128)(2,1)}, s32[32,128]{1,0:T(8,128)}, bf16[2048,2...) custom-call(bf16[256,1024]{1,0:T(8,128)(2,1)} %get-tuple-element.281.conv_ref, bf16[256,1024]{1,0:T(8,128)(2,1)} %get-tuple-element.280.gate_ref, ...), custom_call_target="tpu_custom_call" | custom-call | flops 80000000000 | tf_op jit(solution)/shard_map/link_open/pallas_call | solution.py:832
  89.4 14.5 %fusion.65 = (bf16[2048,1024]{1,0:T(8,128)(2,1)S(1)}, f32[2048,1024]{1,0:T(8,128)}) fusion(bf16[2048,2048]{1,0:T(8,128)(2,1)} %get-tuple-element.57, bf16[2048,1024]{1,0:T(8,128)(2,1)} %get-tuple-element.58), kind=kOutput, calls=%fused_computation.216 | convolution fusion | flops 8592031744 | bytes 25165824 | tf_op jit(solution)/shard_map/dot_general | solution.py:1064
  114.0 12.3 %conv_fwd.1 = (bf16[2048,1024]{1,0:T(8,128)(2,1)}, bf16[2048,1024]{1,0:T(8,128)(2,1)}) custom-call(f32[2048,1024]{1,0:T(8,128)} %get-tuple-element.278.x_ref, f32[32,1024]{1,0:T(8,128)} %bitcast_convert_fusion.1.early_ref, f32[2048,8]{1,0:T(8,128)} %bitcast.270, f32[8,1024]{1,0:T(8,128)} %fusion.47.taps_ref), custom_call_target="tpu_custom_call" | custom-call | flops 8388608000 | bytes 16777216 | tf_op jit(solution)/shard_map/conv_fwd/pallas_call | solution.py:912
  126.2 4.6 convolution_convert_fusion.4.own_ref
  130.8 16.2 %link_sum.2 = f32[160,2048]{1,0:T(8,128)} custom-call(bf16[160,2048]{1,0:T(8,128)(2,1)} %convolution_convert_fusion.4.own_ref), custom_call_target="tpu_custom_call" | custom-call | flops 20000000000 | tf_op jit(solution)/shard_map/link_sum/pallas_call | solution.py:750
  151.6 9.3 %bitcast_reduce_fusion = (f32[4,1024]{1,0:T(4,128)S(1)}, f32[2048,1024]{1,0:T(8,128)}, f32[2048,1024]{1,0:T(8,128)S(1)}) fusion(f32[1024]{0:T(1024)S(1)} %get-tuple-element.217, pred[2048]{0:T(1024)(128)(4,1)S(1)} %bitcast.287, bf16[1024,384]{1,0:T(8,128)(2,1)S(1)} %copy-done.8, f32[160,2048]{1,0:T(8,128)} %link_sum.2), kind=kOutput, calls=%fused_computation.10 | convolution fusion | flops 555741184 | bytes 17586176 | tf_op jit(solution)/shard_map/dot_general | solution.py:1076
  161.0 7.3 convert_multiply_fusion.3.dtx_ref
  168.2 31.4 %fwd_end.1 = f32[64,1024]{1,0:T(8,128)} custom-call(f32[2048,1024]{1,0:T(8,128)} %get-tuple-element.226.dte_ref, f32[2048,1024]{1,0:T(8,128)} %convert_multiply_fusion.3.dtx_ref, f32[2048,16]{1,0:T(8,128)} %bitcast.274, f32[16,1024]{1,0:T(8,128)} %multiply_bitcast_fusion.rate_ref), custom_call_target="tpu_custom_call" | custom-call | flops 33554432000 | bytes 16777216 | tf_op jit(solution)/shard_map/fwd_end/pallas_call | solution.py:82
  201.3 16.1 %link_gather.2 = bf16[640,1024]{1,0:T(8,128)(2,1)} custom-call(bf16[80,1024]{1,0:T(8,128)(2,1)} %pad.47.refs_0_), custom_call_target="tpu_custom_call" | custom-call | flops 20000000000 | tf_op jit(solution)/shard_map/link_gather/pallas_call | solution.py:476
  227.0 42.0 %fwd_full.1 = (f32[2048,1024]{1,0:T(8,128)}, bf16[32896,1024]{1,0:T(8,128)(2,1)}) custom-call(f32[2048,1024]{1,0:T(8,128)} %get-tuple-element.226.dte_ref, f32[2048,1024]{1,0:T(8,128)} %convert_multiply_fusion.3.dtx_ref, f32[2048,16]{1,0:T(8,128)} %bitcast.275, bf16[2048,256]{1,0:T(8,128)(2,1)} %copy.352.read_ref, f32[16,1024]{1,0:T(8,128)} %multiply_bitcast_fusion.rate_ref, ...), custom_call_target="tpu_custom_call" | custom-call | flops 46976204800 | bytes 67108864 | tf_op jit(solution)/shard_map/fwd_full/pallas_call | solution.py:147
  269.1 14.6 %fusion.66 = f32[2048,1024]{1,0:T(8,128)} fusion(bf16[2048,2048]{1,0:T(8,128)(2,1)} %all-gather.8.cloned.1.call-done, bf16[1024,2048]{1,0:T(8,128)(2,1)} %all-gather.6.cloned.1.call-done), kind=kOutput, calls=%fused_computation.217 | convolution fusion | flops 8589934592 | bytes 20971520 | tf_op jit(solution)/shard_map/dot_general | solution.py:978
  283.6 11.3 %all-gather.4.cloned.1.call-done = bf16[2048,1024]{1,0:T(8,128)(2,1)} async-done(((bf16[256,1024]{1,0:T(8,128)(2,1)}), bf16[2048,1024]{1,0:T(8,128)(2,1)}) %all-gather.4.cloned.1.call-update) | async-done | bytes 4194320 | tf_op jit(solution)/shard_map/all_gather | solution.py:1041
  294.9 25.1 %multiply_convert_fusion = (bf16[2048,1024]{1,0:T(8,128)(2,1)}, bf16[2048,1024]{1,0:T(8,128)(2,1)}, f32[2048,1024]{1,0:T(8,128)}) fusion(f32[2048,1024]{1,0:T(8,128)} %fusion.66, f32[2048,1024]{1,0:T(8,128)} %get-tuple-element.61, bf16[2048,1024]{1,0:T(8,128)(2,1)} %get-tuple-element.60, f32[2048]{0:T(1024)S(1)} %bitcast.286, f32[1024]{0:T(1024)S(1)} %copy-done.36, ...), kind=kOutput, calls=%fused_computation.12 | convolution fusion | flops 8629780480 | bytes 50343936 | tf_op jit(solution)/shard_map/dot_general | solution.py:1065
  320.0 14.1 %convolution_convert_fusion = bf16[2048,2048]{1,0:T(8,128)(2,1)} fusion(bf16[2048,1024]{1,0:T(8,128)(2,1)} %get-tuple-element.66, bf16[1024,2048]{1,0:T(8,128)(2,1)} %all-gather.6.cloned.1.call-done), kind=kOutput, calls=%fused_computation.17 | convolution fusion | flops 8594128896 | bytes 16777216 | tf_op jit(solution)/shard_map/dot_general | solution.py:1090
  337.0 14.6 %convolution_convert_fusion.3 = bf16[2048,1024]{1,0:T(8,128)(2,1)} fusion(bf16[2048,2048]{1,0:T(8,128)(2,1)} %get-tuple-element.57, bf16[2048,1024]{1,0:T(8,128)(2,1)} %get-tuple-element.67), kind=kOutput, calls=%fused_computation.34 | convolution fusion | flops 8592031744 | bytes 16777216 | tf_op jit(solution)/shard_map/dot_general | solution.py:974
  351.6 14.1 %convolution_convert_fusion.1 = bf16[1024,2048]{1,0:T(8,128)(2,1)} fusion(bf16[2048,1024]{1,0:T(8,128)(2,1)} %get-tuple-element.66, bf16[2048,2048]{1,0:T(8,128)(2,1)} %all-gather.8.cloned.1.call-done), kind=kOutput, calls=%fused_computation.32 | convolution fusion | flops 8592031744 | bytes 16777216 | tf_op jit(solution)/shard_map/dot_general | solution.py:974
  365.7 31.3 %bwd_end.1 = f32[64,1024]{1,0:T(8,128)} custom-call(f32[2048,1024]{1,0:T(8,128)} %get-tuple-element.226.dte_ref, f32[2048,1024]{1,0:T(8,128)} %get-tuple-element.68.grad_ref, f32[2048,16]{1,0:T(8,128)} %bitcast.272, f32[16,1024]{1,0:T(8,128)} %multiply_bitcast_fusion.rate_ref), custom_call_target="tpu_custom_call" | custom-call | flops 33554432000 | bytes 16777216 | tf_op jit(solution)/shard_map/bwd_end/pallas_call | solution.py:82
  398.7 9.1 %link_gather.3 = bf16[640,1024]{1,0:T(8,128)(2,1)} custom-call(bf16[80,1024]{1,0:T(8,128)(2,1)} %pad.48.refs_0_), custom_call_target="tpu_custom_call" | custom-call | flops 20000000000 | tf_op jit(solution)/shard_map/link_gather/pallas_call | solution.py:476
  413.1 95.2 %bwd_full.1 = (f32[2048,1024]{1,0:T(8,128)}, f32[2048,1024]{1,0:T(8,128)}, f32[16,1024]{1,0:T(8,128)}, f32[256,256]{1,0:T(8,128)}, f32[256,256]{1,0:T(8,128)}) custom-call(f32[2048,1024]{1,0:T(8,128)} %get-tuple-element.226.dte_ref, f32[2048,1024]{1,0:T(8,128)} %convert_multiply_fusion.3.dtx_ref, f32[2048,1024]{1,0:T(8,128)} %get-tuple-element.68.grad_ref, ...), custom_call_target="tpu_custom_call" | custom-call | flops 107374182400 | bytes 67108864 | tf_op jit(solution)/shard_map/bwd_full/pallas_call | solution.py:249
  508.4 17.3 %fusion.60 = (bf16[1024]{0:T(1024)(128)(2,1)S(1)}, bf16[2048,1024]{1,0:T(8,128)(2,1)}, bf16[1024]{0:T(1024)(128)(2,1)S(1)}) fusion(f32[2048,1024]{1,0:T(8,128)} %get-tuple-element.74, bf16[2048,1024]{1,0:T(8,128)(2,1)S(1)} %copy-done.2, f32[2048,1024]{1,0:T(8,128)} %get-tuple-element.75, f32[2048,1024]{1,0:T(8,128)} %copy-done, f32[1024]{0:T(1024)S(1)} %copy-done.33, ...), kind=kLoop, calls=%fused_computation.212 | loop fusion | flops 48232448 | bytes 41951232 | tf_op jit(solution)/shard_map/reduce_sum | solution.py:1112
  528.8 4.0 convolution_convert_fusion.5
  533.7 18.3 %link_sum.3 = f32[160,2048]{1,0:T(8,128)} custom-call(bf16[160,2048]{1,0:T(8,128)(2,1)} %pad_maximum_fusion.1.own_ref), custom_call_target="tpu_custom_call" | custom-call | flops 20000000000 | tf_op jit(solution)/shard_map/link_sum/pallas_call | solution.py:750
  557.8 12.0 %add_add_fusion.grad_ref = f32[2048,1024]{1,0:T(8,128)S(1)} fusion(f32[2048,1024]{1,0:T(8,128)} %get-tuple-element.68.grad_ref, f32[2048,1024]{1,0:T(8,128)} %get-tuple-element.74, bf16[160,2048]{1,0:T(8,128)(2,1)S(1)} %convert_element_type.268, f32[1024]{0:T(1024)S(1)} %copy-done.37, bf16[1024,384]{1,0:T(8,128)(2,1)S(1)} %copy-done.9, ...), kind=kOutput, calls=%fused_computation.11 | convolution fusion | flops 694157312 | bytes 34742272 | tf_op jit(solution)/shard_map/dot_general | solution.py:1119
  569.8 3.3 copy-done.10
  573.9 7.4 collective-permute-start.1
  583.6 18.7 %conv_bwd.1 = (bf16[2048,1024]{1,0:T(8,128)(2,1)}, f32[32,1024]{1,0:T(8,128)}) custom-call(f32[2048,1024]{1,0:T(8,128)} %copy-done.10, bf16[2048,1024]{1,0:T(8,128)(2,1)} %get-tuple-element.80.slope_ref, f32[32,1024]{1,0:T(8,128)} %bitcast_convert_fusion.late_ref, f32[2048,1024]{1,0:T(8,128)} %get-tuple-element.278.x_ref, f32[2048,8]{1,0:T(8,128)} %bitcast.271, ...), custom_call_target="tpu_custom_call" | custom-call | flops 10485760000 | bytes 25165824 | tf_op jit(solution)/shard_map/conv_bwd/pallas_call | solution.py:934
  602.3 6.5 all-to-all-start
  608.9 15.3 %fusion.67 = f32[2048,2048]{1,0:T(8,128)} fusion(bf16[2048,1024]{1,0:T(8,128)(2,1)} %get-tuple-element.83, bf16[2048,1024]{1,0:T(8,128)(2,1)} %get-tuple-element.58), kind=kOutput, calls=%fused_computation.218 | convolution fusion | flops 8589934592 | bytes 25165824 | tf_op jit(solution)/shard_map/dot_general | solution.py:978
  624.2 15.9 %add_convert_fusion.refs_2_ = bf16[2048,2048]{1,0:T(8,128)(2,1)} fusion(f32[2048,2048]{1,0:T(8,128)} %fusion.67, bf16[2048,1024]{1,0:T(8,128)(2,1)} %get-tuple-element.67, bf16[2048,1024]{1,0:T(8,128)(2,1)S(1)} %copy-done.42), kind=kOutput, calls=%fused_computation.1 | convolution fusion | flops 8598323200 | bytes 33554432 | tf_op jit(solution)/shard_map/dot_general | solution.py:978
  640.1 14.2 %convolution_convert_fusion.2.refs_0_ = bf16[2048,1024]{1,0:T(8,128)(2,1)} fusion(bf16[2048,2048]{1,0:T(8,128)(2,1)} %get-tuple-element.57, bf16[2048,1024]{1,0:T(8,128)(2,1)} %get-tuple-element.83), kind=kOutput, calls=%fused_computation.33 | convolution fusion | flops 8592031744 | bytes 16777216 | tf_op jit(solution)/shard_map/dot_general | solution.py:974
  654.8 3.5 concatenate.34
  660.5 91.9 %link_reduce.1 = (bf16[64,4096]{1,0:T(8,128)(2,1)}, bf16[128,384]{1,0:T(8,128)(2,1)}, bf16[512,2048]{1,0:T(8,128)(2,1)}) custom-call(bf16[2048,1024]{1,0:T(8,128)(2,1)} %convolution_convert_fusion.2.refs_0_, bf16[1024,384]{1,0:T(8,128)(2,1)} %pad.50.refs_1_, bf16[2048,2048]{1,0:T(8,128)(2,1)} %add_convert_fusion.refs_2_), custom_call_target="tpu_custom_call" | custom-call | flops 80000000000 | tf_op jit(solution)/shard_map/link_reduce/pallas_call | solution.py:695
  (247 shorter events, 84.6 us)
Async XLA Ops:
  7.2 261.9 %all-gather.6.cloned.1.call-start = ((), (), s32[]{:S(2)}) async-start(), calls=%async_computation.5 | async-start | bytes 4718592 | tf_op jit(solution)/shard_map/all_gather | solution.py:1042
  7.9 12.6 %copy-start.39 = (f32[64]{0:T(128)}, f32[64]{0:T(128)S(1)}, u32[]{:S(2)}) copy-start(f32[64]{0:T(128)S(1)} %convert_element_type.223) | copy-start | bytes 772
  88.5 180.5 %all-gather.8.cloned.1.call-start = ((), (), s32[]{:S(2)}) async-start(), calls=%async_computation.6 | async-start | bytes 10485760 | tf_op jit(solution)/shard_map/all_gather | solution.py:1043
  89.3 205.6 %all-gather.4.cloned.1.call-start = ((), (), s32[]{:S(2)}) async-start(), calls=%async_computation.4 | async-start | bytes 4718592 | tf_op jit(solution)/shard_map/all_gather | solution.py:1041
  89.3 17.9 %copy-start.8 = (bf16[1024,384]{1,0:T(8,128)(2,1)S(1)}, bf16[1024,384]{1,0:T(8,128)(2,1)}, u32[]{:S(2)}) copy-start(bf16[1024,384]{1,0:T(8,128)(2,1)} %get-tuple-element.54) | copy-start | bytes 2359300
  103.9 9.4 %collective-permute-start = (bf16[4,3,1024]{2,1,0:T(4,128)(2,1)S(1)}, bf16[4,3,1024]{2,1,0:T(4,128)(2,1)S(1)}, u32[]{:S(2)}, u32[]{:S(2)}) collective-permute-start(bf16[4,3,1024]{2,1,0:T(4,128)(2,1)S(1)} %slice.399), channel_id=1, source_target_pairs={{0,4},{4,8},{8,12},{12,16},{16,20},{20,24},{24,28},{1,5},{5,9},{9,... | collective-permute-start | bytes 73736 | tf_op jit(solution)/shard_map/ppermute | solution.py:954
  106.0 304.8 %reduce-scatter.4.cloned.1.call-start = ((), (), s32[]{:S(2)}) async-start(), calls=%async_computation.7 | async-start | bytes 10485760 | tf_op jit(solution)/shard_map/reduce_scatter | solution.py:1096
  108.4 52.6 %copy-start.32 = (f32[1024]{0:T(1024)}, f32[1024]{0:T(1024)S(1)}, u32[]{:S(2)}) copy-start(f32[1024]{0:T(1024)S(1)} %get-tuple-element.217) | copy-start | bytes 12292
  160.9 39.7 %copy-start.27 = (bf16[4,1024]{1,0:T(4,128)(2,1)}, bf16[4,1024]{1,0:T(4,128)(2,1)S(1)}, u32[]{:S(2)}) copy-start(bf16[4,1024]{1,0:T(4,128)(2,1)S(1)} %get-tuple-element.223) | copy-start | bytes 24580
  160.9 39.7 %copy-start.29 = (bf16[4,1024]{1,0:T(4,128)(2,1)}, bf16[4,1024]{1,0:T(4,128)(2,1)S(1)}, u32[]{:S(2)}) copy-start(bf16[4,1024]{1,0:T(4,128)(2,1)S(1)} %get-tuple-element.224) | copy-start | bytes 24580
  201.3 20.8 %copy-start.25 = (pred[2048,16]{0,1:T(8,128)(4,1)S(1)}, pred[2048,16]{0,1:T(8,128)(4,1)}, u32[]{:S(2)}) copy-start(pred[2048,16]{0,1:T(8,128)(4,1)} %iota_compare_fusion) | copy-start | bytes 98308
  269.0 25.9 %copy-start.36 = (f32[1024]{0:T(1024)S(1)}, f32[1024]{0:T(1024)}, u32[]{:S(2)}) copy-start(f32[1024]{0:T(1024)} %get-tuple-element.216) | copy-start | bytes 12292
  269.0 25.9 %copy-start.38 = (f32[1,4,4,128]{3,1,2,0:T(4,128)S(1)}, f32[1,4,4,128]{3,1,2,0:T(4,128)}, u32[]{:S(2)}) copy-start(f32[1,4,4,128]{3,1,2,0:T(4,128)} %copy.376) | copy-start | bytes 24580
  334.1 223.6 %reduce-scatter.6.cloned.1.call-start = ((), (), s32[]{:S(2)}) async-start(), calls=%async_computation.8 | async-start | bytes 4718592 | tf_op jit(solution)/shard_map/reduce_scatter | solution.py:1105
  365.6 32.3 %copy-start.28 = (bf16[4,1024]{1,0:T(4,128)(2,1)S(1)}, bf16[4,1024]{1,0:T(4,128)(2,1)}, u32[]{:S(2)}) copy-start(bf16[4,1024]{1,0:T(4,128)(2,1)} %copy-done.27) | copy-start | bytes 24580
  365.7 32.3 %copy-start.30 = (bf16[4,1024]{1,0:T(4,128)(2,1)S(1)}, bf16[4,1024]{1,0:T(4,128)(2,1)}, u32[]{:S(2)}) copy-start(bf16[4,1024]{1,0:T(4,128)(2,1)} %copy-done.29) | copy-start | bytes 24580
  410.9 191.5 %reduce-scatter.8.cloned.1.call-start = ((), (), s32[]{:S(2)}) async-start(), calls=%async_computation.9 | async-start | bytes 4718592 | tf_op jit(solution)/shard_map/reduce_scatter | solution.py:1106
  413.1 95.3 %copy-start.2 = (bf16[2048,1024]{1,0:T(8,128)(2,1)S(1)}, bf16[2048,1024]{1,0:T(8,128)(2,1)}, u32[]{:S(2)}) copy-start(bf16[2048,1024]{1,0:T(8,128)(2,1)} %get-tuple-element.60) | copy-start | bytes 12582916
  413.1 95.3 %copy-start.33 = (f32[1024]{0:T(1024)S(1)}, f32[1024]{0:T(1024)}, u32[]{:S(2)}) copy-start(f32[1024]{0:T(1024)} %copy-done.32) | copy-start | bytes 12292
  508.4 17.4 %copy-start.24 = (f32[256,256]{1,0:T(8,128)S(1)}, f32[256,256]{1,0:T(8,128)}, u32[]{:S(2)}) copy-start(f32[256,256]{1,0:T(8,128)} %get-tuple-element.76) | copy-start | bytes 786436
  508.4 17.4 %copy-start.23 = (f32[256,256]{1,0:T(8,128)S(1)}, f32[256,256]{1,0:T(8,128)}, u32[]{:S(2)}) copy-start(f32[256,256]{1,0:T(8,128)} %get-tuple-element.77) | copy-start | bytes 786436
  508.4 17.7 %copy-start.31 = (f32[16,1024]{1,0:T(8,128)S(1)}, f32[16,1024]{1,0:T(8,128)}, u32[]{:S(2)}) copy-start(f32[16,1024]{1,0:T(8,128)} %get-tuple-element.88) | copy-start | bytes 196612
  533.7 19.9 %copy-start.7 = (bf16[2048,1024]{1,0:T(8,128)(2,1)S(1)}, bf16[2048,1024]{1,0:T(8,128)(2,1)}, u32[]{:S(2)}) copy-start(bf16[2048,1024]{1,0:T(8,128)(2,1)} %get-tuple-element.222) | copy-start | bytes 12582916
  533.7 19.9 %copy-start.16 = (f32[160,2048]{1,0:T(8,128)S(1)}, f32[160,2048]{1,0:T(8,128)}, u32[]{:S(2)}) copy-start(f32[160,2048]{1,0:T(8,128)} %link_sum.2) | copy-start | bytes 3932164
  557.8 23.5 %copy-start.3 = (bf16[2048,1024]{1,0:T(8,128)(2,1)S(1)}, bf16[2048,1024]{1,0:T(8,128)(2,1)}, u32[]{:S(2)}) copy-start(bf16[2048,1024]{1,0:T(8,128)(2,1)} %get-tuple-element.60) | copy-start | bytes 12582916
  573.9 9.0 %collective-permute-start.1 = (bf16[4,3,1024]{2,1,0:T(4,128)(2,1)S(1)}, bf16[4,3,1024]{2,1,0:T(4,128)(2,1)S(1)}, u32[]{:S(2)}, u32[]{:S(2)}) collective-permute-start(bf16[4,3,1024]{2,1,0:T(4,128)(2,1)S(1)} %fusion.43), channel_id=1, source_target_pairs={{4,0},{8,4},{12,8},{16,12},{20,16},{24,20},{28,24},{5,1},{9,5},{13... | collective-permute-start | bytes 73736 | tf_op jit(solution)/shard_map/ppermute | solution.py:954
  602.3 56.9 %all-to-all-start = ((bf16[4,64,1024]{2,1,0:T(8,128)(2,1)}), bf16[4,64,1024]{2,1,0:T(8,128)(2,1)S(1)}, u32[]{:S(2)}, u32[]{:S(2)}) async-start(bf16[4,64,1024]{2,1,0:T(8,128)(2,1)} %bitcast.279), calls=%async_computation.3 | async-start | bytes 1048576 | tf_op jit(solution)/shard_map/all_to_all | solution.py:1131
  608.8 15.3 %copy-start.42 = (bf16[2048,1024]{1,0:T(8,128)(2,1)S(1)}, bf16[2048,1024]{1,0:T(8,128)(2,1)}, u32[]{:S(2)}) copy-start(bf16[2048,1024]{1,0:T(8,128)(2,1)} %all-gather.4.cloned.1.call-done) | copy-start | bytes 12582916
  640.1 14.2 %copy-start.26 = (f32[32,1024]{1,0:T(8,128)S(1)}, f32[32,1024]{1,0:T(8,128)}, u32[]{:S(2)}) copy-start(f32[32,1024]{1,0:T(8,128)} %get-tuple-element.89) | copy-start | bytes 393220
  640.1 14.6 %copy-start.17 = (bf16[1024,128]{1,0:T(8,128)(2,1)S(1)}, bf16[1024,128]{1,0:T(8,128)(2,1)}, u32[]{:S(2)}) copy-start(bf16[1024,128]{1,0:T(8,128)(2,1)} %fusion.20) | copy-start | bytes 786436
  660.5 95.9 %copy-start.6 = (bf16[1,512,2048]{2,1,0:T(8,128)(2,1)S(1)}, bf16[1,512,2048]{2,1,0:T(8,128)(2,1)}, u32[]{:S(2)}) copy-start(bf16[1,512,2048]{2,1,0:T(8,128)(2,1)} %param.13) | copy-start | bytes 6291460
  660.5 95.8 %copy-start.35 = (f32[512]{0:T(512)S(1)}, f32[512]{0:T(512)}, u32[]{:S(2)}) copy-start(f32[512]{0:T(512)} %copy-done.34) | copy-start | bytes 6148
  (20 other events, 110.1 us)
Sparse Core Ops, SparseCore 0:
  88.7 72.4 all-gather.5
  162.7 57.2 all-gather.7
  222.2 72.6 all-gather.3
  334.3 70.2 reduce-scatter.3
  411.0 98.0 reduce-scatter.5
  512.6 87.6 reduce-scatter.7

commit v9 on v8

--- a/solution.py
+++ b/solution.py
@@ -1040,7 +1040,15 @@
     unit, gate_own, out_own, cot_own = lax.optimization_barrier((unit, gate_own, out_weight, cotangent))
     in_gate = lax.all_gather(gate_own, "seq", axis=0, tiled=True)
     out_full = lax.all_gather(out_own, "seq", axis=0, tiled=True)
-    cot_all = lax.all_gather(cot_own, "stream", axis=0, tiled=True)
+    if seqs == 4:
+        core = lax.ppermute(cot_own, "stream", [(i, i ^ 1) for i in range(4)])
+        far = lax.ppermute(cot_own, "stream", [(i, i ^ 2) for i in range(4)])
+        both = lax.ppermute(far, "stream", [(i, i ^ 1) for i in range(4)])
+        stacked = jnp.stack([cot_own, core, far, both])
+        me = lax.axis_index("stream")
+        cot_all = jnp.concatenate([lax.dynamic_index_in_dim(stacked, me ^ i, 0, False) for i in range(4)])
+    else:
+        cot_all = lax.all_gather(cot_own, "stream", axis=0, tiled=True)
     xproj_full = packed[:, :proj_dim]
     dtw_cols = packed[:, proj_dim : proj_dim + rank_dim]
     at = proj_dim + rank_dim

time: 784 us -> 806 us (1.028)
  Pallas kernels: 446 us -> 476 us
  waiting for transfers between devices: 12.6 us -> 0.29 us
    pallas_call x2, Pallas kernels: 25.2 us -> 57.2 us  [link_gather(): pl.pallas_call(kernel, in_specs=[pl.BlockSpec(memory_space=pl.ANY)] * cou...]
    all_gather x1, waiting for transfers between devices: 11.3 us -> 0.01 us  [local(): in_gate = lax.all_gather(gate_own, 'seq', axis=0, tiled=True)]
    dot_general x1, matrix products: 25.1 us -> 14.4 us  [local(): gate_in = jnp.dot(unit, in_gate, preferred_element_type=f32)]
    dot_general x3, matrix products: 45.8 us -> 55.2 us  [contract_cols(): lax.dot_general(left_mat, right_mat, NT, preferred_element_type=jnp.float32)]
  transfers between devices with their start and end apart: 9 -> 11, of which waited for: 2 -> 1; matrix products, arithmetic and copies ran while one was open for 27% -> 26% of each run, Pallas kernels for 38% -> 40%
where the time goes in v9:
time: 806 us; the launch traced here: 797 us
  Pallas kernels  476 us (59%)
  matrix products  174 us (22%)
  other arithmetic  65.5 us (8%)
  local copies, waits for them, and re-layouts  47.9 us (6%)
  starting transfers between devices  18.3 us (2%)
  between operations  15.3 us (2%)
    pallas_call x1, Pallas kernels, bwd_full(): pl.pallas_call(bwd_full_body, grid=(strips, seqs, blocks), in_specs=[pl.B...  95.1 us
    pallas_call x1, Pallas kernels, link_reduce(): pl.pallas_call(kernel, in_specs=[pl.BlockSpec(memory_space=pl.ANY)] * cou...  91.9 us
    pallas_call x1, Pallas kernels, link_open(): pl.pallas_call(kernel, in_specs=[pl.BlockSpec(memory_space=pl.ANY)] * (co...  63.5 us
    pallas_call x2, Pallas kernels, scan_end(): pl.pallas_call(body, grid=(seqs, chans // width), in_specs=[pl.BlockSpec(...  62.6 us
    pallas_call x2, Pallas kernels, link_gather(): pl.pallas_call(kernel, in_specs=[pl.BlockSpec(memory_space=pl.ANY)] * cou...  57.2 us
    dot_general x3, matrix products, contract_cols(): lax.dot_general(left_mat, right_mat, NT, preferred_element_type=jnp.float32)  55.2 us
    dot_general x3, matrix products, contract_rows(): lax.dot_general(left_mat, right_mat, (((0,), (0,)), ((), ())), preferred_...  44 us
    pallas_call x1, Pallas kernels, fwd_full(): pl.pallas_call(fwd_full_body, grid=(chans // width, seqs, blocks), in_spe...  41.9 us
  transfers between devices with their start and end apart: 11, of which 1 were waited for; matrix products, arithmetic and copies ran while one was open for 26% of the time, Pallas kernels for 40%

profile of v9, /device:TPU:19, one launch (start us, length us, event | category | flops | bytes accessed | tf_op | source)
XLA Modules:
  0.0 797.0 jit_solution(10879777723331377032)
XLA Ops:
  25.0 63.5 %link_open.1 = (bf16[2048,1024]{1,0:T(8,128)(2,1)}, bf16[256,1024]{1,0:T(8,128)(2,1)}, bf16[256,1024]{1,0:T(8,128)(2,1)}, s32[32,128]{1,0:T(8,128)}, bf16[2048,2...) custom-call(bf16[256,1024]{1,0:T(8,128)(2,1)} %get-tuple-element.287.conv_ref, bf16[256,1024]{1,0:T(8,128)(2,1)} %get-tuple-element.286.gate_ref, ...), custom_call_target="tpu_custom_call" | custom-call | flops 80000000000 | tf_op jit(solution)/shard_map/link_open/pallas_call | solution.py:832
  90.0 14.5 %fusion.68 = (bf16[2048,1024]{1,0:T(8,128)(2,1)S(1)}, f32[2048,1024]{1,0:T(8,128)}) fusion(bf16[2048,2048]{1,0:T(8,128)(2,1)} %get-tuple-element.57, bf16[2048,1024]{1,0:T(8,128)(2,1)} %get-tuple-element.58), kind=kOutput, calls=%fused_computation.225 | convolution fusion | flops 8592031744 | bytes 25165824 | tf_op jit(solution)/shard_map/dot_general | solution.py:1072
  114.0 12.3 %conv_fwd.1 = (bf16[2048,1024]{1,0:T(8,128)(2,1)}, bf16[2048,1024]{1,0:T(8,128)(2,1)}) custom-call(f32[2048,1024]{1,0:T(8,128)} %get-tuple-element.282.x_ref, f32[32,1024]{1,0:T(8,128)} %bitcast_convert_fusion.1.early_ref, f32[2048,8]{1,0:T(8,128)} %bitcast.280, f32[8,1024]{1,0:T(8,128)} %fusion.48.taps_ref), custom_call_target="tpu_custom_call" | custom-call | flops 8388608000 | bytes 16777216 | tf_op jit(solution)/shard_map/conv_fwd/pallas_call | solution.py:912
  126.2 4.6 convolution_convert_fusion.4.own_ref
  130.8 16.3 %link_sum.2 = f32[160,2048]{1,0:T(8,128)} custom-call(bf16[160,2048]{1,0:T(8,128)(2,1)} %convolution_convert_fusion.4.own_ref), custom_call_target="tpu_custom_call" | custom-call | flops 20000000000 | tf_op jit(solution)/shard_map/link_sum/pallas_call | solution.py:750
  154.5 8.1 %bitcast_reduce_fusion = (f32[4,1024]{1,0:T(4,128)S(1)}, f32[2048,1024]{1,0:T(8,128)}, f32[2048,1024]{1,0:T(8,128)S(1)}) fusion(f32[1024]{0:T(1024)S(1)} %get-tuple-element.217, pred[2048]{0:T(1024)(128)(4,1)S(1)} %bitcast.297, bf16[1024,384]{1,0:T(8,128)(2,1)S(1)} %copy-done.8, f32[160,2048]{1,0:T(8,128)S(1)} %copy-done.15), kind=kOutput, calls=%fused_computation.12 | convolution fusion | flops 555741184 | bytes 17586176 | tf_op jit(solution)/shard_map/dot_general | solution.py:1084
  162.7 7.3 convert_multiply_fusion.3.dtx_ref
  170.0 31.2 %fwd_end.1 = f32[64,1024]{1,0:T(8,128)} custom-call(f32[2048,1024]{1,0:T(8,128)} %get-tuple-element.226.dte_ref, f32[2048,1024]{1,0:T(8,128)} %convert_multiply_fusion.3.dtx_ref, f32[2048,16]{1,0:T(8,128)} %bitcast.284, f32[16,1024]{1,0:T(8,128)} %multiply_bitcast_fusion.rate_ref), custom_call_target="tpu_custom_call" | custom-call | flops 33554432000 | bytes 16777216 | tf_op jit(solution)/shard_map/fwd_end/pallas_call | solution.py:82
  202.9 39.2 %link_gather.2 = bf16[640,1024]{1,0:T(8,128)(2,1)} custom-call(bf16[80,1024]{1,0:T(8,128)(2,1)} %pad.47.refs_0_), custom_call_target="tpu_custom_call" | custom-call | flops 20000000000 | tf_op jit(solution)/shard_map/link_gather/pallas_call | solution.py:476
  245.9 41.9 %fwd_full.1 = (f32[2048,1024]{1,0:T(8,128)}, bf16[32896,1024]{1,0:T(8,128)(2,1)}) custom-call(f32[2048,1024]{1,0:T(8,128)} %get-tuple-element.226.dte_ref, f32[2048,1024]{1,0:T(8,128)} %convert_multiply_fusion.3.dtx_ref, f32[2048,16]{1,0:T(8,128)} %bitcast.285, bf16[2048,256]{1,0:T(8,128)(2,1)} %copy.352.read_ref, f32[16,1024]{1,0:T(8,128)} %multiply_bitcast_fusion.rate_ref, ...), custom_call_target="tpu_custom_call" | custom-call | flops 46976204800 | bytes 67108864 | tf_op jit(solution)/shard_map/fwd_full/pallas_call | solution.py:147
  287.8 3.8 pad_maximum_fusion
  294.5 14.4 %fusion.69 = f32[2048,1024]{1,0:T(8,128)} fusion(bf16[2048,2048]{1,0:T(8,128)(2,1)} %get-tuple-element.57, bf16[2048,1024]{1,0:T(8,128)(2,1)} %all-gather.3.cloned.1.call-done), kind=kOutput, calls=%fused_computation.226 | convolution fusion | flops 8589934592 | bytes 20971520 | tf_op jit(solution)/shard_map/dot_general | solution.py:1073
  309.0 23.9 %multiply_convert_fusion = (bf16[2048,1024]{1,0:T(8,128)(2,1)}, bf16[2048,1024]{1,0:T(8,128)(2,1)}, f32[2048,1024]{1,0:T(8,128)}) fusion(f32[2048,1024]{1,0:T(8,128)} %fusion.69, f32[2048,1024]{1,0:T(8,128)} %get-tuple-element.61, bf16[2048,1024]{1,0:T(8,128)(2,1)} %get-tuple-element.60, f32[2048]{0:T(1024)S(1)} %bitcast.296, f32[1024]{0:T(1024)S(1)} %copy-done.35, ...), kind=kOutput, calls=%fused_computation.14 | convolution fusion | flops 8663334912 | bytes 50343936 | tf_op jit(solution)/shard_map/dot_general | solution.py:978
  332.9 14.1 %convolution_convert_fusion = bf16[2048,2048]{1,0:T(8,128)(2,1)} fusion(bf16[2048,1024]{1,0:T(8,128)(2,1)} %get-tuple-element.66, bf16[1024,2048]{1,0:T(8,128)(2,1)} %all-gather.5.cloned.1.call-done), kind=kOutput, calls=%fused_computation.19 | convolution fusion | flops 8594128896 | bytes 16777216 | tf_op jit(solution)/shard_map/dot_general | solution.py:1098
  349.9 13.8 %convolution_convert_fusion.1 = bf16[1024,2048]{1,0:T(8,128)(2,1)} fusion(bf16[2048,1024]{1,0:T(8,128)(2,1)} %get-tuple-element.66, bf16[512,2048]{1,0:T(8,128)(2,1)} %get-tuple-element.231, bf16[512,2048]{1,0:T(8,128)(2,1)} %get-tuple-element.232, bf16[512,2048]{1,0:T(8,128)(2,1)} %get-tuple-element.233, bf16[512,2048]{1,0:T(8,128)(2,1)S(1)} %get-tuple-element.230), kind=kOutput, calls=%fused_computation.34 | convolution fusion | flops 8625586176 | bytes 16777216 | tf_op jit(solution)/shard_map/dot_general | solution.py:974
  363.7 16.0 %convolution_convert_fusion.3 = bf16[2048,1024]{1,0:T(8,128)(2,1)} fusion(bf16[2048,2048]{1,0:T(8,128)(2,1)} %get-tuple-element.57, bf16[2048,1024]{1,0:T(8,128)(2,1)} %get-tuple-element.67), kind=kOutput, calls=%fused_computation.36 | convolution fusion | flops 8592031744 | bytes 16777216 | tf_op jit(solution)/shard_map/dot_general | solution.py:974
  379.7 31.3 %bwd_end.1 = f32[64,1024]{1,0:T(8,128)} custom-call(f32[2048,1024]{1,0:T(8,128)} %get-tuple-element.226.dte_ref, f32[2048,1024]{1,0:T(8,128)} %get-tuple-element.68.grad_ref, f32[2048,16]{1,0:T(8,128)} %bitcast.282, f32[16,1024]{1,0:T(8,128)} %multiply_bitcast_fusion.rate_ref), custom_call_target="tpu_custom_call" | custom-call | flops 33554432000 | bytes 16777216 | tf_op jit(solution)/shard_map/bwd_end/pallas_call | solution.py:82
  412.7 18.0 %link_gather.3 = bf16[640,1024]{1,0:T(8,128)(2,1)} custom-call(bf16[80,1024]{1,0:T(8,128)(2,1)} %pad.48.refs_0_), custom_call_target="tpu_custom_call" | custom-call | flops 20000000000 | tf_op jit(solution)/shard_map/link_gather/pallas_call | solution.py:476
  436.0 95.1 %bwd_full.1 = (f32[2048,1024]{1,0:T(8,128)}, f32[2048,1024]{1,0:T(8,128)}, f32[16,1024]{1,0:T(8,128)}, f32[256,256]{1,0:T(8,128)}, f32[256,256]{1,0:T(8,128)}) custom-call(f32[2048,1024]{1,0:T(8,128)} %get-tuple-element.226.dte_ref, f32[2048,1024]{1,0:T(8,128)} %convert_multiply_fusion.3.dtx_ref, f32[2048,1024]{1,0:T(8,128)} %get-tuple-element.68.grad_ref, ...), custom_call_target="tpu_custom_call" | custom-call | flops 107374182400 | bytes 67108864 | tf_op jit(solution)/shard_map/bwd_full/pallas_call | solution.py:249
  531.1 17.5 %fusion.63 = (bf16[1024]{0:T(1024)(128)(2,1)S(1)}, bf16[2048,1024]{1,0:T(8,128)(2,1)}, bf16[1024]{0:T(1024)(128)(2,1)S(1)}) fusion(f32[2048,1024]{1,0:T(8,128)} %get-tuple-element.74, bf16[2048,1024]{1,0:T(8,128)(2,1)S(1)} %copy-done.2, f32[2048,1024]{1,0:T(8,128)} %get-tuple-element.75, f32[2048,1024]{1,0:T(8,128)} %copy-done, f32[1024]{0:T(1024)S(1)} %copy-done.32, ...), kind=kLoop, calls=%fused_computation.221 | loop fusion | flops 48232448 | bytes 41951232 | tf_op jit(solution)/shard_map/reduce_sum | solution.py:1120
  551.8 3.9 convolution_convert_fusion.5
  556.6 16.6 %link_sum.3 = f32[160,2048]{1,0:T(8,128)} custom-call(bf16[160,2048]{1,0:T(8,128)(2,1)} %pad_maximum_fusion.5.own_ref), custom_call_target="tpu_custom_call" | custom-call | flops 20000000000 | tf_op jit(solution)/shard_map/link_sum/pallas_call | solution.py:750
  579.0 12.0 %add_add_fusion.grad_ref = f32[2048,1024]{1,0:T(8,128)S(1)} fusion(f32[2048,1024]{1,0:T(8,128)} %get-tuple-element.68.grad_ref, f32[2048,1024]{1,0:T(8,128)} %get-tuple-element.74, bf16[160,2048]{1,0:T(8,128)(2,1)S(1)} %convert_element_type.268, f32[1024]{0:T(1024)S(1)} %copy-done.36, bf16[1024,384]{1,0:T(8,128)(2,1)S(1)} %copy-done.9, ...), kind=kOutput, calls=%fused_computation.13 | convolution fusion | flops 694157312 | bytes 34742272 | tf_op jit(solution)/shard_map/dot_general | solution.py:1127
  595.2 7.6 collective-permute-start.4
  604.7 18.7 %conv_bwd.1 = (bf16[2048,1024]{1,0:T(8,128)(2,1)}, f32[32,1024]{1,0:T(8,128)}) custom-call(f32[2048,1024]{1,0:T(8,128)} %copy-done.10, bf16[2048,1024]{1,0:T(8,128)(2,1)} %get-tuple-element.80.slope_ref, f32[32,1024]{1,0:T(8,128)} %bitcast_convert_fusion.late_ref, f32[2048,1024]{1,0:T(8,128)} %get-tuple-element.282.x_ref, f32[2048,8]{1,0:T(8,128)} %bitcast.281, ...), custom_call_target="tpu_custom_call" | custom-call | flops 10485760000 | bytes 25165824 | tf_op jit(solution)/shard_map/conv_bwd/pallas_call | solution.py:934
  623.4 6.4 all-to-all-start
  629.8 15.3 %fusion.70 = f32[2048,2048]{1,0:T(8,128)} fusion(bf16[2048,1024]{1,0:T(8,128)(2,1)} %get-tuple-element.83, bf16[2048,1024]{1,0:T(8,128)(2,1)} %get-tuple-element.58), kind=kOutput, calls=%fused_computation.227 | convolution fusion | flops 8589934592 | bytes 25165824 | tf_op jit(solution)/shard_map/dot_general | solution.py:978
  645.2 15.9 %add_convert_fusion.refs_2_ = bf16[2048,2048]{1,0:T(8,128)(2,1)} fusion(f32[2048,2048]{1,0:T(8,128)} %fusion.70, bf16[2048,1024]{1,0:T(8,128)(2,1)} %get-tuple-element.67, bf16[2048,1024]{1,0:T(8,128)(2,1)S(1)} %copy-done.41), kind=kOutput, calls=%fused_computation.1 | convolution fusion | flops 8598323200 | bytes 33554432 | tf_op jit(solution)/shard_map/dot_general | solution.py:978
  661.1 14.2 %convolution_convert_fusion.2.refs_0_ = bf16[2048,1024]{1,0:T(8,128)(2,1)} fusion(bf16[2048,2048]{1,0:T(8,128)(2,1)} %get-tuple-element.57, bf16[2048,1024]{1,0:T(8,128)(2,1)} %get-tuple-element.83), kind=kOutput, calls=%fused_computation.35 | convolution fusion | flops 8592031744 | bytes 16777216 | tf_op jit(solution)/shard_map/dot_general | solution.py:974
  675.7 3.5 concatenate.38
  681.5 91.9 %link_reduce.1 = (bf16[64,4096]{1,0:T(8,128)(2,1)}, bf16[128,384]{1,0:T(8,128)(2,1)}, bf16[512,2048]{1,0:T(8,128)(2,1)}) custom-call(bf16[2048,1024]{1,0:T(8,128)(2,1)} %convolution_convert_fusion.2.refs_0_, bf16[1024,384]{1,0:T(8,128)(2,1)} %pad.50.refs_1_, bf16[2048,2048]{1,0:T(8,128)(2,1)} %add_convert_fusion.refs_2_), custom_call_target="tpu_custom_call" | custom-call | flops 80000000000 | tf_op jit(solution)/shard_map/link_reduce/pallas_call | solution.py:695
  779.5 4.3 fusion.16
  (250 shorter events, 84.3 us)
Async XLA Ops:
  7.2 287.3 %all-gather.3.cloned.1.call-start = ((), (), s32[]{:S(2)}) async-start(), calls=%async_computation.4 | async-start | bytes 4718592 | tf_op jit(solution)/shard_map/all_gather | solution.py:1041
  88.5 220.4 %all-gather.5.cloned.1.call-start = ((), (), s32[]{:S(2)}) async-start(), calls=%async_computation.5 | async-start | bytes 4718592 | tf_op jit(solution)/shard_map/all_gather | solution.py:1042
  88.6 156.6 %collective-permute-start.2 = (bf16[512,2048]{1,0:T(8,128)(2,1)}, bf16[512,2048]{1,0:T(8,128)(2,1)}, u32[]{:S(2)}, u32[]{:S(2)}) collective-permute-start(bf16[512,2048]{1,0:T(8,128)(2,1)} %bitcast.8), channel_id=1, source_target_pairs={{0,2},{1,3},{2,0},{3,1},{4,6},{5,7},{6,4},{7,5},{8,10},{9,11},{10,... | collective-permute-start | bytes 6291464 | tf_op jit(solution)/shard_map/ppermute | solution.py:1045
  89.9 197.8 %collective-permute-start.1 = (bf16[512,2048]{1,0:T(8,128)(2,1)}, bf16[512,2048]{1,0:T(8,128)(2,1)}, u32[]{:S(2)}, u32[]{:S(2)}) collective-permute-start(bf16[512,2048]{1,0:T(8,128)(2,1)} %bitcast.8), channel_id=1, source_target_pairs={{0,1},{1,0},{2,3},{3,2},{4,5},{5,4},{6,7},{7,6},{8,9},{9,8},{10,11... | collective-permute-start | bytes 6291464 | tf_op jit(solution)/shard_map/ppermute | solution.py:1044
  90.0 17.9 %copy-start.8 = (bf16[1024,384]{1,0:T(8,128)(2,1)S(1)}, bf16[1024,384]{1,0:T(8,128)(2,1)}, u32[]{:S(2)}) copy-start(bf16[1024,384]{1,0:T(8,128)(2,1)} %get-tuple-element.54) | copy-start | bytes 2359300
  104.5 8.8 %collective-permute-start = (bf16[4,3,1024]{2,1,0:T(4,128)(2,1)S(1)}, bf16[4,3,1024]{2,1,0:T(4,128)(2,1)S(1)}, u32[]{:S(2)}, u32[]{:S(2)}) collective-permute-start(bf16[4,3,1024]{2,1,0:T(4,128)(2,1)S(1)} %slice.399), channel_id=1, source_target_pairs={{0,4},{4,8},{8,12},{12,16},{16,20},{20,24},{24,28},{1,5},{5,9},{9,... | collective-permute-start | bytes 73736 | tf_op jit(solution)/shard_map/ppermute | solution.py:954
  106.6 327.1 %reduce-scatter.4.cloned.1.call-start = ((), (), s32[]{:S(2)}) async-start(), calls=%async_computation.6 | async-start | bytes 10485760 | tf_op jit(solution)/shard_map/reduce_scatter | solution.py:1104
  109.0 53.7 %copy-start.31 = (f32[1024]{0:T(1024)}, f32[1024]{0:T(1024)S(1)}, u32[]{:S(2)}) copy-start(f32[1024]{0:T(1024)S(1)} %get-tuple-element.217) | copy-start | bytes 12292
  162.7 39.5 %copy-start.26 = (bf16[4,1024]{1,0:T(4,128)(2,1)}, bf16[4,1024]{1,0:T(4,128)(2,1)S(1)}, u32[]{:S(2)}) copy-start(bf16[4,1024]{1,0:T(4,128)(2,1)S(1)} %get-tuple-element.223) | copy-start | bytes 24580
  162.7 39.5 %copy-start.28 = (bf16[4,1024]{1,0:T(4,128)(2,1)}, bf16[4,1024]{1,0:T(4,128)(2,1)S(1)}, u32[]{:S(2)}) copy-start(bf16[4,1024]{1,0:T(4,128)(2,1)S(1)} %get-tuple-element.224) | copy-start | bytes 24580
  202.9 40.9 %copy-start.18 = (f32[16,1024]{1,0:T(8,128)S(1)}, f32[16,1024]{1,0:T(8,128)}, u32[]{:S(2)}) copy-start(f32[16,1024]{1,0:T(8,128)} %multiply_bitcast_fusion.rate_ref) | copy-start | bytes 196612
  245.2 42.6 %collective-permute-start.3 = (bf16[512,2048]{1,0:T(8,128)(2,1)}, bf16[512,2048]{1,0:T(8,128)(2,1)S(1)}, u32[]{:S(2)}, u32[]{:S(2)}) collective-permute-start(bf16[512,2048]{1,0:T(8,128)(2,1)} %collective-permute-done.2), channel_id=1, source_target_pairs={{0,1},{1,0},{2,3},{3,2},{4,5},{5,4},{6,7},{7,6},{8,9},{9,8},{10,11... | collective-permute-start | bytes 6291464 | tf_op jit(solution)/shard_map/ppermute | solution.py:1046
  294.5 14.4 %copy-start.37 = (f32[1,4,4,128]{3,1,2,0:T(4,128)S(1)}, f32[1,4,4,128]{3,1,2,0:T(4,128)}, u32[]{:S(2)}) copy-start(f32[1,4,4,128]{3,1,2,0:T(4,128)} %copy.376) | copy-start | bytes 24580
  347.0 232.0 %reduce-scatter.6.cloned.1.call-start = ((), (), s32[]{:S(2)}) async-start(), calls=%async_computation.7 | async-start | bytes 4718592 | tf_op jit(solution)/shard_map/reduce_scatter | solution.py:1113
  379.7 32.3 %copy-start.27 = (bf16[4,1024]{1,0:T(4,128)(2,1)S(1)}, bf16[4,1024]{1,0:T(4,128)(2,1)}, u32[]{:S(2)}) copy-start(bf16[4,1024]{1,0:T(4,128)(2,1)} %copy-done.26) | copy-start | bytes 24580
  379.7 32.3 %copy-start.29 = (bf16[4,1024]{1,0:T(4,128)(2,1)S(1)}, bf16[4,1024]{1,0:T(4,128)(2,1)}, u32[]{:S(2)}) copy-start(bf16[4,1024]{1,0:T(4,128)(2,1)} %copy-done.28) | copy-start | bytes 24580
  412.7 19.7 %copy-start.19 = (f32[16,1024]{1,0:T(8,128)S(1)}, f32[16,1024]{1,0:T(8,128)}, u32[]{:S(2)}) copy-start(f32[16,1024]{1,0:T(8,128)} %multiply_bitcast_fusion.rate_ref) | copy-start | bytes 196612
  433.8 189.6 %reduce-scatter.8.cloned.1.call-start = ((), (), s32[]{:S(2)}) async-start(), calls=%async_computation.8 | async-start | bytes 4718592 | tf_op jit(solution)/shard_map/reduce_scatter | solution.py:1114
  436.0 95.1 %copy-start.2 = (bf16[2048,1024]{1,0:T(8,128)(2,1)S(1)}, bf16[2048,1024]{1,0:T(8,128)(2,1)}, u32[]{:S(2)}) copy-start(bf16[2048,1024]{1,0:T(8,128)(2,1)} %get-tuple-element.60) | copy-start | bytes 12582916
  436.0 95.1 %copy-start.32 = (f32[1024]{0:T(1024)S(1)}, f32[1024]{0:T(1024)}, u32[]{:S(2)}) copy-start(f32[1024]{0:T(1024)} %copy-done.31) | copy-start | bytes 12292
  531.1 17.6 %copy-start.24 = (f32[256,256]{1,0:T(8,128)S(1)}, f32[256,256]{1,0:T(8,128)}, u32[]{:S(2)}) copy-start(f32[256,256]{1,0:T(8,128)} %get-tuple-element.76) | copy-start | bytes 786436
  531.1 17.6 %copy-start.23 = (f32[256,256]{1,0:T(8,128)S(1)}, f32[256,256]{1,0:T(8,128)}, u32[]{:S(2)}) copy-start(f32[256,256]{1,0:T(8,128)} %get-tuple-element.77) | copy-start | bytes 786436
  531.1 17.8 %copy-start.30 = (f32[16,1024]{1,0:T(8,128)S(1)}, f32[16,1024]{1,0:T(8,128)}, u32[]{:S(2)}) copy-start(f32[16,1024]{1,0:T(8,128)} %get-tuple-element.88) | copy-start | bytes 196612
  556.6 18.2 %copy-start.7 = (bf16[2048,1024]{1,0:T(8,128)(2,1)S(1)}, bf16[2048,1024]{1,0:T(8,128)(2,1)}, u32[]{:S(2)}) copy-start(bf16[2048,1024]{1,0:T(8,128)(2,1)} %get-tuple-element.222) | copy-start | bytes 12582916
  556.6 18.2 %copy-start.16 = (f32[160,2048]{1,0:T(8,128)S(1)}, f32[160,2048]{1,0:T(8,128)}, u32[]{:S(2)}) copy-start(f32[160,2048]{1,0:T(8,128)} %link_sum.2) | copy-start | bytes 3932164
  579.0 23.7 %copy-start.3 = (bf16[2048,1024]{1,0:T(8,128)(2,1)S(1)}, bf16[2048,1024]{1,0:T(8,128)(2,1)}, u32[]{:S(2)}) copy-start(bf16[2048,1024]{1,0:T(8,128)(2,1)} %get-tuple-element.60) | copy-start | bytes 12582916
  595.2 8.9 %collective-permute-start.4 = (bf16[4,3,1024]{2,1,0:T(4,128)(2,1)S(1)}, bf16[4,3,1024]{2,1,0:T(4,128)(2,1)S(1)}, u32[]{:S(2)}, u32[]{:S(2)}) collective-permute-start(bf16[4,3,1024]{2,1,0:T(4,128)(2,1)S(1)} %fusion.44), channel_id=1, source_target_pairs={{4,0},{8,4},{12,8},{16,12},{20,16},{24,20},{28,24},{5,1},{9,5},{13... | collective-permute-start | bytes 73736 | tf_op jit(solution)/shard_map/ppermute | solution.py:954
  623.4 56.8 %all-to-all-start = ((bf16[4,64,1024]{2,1,0:T(8,128)(2,1)}), bf16[4,64,1024]{2,1,0:T(8,128)(2,1)S(1)}, u32[]{:S(2)}, u32[]{:S(2)}) async-start(bf16[4,64,1024]{2,1,0:T(8,128)(2,1)} %bitcast.289), calls=%async_computation.3 | async-start | bytes 1048576 | tf_op jit(solution)/shard_map/all_to_all | solution.py:1139
  629.8 15.3 %copy-start.41 = (bf16[2048,1024]{1,0:T(8,128)(2,1)S(1)}, bf16[2048,1024]{1,0:T(8,128)(2,1)}, u32[]{:S(2)}) copy-start(bf16[2048,1024]{1,0:T(8,128)(2,1)} %all-gather.3.cloned.1.call-done) | copy-start | bytes 12582916
  661.1 14.6 %copy-start.17 = (bf16[1024,128]{1,0:T(8,128)(2,1)S(1)}, bf16[1024,128]{1,0:T(8,128)(2,1)}, u32[]{:S(2)}) copy-start(bf16[1024,128]{1,0:T(8,128)(2,1)} %fusion.21) | copy-start | bytes 786436
  681.5 95.6 %copy-start.6 = (bf16[1,512,2048]{2,1,0:T(8,128)(2,1)S(1)}, bf16[1,512,2048]{2,1,0:T(8,128)(2,1)}, u32[]{:S(2)}) copy-start(bf16[1,512,2048]{2,1,0:T(8,128)(2,1)} %param.13) | copy-start | bytes 6291460
  681.5 95.6 %copy-start.34 = (f32[512]{0:T(512)S(1)}, f32[512]{0:T(512)}, u32[]{:S(2)}) copy-start(f32[512]{0:T(512)} %copy-done.33) | copy-start | bytes 6148
  (21 other events, 139.6 us)
Sparse Core Ops, SparseCore 0:
  88.7 72.5 all-gather.2
  163.3 80.3 all-gather.4
  347.2 77.8 reduce-scatter.3
  433.9 96.0 reduce-scatter.5
  533.5 87.8 reduce-scatter.7
